TPU v7x, 32 devices: a whole 2x2x4 slice. The times are simulated.
32 devices in a mesh: dp: 8 (over z, x), heads: 4 (over y, core).
Axes of the slice: x: 2, y: 2, z: 4, core: 2. Of those that a mesh axis runs over, the one named last changes fastest.
Arguments:
- tokens: bfloat16 [2, 8, 1024, 1024], P(None, 'dp', 'heads'), may hold values from -6 to 6
- counts: int32 [2, 8], P(None, 'dp'), may hold values from 64 to 512, as said below
- token_weights: bfloat16 [1024, 3, 1024], P('dp', None, 'heads'), may hold values from -0.1875 to 0.1875
- token_output: bfloat16 [1024, 1024], P('dp', 'heads'), may hold values from -3 to 3
- state_weights: bfloat16 [1024, 3, 1024], P('dp', None, 'heads'), may hold values from -0.1875 to 0.1875
- state_output: bfloat16 [1024, 1024], P('dp', 'heads'), may hold values from -3 to 3
- hidden_up: bfloat16 [1024, 4096], P('dp', 'heads'), may hold values from -0.1875 to 0.1875
- hidden_down: bfloat16 [1024, 4096], P('dp', 'heads'), may hold values from -0.09375 to 0.09375
- norm_gains: bfloat16 [3, 1024], P(None, 'dp'), may hold values from 0.5 to 1.5
- gate_bias: bfloat16 [1024], P('dp'), may hold values from -2 to 2
- init_state: bfloat16 [512, 1024], P(None, 'dp'), may hold values from -6 to 6
- cotangent: bfloat16 [2, 8, 1024, 1024], P(None, 'dp', 'heads'), may hold values from -6 to 6
- state_cotangent: bfloat16 [2, 8, 512, 1024], P(None, 'dp'), may hold values from -6 to 6
Outputs:
- output: bfloat16 [2, 8, 1024, 1024], P(None, 'dp', 'heads')
- final_state: bfloat16 [2, 8, 512, 1024], P(None, 'dp')
- input_grad: float32 [2, 8, 1024, 1024], P(None, 'dp', 'heads')
- grad_token_weights: float32 [1024, 3, 1024], P('dp', None, 'heads')
- grad_token_output: float32 [1024, 1024], P('dp', 'heads')
- grad_state_weights: float32 [1024, 3, 1024], P('dp', None, 'heads')
- grad_state_output: float32 [1024, 1024], P('dp', 'heads')
- grad_hidden_up: float32 [1024, 4096], P('dp', 'heads')
- grad_hidden_down: float32 [1024, 4096], P('dp', 'heads')
- grad_norm_gains: float32 [3, 1024], P(None, 'dp')
- grad_gate_bias: float32 [1024], P('dp')
- grad_init_state: float32 [512, 1024], P(None, 'dp')
Inputs may be any that keep to these rules, and one draw needn't show every extreme that they name: `counts`: for every sequence index of a micro-batch, one of its 2 micro-batches has all 512 tokens of the final block valid.
All inputs are finite; a program needn't handle non-finite values.
Results may differ from a plain program's by a relative error of at most 0.019.
Values may be sent and summed in bfloat16 or wider, within the bound.
No kernel may reach another device: no remote copies, remote signals or barrier semaphores. Data moves between devices by JAX's collectives and lax.ppermute only.
A program may use at most 320 MiB of HBM per device.

v0:
```python
import jax
import jax.numpy as jnp
from jax import lax
from jax.sharding import PartitionSpec as P

HEAD_DIM = 128
BLOCK = 512


EPSILON = 1e-06
MASKED = -1e30


def rms_forward(values, gain):
    inverse = lax.rsqrt(jnp.mean(values * values, axis=-1, keepdims=True) + EPSILON)
    return values * inverse * gain


def rms_backward(values, gain, grad_out):
    unused, pullback = jax.vjp(rms_forward, values, gain)
    return pullback(grad_out)


def gelu_tanh(values):
    return jax.nn.gelu(values, approximate=True)


def split_heads(flat):
    return flat.reshape(flat.shape[0], flat.shape[1] // HEAD_DIM, HEAD_DIM).transpose(1, 0, 2)


def merge_heads(split):
    return split.transpose(1, 0, 2).reshape(split.shape[1], split.shape[0] * HEAD_DIM)


def attend_forward(queries, key_rows, value_rows, allowed):
    scale = HEAD_DIM ** (-0.5)
    scores = (
        jnp.einsum("hqe,hke->hqk", queries, key_rows, preferred_element_type=jnp.float32) * scale
    )
    scores = jnp.where(allowed[None], scores, MASKED)
    row_top = jnp.max(scores, axis=-1, keepdims=True)
    weights = jnp.exp(scores - row_top)
    row_total = jnp.sum(weights, axis=-1, keepdims=True)
    probs = (weights / row_total).astype(jnp.bfloat16)
    mixed = jnp.einsum("hqk,hke->hqe", probs, value_rows, preferred_element_type=jnp.float32)
    return (mixed, row_top + jnp.log(row_total))


def attend_backward(queries, key_rows, value_rows, allowed, log_total, grad_mixed):
    scale = HEAD_DIM ** (-0.5)
    scores = (
        jnp.einsum("hqe,hke->hqk", queries, key_rows, preferred_element_type=jnp.float32) * scale
    )
    scores = jnp.where(allowed[None], scores, MASKED)
    probs = jnp.exp(scores - log_total)
    grad_probs = jnp.einsum(
        "hqe,hke->hqk", grad_mixed, value_rows, preferred_element_type=jnp.float32
    )
    grad_scores = probs * (grad_probs - jnp.sum(grad_probs * probs, axis=-1, keepdims=True))
    low_scores = grad_scores.astype(jnp.bfloat16)
    grad_queries = (
        jnp.einsum("hqk,hke->hqe", low_scores, key_rows, preferred_element_type=jnp.float32) * scale
    )
    grad_keys = (
        jnp.einsum("hqk,hqe->hke", low_scores, queries, preferred_element_type=jnp.float32) * scale
    )
    grad_values = jnp.einsum(
        "hqk,hqe->hke", probs.astype(jnp.bfloat16), grad_mixed, preferred_element_type=jnp.float32
    )
    return (grad_queries, grad_keys, grad_values)


def block_masks(valid_mask, block_index, state_row_block):
    begin_row = block_index * BLOCK
    first_key = max(block_index - 1, 0) * BLOCK
    final_row = begin_row + BLOCK
    query_pos = jnp.arange(begin_row, final_row)
    key_pos = jnp.arange(first_key, final_row)
    nearby = (
        (key_pos[None, :] <= query_pos[:, None])
        & (key_pos[None, :] > query_pos[:, None] - BLOCK)
        & valid_mask[None, first_key:final_row]
    )
    allowed = jnp.concatenate([nearby, jnp.ones((BLOCK, state_row_block), jnp.bool_)], axis=1)
    state_allowed = jnp.concatenate(
        [
            jnp.ones((state_row_block, state_row_block), jnp.bool_),
            jnp.broadcast_to(valid_mask[None, begin_row:final_row], (state_row_block, BLOCK)),
        ],
        axis=1,
    )
    return (allowed, state_allowed)


def fetch_weights(shards):
    (
        token_weights,
        token_output,
        state_weights,
        state_output,
        hidden_up,
        hidden_down,
        norm_gains,
        gate_bias,
        init_state,
    ) = shards
    return (
        lax.all_gather(token_weights, "dp", axis=0, tiled=True),
        lax.all_gather(token_output, "dp", axis=0, tiled=True),
        lax.all_gather(state_weights, "dp", axis=0, tiled=True),
        lax.all_gather(state_output, "dp", axis=0, tiled=True),
        lax.all_gather(hidden_up, "dp", axis=0, tiled=True),
        lax.all_gather(hidden_down, "dp", axis=0, tiled=True),
        lax.all_gather(norm_gains, "dp", axis=1, tiled=True),
        lax.all_gather(gate_bias, "dp", axis=0, tiled=True),
        lax.all_gather(init_state, "dp", axis=1, tiled=True),
    )


def reduce_grads(grads):
    (
        grad_token_weights,
        grad_token_output,
        grad_state_weights,
        grad_state_output,
        grad_hidden_up,
        grad_hidden_down,
        gain_token,
        gain_state,
        gain_hidden,
        grad_gate,
        grad_init,
    ) = grads
    summed = lax.psum(jnp.stack([gain_token, gain_hidden]), "heads")
    grad_gains = jnp.stack([summed[0], gain_state, summed[1]])
    return (
        lax.psum_scatter(grad_token_weights, "dp", scatter_dimension=0, tiled=True),
        lax.psum_scatter(grad_token_output, "dp", scatter_dimension=0, tiled=True),
        lax.psum_scatter(grad_state_weights, "dp", scatter_dimension=0, tiled=True),
        lax.psum_scatter(grad_state_output, "dp", scatter_dimension=0, tiled=True),
        lax.psum_scatter(grad_hidden_up, "dp", scatter_dimension=0, tiled=True),
        lax.psum_scatter(grad_hidden_down, "dp", scatter_dimension=0, tiled=True),
        lax.psum_scatter(grad_gains, "dp", scatter_dimension=1, tiled=True),
        lax.psum_scatter(grad_gate, "dp", scatter_dimension=0, tiled=True),
        lax.psum_scatter(grad_init, "dp", scatter_dimension=1, tiled=True),
    )


def run_sequence(weights, token_rows, valid_count, grad_out, grad_final):
    (
        w_token,
        w_token_out,
        w_state,
        w_state_out,
        w_hidden_up,
        w_hidden_down,
        gain_rows,
        gate_bias,
        init_rows,
    ) = weights
    gain_values = gain_rows.astype(jnp.float32)
    gate_open = jax.nn.sigmoid(gate_bias.astype(jnp.float32))
    local_rows = token_rows.shape[0]
    seq_length = local_rows * lax.axis_size("heads")
    block_total = seq_length // BLOCK
    state_row_block = init_rows.shape[0]
    head_local = w_token.shape[2] // HEAD_DIM
    token_values = token_rows.astype(jnp.float32)
    normed = rms_forward(token_values, gain_values[0]).astype(jnp.bfloat16)
    normed_all = lax.all_gather(normed, "heads", axis=0, tiled=True)
    projected = jnp.einsum(
        "nd,dcf->cnf", normed_all, w_token, preferred_element_type=jnp.float32
    ).astype(jnp.bfloat16)
    queries = split_heads(projected[0])
    key_rows = split_heads(projected[1])
    value_rows = split_heads(projected[2])
    valid_mask = jnp.arange(seq_length) < (block_total - 1) * BLOCK + valid_count
    state_now = init_rows.astype(jnp.float32)
    kept_blocks = []
    mixed_parts = []
    for block_index in range(block_total):
        begin_row = block_index * BLOCK
        first_key = max(block_index - 1, 0) * BLOCK
        final_row = begin_row + BLOCK
        state_norm = rms_forward(state_now, gain_values[1]).astype(jnp.bfloat16)
        state_proj = jnp.einsum(
            "nd,dcf->cnf", state_norm, w_state, preferred_element_type=jnp.float32
        ).astype(jnp.bfloat16)
        state_queries = split_heads(state_proj[0])
        state_keys = split_heads(state_proj[1])
        state_values = split_heads(state_proj[2])
        allowed, state_allowed = block_masks(valid_mask, block_index, state_row_block)
        mixed, log_total = attend_forward(
            queries[:, begin_row:final_row],
            jnp.concatenate([key_rows[:, first_key:final_row], state_keys], axis=1),
            jnp.concatenate([value_rows[:, first_key:final_row], state_values], axis=1),
            allowed,
        )
        mixed_parts.append(mixed)
        state_mixed, state_log_total = attend_forward(
            state_queries,
            jnp.concatenate([state_keys, key_rows[:, begin_row:final_row]], axis=1),
            jnp.concatenate([state_values, value_rows[:, begin_row:final_row]], axis=1),
            state_allowed,
        )
        state_flat = merge_heads(state_mixed).astype(jnp.bfloat16)
        partial_update = jnp.einsum(
            "nf,df->nd", state_flat, w_state_out, preferred_element_type=jnp.float32
        )
        update = lax.psum(partial_update, "heads")
        kept_blocks.append(
            (
                state_now,
                state_norm,
                state_queries,
                state_keys,
                state_values,
                log_total,
                state_log_total,
                state_flat,
                update,
            )
        )
        state_now = gate_open * state_now + (1.0 - gate_open) * update
    mixed_all = merge_heads(jnp.concatenate(mixed_parts, axis=1)).astype(jnp.bfloat16)
    rows_here = mixed_all
    hidden = token_values + lax.psum_scatter(
        jnp.einsum("nf,df->nd", rows_here, w_token_out, preferred_element_type=jnp.float32).astype(
            jnp.bfloat16
        ),
        "heads",
        scatter_dimension=0,
        tiled=True,
    ).astype(jnp.float32)
    hidden_norm = rms_forward(hidden, gain_values[2]).astype(jnp.bfloat16)
    hidden_all = lax.all_gather(hidden_norm, "heads", axis=0, tiled=True)
    up_value = jnp.dot(hidden_all, w_hidden_up, preferred_element_type=jnp.float32)
    activated = gelu_tanh(up_value).astype(jnp.bfloat16)
    rows_here = activated
    result_rows = (
        hidden
        + lax.psum_scatter(
            jnp.einsum(
                "nf,df->nd", rows_here, w_hidden_down, preferred_element_type=jnp.float32
            ).astype(jnp.bfloat16),
            "heads",
            scatter_dimension=0,
            tiled=True,
        ).astype(jnp.float32)
    ).astype(jnp.bfloat16)
    final_rows = state_now.astype(jnp.bfloat16)
    grad_out_all = lax.all_gather(grad_out, "heads", axis=0, tiled=True)
    grad_hidden_down = jnp.einsum(
        "nd,nf->df", grad_out_all, activated, preferred_element_type=jnp.float32
    )
    grad_activated = jnp.einsum(
        "nd,df->nf", grad_out_all, w_hidden_down, preferred_element_type=jnp.float32
    ).astype(jnp.bfloat16)
    unused, gelu_pull = jax.vjp(gelu_tanh, up_value)
    grad_up = gelu_pull(grad_activated.astype(jnp.float32))[0].astype(jnp.bfloat16)
    grad_hidden_up = jnp.einsum(
        "nd,nf->df", hidden_all, grad_up, preferred_element_type=jnp.float32
    )
    rows_here = grad_up
    grad_hidden_norm = lax.psum_scatter(
        jnp.einsum("nf,df->nd", rows_here, w_hidden_up, preferred_element_type=jnp.float32).astype(
            jnp.bfloat16
        ),
        "heads",
        scatter_dimension=0,
        tiled=True,
    ).astype(jnp.float32)
    grad_through, gain_hidden = rms_backward(hidden, gain_values[2], grad_hidden_norm)
    grad_hidden = grad_out.astype(jnp.float32) + grad_through
    grad_branch_all = lax.all_gather(grad_hidden.astype(jnp.bfloat16), "heads", axis=0, tiled=True)
    grad_token_output = jnp.einsum(
        "nd,nf->df", grad_branch_all, mixed_all, preferred_element_type=jnp.float32
    )
    grad_mixed = split_heads(
        jnp.einsum(
            "nd,df->nf", grad_branch_all, w_token_out, preferred_element_type=jnp.float32
        ).astype(jnp.bfloat16)
    )
    grad_key_sum = jnp.zeros((head_local, seq_length, HEAD_DIM), jnp.float32)
    grad_value_sum = jnp.zeros((head_local, seq_length, HEAD_DIM), jnp.float32)
    grad_query_parts = [None] * block_total
    grad_state = grad_final.astype(jnp.float32)
    grad_state_output = jnp.zeros(w_state_out.shape, jnp.float32)
    grad_state_weights = jnp.zeros(w_state.shape, jnp.float32)
    grad_gate = jnp.zeros(gate_open.shape, jnp.float32)
    gain_state = jnp.zeros(gate_open.shape, jnp.float32)
    for block_index in reversed(range(block_total)):
        (
            state_before,
            state_norm,
            state_queries,
            state_keys,
            state_values,
            log_total,
            state_log_total,
            state_flat,
            update,
        ) = kept_blocks[block_index]
        begin_row = block_index * BLOCK
        first_key = max(block_index - 1, 0) * BLOCK
        final_row = begin_row + BLOCK
        neighbor_count = final_row - first_key
        allowed, state_allowed = block_masks(valid_mask, block_index, state_row_block)
        grad_update = ((1.0 - gate_open) * grad_state).astype(jnp.bfloat16)
        grad_gate = grad_gate + jnp.sum(
            grad_state * (state_before - update), axis=0
        ) * gate_open * (1.0 - gate_open)
        grad_carry = gate_open * grad_state
        grad_state_output = grad_state_output + jnp.einsum(
            "nd,nf->df", grad_update, state_flat, preferred_element_type=jnp.float32
        )
        grad_state_mixed = split_heads(
            jnp.einsum(
                "nd,df->nf", grad_update, w_state_out, preferred_element_type=jnp.float32
            ).astype(jnp.bfloat16)
        )
        state_query_width, state_key_width, state_dv = attend_backward(
            state_queries,
            jnp.concatenate([state_keys, key_rows[:, begin_row:final_row]], axis=1),
            jnp.concatenate([state_values, value_rows[:, begin_row:final_row]], axis=1),
            state_allowed,
            state_log_total,
            grad_state_mixed,
        )
        token_dq, token_key_width, token_dv = attend_backward(
            queries[:, begin_row:final_row],
            jnp.concatenate([key_rows[:, first_key:final_row], state_keys], axis=1),
            jnp.concatenate([value_rows[:, first_key:final_row], state_values], axis=1),
            allowed,
            log_total,
            grad_mixed[:, begin_row:final_row],
        )
        grad_query_parts[block_index] = token_dq
        grad_key_sum = grad_key_sum.at[:, first_key:final_row].add(
            token_key_width[:, :neighbor_count]
        )
        grad_value_sum = grad_value_sum.at[:, first_key:final_row].add(token_dv[:, :neighbor_count])
        grad_key_sum = grad_key_sum.at[:, begin_row:final_row].add(
            state_key_width[:, state_row_block:]
        )
        grad_value_sum = grad_value_sum.at[:, begin_row:final_row].add(
            state_dv[:, state_row_block:]
        )
        state_key_gradient = (
            state_key_width[:, :state_row_block] + token_key_width[:, neighbor_count:]
        )
        state_value_gradient = state_dv[:, :state_row_block] + token_dv[:, neighbor_count:]
        grad_state_proj = jnp.stack(
            [
                merge_heads(state_query_width),
                merge_heads(state_key_gradient),
                merge_heads(state_value_gradient),
            ]
        ).astype(jnp.bfloat16)
        grad_state_weights = grad_state_weights + jnp.einsum(
            "nd,cnf->dcf", state_norm, grad_state_proj, preferred_element_type=jnp.float32
        )
        partial_norm = jnp.einsum(
            "cnf,dcf->nd", grad_state_proj, w_state, preferred_element_type=jnp.float32
        )
        grad_state_norm = lax.psum(partial_norm.astype(jnp.bfloat16), "heads").astype(jnp.float32)
        grad_previous, gain_piece = rms_backward(state_before, gain_values[1], grad_state_norm)
        gain_state = gain_state + gain_piece
        grad_state = grad_carry + grad_previous
    grad_projected = jnp.stack(
        [
            merge_heads(jnp.concatenate(grad_query_parts, axis=1)),
            merge_heads(grad_key_sum),
            merge_heads(grad_value_sum),
        ]
    ).astype(jnp.bfloat16)
    grad_token_weights = jnp.einsum(
        "nd,cnf->dcf", normed_all, grad_projected, preferred_element_type=jnp.float32
    )
    rows_here = grad_projected
    grad_normed = lax.psum_scatter(
        jnp.einsum("cnf,dcf->nd", rows_here, w_token, preferred_element_type=jnp.float32).astype(
            jnp.bfloat16
        ),
        "heads",
        scatter_dimension=0,
        tiled=True,
    ).astype(jnp.float32)
    grad_token_norm, gain_token = rms_backward(token_values, gain_values[0], grad_normed)
    input_rows = grad_hidden + grad_token_norm
    grads = (
        grad_token_weights,
        grad_token_output,
        grad_state_weights,
        grad_state_output,
        grad_hidden_up,
        grad_hidden_down,
        gain_token,
        gain_state,
        gain_hidden,
        grad_gate,
        grad_state,
    )
    return (result_rows, final_rows, input_rows, grads)


def body(
    tokens,
    counts,
    token_weights,
    token_output,
    state_weights,
    state_output,
    hidden_up,
    hidden_down,
    norm_gains,
    gate_bias,
    init_state,
    cotangent,
    state_cotangent,
):
    shards = (
        token_weights,
        token_output,
        state_weights,
        state_output,
        hidden_up,
        hidden_down,
        norm_gains,
        gate_bias,
        init_state,
    )
    micro_count = tokens.shape[0]
    result_list = []
    final_list = []
    input_list = []
    sharded_total = None
    full_total = None
    for micro_index in range(micro_count):
        weights_now = fetch_weights(shards)
        result_rows, final_rows, input_rows, grads = run_sequence(
            weights_now,
            tokens[micro_index, 0],
            counts[micro_index, 0],
            cotangent[micro_index, 0],
            state_cotangent[micro_index, 0],
        )
        result_list.append(result_rows)
        final_list.append(final_rows)
        input_list.append(input_rows)
        full_total = grads if full_total is None else jax.tree.map(jnp.add, full_total, grads)
    sharded_total = reduce_grads(full_total)
    output = jnp.stack(result_list)[:, None]
    final_state = jnp.stack(final_list)[:, None]
    input_grad = jnp.stack(input_list)[:, None]
    return (
        output,
        final_state,
        input_grad,
        sharded_total[0],
        sharded_total[1],
        sharded_total[2],
        sharded_total[3],
        sharded_total[4],
        sharded_total[5],
        sharded_total[6],
        sharded_total[7],
        sharded_total[8],
    )


def solution(mesh):
    placed = (
        P(None, "dp", "heads", None),
        P(None, "dp"),
        P("dp", None, "heads"),
        P("dp", "heads"),
        P("dp", None, "heads"),
        P("dp", "heads"),
        P("dp", "heads"),
        P("dp", "heads"),
        P(None, "dp"),
        P("dp"),
        P(None, "dp"),
        P(None, "dp", "heads", None),
        P(None, "dp", None, None),
    )
    return jax.shard_map(
        body,
        mesh=mesh,
        in_specs=placed,
        out_specs=(
            P(None, "dp", "heads", None),
            P(None, "dp", None, None),
            P(None, "dp", "heads", None),
            P("dp", None, "heads"),
            P("dp", "heads"),
            P("dp", None, "heads"),
            P("dp", "heads"),
            P("dp", "heads"),
            P("dp", "heads"),
            P(None, "dp"),
            P("dp"),
            P(None, "dp"),
        ),
        check_vma=False,
    )
```

profile of v0, /device:TPU:0, one launch (start us, length us, event | category | flops | bytes accessed | tf_op | source)
XLA Modules:
  0.0 1710.5 jit_solution(12839193916816799299)
XLA Ops:
  11.6 22.5 %all_gather.60 = bf16[3,1024]{1,0:T(4,128)(2,1)S(1)} all-gather(bf16[3,128]{1,0:T(4,128)(2,1)} %param.61), channel_id=1, replica_groups=mesh['dp'=8,'heads'=4] {'dp'}, dimensions={1}, use_global_device_ids=true | all-gather | bytes 6912 | tf_op jit(solution)/shard_map/all_gather | solution.py:115
  42.2 32.0 %all_gather.66 = bf16[1024,256]{1,0:T(8,128)(2,1)S(1)} all-gather(bf16[128,256]{1,0:T(8,128)(2,1)S(1)} %copy-done.182), channel_id=1, replica_groups=mesh['dp'=8,'heads'=4] {'dp'}, dimensions={0}, use_global_device_ids=true | all-gather | bytes 589824 | tf_op jit(solution)/shard_map/all_gather | solution.py:112
  76.0 26.4 %all-gather.23.cloned.1.call-done = bf16[1024,3,256]{0,2,1:T(8,128)(2,1)} async-done(((bf16[128,3,256]{0,2,1:T(8,128)(2,1)}), bf16[1024,3,256]{0,2,1:T(8,128)(2,1)}) %all-gather.23.cloned.1.call-update) | async-done | bytes 1572880 | tf_op jit(solution)/shard_map/all_gather | solution.py:111
  107.1 41.4 %all-gather.19.cloned.1.call-done = bf16[1024,3,256]{0,2,1:T(8,128)(2,1)} async-done(((bf16[128,3,256]{0,2,1:T(8,128)(2,1)}), bf16[1024,3,256]{0,2,1:T(8,128)(2,1)}) %all-gather.19.cloned.1.call-update) | async-done | bytes 1572880 | tf_op jit(solution)/shard_map/all_gather | solution.py:109
  148.5 22.8 %all-gather.31.cloned.1.call-done = bf16[1024,1024]{1,0:T(8,128)(2,1)} async-done(((bf16[256,1024]{1,0:T(8,128)(2,1)}), bf16[1024,1024]{1,0:T(8,128)(2,1)}) %all-gather.31.cloned.1.call-update) | async-done | bytes 2097168 | tf_op jit(solution)/shard_map/all_gather | solution.py:171
  223.9 20.4 %all-gather.2 = bf16[8,1,128]{2,1,0:T(2,128)(2,1)S(1)} all-gather(bf16[1,1,128]{2,1,0:T(2,128)(2,1)S(1)} %bitcast.581), channel_id=1, replica_groups=mesh['dp'=8,'heads'=4] {'dp'}, dimensions={0}, use_global_device_ids=true | all-gather | bytes 2304 | tf_op jit(solution)/shard_map/all_gather | solution.py:116
  244.3 33.4 %all_gather.67 = bf16[1024,256]{1,0:T(8,128)(2,1)} all-gather(bf16[128,256]{1,0:T(8,128)(2,1)S(1)} %copy-done.183), channel_id=1, replica_groups=mesh['dp'=8,'heads'=4] {'dp'}, dimensions={0}, use_global_device_ids=true | all-gather | bytes 589824 | tf_op jit(solution)/shard_map/all_gather | solution.py:110
  286.3 20.7 %all-reduce.20.cloned.1.call-done = (f32[512,1024]{1,0:T(8,128)}, f32[512,1024]{1,0:T(8,128)}) async-done(((f32[512,1024]{1,0:T(8,128)}, f32[512,1024]{1,0:T(8,128)}), (f32[512,1024]{1,0:T(8,128)}, f32[512,1024]{1,0:T(8,128)})) %all-reduce.20.cloned.1.call-update) | async-done | bytes 4194320 | tf_op jit(solution)/shard_map/psum | solution.py:211
  358.4 34.0 %reduce-scatter.23.cloned.1.call-done = bf16[256,1024]{1,0:T(8,128)(2,1)} async-done(((bf16[1024,1024]{1,0:T(8,128)(2,1)}), bf16[256,1024]{1,0:T(8,128)(2,1)}) %reduce-scatter.23.cloned.1.call-update) | async-done | bytes 524304 | tf_op jit(solution)/shard_map/reduce_scatter | solution.py:228
  400.1 44.0 %all-gather.27.cloned.1.call-done = bf16[1024,1024]{1,0:T(8,128)(2,1)} async-done(((bf16[128,1024]{1,0:T(8,128)(2,1)}), bf16[1024,1024]{1,0:T(8,128)(2,1)}) %all-gather.27.cloned.1.call-update) | async-done | bytes 2097168 | tf_op jit(solution)/shard_map/all_gather | solution.py:113
  444.1 23.2 %all-gather.33.cloned.1.call-done = bf16[1024,1024]{1,0:T(8,128)(2,1)} async-done(((bf16[256,1024]{1,0:T(8,128)(2,1)}), bf16[1024,1024]{1,0:T(8,128)(2,1)}) %all-gather.33.cloned.1.call-update) | async-done | bytes 2097168 | tf_op jit(solution)/shard_map/all_gather | solution.py:237
  492.1 51.5 %all-gather.29.cloned.1.call-done = bf16[1024,1024]{1,0:T(8,128)(2,1)} async-done(((bf16[128,1024]{1,0:T(8,128)(2,1)}), bf16[1024,1024]{1,0:T(8,128)(2,1)}) %all-gather.29.cloned.1.call-update) | async-done | bytes 2097168 | tf_op jit(solution)/shard_map/all_gather | solution.py:114
  626.0 33.5 %reduce-scatter.27.cloned.1.call-done = bf16[256,1024]{1,0:T(8,128)(2,1)} async-done(((bf16[1024,1024]{1,0:T(8,128)(2,1)}), bf16[256,1024]{1,0:T(8,128)(2,1)}) %reduce-scatter.27.cloned.1.call-update) | async-done | bytes 524304 | tf_op jit(solution)/shard_map/reduce_scatter | solution.py:266
  662.3 31.2 %reduce-scatter.25.cloned.1.call-done = bf16[256,1024]{1,0:T(8,128)(2,1)} async-done(((bf16[1024,1024]{1,0:T(8,128)(2,1)}), bf16[256,1024]{1,0:T(8,128)(2,1)}) %reduce-scatter.25.cloned.1.call-update) | async-done | bytes 524304 | tf_op jit(solution)/shard_map/reduce_scatter | solution.py:243
  832.1 54.3 %all-reduce.24.cloned.1.call-done = (bf16[512,1024]{1,0:T(8,128)(2,1)}, bf16[512,1024]{1,0:T(8,128)(2,1)}) async-done(((bf16[512,1024]{1,0:T(8,128)(2,1)}, bf16[512,1024]{1,0:T(8,128)(2,1)}), (bf16[512,1024]{1,0:T(8,128)(2,1)}, bf16[512,1024]{1,0:T(8,128)(2,1)})) %all-reduce.24.cloned.1.call-update) | async-done | bytes 2097168 | tf_op jit(solution)/shard_map/psum | solution.py:367
  1022.9 34.4 %reduce-scatter.29.cloned.1.call-done = bf16[256,1024]{1,0:T(8,128)(2,1)} async-done(((bf16[1024,1024]{1,0:T(8,128)(2,1)}), bf16[256,1024]{1,0:T(8,128)(2,1)}) %reduce-scatter.29.cloned.1.call-update) | async-done | bytes 524304 | tf_op jit(solution)/shard_map/reduce_scatter | solution.py:382
  1111.0 38.8 %reduce-scatter.45.cloned.1.call-done = f32[128,1024]{0,1:T(8,128)} async-done(((f32[1024,1024]{0,1:T(8,128)}), f32[128,1024]{0,1:T(8,128)}) %reduce-scatter.45.cloned.1.call-update) | async-done | bytes 524304 | tf_op jit(solution)/shard_map/reduce_scatter | solution.py:143
  1189.5 59.5 %reduce-scatter.49.cloned.1.call-done = f32[128,3]{1,0:T(8,128)} async-done(((f32[1024,3]{1,0:T(8,128)}), f32[128,3]{1,0:T(8,128)}) %reduce-scatter.49.cloned.1.call-update) | async-done | bytes 1552
  1250.4 89.8 %reduce-scatter.43.cloned.1.call-done = f32[128,1024]{1,0:T(8,128)} async-done(((f32[1024,1024]{1,0:T(8,128)}), f32[128,1024]{1,0:T(8,128)}) %reduce-scatter.43.cloned.1.call-update) | async-done | bytes 524304 | tf_op jit(solution)/shard_map/reduce_scatter | solution.py:142
  1340.2 67.5 %reduce-scatter.37.cloned.1.call-done = f32[128,256]{1,0:T(8,128)} async-done(((f32[1024,256]{1,0:T(8,128)}), f32[128,256]{1,0:T(8,128)}) %reduce-scatter.37.cloned.1.call-update) | async-done | bytes 131088 | tf_op jit(solution)/shard_map/reduce_scatter | solution.py:139
  1407.8 66.3 %reduce-scatter.41.cloned.1.call-done = f32[128,256]{1,0:T(8,128)} async-done(((f32[1024,256]{1,0:T(8,128)}), f32[128,256]{1,0:T(8,128)}) %reduce-scatter.41.cloned.1.call-update) | async-done | bytes 131088 | tf_op jit(solution)/shard_map/reduce_scatter | solution.py:141
  1474.1 71.6 %reduce-scatter.47.cloned.1.call-done = f32[512,128]{1,0:T(8,128)} async-done(((f32[512,1024]{1,0:T(8,128)}), f32[512,128]{1,0:T(8,128)}) %reduce-scatter.47.cloned.1.call-update) | async-done | bytes 262160 | tf_op jit(solution)/shard_map/reduce_scatter | solution.py:146
  1545.7 78.7 %reduce-scatter.35.cloned.1.call-done = f32[128,3,256]{2,0,1:T(8,128)} async-done(((f32[1024,3,256]{2,0,1:T(8,128)}), f32[128,3,256]{2,0,1:T(8,128)}) %reduce-scatter.35.cloned.1.call-update) | async-done | bytes 393232 | tf_op jit(solution)/shard_map/reduce_scatter | solution.py:138
  1624.3 78.9 %reduce-scatter.39.cloned.1.call-done = f32[128,3,256]{2,0,1:T(8,128)} async-done(((f32[1024,3,256]{2,0,1:T(8,128)}), f32[128,3,256]{2,0,1:T(8,128)}) %reduce-scatter.39.cloned.1.call-update) | async-done | bytes 393232 | tf_op jit(solution)/shard_map/reduce_scatter | solution.py:140
  (829 shorter events, 613.9 us)
Async XLA Ops:
  9.7 138.8 %all-gather.19.cloned.1.call-start = ((), (), s32[]{:S(2)}) async-start(), calls=%async_computation.17 | async-start | bytes 1769472 | tf_op jit(solution)/shard_map/all_gather | solution.py:109
  11.6 159.8 %all-gather.31.cloned.1.call-start = ((), (), s32[]{:S(2)}) async-start(), calls=%async_computation.25 | async-start | bytes 2621440 | tf_op jit(solution)/shard_map/all_gather | solution.py:171
  37.5 158.4 %all-gather.17.cloned.1.call-start = ((), (), s32[]{:S(2)}) async-start(), calls=%async_computation.16 | async-start | bytes 2621440 | tf_op jit(solution)/shard_map/all_gather | solution.py:171
  38.1 269.0 %all-reduce.20.cloned.1.call-start = ((), (), s32[]{:S(2)}) async-start(), calls=%async_computation.46 | async-start | bytes 8388608 | tf_op jit(solution)/shard_map/psum | solution.py:211
  221.2 137.2 %reduce-scatter.19.cloned.1.call-start = ((), (), s32[]{:S(2)}) async-start(), calls=%async_computation.20 | async-start | bytes 2621440 | tf_op jit(solution)/shard_map/reduce_scatter | solution.py:228
  349.5 117.8 %all-gather.33.cloned.1.call-start = ((), (), s32[]{:S(2)}) async-start(), calls=%async_computation.27 | async-start | bytes 2621440 | tf_op jit(solution)/shard_map/all_gather | solution.py:237
  397.9 145.7 %all-gather.29.cloned.1.call-start = ((), (), s32[]{:S(2)}) async-start(), calls=%async_computation.23 | async-start | bytes 2359296 | tf_op jit(solution)/shard_map/all_gather | solution.py:114
  398.5 168.4 %all-gather.25.cloned.1.call-start = ((), (), s32[]{:S(2)}) async-start(), calls=%async_computation.21 | async-start | bytes 2621440 | tf_op jit(solution)/shard_map/all_gather | solution.py:237
  399.3 191.8 %all-gather.39.cloned.1.call-start = ((), (), s32[]{:S(2)}) async-start(), calls=%async_computation.42 | async-start | bytes 2621440 | tf_op jit(solution)/shard_map/all_gather | solution.py:253
  399.8 226.2 %reduce-scatter.31.cloned.1.call-start = ((), (), s32[]{:S(2)}) async-start(), calls=%async_computation.32 | async-start | bytes 2621440 | tf_op jit(solution)/shard_map/reduce_scatter | solution.py:266
  556.8 102.7 %reduce-scatter.27.cloned.1.call-start = ((), (), s32[]{:S(2)}) async-start(), calls=%async_computation.29 | async-start | bytes 2621440 | tf_op jit(solution)/shard_map/reduce_scatter | solution.py:266
  611.1 126.6 %all-gather.35.cloned.1.call-start = ((), (), s32[]{:S(2)}) async-start(), calls=%async_computation.30 | async-start | bytes 2621440 | tf_op jit(solution)/shard_map/all_gather | solution.py:276
  719.4 112.6 %all-reduce.18.cloned.1.call-start = ((), (), s32[]{:S(2)}) async-start(), calls=%async_computation.45 | async-start | bytes 8388608 | tf_op jit(solution)/shard_map/psum | solution.py:211
  737.5 148.9 %all-reduce.24.cloned.1.call-start = ((), (), s32[]{:S(2)}) async-start(), calls=%async_computation.48 | async-start | bytes 4194304 | tf_op jit(solution)/shard_map/psum | solution.py:367
  807.2 192.8 %all-reduce.22.cloned.1.call-start = ((), (), s32[]{:S(2)}) async-start(), calls=%async_computation.47 | async-start | bytes 4194304 | tf_op jit(solution)/shard_map/psum | solution.py:367
  975.3 174.6 %reduce-scatter.45.cloned.1.call-start = ((), (), s32[]{:S(2)}) async-start(), calls=%async_computation.40 | async-start | bytes 4718592 | tf_op jit(solution)/shard_map/reduce_scatter | solution.py:143
  986.0 197.4 %reduce-scatter.21.cloned.1.call-start = ((), (), s32[]{:S(2)}) async-start(), calls=%async_computation.24 | async-start | bytes 2621440 | tf_op jit(solution)/shard_map/reduce_scatter | solution.py:243
  993.0 255.9 %reduce-scatter.49.cloned.1.call-start = ((), (), s32[]{:S(2)}) async-start(), calls=%async_computation.44 | async-start | bytes 589824
  1066.4 273.8 %reduce-scatter.43.cloned.1.call-start = ((), (), s32[]{:S(2)}) async-start(), calls=%async_computation.39 | async-start | bytes 4718592 | tf_op jit(solution)/shard_map/reduce_scatter | solution.py:142
  1074.8 333.0 %reduce-scatter.37.cloned.1.call-start = ((), (), s32[]{:S(2)}) async-start(), calls=%async_computation.36 | async-start | bytes 1179648 | tf_op jit(solution)/shard_map/reduce_scatter | solution.py:139
  1079.3 394.8 %reduce-scatter.41.cloned.1.call-start = ((), (), s32[]{:S(2)}) async-start(), calls=%async_computation.38 | async-start | bytes 1179648 | tf_op jit(solution)/shard_map/reduce_scatter | solution.py:141
  1086.0 459.7 %reduce-scatter.47.cloned.1.call-start = ((), (), s32[]{:S(2)}) async-start(), calls=%async_computation.41 | async-start | bytes 2359296 | tf_op jit(solution)/shard_map/reduce_scatter | solution.py:146
  1091.8 532.6 %reduce-scatter.35.cloned.1.call-start = ((), (), s32[]{:S(2)}) async-start(), calls=%async_computation.35 | async-start | bytes 3538944 | tf_op jit(solution)/shard_map/reduce_scatter | solution.py:138
  1100.6 602.6 %reduce-scatter.39.cloned.1.call-start = ((), (), s32[]{:S(2)}) async-start(), calls=%async_computation.37 | async-start | bytes 3538944 | tf_op jit(solution)/shard_map/reduce_scatter | solution.py:140
  (249 other events, 5035.9 us)
Sparse Core Ops, SparseCore 0:
  10.1 45.1 all-gather.20
  57.9 44.4 all-gather.22
  105.0 43.4 all-gather.18
  221.3 85.6 all-reduce.19
  326.9 31.5 reduce-scatter.18
  360.9 31.4 reduce-scatter.22
  394.8 49.2 all-gather.26
  494.3 49.2 all-gather.28
  593.6 31.4 reduce-scatter.30
  628.0 31.4 reduce-scatter.26
  662.0 31.3 reduce-scatter.24
  746.3 85.6 all-reduce.17
  834.7 51.6 all-reduce.23
  937.0 51.6 all-reduce.21
  991.3 31.4 reduce-scatter.32
  1025.8 31.4 reduce-scatter.28
  1061.3 88.4 reduce-scatter.44
  1187.0 61.9 reduce-scatter.48
  1253.1 87.0 reduce-scatter.42
  1344.6 63.1 reduce-scatter.36
  1411.6 62.4 reduce-scatter.40
  1478.6 66.9 reduce-scatter.46
  1550.3 74.0 reduce-scatter.34
  1628.8 74.3 reduce-scatter.38
  (9 shorter events, 206.5 us)
where the time goes:
time: 1720 us; the launch traced here: 1710 us
  waiting for transfers between devices  1090 us (63%)
  matrix products  249 us (14%)
  blocking collectives  134 us (8%)
  local copies, waits for them, and re-layouts  119 us (7%)
  other arithmetic  98.5 us (6%)
  between operations  19.8 us (1%)
    reduce_scatter x1, waiting for transfers between devices, reduce_grads(): lax.psum_scatter(grad_hidden_up, 'dp', scatter_dimension=0, tiled=True)  89.8 us
    reduce_scatter x1, waiting for transfers between devices, reduce_grads(): lax.psum_scatter(grad_state_weights, 'dp', scatter_dimension=0, tiled=True)  78.9 us
    reduce_scatter x1, waiting for transfers between devices, reduce_grads(): lax.psum_scatter(grad_token_weights, 'dp', scatter_dimension=0, tiled=True)  78.7 us
    reduce_scatter x1, waiting for transfers between devices, reduce_grads(): lax.psum_scatter(grad_init, 'dp', scatter_dimension=1, tiled=True)  71.6 us
    reduce_scatter x1, waiting for transfers between devices, reduce_grads(): lax.psum_scatter(grad_token_output, 'dp', scatter_dimension=0, tiled=True)  67.5 us
    reduce_scatter x1, waiting for transfers between devices, reduce_grads(): lax.psum_scatter(grad_state_output, 'dp', scatter_dimension=0, tiled=True)  66.3 us
    unnamed x34, waiting for transfers between devices  63.6 us
    psum x2, waiting for transfers between devices, run_sequence(): lax.psum(partial_norm.astype(jnp.bfloat16), 'heads').astype(jnp.float32)  54.4 us
  transfers between devices with their start and end apart: 33, of which 28 were waited for; matrix products, arithmetic and copies ran while one was open for 20% of the time, Pallas kernels for 0%

commit v1 on v0

v1 whole, which is shorter than its diff:
```python
import functools

import jax
import jax.numpy as jnp
from jax import lax
from jax.sharding import Mesh
from jax.sharding import PartitionSpec as P

HEAD_DIM = 128
BLOCK = 512
EPSILON = 1e-06
MASKED = -1e30
RING = 4
BF = jnp.bfloat16
F32 = jnp.float32


def swap(array, axis):
    return lax.ppermute(array, axis, [(0, 1), (1, 0)])


def turn(array, steps):
    return lax.ppermute(array, "z", [(i, (i + steps) % RING) for i in range(RING)])


def matmul(left, right, contract):
    return lax.dot_general(
        left, right, (contract, ((), ())), preferred_element_type=jnp.float32
    )


def mm(left, right):
    return matmul(left, right, ((1,), (0,)))


def mm_nt(left, right):
    return matmul(left, right, ((1,), (1,)))


def mm_tn(left, right):
    return matmul(left, right, ((0,), (0,)))


def width_places():
    z, x = lax.axis_index("z"), lax.axis_index("x")
    return [lax.rem(z - k + RING, RING) * 2 + jnp.bitwise_xor(x, dx) for dx in range(2) for k in range(RING)]


def take_pieces(array, places):
    groups = lax.axis_size("r")
    lead, width = array.shape[:-1], array.shape[-1]
    split = array.reshape(lead + (groups, len(places), width // (groups * len(places))))
    axis = len(lead) + 1
    return [lax.dynamic_index_in_dim(split, place, axis, keepdims=False) for place in places]


def to_local(array):
    pieces = take_pieces(array, width_places())
    lead = array.shape[:-1]
    return jnp.concatenate([p.reshape(lead + (-1,)) for p in pieces], axis=-1)


def from_local(array):
    z, x = lax.axis_index("z"), lax.axis_index("x")
    groups = lax.axis_size("r")
    lead, width = array.shape[:-1], array.shape[-1]
    split = array.reshape(lead + (2 * RING, groups, width // (groups * 2 * RING)))
    axis = len(lead)
    pieces = []
    for z_to in range(RING):
        for x_to in range(2):
            place = jnp.bitwise_xor(x, x_to) * RING + lax.rem(z - z_to + RING, RING)
            pieces.append(lax.dynamic_index_in_dim(split, place, axis, keepdims=False))
    return jnp.stack(pieces, axis=axis + 1).reshape(array.shape)


def gather_groups(array, axis):
    if lax.axis_size("r") == 1:
        return array
    return lax.all_gather(array, "r", axis=axis, tiled=True)


def gather_weight(shard):
    shard = gather_groups(shard, 1)
    half = shard.shape[2] // 2
    ring = [shard] + [turn(shard, k) for k in range(1, RING)]
    near_a = jnp.concatenate([piece[..., :half] for piece in ring], axis=1)
    near_b = jnp.concatenate([piece[..., half:] for piece in ring], axis=1)
    a_x, a_y = swap(near_a, "x"), swap(near_a, "y")
    b_y, b_x = swap(near_b, "y"), swap(near_b, "x")
    a_xy, b_xy = swap(a_x, "y"), swap(b_y, "x")
    top = jnp.concatenate([near_a, a_y, near_b, b_y], axis=2)
    bottom = jnp.concatenate([a_x, a_xy, b_x, b_xy], axis=2)
    return jnp.concatenate([top, bottom], axis=1)


def gather_rows(shard):
    if lax.axis_size("r") > 1:
        shard = lax.all_gather(shard, "r", axis=1, tiled=True)
    near = jnp.concatenate([shard] + [turn(shard, k) for k in range(1, RING)], axis=1)
    return jnp.concatenate([near, swap(near, "x")], axis=1)


def add_low(left, right):
    return (left.astype(F32) + right.astype(F32)).astype(BF)


def scatter_groups(array, axis):
    if lax.axis_size("r") == 1:
        return array
    return lax.psum_scatter(array, "r", scatter_dimension=axis, tiled=True)


def scatter_ring(near):
    groups, rows, width = near.shape
    split = near.reshape(groups, RING, rows // RING, width)
    total = split[:, 0].astype(F32)
    for k in range(1, RING):
        total = total + turn(split[:, k], RING - k).astype(F32)
    return total


def weight_grad(left, rights):
    width = left.shape[1]
    quarter = rights[0].shape[1] // 4
    half_rows = width // 2

    def part(rows, columns):
        return jnp.stack([mm_tn(left[:, rows], right[:, columns]).astype(BF) for right in rights])

    everything = slice(0, width)
    near, far = slice(0, half_rows), slice(half_rows, width)
    a_send = part(everything, slice(quarter, 2 * quarter))
    b_send = part(far, slice(2 * quarter, 4 * quarter))
    a_got, b_got = swap(a_send, "y"), swap(b_send, "x")
    a_sum = add_low(part(everything, slice(0, quarter)), a_got)
    b_sum = add_low(part(near, slice(2 * quarter, 4 * quarter)), b_got)
    a_got2 = swap(a_sum[:, half_rows:], "x")
    b_got2 = swap(b_sum[:, :, quarter:], "y")
    a_near = add_low(a_sum[:, :half_rows], a_got2)
    b_near = add_low(b_sum[:, :, :quarter], b_got2)
    total = scatter_ring(jnp.concatenate([a_near, b_near], axis=2))
    return scatter_groups(total, 1)


def rms_inverse(values):
    return lax.rsqrt(jnp.mean(values * values, axis=-1, keepdims=True) + EPSILON)


def rms_forward(values, gain):
    return (values * rms_inverse(values) * gain).astype(BF)


def rms_backward(values, gain, grad):
    inverse = rms_inverse(values)
    scaled = values * inverse
    weighted = grad * gain
    grad_values = inverse * (weighted - scaled * jnp.mean(scaled * weighted, axis=-1, keepdims=True))
    return grad_values, jnp.sum(grad * scaled, axis=0)


def gelu_tanh(values):
    return jax.nn.gelu(values, approximate=True)


def join(own):
    return jnp.concatenate([own, swap(own, "c")], axis=0)


def fold(partial):
    rows = partial.shape[0] // 2
    return partial[:rows].astype(F32) + swap(partial[rows:].astype(BF), "c").astype(F32)


def split_heads(flat):
    return flat.reshape(flat.shape[0], flat.shape[1] // HEAD_DIM, HEAD_DIM).transpose(1, 0, 2)


def merge_heads(split):
    return split.transpose(1, 0, 2).reshape(split.shape[1], split.shape[0] * HEAD_DIM)


def attend_forward(queries, key_rows, value_rows, allowed):
    scale = HEAD_DIM ** (-0.5)
    scores = jnp.einsum("hqe,hke->hqk", queries, key_rows, preferred_element_type=F32) * scale
    scores = jnp.where(allowed[None], scores, MASKED)
    row_top = jnp.max(scores, axis=-1, keepdims=True)
    weights = jnp.exp(scores - row_top)
    row_total = jnp.sum(weights, axis=-1, keepdims=True)
    probs = (weights / row_total).astype(BF)
    mixed = jnp.einsum("hqk,hke->hqe", probs, value_rows, preferred_element_type=F32)
    return (mixed, row_top + jnp.log(row_total))


def attend_backward(queries, key_rows, value_rows, allowed, log_total, grad_mixed):
    scale = HEAD_DIM ** (-0.5)
    scores = jnp.einsum("hqe,hke->hqk", queries, key_rows, preferred_element_type=F32) * scale
    scores = jnp.where(allowed[None], scores, MASKED)
    probs = jnp.exp(scores - log_total)
    grad_probs = jnp.einsum("hqe,hke->hqk", grad_mixed, value_rows, preferred_element_type=F32)
    grad_scores = probs * (grad_probs - jnp.sum(grad_probs * probs, axis=-1, keepdims=True))
    low_scores = grad_scores.astype(BF)
    grad_queries = jnp.einsum("hqk,hke->hqe", low_scores, key_rows, preferred_element_type=F32) * scale
    grad_keys = jnp.einsum("hqk,hqe->hke", low_scores, queries, preferred_element_type=F32) * scale
    grad_values = jnp.einsum("hqk,hqe->hke", probs.astype(BF), grad_mixed, preferred_element_type=F32)
    return (grad_queries, grad_keys, grad_values)


def rows_of_block(array, block_index, blocks):
    lead = array.shape[:-2]
    rows, width = array.shape[-2:]
    per = rows // (2 * blocks)
    split = array.reshape(lead + (2, blocks, per, width))
    return split[..., block_index, :, :].reshape(lead + (2 * per, width))


def rows_from_blocks(parts):
    blocks = len(parts)
    lead = parts[0].shape[:-2]
    rows, width = parts[0].shape[-2:]
    split = [part.reshape(lead + (2, 1, rows // 2, width)) for part in parts]
    joined = jnp.concatenate(split, axis=-3)
    return joined.reshape(lead + (blocks * rows, width))


def body(
    tokens,
    counts,
    token_weights,
    token_output,
    state_weights,
    state_output,
    hidden_up,
    hidden_down,
    norm_gains,
    gate_bias,
    init_state,
    cotangent,
    state_cotangent,
):
    y, c = lax.axis_index("y"), lax.axis_index("c")
    micro, rows_local, width = tokens.shape[0], tokens.shape[2], tokens.shape[3]
    state_rows = init_state.shape[0]
    state_half = state_rows // 2

    def own_rows(array):
        keep = lax.dynamic_index_in_dim(array[:, 0], y, 0, keepdims=False)
        send = lax.dynamic_index_in_dim(array[:, 0], 1 - y, 0, keepdims=False)
        got = swap(send, "y")
        return jnp.where(y == 0, jnp.concatenate([keep, got]), jnp.concatenate([got, keep]))

    def to_owner(rows, wide):
        split = rows.reshape(2, rows_local, width)
        keep = lax.dynamic_index_in_dim(split, y, 0, keepdims=False)
        send = lax.dynamic_index_in_dim(split, 1 - y, 0, keepdims=False)
        got = swap(send.astype(BF), "y").astype(wide)
        keep = keep.astype(wide)
        return jnp.where(y == 0, jnp.stack([keep, got]), jnp.stack([got, keep]))[:, None]

    x_rows = to_local(own_rows(tokens))
    valid_count = lax.dynamic_index_in_dim(counts[:, 0], y, 0, keepdims=False)

    small = jnp.concatenate(
        [
            lax.dynamic_slice_in_dim(init_state, c * state_half, state_half, 0),
            norm_gains,
            gate_bias[None],
            jnp.zeros((12, init_state.shape[1]), BF),
        ],
        axis=0,
    )
    w_token = gather_weight(token_weights.transpose(1, 0, 2))
    small = gather_rows(small)
    w_state = gather_weight(state_weights.transpose(1, 0, 2))
    w_state_out = gather_weight(state_output[None])[0]
    w_token_out = gather_weight(token_output[None])[0]
    w_up = gather_weight(hidden_up[None])[0]
    w_down = gather_weight(hidden_down[None])[0]
    gains = small[state_half : state_half + 3].astype(F32)
    gate_open = jax.nn.sigmoid(small[state_half + 3].astype(F32))
    state_now = small[:state_half].astype(F32)

    dy_rows = to_local(own_rows(cotangent))
    dy_all = join(dy_rows)
    grad_final = lax.dynamic_slice(
        state_cotangent, (y, 0, c * state_half, 0), (1, 1, state_half, width)
    )[0, 0]
    grad_final = to_local(grad_final)

    seq_length = 4 * rows_local
    blocks = seq_length // BLOCK
    x_values = x_rows.astype(F32)
    normed_all = join(rms_forward(x_values, gains[0]))
    queries, key_rows, value_rows = [
        split_heads(mm(normed_all, w_token[part]).astype(BF)) for part in range(3)
    ]
    core_of = jnp.bitwise_xor(jnp.arange(2), c)
    block_pos = (core_of[:, None] * rows_local + jnp.arange(rows_local)[None]).reshape(-1)

    def masks(block_index):
        query_pos = block_index * BLOCK + block_pos
        key_blocks = range(max(block_index - 1, 0), block_index + 1)
        key_pos = jnp.concatenate([k * BLOCK + block_pos for k in key_blocks])
        nearby = (
            (key_pos[None, :] <= query_pos[:, None])
            & (key_pos[None, :] > query_pos[:, None] - BLOCK)
            & (key_pos < (blocks - 1) * BLOCK + valid_count)[None]
        )
        own_valid = query_pos < (blocks - 1) * BLOCK + valid_count
        allowed = jnp.concatenate([nearby, jnp.ones((BLOCK, state_rows), jnp.bool_)], axis=1)
        state_allowed = jnp.concatenate(
            [
                jnp.ones((state_rows, state_rows), jnp.bool_),
                jnp.broadcast_to(own_valid[None], (state_rows, BLOCK)),
            ],
            axis=1,
        )
        return allowed, state_allowed

    def block_keys(array, block_index):
        first = max(block_index - 1, 0)
        return jnp.concatenate(
            [rows_of_block(array, k, blocks) for k in range(first, block_index + 1)], axis=1
        )

    kept = []
    mixed_parts = []
    for b in range(blocks):
        state_norm = join(rms_forward(state_now, gains[1]))
        s_query, s_key, s_value = [
            split_heads(mm(state_norm, w_state[part]).astype(BF)) for part in range(3)
        ]
        allowed, state_allowed = masks(b)
        token_in = (
            rows_of_block(queries, b, blocks),
            jnp.concatenate([block_keys(key_rows, b), s_key], axis=1),
            jnp.concatenate([block_keys(value_rows, b), s_value], axis=1),
            allowed,
        )
        state_in = (
            s_query,
            jnp.concatenate([s_key, rows_of_block(key_rows, b, blocks)], axis=1),
            jnp.concatenate([s_value, rows_of_block(value_rows, b, blocks)], axis=1),
            state_allowed,
        )
        mixed, log_total = attend_forward(*token_in)
        mixed_parts.append(mixed)
        state_mixed, state_log = attend_forward(*state_in)
        state_flat = merge_heads(state_mixed).astype(BF)
        update = fold(mm_nt(state_flat, w_state_out))
        kept.append((state_now, state_norm, token_in, state_in, log_total, state_log, state_flat, update))
        state_now = gate_open * state_now + (1.0 - gate_open) * update
    mixed_all = merge_heads(rows_from_blocks(mixed_parts)).astype(BF)
    hidden = x_values + fold(mm_nt(mixed_all, w_token_out))
    hidden_all = join(rms_forward(hidden, gains[2]))
    up_value = mm(hidden_all, w_up)
    activated = gelu_tanh(up_value).astype(BF)
    result = (hidden + fold(mm_nt(activated, w_down))).astype(BF)
    output = to_owner(from_local(result), BF)

    final_half = from_local(state_now.astype(BF))
    final_pair = jnp.stack([final_half, swap(final_half, "y")])
    final_pair = jnp.where(y == 0, final_pair, final_pair[::-1])
    final_other = swap(final_pair, "c")
    final_state = jnp.where(
        c == 0,
        jnp.concatenate([final_pair, final_other], axis=1),
        jnp.concatenate([final_other, final_pair], axis=1),
    )[:, None]

    grad_activated = mm(dy_all, w_down).astype(BF)
    unused, gelu_pull = jax.vjp(gelu_tanh, up_value)
    grad_up = gelu_pull(grad_activated.astype(F32))[0].astype(BF)
    grad_hidden_norm = fold(mm_nt(grad_up, w_up))
    grad_hidden_down = weight_grad(dy_all, [activated])[0]
    grad_hidden_up = weight_grad(hidden_all, [grad_up])[0]
    through, gain_hidden = rms_backward(hidden, gains[2], grad_hidden_norm)
    grad_hidden = dy_rows.astype(F32) + through
    branch_all = join(grad_hidden.astype(BF))
    grad_mixed = split_heads(mm(branch_all, w_token_out).astype(BF))
    grad_token_output = weight_grad(branch_all, [mixed_all])[0]

    grad_state = grad_final.astype(F32)
    grad_gate = jnp.zeros((width,), F32)
    gain_state = jnp.zeros((width,), F32)
    query_parts = [None] * blocks
    key_parts = [0.0] * blocks
    value_parts = [0.0] * blocks
    update_all, flat_all, norm_all, proj_all = [], [], [], []
    for b in reversed(range(blocks)):
        state_before, state_norm, token_in, state_in, log_total, state_log, state_flat, update = kept[b]
        grad_update = join(((1.0 - gate_open) * grad_state).astype(BF))
        grad_gate = grad_gate + jnp.sum(grad_state * (state_before - update), axis=0)
        grad_state_mixed = split_heads(mm(grad_update, w_state_out).astype(BF))
        update_all.append(grad_update)
        flat_all.append(state_flat)
        s_dq, s_dk, s_dv = attend_backward(*state_in, state_log, grad_state_mixed)
        t_dq, t_dk, t_dv = attend_backward(*token_in, log_total, rows_of_block(grad_mixed, b, blocks))
        query_parts[b] = t_dq
        first = max(b - 1, 0)
        for k in range(first, b + 1):
            rows = slice((k - first) * BLOCK, (k - first + 1) * BLOCK)
            key_parts[k] = key_parts[k] + t_dk[:, rows]
            value_parts[k] = value_parts[k] + t_dv[:, rows]
        near = (b + 1 - first) * BLOCK
        key_parts[b] = key_parts[b] + s_dk[:, state_rows:]
        value_parts[b] = value_parts[b] + s_dv[:, state_rows:]
        grad_proj = [
            merge_heads(s_dq).astype(BF),
            merge_heads(s_dk[:, :state_rows] + t_dk[:, near:]).astype(BF),
            merge_heads(s_dv[:, :state_rows] + t_dv[:, near:]).astype(BF),
        ]
        norm_all.append(state_norm)
        proj_all.append(grad_proj)
        partial = sum(mm_nt(grad_proj[part], w_state[part]) for part in range(3))
        previous, gain_piece = rms_backward(state_before, gains[1], fold(partial))
        gain_state = gain_state + gain_piece
        grad_state = gate_open * grad_state + previous
    grad_gate = grad_gate * gate_open * (1.0 - gate_open)
    grad_state_output = weight_grad(jnp.concatenate(update_all), [jnp.concatenate(flat_all)])[0]
    grad_state_weights = weight_grad(
        jnp.concatenate(norm_all),
        [jnp.concatenate([proj[part] for proj in proj_all]) for part in range(3)],
    ).transpose(1, 0, 2)
    grad_projected = [
        merge_heads(rows_from_blocks(parts)).astype(BF)
        for parts in (query_parts, key_parts, value_parts)
    ]
    grad_normed = fold(sum(mm_nt(grad_projected[part], w_token[part]) for part in range(3)))
    grad_token_weights = weight_grad(normed_all, grad_projected).transpose(1, 0, 2)
    through, gain_token = rms_backward(x_values, gains[0], grad_normed)
    input_grad = to_owner(from_local(grad_hidden + through), F32)

    vectors = from_local(jnp.stack([gain_token, gain_state, gain_hidden, grad_gate]))
    vectors = lax.psum_scatter(vectors, ("r", "z", "x"), scatter_dimension=1, tiled=True)
    vectors = lax.psum(vectors, ("y", "c"))
    init_grad = from_local(grad_state)
    init_grad = lax.psum_scatter(init_grad, ("r", "z", "x"), scatter_dimension=1, tiled=True)
    init_grad = lax.psum(init_grad, "y")
    init_grad = lax.all_gather(init_grad, "c", axis=0, tiled=True)
    return (
        output,
        final_state,
        input_grad,
        grad_token_weights,
        grad_token_output,
        grad_state_weights,
        grad_state_output,
        grad_hidden_up,
        grad_hidden_down,
        vectors[:3],
        vectors[3],
        init_grad,
    )


def solution(mesh):
    dp, heads = mesh.devices.shape
    fine = Mesh(mesh.devices.reshape(dp // (2 * RING), RING, 2, heads // 2, 2), ("r", "z", "x", "y", "c"))
    d, h = ("r", "z", "x"), ("y", "c")
    return jax.shard_map(
        body,
        mesh=fine,
        in_specs=(
            P(None, d, h, None),
            P(None, d),
            P(d, None, h),
            P(d, h),
            P(d, None, h),
            P(d, h),
            P(d, h),
            P(d, h),
            P(None, d),
            P(d),
            P(None, d),
            P(None, d, h, None),
            P(None, d, None, None),
        ),
        out_specs=(
            P(None, d, h, None),
            P(None, d, None, None),
            P(None, d, h, None),
            P(d, None, h),
            P(d, h),
            P(d, None, h),
            P(d, h),
            P(d, h),
            P(d, h),
            P(None, d),
            P(d),
            P(None, d),
        ),
        check_vma=False,
    )
```

time: 1720 us -> 1120 us (0.65)
  waiting for transfers between devices: 1090 us -> 273 us
  other arithmetic: 98.5 us -> 256 us
  blocking collectives: 134 us -> 7.84 us
  starting transfers between devices: 3.67 us -> 125 us
  local copies, waits for them, and re-layouts: 119 us -> 181 us
    reduce_scatter x15 -> x1, waiting for transfers between devices: 658 us -> 12.1 us  [body(): lax.psum_scatter(init_grad, ('r', 'z', 'x'), scatter_dimension=1, tiled=T...]
    all_gather x13 -> x0, waiting for transfers between devices: 273 us -> none  [the longest x1 51.5 us: fetch_weights(): lax.all_gather(hidden_down, 'dp', axis=0, tiled=True)]
    ppermute x0 -> x122, waiting for transfers between devices: none -> 236 us  [the longest x83 120 us: swap(): return lax.ppermute(array, axis, [(0, 1), (1, 0)])]
    squeeze x0 -> x7, other arithmetic: none -> 136 us  [the longest x1 71.9 us: body(): w_down = gather_weight(hidden_down[None])[0]]
    ppermute x0 -> x122, starting transfers between devices: none -> 125 us  [the longest x83 71.7 us: swap(): return lax.ppermute(array, axis, [(0, 1), (1, 0)])]
    all_gather x4 -> x1, blocking collectives: 108 us -> 2.19 us  [body(): init_grad = lax.all_gather(init_grad, 'c', axis=0, tiled=True)]
    psum x4 -> x1, waiting for transfers between devices: 92.5 us -> 19.5 us  [body(): init_grad = lax.psum(init_grad, 'y')]
    unnamed x34 -> x4, waiting for transfers between devices: 63.6 us -> 5.42 us
  transfers between devices with their start and end apart: 33 -> 125, of which waited for: 28 -> 42; matrix products, arithmetic and copies ran while one was open for 20% -> 60% of each run, Pallas kernels for 0% -> 0%
where the time goes in v1:
time: 1120 us; the launch traced here: 1110 us
  waiting for transfers between devices  273 us (24%)
  other arithmetic  256 us (23%)
  matrix products  247 us (22%)
  local copies, waits for them, and re-layouts  181 us (16%)
  starting transfers between devices  125 us (11%)
  between operations  18.8 us (2%)
    dot_general x68, matrix products, matmul(): lax.dot_general(left, right, (contract, ((), ())), preferred_element_type...  157 us
    ppermute x83, waiting for transfers between devices, swap(): return lax.ppermute(array, axis, [(0, 1), (1, 0)])  120 us
    ppermute x39, waiting for transfers between devices, turn(): lax.ppermute(array, 'z', [(i, (i + steps) % RING) for i in range(RING)])  116 us
    squeeze x1, other arithmetic, body(): w_down = gather_weight(hidden_down[None])[0]  71.9 us
    unnamed x677, local copies, waits for them, and re-layouts  71.9 us
    ppermute x83, starting transfers between devices, swap(): return lax.ppermute(array, axis, [(0, 1), (1, 0)])  71.7 us
    squeeze x1, other arithmetic, body(): w_up = gather_weight(hidden_up[None])[0]  55.4 us
    ppermute x39, starting transfers between devices, turn(): lax.ppermute(array, 'z', [(i, (i + steps) % RING) for i in range(RING)])  53.5 us
  transfers between devices with their start and end apart: 125, of which 42 were waited for; matrix products, arithmetic and copies ran while one was open for 60% of the time, Pallas kernels for 0%

profile of v1, /device:TPU:0, one launch (start us, length us, event | category | flops | bytes accessed | tf_op | source)
XLA Modules:
  0.0 1108.9 jit_solution(6698468377627851957)
XLA Ops:
  56.7 7.5 collective-permute-done.1
  81.0 11.9 %collective-permute-done.17 = bf16[3,128,256]{2,1,0:T(8,128)(2,1)S(1)} collective-permute-done((bf16[3,128,256]{2,1,0:T(8,128)(2,1)}, bf16[3,128,256]{2,1,0:T(8,128)(2,1)S(1)}, u32[]{:S(2)}, u32[]{:S(2)}) %collective-permute-start.17) | collective-permute-done | bytes 196640 | tf_op jit(solution)/shard_map/ppermute | solution.py:23
  103.7 13.3 %collective-permute-done.48 = bf16[1,128,1024]{2,1,0:T(8,128)(2,1)S(1)} collective-permute-done((bf16[1,128,1024]{2,1,0:T(8,128)(2,1)}, bf16[1,128,1024]{2,1,0:T(8,128)(2,1)S(1)}, u32[]{:S(2)}, u32[]{:S(2)}) %collective-permute-start.48) | collective-permute-done | bytes 262176 | tf_op jit(solution)/shard_map/ppermute | solution.py:23
  120.3 18.3 %collective-permute-done.57 = bf16[1,128,1024]{2,1,0:T(8,128)(2,1)S(1)} collective-permute-done((bf16[1,128,1024]{2,1,0:T(8,128)(2,1)S(1)}, bf16[1,128,1024]{2,1,0:T(8,128)(2,1)S(1)}, u32[]{:S(2)}, u32[]{:S(2)}) %collective-permute-start.57) | collective-permute-done | bytes 262176 | tf_op jit(solution)/shard_map/ppermute | solution.py:23
  182.1 11.8 %collective-permute-done.24 = bf16[3,512,128]{2,1,0:T(8,128)(2,1)S(1)} collective-permute-done((bf16[3,512,128]{2,1,0:T(8,128)(2,1)}, bf16[3,512,128]{2,1,0:T(8,128)(2,1)S(1)}, u32[]{:S(2)}, u32[]{:S(2)}) %collective-permute-start.24) | collective-permute-done | bytes 393248 | tf_op jit(solution)/shard_map/ppermute | solution.py:19
  200.1 7.5 collective-permute-done.40
  225.5 8.5 collective-permute-done.52
  234.8 7.6 collective-permute-done.14
  256.5 8.3 collective-permute-done.55
  266.6 55.4 %maximum_bitcast_fusion = bf16[1024,2048]{1,0:T(8,128)(2,1)} fusion(bf16[1,512,512]{2,1,0:T(8,128)(2,1)S(1)} %collective-permute-done.55, bf16[1,512,512]{2,1,0:T(8,128)(2,1)} %collective-permute-done.54, bf16[1,512,512]{2,1,0:T(8,128)(2,1)S(1)} %collective-permute-done.53, bf16[1,512,512]{2,1,0:T(8,128)(2,1)} %collective-permute-done.52, ...), kind=kLoop, calls=%fused_computation.53 | loop fusion | flops 58720256 | bytes 8388608 | tf_op jit(solution)/shard_map/squeeze | solution.py:277
  326.2 71.9 %maximum_bitcast_fusion.1 = bf16[1024,2048]{1,0:T(8,128)(2,1)} fusion(bf16[1,512,512]{2,1,0:T(8,128)(2,1)S(1)} %collective-permute-done.64, bf16[1,512,512]{2,1,0:T(8,128)(2,1)S(1)} %collective-permute-done.63, bf16[1,512,512]{2,1,0:T(8,128)(2,1)S(1)} %collective-permute-done.62, bf16[1,512,512]{2,1,0:T(8,128)(2,1)S(1)} %collective-permute-done.61, ...), kind=kLoop, calls=%fused_computation.54 | loop fusion | flops 58720256 | bytes 8388608 | tf_op jit(solution)/shard_map/squeeze | solution.py:278
  545.0 8.9 multiply_convert_fusion.4
  553.9 14.1 %fusion.4 = bf16[1024,2048]{1,0:T(8,128)(2,1)S(1)} fusion(f32[1024,2048]{1,0:T(8,128)} %get-tuple-element.145, bf16[1024,2048]{1,0:T(8,128)(2,1)S(1)} %copy-done.87, bf16[512,1024]{0,1:T(8,128)(2,1)} %collective-permute-done.71, bf16[512,1024]{0,1:T(8,128)(2,1)S(1)} %copy-done.120), kind=kOutput, calls=%fused_computation.14 | convolution fusion | flops 4345298944 | bytes 18874368 | tf_op jit(solution)/shard_map/dot_general | solution.py:27
  589.8 16.4 %collective-permute-done.114 = bf16[1,1024,512]{1,2,0:T(8,128)(2,1)S(1)} collective-permute-done((bf16[1,1024,512]{1,2,0:T(8,128)(2,1)S(1)}, bf16[1,1024,512]{1,2,0:T(8,128)(2,1)S(1)}, u32[]{:S(2)}, u32[]{:S(2)}) %collective-permute-start.114) | collective-permute-done | bytes 1048608 | tf_op jit(solution)/shard_map/ppermute | solution.py:19
  612.5 15.0 %collective-permute-done.107 = bf16[1,1024,512]{1,2,0:T(8,128)(2,1)S(1)} collective-permute-done((bf16[1,1024,512]{1,2,0:T(8,128)(2,1)S(1)}, bf16[1,1024,512]{1,2,0:T(8,128)(2,1)S(1)}, u32[]{:S(2)}, u32[]{:S(2)}) %collective-permute-start.107) | collective-permute-done | bytes 1048608 | tf_op jit(solution)/shard_map/ppermute | solution.py:19
  675.2 8.6 collective-permute-done.119
  690.7 14.8 %collective-permute-done.112 = bf16[1,128,1024]{2,1,0:T(8,128)(2,1)S(1)} collective-permute-done((bf16[1,128,1024]{2,1,0:T(8,128)(2,1)S(1)}, bf16[1,128,1024]{2,1,0:T(8,128)(2,1)S(1)}, u32[]{:S(2)}, u32[]{:S(2)}) %collective-permute-start.112) | collective-permute-done | bytes 262176 | tf_op jit(solution)/shard_map/ppermute | solution.py:23
  712.3 6.8 fusion.26
  738.5 10.1 multiply_reduce_fusion
  953.0 10.8 collective-permute-done.79
  1036.3 12.4 %collective-permute-done.98 = bf16[3,128,256]{2,1,0:T(8,128)(2,1)} collective-permute-done((bf16[3,128,256]{2,1,0:T(8,128)(2,1)}, bf16[3,128,256]{2,1,0:T(8,128)(2,1)}, u32[]{:S(2)}, u32[]{:S(2)}) %collective-permute-start.98) | collective-permute-done | bytes 196640 | tf_op jit(solution)/shard_map/ppermute | solution.py:23
  1050.7 9.6 collective-permute-done.84
  1064.3 12.1 %reduce-scatter.5.cloned.1.call-done = f32[256,128]{1,0:T(8,128)} async-done(((f32[256,1024]{1,0:T(8,128)}), f32[256,128]{1,0:T(8,128)}) %reduce-scatter.5.cloned.1.call-update) | async-done | bytes 131088 | tf_op jit(solution)/shard_map/reduce_scatter | solution.py:438
  1079.8 19.5 %all-reduce.6.cloned.1.call-done = f32[256,128]{1,0:T(8,128)} async-done(((f32[256,128]{1,0:T(8,128)}), f32[256,128]{1,0:T(8,128)}) %all-reduce.6.cloned.1.call-update) | async-done | bytes 131088 | tf_op jit(solution)/shard_map/psum | solution.py:439
  (1250 shorter events, 709.0 us)
Async XLA Ops:
  7.2 993.9 %reduce-scatter.7.cloned.1.call-start = ((), (), s32[]{:S(2)}) async-start(), calls=%async_computation.4 | async-start | bytes 589824
  42.0 52.8 %collective-permute-start.8 = (bf16[3,128,256]{2,1,0:T(8,128)(2,1)}, bf16[3,128,256]{2,1,0:T(8,128)(2,1)S(1)}, u32[]{:S(2)}, u32[]{:S(2)}) collective-permute-start(bf16[3,128,256]{2,1,0:T(8,128)(2,1)} %bitcast.759), channel_id=1, source_target_pairs={{0,24},{8,0},{16,8},{24,16},{1,25},{9,1},{17,9},{25,17},{2,26},{10... | collective-permute-start | bytes 589832 | tf_op jit(solution)/shard_map/ppermute | solution.py:23
  247.0 75.0 %collective-permute-start.41 = (bf16[1,512,128]{2,1,0:T(8,128)(2,1)}, bf16[1,512,128]{2,1,0:T(8,128)(2,1)}, u32[]{:S(2)}, u32[]{:S(2)}) collective-permute-start(bf16[1,512,128]{2,1,0:T(8,128)(2,1)} %pad_maximum_fusion.71), channel_id=1, source_target_pairs={{0,4},{4,0},{1,5},{5,1},{2,6},{6,2},{3,7},{7,3},{8,12},{12,8},{9,1... | collective-permute-start | bytes 393224 | tf_op jit(solution)/shard_map/ppermute | solution.py:19
  254.4 68.8 %collective-permute-start.63 = (bf16[1,512,512]{2,1,0:T(8,128)(2,1)S(1)}, bf16[1,512,512]{2,1,0:T(8,128)(2,1)S(1)}, u32[]{:S(2)}, u32[]{:S(2)}) collective-permute-start(bf16[1,512,512]{2,1,0:T(8,128)(2,1)S(1)} %copy-done.205), channel_id=1, source_target_pairs={{0,4},{4,0},{1,5},{5,1},{2,6},{6,2},{3,7},{7,3},{8,12},{12,8},{9,1... | collective-permute-start | bytes 1572872 | tf_op jit(solution)/shard_map/ppermute | solution.py:19
  255.6 68.7 %collective-permute-start.59 = (bf16[1,512,512]{2,1,0:T(8,128)(2,1)S(1)}, bf16[1,512,512]{2,1,0:T(8,128)(2,1)S(1)}, u32[]{:S(2)}, u32[]{:S(2)}) collective-permute-start(bf16[1,512,512]{2,1,0:T(8,128)(2,1)S(1)} %copy-done.204), channel_id=1, source_target_pairs={{0,2},{2,0},{1,3},{3,1},{4,6},{6,4},{5,7},{7,5},{8,10},{10,8},{9,1... | collective-permute-start | bytes 1572872 | tf_op jit(solution)/shard_map/ppermute | solution.py:19
  264.8 60.4 %collective-permute-start.64 = (bf16[1,512,512]{2,1,0:T(8,128)(2,1)S(1)}, bf16[1,512,512]{2,1,0:T(8,128)(2,1)S(1)}, u32[]{:S(2)}, u32[]{:S(2)}) collective-permute-start(bf16[1,512,512]{2,1,0:T(8,128)(2,1)S(1)} %collective-permute-done.60), channel_id=1, source_target_pairs={{0,4},{4,0},{1,5},{5,1},{2,6},{6,2},{3,7},{7,3},{8,12},{12,8},{9,1... | collective-permute-start | bytes 1572872 | tf_op jit(solution)/shard_map/ppermute | solution.py:19
  265.6 60.5 %collective-permute-start.62 = (bf16[1,512,512]{2,1,0:T(8,128)(2,1)S(1)}, bf16[1,512,512]{2,1,0:T(8,128)(2,1)S(1)}, u32[]{:S(2)}, u32[]{:S(2)}) collective-permute-start(bf16[1,512,512]{2,1,0:T(8,128)(2,1)S(1)} %collective-permute-done.61), channel_id=1, source_target_pairs={{0,2},{2,0},{1,3},{3,1},{4,6},{6,4},{5,7},{7,5},{8,10},{10,8},{9,1... | collective-permute-start | bytes 1572872 | tf_op jit(solution)/shard_map/ppermute | solution.py:19
  322.1 188.3 %collective-permute-start.43 = (bf16[1,512,128]{2,1,0:T(8,128)(2,1)}, bf16[1,512,128]{2,1,0:T(8,128)(2,1)}, u32[]{:S(2)}, u32[]{:S(2)}) collective-permute-start(bf16[1,512,128]{2,1,0:T(8,128)(2,1)} %pad_maximum_fusion.72), channel_id=1, source_target_pairs={{0,4},{4,0},{1,5},{5,1},{2,6},{6,2},{3,7},{7,3},{8,12},{12,8},{9,1... | collective-permute-start | bytes 393224 | tf_op jit(solution)/shard_map/ppermute | solution.py:19
  323.2 187.3 %collective-permute-start.39 = (bf16[1,512,128]{2,1,0:T(8,128)(2,1)}, bf16[1,512,128]{2,1,0:T(8,128)(2,1)}, u32[]{:S(2)}, u32[]{:S(2)}) collective-permute-start(bf16[1,512,128]{2,1,0:T(8,128)(2,1)} %pad_maximum_fusion.71), channel_id=1, source_target_pairs={{0,2},{2,0},{1,3},{3,1},{4,6},{6,4},{5,7},{7,5},{8,10},{10,8},{9,1... | collective-permute-start | bytes 393224 | tf_op jit(solution)/shard_map/ppermute | solution.py:19
  324.4 186.1 %collective-permute-start.44 = (bf16[1,512,128]{2,1,0:T(8,128)(2,1)}, bf16[1,512,128]{2,1,0:T(8,128)(2,1)}, u32[]{:S(2)}, u32[]{:S(2)}) collective-permute-start(bf16[1,512,128]{2,1,0:T(8,128)(2,1)} %collective-permute-done.40), channel_id=1, source_target_pairs={{0,4},{4,0},{1,5},{5,1},{2,6},{6,2},{3,7},{7,3},{8,12},{12,8},{9,1... | collective-permute-start | bytes 393224 | tf_op jit(solution)/shard_map/ppermute | solution.py:19
  325.2 185.3 %collective-permute-start.42 = (bf16[1,512,128]{2,1,0:T(8,128)(2,1)}, bf16[1,512,128]{2,1,0:T(8,128)(2,1)}, u32[]{:S(2)}, u32[]{:S(2)}) collective-permute-start(bf16[1,512,128]{2,1,0:T(8,128)(2,1)} %collective-permute-done.41), channel_id=1, source_target_pairs={{0,2},{2,0},{1,3},{3,1},{4,6},{6,4},{5,7},{7,5},{8,10},{10,8},{9,1... | collective-permute-start | bytes 393224 | tf_op jit(solution)/shard_map/ppermute | solution.py:19
  326.1 72.0 %collective-permute-start.5 = (bf16[512,1024]{0,1:T(8,128)(2,1)S(1)}, bf16[512,1024]{0,1:T(8,128)(2,1)S(1)}, u32[]{:S(2)}, u32[]{:S(2)}) collective-permute-start(bf16[512,1024]{0,1:T(8,128)(2,1)S(1)} %copy-done.146), channel_id=1, source_target_pairs={{0,1},{1,0},{2,3},{3,2},{4,5},{5,4},{6,7},{7,6},{8,9},{9,8},{10,11... | collective-permute-start | bytes 3145736 | tf_op jit(solution)/shard_map/ppermute | solution.py:19
  481.2 72.6 %collective-permute-start.71 = (bf16[512,1024]{0,1:T(8,128)(2,1)}, bf16[512,1024]{0,1:T(8,128)(2,1)}, u32[]{:S(2)}, u32[]{:S(2)}) collective-permute-start(bf16[512,1024]{0,1:T(8,128)(2,1)} %copy-done.119), channel_id=1, source_target_pairs={{0,1},{1,0},{2,3},{3,2},{4,5},{5,4},{6,7},{7,6},{8,9},{9,8},{10,11... | collective-permute-start | bytes 3145736 | tf_op jit(solution)/shard_map/ppermute | solution.py:19
  510.4 297.0 %collective-permute-start.67 = (bf16[256,1024]{1,0:T(8,128)(2,1)}, bf16[256,1024]{1,0:T(8,128)(2,1)}, u32[]{:S(2)}, u32[]{:S(2)}) collective-permute-start(bf16[256,1024]{1,0:T(8,128)(2,1)} %slice.1355), channel_id=1, source_target_pairs={{0,1},{1,0},{2,3},{3,2},{4,5},{5,4},{6,7},{7,6},{8,9},{9,8},{10,11... | collective-permute-start | bytes 1572872 | tf_op jit(solution)/shard_map/ppermute | solution.py:19
  651.6 54.8 %collective-permute-start.73 = (bf16[512,1024]{0,1:T(8,128)(2,1)}, bf16[512,1024]{0,1:T(8,128)(2,1)}, u32[]{:S(2)}, u32[]{:S(2)}) collective-permute-start(bf16[512,1024]{0,1:T(8,128)(2,1)} %get-tuple-element.24), channel_id=1, source_target_pairs={{0,1},{1,0},{2,3},{3,2},{4,5},{5,4},{6,7},{7,6},{8,9},{9,8},{10,11... | collective-permute-start | bytes 3145736 | tf_op jit(solution)/shard_map/ppermute | solution.py:19
  816.5 63.9 %collective-permute-start.68 = (bf16[256,1024]{1,0:T(8,128)(2,1)}, bf16[256,1024]{1,0:T(8,128)(2,1)}, u32[]{:S(2)}, u32[]{:S(2)}) collective-permute-start(bf16[256,1024]{1,0:T(8,128)(2,1)} %bitcast.548), channel_id=1, source_target_pairs={{0,2},{2,0},{1,3},{3,1},{4,6},{6,4},{5,7},{7,5},{8,10},{10,8},{9,1... | collective-permute-start | bytes 1572872 | tf_op jit(solution)/shard_map/ppermute | solution.py:19
  883.0 107.3 %collective-permute-start.69 = (bf16[2,256,1024]{2,1,0:T(8,128)(2,1)}, bf16[2,256,1024]{2,1,0:T(8,128)(2,1)}, u32[]{:S(2)}, u32[]{:S(2)}) collective-permute-start(bf16[2,256,1024]{2,1,0:T(8,128)(2,1)} %reverse_select_fusion), channel_id=1, source_target_pairs={{0,1},{1,0},{2,3},{3,2},{4,5},{5,4},{6,7},{7,6},{8,9},{9,8},{10,11... | collective-permute-start | bytes 3145736 | tf_op jit(solution)/shard_map/ppermute | solution.py:19
  938.4 138.0 %reduce-scatter.5.cloned.1.call-start = ((), (), s32[]{:S(2)}) async-start(), calls=%async_computation.2 | async-start | bytes 1179648 | tf_op jit(solution)/shard_map/reduce_scatter | solution.py:438
  940.7 158.6 %all-reduce.6.cloned.1.call-start = ((), (), s32[]{:S(2)}) async-start(), calls=%async_computation.3 | async-start | bytes 262144 | tf_op jit(solution)/shard_map/psum | solution.py:439
  948.4 59.8 %collective-permute-start.94 = (bf16[3,512,128]{1,2,0:T(8,128)(2,1)S(1)}, bf16[3,512,128]{1,2,0:T(8,128)(2,1)}, u32[]{:S(2)}, u32[]{:S(2)}) collective-permute-start(bf16[3,512,128]{1,2,0:T(8,128)(2,1)S(1)} %slice.962), channel_id=1, source_target_pairs={{0,4},{4,0},{1,5},{5,1},{2,6},{6,2},{3,7},{7,3},{8,12},{12,8},{9,1... | collective-permute-start | bytes 1179656 | tf_op jit(solution)/shard_map/ppermute | solution.py:19
  952.4 56.9 %collective-permute-start.96 = (bf16[3,512,128]{1,2,0:T(8,128)(2,1)}, bf16[3,512,128]{1,2,0:T(8,128)(2,1)}, u32[]{:S(2)}, u32[]{:S(2)}) collective-permute-start(bf16[3,512,128]{1,2,0:T(8,128)(2,1)} %slice.966), channel_id=1, source_target_pairs={{0,2},{2,0},{1,3},{3,1},{4,6},{6,4},{5,7},{7,5},{8,10},{10,8},{9,1... | collective-permute-start | bytes 1179656 | tf_op jit(solution)/shard_map/ppermute | solution.py:19
  966.0 55.6 %collective-permute-start.80 = (bf16[3,512,128]{1,2,0:T(8,128)(2,1)}, bf16[3,512,128]{1,2,0:T(8,128)(2,1)}, u32[]{:S(2)}, u32[]{:S(2)}) collective-permute-start(bf16[3,512,128]{1,2,0:T(8,128)(2,1)} %slice.928), channel_id=1, source_target_pairs={{0,4},{4,0},{1,5},{5,1},{2,6},{6,2},{3,7},{7,3},{8,12},{12,8},{9,1... | collective-permute-start | bytes 1179656 | tf_op jit(solution)/shard_map/ppermute | solution.py:19
  969.7 53.1 %collective-permute-start.82 = (bf16[3,512,128]{1,2,0:T(8,128)(2,1)}, bf16[3,512,128]{1,2,0:T(8,128)(2,1)}, u32[]{:S(2)}, u32[]{:S(2)}) collective-permute-start(bf16[3,512,128]{1,2,0:T(8,128)(2,1)} %slice.937), channel_id=1, source_target_pairs={{0,2},{2,0},{1,3},{3,1},{4,6},{6,4},{5,7},{7,5},{8,10},{10,8},{9,1... | collective-permute-start | bytes 1179656 | tf_op jit(solution)/shard_map/ppermute | solution.py:19
  990.3 71.9 %collective-permute-start.78 = (bf16[256,1024]{1,0:T(8,128)(2,1)}, bf16[256,1024]{1,0:T(8,128)(2,1)}, u32[]{:S(2)}, u32[]{:S(2)}) collective-permute-start(bf16[256,1024]{1,0:T(8,128)(2,1)} %bitcast.719), channel_id=1, source_target_pairs={{0,2},{2,0},{1,3},{3,1},{4,6},{6,4},{5,7},{7,5},{8,10},{10,8},{9,1... | collective-permute-start | bytes 1572872 | tf_op jit(solution)/shard_map/ppermute | solution.py:19
  (395 other events, 8147.5 us)
Sparse Core Ops, SparseCore 0:
  938.5 62.5 reduce-scatter.6
  1004.9 71.4 reduce-scatter.4
  1078.7 20.4 all-reduce.5

commit v2 on v1

v2 whole, which is shorter than its diff:
```python
import functools

import jax
import jax.numpy as jnp
from jax import lax
from jax.experimental import pallas as pl
from jax.experimental.pallas import tpu as pltpu
from jax.sharding import Mesh
from jax.sharding import PartitionSpec as P

HEAD_DIM = 128
BLOCK = 512
EPSILON = 1e-06
MASKED = -1e30
GELU = 0.7978845608028654
RING = 4
BF = jnp.bfloat16
F32 = jnp.float32


def swap(array, axis):
    return lax.ppermute(array, axis, [(0, 1), (1, 0)])


def turn(array, steps):
    return lax.ppermute(array, "z", [(i, (i + steps) % RING) for i in range(RING)])


def matmul(left, right, contract):
    return lax.dot_general(
        left, right, (contract, ((), ())), preferred_element_type=jnp.float32
    )


def mm(left, right):
    return matmul(left, right, ((1,), (0,)))


def mm_nt(left, right):
    return matmul(left, right, ((1,), (1,)))


def mm_tn(left, right):
    return matmul(left, right, ((0,), (0,)))


def width_places():
    z, x = lax.axis_index("z"), lax.axis_index("x")
    return [lax.rem(z - k + RING, RING) * 2 + jnp.bitwise_xor(x, dx) for dx in range(2) for k in range(RING)]


def take_pieces(array, places):
    groups = lax.axis_size("r")
    lead, width = array.shape[:-1], array.shape[-1]
    split = array.reshape(lead + (groups, len(places), width // (groups * len(places))))
    axis = len(lead) + 1
    return [lax.dynamic_index_in_dim(split, place, axis, keepdims=False) for place in places]


def to_local(array):
    pieces = take_pieces(array, width_places())
    lead = array.shape[:-1]
    return jnp.concatenate([p.reshape(lead + (-1,)) for p in pieces], axis=-1)


def from_local(array):
    z, x = lax.axis_index("z"), lax.axis_index("x")
    groups = lax.axis_size("r")
    lead, width = array.shape[:-1], array.shape[-1]
    split = array.reshape(lead + (2 * RING, groups, width // (groups * 2 * RING)))
    axis = len(lead)
    pieces = []
    for z_to in range(RING):
        for x_to in range(2):
            place = jnp.bitwise_xor(x, x_to) * RING + lax.rem(z - z_to + RING, RING)
            pieces.append(lax.dynamic_index_in_dim(split, place, axis, keepdims=False))
    return jnp.stack(pieces, axis=axis + 1).reshape(array.shape)


def gather_groups(array, axis):
    if lax.axis_size("r") == 1:
        return array
    return lax.all_gather(array, "r", axis=axis, tiled=True)


def scatter_groups(array, axis):
    if lax.axis_size("r") == 1:
        return array
    return lax.psum_scatter(array, "r", scatter_dimension=axis, tiled=True)


def call(kernel, grid, inputs, in_specs, outputs, out_specs, flops=0, exps=0, **more):
    block_bytes = sum(a.size * a.dtype.itemsize for a in inputs)
    shapes = [jax.ShapeDtypeStruct(shape, dtype) for shape, dtype in outputs]
    out_bytes = sum(s.size * s.dtype.itemsize for s in shapes)
    return pl.pallas_call(
        kernel,
        grid=grid,
        in_specs=in_specs,
        out_specs=out_specs,
        out_shape=shapes,
        compiler_params=pltpu.CompilerParams(vmem_limit_bytes=48 * 2**20),
        cost_estimate=pl.CostEstimate(
            flops=flops, bytes_accessed=block_bytes + out_bytes, transcendentals=exps
        ),
        **more,
    )(*inputs)


def whole(array):
    return pl.BlockSpec(array.shape, lambda *_: (0,) * array.ndim)


def whole_out(shape):
    return pl.BlockSpec(shape, lambda *_: (0,) * len(shape))


def stack_rows(pieces):
    half = len(pieces) // 2
    rows, width = pieces[0].shape

    def kernel(*refs):
        ins, outs, sem = refs[: len(pieces)], refs[len(pieces) : -1], refs[-1]
        copies = [
            pltpu.make_async_copy(
                piece, outs[i // half].at[pl.ds((i % half) * rows, rows)], sem.at[i]
            )
            for i, piece in enumerate(ins)
        ]
        for copy in copies:
            copy.start()
        for copy in copies:
            copy.wait()

    anywhere = pl.BlockSpec(memory_space=pl.ANY)
    return call(
        kernel,
        (),
        pieces,
        [anywhere] * len(pieces),
        [((half * rows, width), BF)] * 2,
        [anywhere] * 2,
        scratch_shapes=[pltpu.SemaphoreType.DMA((len(pieces),))],
    )


def gather_weight(shard):
    shard = gather_groups(shard, 0)
    low, high = stack_rows([shard] + [turn(shard, k) for k in range(1, RING)])
    low_x, low_y = swap(low, "x"), swap(low, "y")
    high_y, high_x = swap(high, "y"), swap(high, "x")
    low_xy, high_xy = swap(low_x, "y"), swap(high_y, "x")
    return [[[low, high], [low_x, high_x]], [[low_y, high_y], [low_xy, high_xy]]]


def flat_pieces(pieces):
    return [pieces[y][x][half] for y in range(2) for x in range(2) for half in range(2)]


def gather_rows(shard):
    if lax.axis_size("r") > 1:
        shard = lax.all_gather(shard, "r", axis=1, tiled=True)
    near = jnp.concatenate([shard] + [turn(shard, k) for k in range(1, RING)], axis=1)
    return jnp.concatenate([near, swap(near, "x")], axis=1)


def row_order(own, other, blocks):
    per = own.shape[0] // blocks
    parts = []
    for b in range(blocks):
        parts += [own[b * per : (b + 1) * per], other[b * per : (b + 1) * per]]
    return jnp.concatenate(parts, axis=0)


def project(own, other, pieces, column, width, block, blocks=1, gate=None, activate=False):
    rows = own.shape[0] * 2
    refs = flat_pieces(pieces)
    first = column // block

    def kernel(*args):
        own_ref, other_ref, weights = args[0], args[1], args[2:10]
        left = row_order(own_ref[...], other_ref[...], blocks)
        for y in range(2):
            weight = jnp.concatenate([ref[...] for ref in weights[4 * y : 4 * y + 4]], axis=0)
            total = mm(left, weight)
            if gate is not None:
                gate_ref, out_ref = args[10], args[11]
                low = total.astype(BF).astype(F32)
                out_ref[y] = (low * gate_ref[y].astype(F32)).astype(BF)
            elif activate:
                act_ref, slope_ref = args[10], args[11]
                cubic = 0.044715 * total * total * total
                inner = GELU * (total + cubic)
                curve = jnp.tanh(inner)
                act_ref[y] = (0.5 * total * (1.0 + curve)).astype(BF)
                slope = 0.5 * (1.0 + curve) + 0.5 * total * (1.0 - curve * curve) * (
                    GELU * (1.0 + 3.0 * 0.044715 * total * total)
                )
                slope_ref[y] = slope.astype(BF)
            else:
                args[10][y] = total.astype(BF)

    spec = pl.BlockSpec((2, rows, block), lambda j: (0, 0, j))
    weight_spec = [pl.BlockSpec((ref.shape[0], block), lambda j: (0, first + j)) for ref in refs]
    extra = [] if gate is None else [gate]
    count = 2 if activate else 1
    out = call(
        kernel,
        (width // block,),
        [own, other] + refs + extra,
        [whole(own), whole(other)] + weight_spec + [spec] * len(extra),
        [((2, rows, width), BF)] * count,
        [spec] * count,
        flops=4 * rows * own.shape[1] * width,
    )
    return out if activate else out[0]


def merge(lefts, pieces, column, blocks=1):
    refs = flat_pieces(pieces)
    columns = lefts[0].shape[2]
    rows = sum(left.shape[1] for left in lefts)
    width = 8 * refs[0].shape[0] // 2
    first = column // columns
    count = len(lefts)

    def kernel(*args):
        left_refs, weights = args[:count], args[count : count + 8]
        own_ref, other_ref = args[count + 8 :]
        sides = [
            jnp.concatenate([ref[...] for ref in weights[4 * y : 4 * y + 4]], axis=0) for y in range(2)
        ]
        per = rows // (2 * blocks)
        for core, out_ref in ((1, other_ref), (0, own_ref)):
            total = None
            for y in range(2):
                parts = []
                for b in range(blocks):
                    begin = (2 * b + core) * per
                    index, within = begin // left_refs[0].shape[1], begin % left_refs[0].shape[1]
                    parts.append(left_refs[index][y, within : within + per])
                piece = mm_nt(jnp.concatenate(parts, axis=0), sides[y])
                total = piece if total is None else total + piece
            out_ref[...] = total.astype(out_ref.dtype)

    weight_spec = [pl.BlockSpec((ref.shape[0], columns), lambda i: (0, first)) for ref in refs]
    return call(
        kernel,
        (1,),
        list(lefts) + refs,
        [whole(left) for left in lefts] + weight_spec,
        [((rows // 2, width), F32), ((rows // 2, width), BF)],
        [whole_out((rows // 2, width))] * 2,
        flops=4 * rows * width * columns,
    )


def outer(lefts, rights, block, blocks=1):
    width = lefts[0][0].shape[1]
    columns = rights[0].shape[2]
    half = width // 2
    count = len(lefts)
    flat = [array for pair in lefts for array in pair]

    def kernel(*args):
        left_refs, right_refs = args[: 2 * count], args[2 * count : 3 * count]
        low11, high11, out10, out01, out00 = args[3 * count :]
        left = jnp.concatenate(
            [row_order(left_refs[2 * i][...], left_refs[2 * i + 1][...], blocks) for i in range(count)], axis=0
        )
        for y in (1, 0):
            right = jnp.concatenate([ref[y] for ref in right_refs], axis=0)
            for x in (1, 0):
                total = mm_tn(left[:, x * half : (x + 1) * half], right).astype(BF)
                if x and y:
                    low11[...] = total[: half // 2]
                    high11[...] = total[half // 2 :]
                else:
                    {(1, 0): out10, (0, 1): out01, (0, 0): out00}[(x, y)][...] = total

    return call(
        kernel,
        (columns // block,),
        flat + list(rights),
        [whole(array) for array in flat]
        + [pl.BlockSpec((2, right.shape[1], block), lambda j: (0, 0, j)) for right in rights],
        [((half // 2, columns), BF)] * 2 + [((half, columns), BF)] * 3,
        [pl.BlockSpec((half // 2, block), lambda j: (0, j))] * 2
        + [pl.BlockSpec((half, block), lambda j: (0, j))] * 3,
        flops=4 * width * columns * sum(right.shape[1] for right in rights),
    )


def add_into(array, piece, half):
    rows, columns = piece.shape

    def kernel(array_ref, piece_ref, out_ref):
        out_ref[...] = (array_ref[...].astype(F32) + piece_ref[...].astype(F32)).astype(BF)

    return call(
        kernel,
        (1,),
        [array, piece],
        [pl.BlockSpec((rows, columns), lambda i: (half, 0)), pl.BlockSpec((rows, columns), lambda i: (0, 0))],
        [(array.shape, BF)],
        [pl.BlockSpec((rows, columns), lambda i: (half, 0))],
        input_output_aliases={0: 0},
    )[0]


def add_split(first, second, third):
    rows, columns = first.shape
    part = rows // RING

    def kernel(a_ref, b_ref, c_ref, *outs):
        for k, out_ref in enumerate(outs):
            piece = slice(k * part, (k + 1) * part)
            total = a_ref[piece].astype(F32) + b_ref[piece].astype(F32) + c_ref[piece].astype(F32)
            out_ref[...] = total.astype(out_ref.dtype)

    return call(
        kernel,
        (),
        [first, second, third],
        [whole(first)] * 3,
        [((part, columns), F32)] + [((part, columns), BF)] * (RING - 1),
        [whole_out((part, columns))] * RING,
    )


def reduce_weight(quarters):
    low11, high11, out10, out01, out00 = quarters
    low_got, high_got = swap(low11, "y"), swap(high11, "x")
    x_got = swap(add_into(out10, low_got, 0), "x")
    y_got = swap(add_into(out01, high_got, 1), "y")
    pieces = add_split(out00, x_got, y_got)
    total = pieces[0]
    for k in range(1, RING):
        total = total + turn(pieces[k], RING - k).astype(F32)
    return scatter_groups(total, 0)


def rms_inverse(values):
    return lax.rsqrt(jnp.mean(values * values, axis=-1, keepdims=True) + EPSILON)


def rms_forward(values, gain):
    return (values * rms_inverse(values) * gain).astype(BF)


def rms_backward(values, gain, grad):
    inverse = rms_inverse(values)
    scaled = values * inverse
    weighted = grad * gain
    grad_values = inverse * (weighted - scaled * jnp.mean(scaled * weighted, axis=-1, keepdims=True))
    return grad_values, jnp.sum(grad * scaled, axis=0)


def pair(own):
    return own, swap(own, "c")


def fold(both):
    own, other = both
    return own + swap(other, "c").astype(F32)


SCALE = HEAD_DIM ** (-0.5)


def key_tiles(b, j):
    tiles = []
    if b > 0:
        tiles += [(b - 1, jj, "after" if jj == j else "all") for jj in range(j, 2)]
    tiles += [(b, jj, "until" if jj == j else "all") for jj in range(j + 1)]
    return tiles


def tile_mask(kind, size, limit):
    rows = lax.broadcasted_iota(jnp.int32, (size, size), 0)
    columns = lax.broadcasted_iota(jnp.int32, (size, size), 1)
    mask = None
    if kind == "after":
        mask = columns > rows
    if kind == "until":
        mask = columns <= rows
    if limit is not None:
        inside = columns < limit
        mask = inside if mask is None else mask & inside
    return mask


def masked_scores(queries, keys, masks):
    scores = mm_nt(queries, keys) * SCALE
    parts, place = [], 0
    for size, mask in masks:
        part = scores[:, place : place + size]
        parts.append(part if mask is None else jnp.where(mask, part, MASKED))
        place += size
    return jnp.concatenate(parts, axis=1)


def attention_plan(b, last, size, core, count, states):
    def start(block, j):
        return pl.multiple_of(block * 2 * size + jnp.bitwise_xor(core, j) * size, size)

    plan = []
    for j in range(2):
        tiles, masks = [], []
        for block, jj, kind in key_tiles(b, j):
            limit = count - jj * size if block == b and last else None
            tiles.append((block, jj))
            masks.append((size, tile_mask(kind, size, limit)))
        plan.append((tiles, masks + [(states, None)]))
    state_masks = [(states, None)]
    for jj in range(2):
        state_masks.append((size, tile_mask("all", size, count - jj * size if last else None)))
    return start, plan, state_masks


def attend_forward(b, blocks, info, tokens, states):
    lanes = tokens.shape[2] // 3
    heads = lanes // HEAD_DIM
    size = BLOCK // 2
    count_states = states.shape[1]

    def one(queries, keys, values, masks):
        scores = masked_scores(queries, keys, masks)
        top = jnp.max(scores, axis=1, keepdims=True)
        weights = jnp.exp(scores - top)
        total = jnp.sum(weights, axis=1, keepdims=True)
        mixed = mm(weights.astype(BF), values) / total
        return mixed.astype(BF), top + jnp.log(total)

    def kernel(info_ref, token_ref, state_ref, mixed_ref, state_mixed_ref, log_ref):
        start, plan, state_masks = attention_plan(
            b, b == blocks - 1, size, info_ref[0], info_ref[1], count_states
        )
        for h in range(heads):
            query, key, value = [slice(p * lanes + h * HEAD_DIM, p * lanes + (h + 1) * HEAD_DIM) for p in range(3)]
            own = slice(h * HEAD_DIM, (h + 1) * HEAD_DIM)

            def token_rows(places, columns):
                return [token_ref[0, pl.ds(start(*place), size), columns] for place in places]

            for j, (tiles, masks) in enumerate(plan):
                keys = jnp.concatenate(token_rows(tiles, key) + [state_ref[0, :, key]], axis=0)
                values = jnp.concatenate(token_rows(tiles, value) + [state_ref[0, :, value]], axis=0)
                mixed, log_total = one(token_ref[0, pl.ds(start(b, j), size), query], keys, values, masks)
                mixed_ref[0, pl.ds(start(0, j), size), own] = mixed
                log_ref[0, pl.ds(start(0, j), size), h : h + 1] = log_total
            tiles = [(b, 0), (b, 1)]
            keys = jnp.concatenate([state_ref[0, :, key]] + token_rows(tiles, key), axis=0)
            values = jnp.concatenate([state_ref[0, :, value]] + token_rows(tiles, value), axis=0)
            for begin in range(0, count_states, size):
                rows = slice(begin, begin + size)
                mixed, log_total = one(state_ref[0, rows, query], keys, values, state_masks)
                state_mixed_ref[0, rows, own] = mixed
                log_ref[0, rows, heads + h : heads + h + 1] = log_total

    rows = (b + 1) * BLOCK
    pairs = 2 * heads * (BLOCK * (BLOCK * (2 if b else 1) + count_states) + count_states * (count_states + BLOCK))
    spec = lambda n, w: pl.BlockSpec((1, n, w), lambda y: (y, 0, 0))
    return call(
        kernel,
        (2,),
        [info, tokens, states],
        [pl.BlockSpec(memory_space=pltpu.SMEM), spec(rows, 3 * lanes), spec(count_states, 3 * lanes)],
        [((2, BLOCK, lanes), BF), ((2, count_states, lanes), BF), ((2, BLOCK, 128), F32)],
        [spec(BLOCK, lanes), spec(count_states, lanes), spec(BLOCK, 128)],
        flops=4 * pairs * HEAD_DIM,
        exps=pairs,
    )


def attend_backward(b, blocks, info, tokens, states, logs, grad_mixed, grad_state_mixed, later):
    lanes = tokens.shape[2] // 3
    heads = lanes // HEAD_DIM
    size = BLOCK // 2
    count_states = states.shape[1]
    is_last = b == blocks - 1

    def one(queries, keys, values, masks, log_total, grad):
        scores = masked_scores(queries, keys, masks)
        probs = jnp.exp(scores - log_total)
        grad_probs = mm_nt(grad, values)
        row_sum = jnp.sum(grad_probs * probs, axis=1, keepdims=True)
        low = (probs * (grad_probs - row_sum)).astype(BF)
        return mm(low, keys) * SCALE, mm_tn(low, queries) * SCALE, mm_tn(probs.astype(BF), grad)

    def kernel(*args):
        info_ref, token_ref, state_ref, log_ref, grad_ref, state_grad_ref = args[:6]
        rest = list(args[6:])
        later_ref = None if is_last else rest.pop(0)
        out_ref, state_out_ref = rest.pop(0), rest.pop(0)
        before_ref = rest.pop(0) if b > 0 else None
        start, plan, state_masks = attention_plan(b, is_last, size, info_ref[0], info_ref[1], count_states)
        for h in range(heads):
            query, key, value = [slice(p * lanes + h * HEAD_DIM, p * lanes + (h + 1) * HEAD_DIM) for p in range(3)]
            own = slice(h * HEAD_DIM, (h + 1) * HEAD_DIM)

            def token_rows(places, columns):
                return [token_ref[0, pl.ds(start(*place), size), columns] for place in places]

            sums = {}

            def gather(places, grads):
                begin = 0
                for place in places:
                    rows = count_states if place == "state" else size
                    part = grads[begin : begin + rows]
                    begin += rows
                    yield place, part

            def collect(name, places, grads):
                for place, part in gather(places, grads):
                    full = (name, place)
                    sums[full] = part if full not in sums else sums[full] + part

            places = ["state", (b, 0), (b, 1)]
            keys = jnp.concatenate([state_ref[0, :, key]] + token_rows(places[1:], key), axis=0)
            values = jnp.concatenate([state_ref[0, :, value]] + token_rows(places[1:], value), axis=0)
            for begin in range(0, count_states, size):
                rows = slice(begin, begin + size)
                dq, dk, dv = one(
                    state_ref[0, rows, query],
                    keys,
                    values,
                    state_masks,
                    log_ref[0, rows, heads + h : heads + h + 1],
                    state_grad_ref[0, rows, own],
                )
                state_out_ref[0, rows, query] = dq.astype(BF)
                collect("k", places, dk)
                collect("v", places, dv)
            for j, (tiles, masks) in enumerate(plan):
                keys = jnp.concatenate(token_rows(tiles, key) + [state_ref[0, :, key]], axis=0)
                values = jnp.concatenate(token_rows(tiles, value) + [state_ref[0, :, value]], axis=0)
                here = pl.ds(start(0, j), size)
                dq, dk, dv = one(
                    token_ref[0, pl.ds(start(b, j), size), query],
                    keys,
                    values,
                    masks,
                    log_ref[0, here, h : h + 1],
                    grad_ref[0, here, own],
                )
                out_ref[0, here, query] = dq.astype(BF)
                collect("k", tiles + ["state"], dk)
                collect("v", tiles + ["state"], dv)
            state_out_ref[0, :, key] = sums[("k", "state")].astype(BF)
            state_out_ref[0, :, value] = sums[("v", "state")].astype(BF)
            for name, columns in (("k", key), ("v", value)):
                shift = slice(columns.start - lanes, columns.stop - lanes)
                for j in range(2):
                    here = pl.ds(start(0, j), size)
                    total = sums[(name, (b, j))]
                    if later_ref is not None:
                        total = total + later_ref[0, here, shift]
                    out_ref[0, here, columns] = total.astype(BF)
                    if before_ref is not None:
                        before_ref[0, here, shift] = sums[(name, (b - 1, j))]

    rows = (b + 1) * BLOCK
    pairs = 2 * heads * (BLOCK * (BLOCK * (2 if b else 1) + count_states) + count_states * (count_states + BLOCK))
    spec = lambda n, w: pl.BlockSpec((1, n, w), lambda y: (y, 0, 0))
    inputs = [info, tokens, states, logs, grad_mixed, grad_state_mixed]
    in_specs = [
        pl.BlockSpec(memory_space=pltpu.SMEM),
        spec(rows, 3 * lanes),
        spec(count_states, 3 * lanes),
        spec(BLOCK, 128),
        pl.BlockSpec((1, BLOCK, lanes), lambda y: (y, b, 0)),
        spec(count_states, lanes),
    ]
    outputs = [((2, BLOCK, 3 * lanes), BF), ((2, count_states, 3 * lanes), BF)]
    out_specs = [spec(BLOCK, 3 * lanes), spec(count_states, 3 * lanes)]
    if not is_last:
        inputs.append(later)
        in_specs.append(spec(BLOCK, 2 * lanes))
    if b > 0:
        outputs.append(((2, BLOCK, 2 * lanes), F32))
        out_specs.append(spec(BLOCK, 2 * lanes))
    out = call(
        kernel, (2,), inputs, in_specs, outputs, out_specs, flops=10 * pairs * HEAD_DIM, exps=pairs
    )
    return out if b > 0 else (out[0], out[1], None)


def body(
    tokens,
    counts,
    token_weights,
    token_output,
    state_weights,
    state_output,
    hidden_up,
    hidden_down,
    norm_gains,
    gate_bias,
    init_state,
    cotangent,
    state_cotangent,
):
    y, c = lax.axis_index("y"), lax.axis_index("c")
    micro, rows_local, width = tokens.shape[0], tokens.shape[2], tokens.shape[3]
    state_rows = init_state.shape[0]
    state_half = state_rows // 2

    def own_rows(array):
        keep = lax.dynamic_index_in_dim(array[:, 0], y, 0, keepdims=False)
        send = lax.dynamic_index_in_dim(array[:, 0], 1 - y, 0, keepdims=False)
        got = swap(send, "y")
        return jnp.where(y == 0, jnp.concatenate([keep, got]), jnp.concatenate([got, keep]))

    def to_owner(rows, wide):
        split = rows.reshape(2, rows_local, width)
        keep = lax.dynamic_index_in_dim(split, y, 0, keepdims=False)
        send = lax.dynamic_index_in_dim(split, 1 - y, 0, keepdims=False)
        got = swap(send.astype(BF), "y").astype(wide)
        keep = keep.astype(wide)
        return jnp.where(y == 0, jnp.stack([keep, got]), jnp.stack([got, keep]))[:, None]

    x_rows = to_local(own_rows(tokens))
    valid_count = lax.dynamic_index_in_dim(counts[:, 0], y, 0, keepdims=False)

    small = jnp.concatenate(
        [
            lax.dynamic_slice_in_dim(init_state, c * state_half, state_half, 0),
            norm_gains,
            gate_bias[None],
            jnp.zeros((12, init_state.shape[1]), BF),
        ],
        axis=0,
    )
    shard_rows = token_output.shape[0]
    flat = lambda array: array.reshape(shard_rows, -1)
    small = gather_rows(small)
    w_token = gather_weight(flat(token_weights))
    w_mid = gather_weight(jnp.concatenate([flat(state_weights), state_output, token_output], axis=1))
    w_up = gather_weight(hidden_up)
    w_down = gather_weight(hidden_down)
    head = token_output.shape[1]
    at_state, at_state_out, at_token_out = 0, 3 * head, 4 * head
    gains = small[state_half : state_half + 3].astype(F32)
    gate_open = jax.nn.sigmoid(small[state_half + 3].astype(F32))
    state_now = small[:state_half].astype(F32)

    dy_rows = to_local(own_rows(cotangent))
    dy_pair = pair(dy_rows)
    grad_final = lax.dynamic_slice(
        state_cotangent, (y, 0, c * state_half, 0), (1, 1, state_half, width)
    )[0, 0]
    grad_final = to_local(grad_final)

    seq_length = 4 * rows_local
    blocks = seq_length // BLOCK
    info = jnp.stack([c, valid_count]).astype(jnp.int32)
    x_values = x_rows.astype(F32)
    normed = pair(rms_forward(x_values, gains[0]))
    token_proj = project(*normed, w_token, 0, 3 * head, 3 * head // 2, blocks=blocks)

    kept = []
    mixed = []
    for b in range(blocks):
        state_norm = pair(rms_forward(state_now, gains[1]))
        state_proj = project(*state_norm, w_mid, at_state, 3 * head, 3 * head)
        mixed_b, state_flat, logs = attend_forward(b, blocks, info, token_proj, state_proj)
        mixed.append(mixed_b)
        update = fold(merge([state_flat], w_mid, at_state_out))
        kept.append((state_now, state_norm, state_proj, logs, state_flat, update))
        state_now = gate_open * state_now + (1.0 - gate_open) * update
    hidden = x_values + fold(merge(mixed, w_mid, at_token_out, blocks=blocks))
    hidden_norm = pair(rms_forward(hidden, gains[2]))
    ff = hidden_up.shape[1]
    activated, slope = project(*hidden_norm, w_up, 0, ff, ff // 2, activate=True)
    result = (hidden + fold(merge([activated], w_down, 0))).astype(BF)
    output = to_owner(from_local(result), BF)

    final_half = from_local(state_now.astype(BF))
    final_pair = jnp.stack([final_half, swap(final_half, "y")])
    final_pair = jnp.where(y == 0, final_pair, final_pair[::-1])
    final_other = swap(final_pair, "c")
    final_state = jnp.where(
        c == 0,
        jnp.concatenate([final_pair, final_other], axis=1),
        jnp.concatenate([final_other, final_pair], axis=1),
    )[:, None]

    grad_hidden_down = reduce_weight(outer([dy_pair], [activated], ff // 2))
    grad_up = project(*dy_pair, w_down, 0, ff, ff // 2, gate=slope)
    grad_hidden_norm = fold(merge([grad_up], w_up, 0))
    grad_hidden_up = reduce_weight(outer([hidden_norm], [grad_up], ff // 2))
    through, gain_hidden = rms_backward(hidden, gains[2], grad_hidden_norm)
    grad_hidden = dy_rows.astype(F32) + through
    branch = pair(grad_hidden.astype(BF))
    grad_mixed = project(*branch, w_mid, at_token_out, head, head, blocks=blocks)
    grad_token_output = reduce_weight(
        outer([branch], [jnp.concatenate(mixed, axis=1)], head, blocks=blocks)
    )

    grad_state = grad_final.astype(F32)
    grad_gate = jnp.zeros((width,), F32)
    gain_state = jnp.zeros((width,), F32)
    proj_grads = [None] * blocks
    update_all, flat_all, norm_all, state_grads = [], [], [], []
    later = None
    for b in reversed(range(blocks)):
        state_before, state_norm, state_proj, logs, state_flat, update = kept[b]
        grad_update = pair(((1.0 - gate_open) * grad_state).astype(BF))
        grad_gate = grad_gate + jnp.sum(grad_state * (state_before - update), axis=0)
        grad_state_mixed = project(*grad_update, w_mid, at_state_out, head, head)
        proj_grads[b], state_grad, later = attend_backward(
            b, blocks, info, token_proj, state_proj, logs, grad_mixed, grad_state_mixed, later
        )
        update_all.append(grad_update)
        flat_all.append(state_flat)
        norm_all.append(state_norm)
        state_grads.append(state_grad)
        partial = merge([state_grad], w_mid, at_state)
        previous, gain_piece = rms_backward(state_before, gains[1], fold(partial))
        gain_state = gain_state + gain_piece
        grad_state = gate_open * grad_state + previous
    grad_gate = grad_gate * gate_open * (1.0 - gate_open)
    grad_state_output = reduce_weight(outer(update_all, flat_all, head))
    grad_state_weights = reduce_weight(outer(norm_all, state_grads, 3 * head)).reshape(-1, 3, head)
    grad_normed = fold(merge(proj_grads, w_token, 0, blocks=blocks))
    grad_token_weights = reduce_weight(
        outer([normed], [jnp.concatenate(proj_grads, axis=1)], 3 * head, blocks=blocks)
    ).reshape(-1, 3, head)
    through, gain_token = rms_backward(x_values, gains[0], grad_normed)
    input_grad = to_owner(from_local(grad_hidden + through), F32)

    vectors = from_local(jnp.stack([gain_token, gain_state, gain_hidden, grad_gate]))
    vectors = lax.psum_scatter(vectors, ("r", "z", "x"), scatter_dimension=1, tiled=True)
    vectors = lax.psum(vectors, ("y", "c"))
    init_grad = from_local(grad_state)
    init_grad = lax.psum_scatter(init_grad, ("r", "z", "x"), scatter_dimension=1, tiled=True)
    init_grad = lax.psum(init_grad, "y")
    init_grad = lax.all_gather(init_grad, "c", axis=0, tiled=True)
    return (
        output,
        final_state,
        input_grad,
        grad_token_weights,
        grad_token_output,
        grad_state_weights,
        grad_state_output,
        grad_hidden_up,
        grad_hidden_down,
        vectors[:3],
        vectors[3],
        init_grad,
    )


def solution(mesh):
    dp, heads = mesh.devices.shape
    fine = Mesh(mesh.devices.reshape(dp // (2 * RING), RING, 2, heads // 2, 2), ("r", "z", "x", "y", "c"))
    d, h = ("r", "z", "x"), ("y", "c")
    return jax.shard_map(
        body,
        mesh=fine,
        in_specs=(
            P(None, d, h, None),
            P(None, d),
            P(d, None, h),
            P(d, h),
            P(d, None, h),
            P(d, h),
            P(d, h),
            P(d, h),
            P(None, d),
            P(d),
            P(None, d),
            P(None, d, h, None),
            P(None, d, None, None),
        ),
        out_specs=(
            P(None, d, h, None),
            P(None, d, None, None),
            P(None, d, h, None),
            P(d, None, h),
            P(d, h),
            P(d, None, h),
            P(d, h),
            P(d, h),
            P(d, h),
            P(None, d),
            P(d),
            P(None, d),
        ),
        check_vma=False,
    )
```

time: 1120 us -> 837 us (0.75)
  Pallas kernels: 0 us -> 257 us
  matrix products: 247 us -> 0 us
  other arithmetic: 256 us -> 64.5 us
  waiting for transfers between devices: 273 us -> 211 us
  local copies, waits for them, and re-layouts: 181 us -> 125 us
  starting transfers between devices: 125 us -> 147 us
    pallas_call x0 -> x48, Pallas kernels: none -> 257 us  [call(): pl.pallas_call(kernel, grid=grid, in_specs=in_specs, out_specs=out_specs,...]
    dot_general x92 -> x0, matrix products: 247 us -> none  [the longest x68 157 us: matmul(): lax.dot_general(left, right, (contract, ((), ())), preferred_element_type...]
    squeeze x7 -> x0, other arithmetic: 136 us -> none  [the longest x1 71.9 us: body(): w_down = gather_weight(hidden_down[None])[0]]
    ppermute x39 -> x33, waiting for transfers between devices: 116 us -> 42.4 us  [turn(): lax.ppermute(array, 'z', [(i, (i + steps) % RING) for i in range(RING)])]
    slice x51 -> x1, local copies, waits for them, and re-layouts: 41.9 us -> 0.6 us  [body(): hidden_norm = pair(rms_forward(hidden, gains[2]))]
    ppermute x39 -> x33, starting transfers between devices: 53.5 us -> 89.4 us  [turn(): lax.ppermute(array, 'z', [(i, (i + steps) % RING) for i in range(RING)])]
    convert_element_type x30 -> x2, other arithmetic: 40.8 us -> 7.49 us  [the longest x1 4.89 us: body(): branch = pair(grad_hidden.astype(BF))]
    ppermute x83 -> x71, waiting for transfers between devices: 120 us -> 87.4 us  [swap(): return lax.ppermute(array, axis, [(0, 1), (1, 0)])]
  transfers between devices with their start and end apart: 125 -> 107, of which waited for: 42 -> 23; matrix products, arithmetic and copies ran while one was open for 60% -> 19% of each run, Pallas kernels for 0% -> 29%
where the time goes in v2:
time: 837 us; the launch traced here: 827 us
  Pallas kernels  257 us (31%)
  waiting for transfers between devices  211 us (25%)
  starting transfers between devices  147 us (18%)
  local copies, waits for them, and re-layouts  125 us (15%)
  other arithmetic  64.5 us (8%)
  between operations  15.6 us (2%)
    pallas_call x48, Pallas kernels, call(): pl.pallas_call(kernel, grid=grid, in_specs=in_specs, out_specs=out_specs,...  257 us
    ppermute x33, starting transfers between devices, turn(): lax.ppermute(array, 'z', [(i, (i + steps) % RING) for i in range(RING)])  89.4 us
    ppermute x71, waiting for transfers between devices, swap(): return lax.ppermute(array, axis, [(0, 1), (1, 0)])  87.4 us
    unnamed x309, local copies, waits for them, and re-layouts  64 us
    ppermute x71, starting transfers between devices, swap(): return lax.ppermute(array, axis, [(0, 1), (1, 0)])  57.2 us
    ppermute x33, waiting for transfers between devices, turn(): lax.ppermute(array, 'z', [(i, (i + steps) % RING) for i in range(RING)])  42.4 us
    unnamed x4, waiting for transfers between devices  34.6 us
    reduce_scatter x1, waiting for transfers between devices, body(): lax.psum_scatter(init_grad, ('r', 'z', 'x'), scatter_dimension=1, tiled=T...  26.7 us
  transfers between devices with their start and end apart: 107, of which 23 were waited for; matrix products, arithmetic and copies ran while one was open for 19% of the time, Pallas kernels for 29%

profile of v2, /device:TPU:0, one launch (start us, length us, event | category | flops | bytes accessed | tf_op | source)
XLA Modules:
  0.0 827.1 jit_solution(15935483445226145770)
XLA Ops:
  97.1 16.8 %collective-permute-done.13.args_8_ = bf16[256,768]{1,0:T(8,128)(2,1)} collective-permute-done((bf16[256,768]{1,0:T(8,128)(2,1)S(1)}, bf16[256,768]{1,0:T(8,128)(2,1)}, u32[]{:S(2)}, u32[]{:S(2)}) %collective-permute-start.13) | collective-permute-done | bytes 393248 | tf_op jit(solution)/shard_map/ppermute | solution.py:22
  121.0 8.1 shard_map.221.token_ref.args_1_
  156.4 9.6 %shard_map.224 = (bf16[2,512,256]{2,1,0:T(8,128)(2,1)S(1)}, bf16[2,512,256]{2,1,0:T(8,128)(2,1)S(1)}, f32[2,512,128]{2,1,0:T(8,128)S(1)}) custom-call(s32[2]{0:T(128)S(1)} %pad_add_fusion.info_ref.args_0_, bf16[2,1024,768]{2,1,0:T(8,128)(2,1)} %shard_map.221.token_ref.args_1_, bf16[2,512,768]{2,1,0:T(8,128)(2,1)S(1)} %copy-done.31), custom_call_target="tpu_custom_call" | custom-call | flops 2147483648 | bytes 6291464 | tf_op jit(solution)/shard_map/pallas_call | solution.py:96
  183.3 10.7 %collective-permute-done.31.refs_3_ = bf16[128,1024]{1,0:T(8,128)(2,1)S(1)} collective-permute-done((bf16[128,1024]{1,0:T(8,128)(2,1)S(1)}, bf16[128,1024]{1,0:T(8,128)(2,1)S(1)}, u32[]{:S(2)}, u32[]{:S(2)}) %collective-permute-start.31) | collective-permute-done | bytes 262176 | tf_op jit(solution)/shard_map/ppermute | solution.py:26
  197.7 17.0 %shard_map.229 = (bf16[256,1024]{1,0:T(8,128)(2,1)}, bf16[256,1024]{1,0:T(8,128)(2,1)}) custom-call(bf16[128,1024]{1,0:T(8,128)(2,1)S(1)} %copy-done.57, bf16[128,1024]{1,0:T(8,128)(2,1)} %collective-permute-done.29.refs_1_, bf16[128,1024]{1,0:T(8,128)(2,1)} %collective-permute-done.30.refs_2_, bf16[128,1024]{1,0:T(8,128)(2,1)S(1)} %copy-done.59), custom_call_target="tpu_custom_call" | custom-call | bytes 2097152 | tf_op jit(solution)/shard_map/pallas_call | solution.py:96
  216.8 32.9 %shard_map.231 = (bf16[256,1024]{1,0:T(8,128)(2,1)}, bf16[256,1024]{1,0:T(8,128)(2,1)}) custom-call(bf16[128,1024]{1,0:T(8,128)(2,1)} %refs_0_.3, bf16[128,1024]{1,0:T(8,128)(2,1)} %collective-permute-done.38.refs_1_, bf16[128,1024]{1,0:T(8,128)(2,1)} %collective-permute-done.39.refs_2_, bf16[128,1024]{1,0:T(8,128)(2,1)} %collective-permute-done.40.refs_3_), custom_call_target="tpu_custom_call" | custom-call | bytes 2097152 | tf_op jit(solution)/shard_map/pallas_call | solution.py:96
  272.3 11.2 %shard_map.227 = (bf16[2,512,256]{2,1,0:T(8,128)(2,1)S(1)}, bf16[2,512,256]{2,1,0:T(8,128)(2,1)S(1)}, f32[2,512,128]{2,1,0:T(8,128)S(1)}) custom-call(s32[2]{0:T(128)S(1)} %pad_add_fusion.info_ref.args_0_, bf16[2,1024,768]{2,1,0:T(8,128)(2,1)} %shard_map.221.token_ref.args_1_, bf16[2,512,768]{2,1,0:T(8,128)(2,1)S(1)} %copy-done.32), custom_call_target="tpu_custom_call" | custom-call | flops 2684354560 | bytes 6291464 | tf_op jit(solution)/shard_map/pallas_call | solution.py:96
  308.9 8.7 %collective-permute-done.34.args_6_.args_5_ = bf16[256,1024]{1,0:T(8,128)(2,1)S(1)} collective-permute-done((bf16[256,1024]{1,0:T(8,128)(2,1)}, bf16[256,1024]{1,0:T(8,128)(2,1)S(1)}, u32[]{:S(2)}, u32[]{:S(2)}) %collective-permute-start.34) | collective-permute-done | bytes 524320 | tf_op jit(solution)/shard_map/ppermute | solution.py:22
  318.1 10.1 %collective-permute-done.36.args_8_.args_7_ = bf16[256,1024]{1,0:T(8,128)(2,1)S(1)} collective-permute-done((bf16[256,1024]{1,0:T(8,128)(2,1)}, bf16[256,1024]{1,0:T(8,128)(2,1)S(1)}, u32[]{:S(2)}, u32[]{:S(2)}) %collective-permute-start.36) | collective-permute-done | bytes 524320 | tf_op jit(solution)/shard_map/ppermute | solution.py:22
  330.7 12.9 %shard_map.230 = (bf16[2,1024,1024]{2,1,0:T(8,128)(2,1)}, bf16[2,1024,1024]{2,1,0:T(8,128)(2,1)}) custom-call(bf16[512,1024]{1,0:T(8,128)(2,1)} %multiply_convert_fusion.args_0_, bf16[512,1024]{1,0:T(8,128)(2,1)} %collective-permute-done.28.args_1_, bf16[256,1024]{1,0:T(8,128)(2,1)} %get-tuple-element.114.args_2_.args_1_, ...), custom_call_target="tpu_custom_call" | custom-call | flops 4294967296 | bytes 14680064 | tf_op jit(solution)/shard_map/pallas_call | solution.py:96
  343.7 9.3 %collective-permute-done.45.args_7_.args_8_ = bf16[256,1024]{1,0:T(8,128)(2,1)S(1)} collective-permute-done((bf16[256,1024]{1,0:T(8,128)(2,1)}, bf16[256,1024]{1,0:T(8,128)(2,1)S(1)}, u32[]{:S(2)}, u32[]{:S(2)}) %collective-permute-start.45) | collective-permute-done | bytes 524320 | tf_op jit(solution)/shard_map/ppermute | solution.py:22
  353.9 8.8 %shard_map.234.args_0_.args_2_ = bf16[2,1024,1024]{2,1,0:T(8,128)(2,1)} custom-call(bf16[512,1024]{1,0:T(8,128)(2,1)} %bitcast_dynamic-update-slice_fusion.args_0_, bf16[512,1024]{1,0:T(8,128)(2,1)} %copy-done.118, bf16[256,1024]{1,0:T(8,128)(2,1)} %get-tuple-element.117.args_1_.args_2_, bf16[256,1024]{1,0:T(8,128)(2,1)} %get-tuple-element.118.args_2_.args_3_, ...), custom_call_target="tpu_custom_call" | custom-call | flops 4294967296 | bytes 14680064 | tf_op jit(solution)/shard_map/pallas_call | solution.py:96
  362.8 8.8 %shard_map.235 = (f32[512,1024]{1,0:T(8,128)}, bf16[512,1024]{1,0:T(8,128)(2,1)S(1)}) custom-call(bf16[2,1024,1024]{2,1,0:T(8,128)(2,1)} %shard_map.234.args_0_.args_2_, bf16[256,1024]{1,0:T(8,128)(2,1)} %get-tuple-element.114.args_2_.args_1_, bf16[256,1024]{1,0:T(8,128)(2,1)} %get-tuple-element.115.args_3_.args_2_, ...), custom_call_target="tpu_custom_call" | custom-call | flops 4294967296 | bytes 11534336 | tf_op jit(solution)/shard_map/pallas_call | solution.py:96
  382.8 8.7 %shard_map.232 = (f32[512,1024]{1,0:T(8,128)}, bf16[512,1024]{1,0:T(8,128)(2,1)S(1)}) custom-call(bf16[2,1024,1024]{2,1,0:T(8,128)(2,1)} %get-tuple-element.116.args_0_.args_2_, bf16[256,1024]{1,0:T(8,128)(2,1)} %get-tuple-element.117.args_1_.args_2_, bf16[256,1024]{1,0:T(8,128)(2,1)} %get-tuple-element.118.args_2_.args_3_, ...), custom_call_target="tpu_custom_call" | custom-call | flops 4294967296 | bytes 11534336 | tf_op jit(solution)/shard_map/pallas_call | solution.py:96
  392.1 8.5 %shard_map.263 = (bf16[256,1024]{1,0:T(8,128)(2,1)S(1)}, bf16[256,1024]{1,0:T(8,128)(2,1)S(1)}, bf16[512,1024]{1,0:T(8,128)(2,1)}, bf16[512,1024]{1,0:T(8,128)(2,1)}, bf16[512,1024]{1,0:T(8,128)(2,1)S(1)}) custom-call(bf16[512,1024]{1,0:T(8,128)(2,1)} %bitcast_dynamic-update-slice_fusion.args_0_, bf16[512,1024]{1,0:T(8,128)(2,1)} %copy-done.118, ...), custom_call_target="tpu_custom_call" | custom-call | flops 4294967296 | bytes 10485760 | tf_op jit(solution)/shard_map/pallas_call | solution.py:96
  457.6 14.2 %collective-permute-done.48 = bf16[256,1024]{1,0:T(8,128)(2,1)} collective-permute-done((bf16[256,1024]{1,0:T(8,128)(2,1)}, bf16[256,1024]{1,0:T(8,128)(2,1)}, u32[]{:S(2)}, u32[]{:S(2)}) %collective-permute-start.48) | collective-permute-done | bytes 524320 | tf_op jit(solution)/shard_map/ppermute | solution.py:22
  488.8 19.9 %shard_map.238 = (bf16[2,512,768]{2,1,0:T(8,128)(2,1)S(1)}, bf16[2,512,768]{2,1,0:T(8,128)(2,1)S(1)}, f32[2,512,512]{2,1,0:T(8,128)}) custom-call(s32[2]{0:T(128)S(1)} %pad_add_fusion.info_ref.args_0_, bf16[2,1024,768]{2,1,0:T(8,128)(2,1)} %shard_map.221.token_ref.args_1_, bf16[2,512,768]{2,1,0:T(8,128)(2,1)} %shard_map.226.state_ref.args_2_, ...), custom_call_target="tpu_custom_call" | custom-call | flops 6710886400 | bytes 12058632 | tf_op jit(solution)/shard_map/pallas_call | solution.py:96
  525.8 9.2 %collective-permute-start.74 = (bf16[128,256]{1,0:T(8,128)(2,1)S(1)}, bf16[128,256]{1,0:T(8,128)(2,1)S(1)}, u32[]{:S(2)}, u32[]{:S(2)}) collective-permute-start(bf16[128,256]{1,0:T(8,128)(2,1)S(1)} %get-tuple-element.154), channel_id=1, source_target_pairs={{0,8},{8,16},{16,24},{24,0},{1,9},{9,17},{17,25},{25,1},{2,10},{10... | collective-permute-start | bytes 196616 | tf_op jit(solution)/shard_map/ppermute | solution.py:26
  537.1 8.1 collective-permute-start.72
  566.2 18.1 %shard_map.241 = (bf16[2,512,768]{2,1,0:T(8,128)(2,1)S(1)}, bf16[2,512,768]{2,1,0:T(8,128)(2,1)S(1)}) custom-call(s32[2]{0:T(128)S(1)} %pad_add_fusion.info_ref.args_0_, bf16[2,1024,768]{2,1,0:T(8,128)(2,1)} %shard_map.221.token_ref.args_1_, bf16[2,512,768]{2,1,0:T(8,128)(2,1)} %shard_map.223.state_ref.args_2_, f32[2,512,128]{2,1,0:T(8,128)S(1)} %copy-done.64, ...), custom_call_target="tpu_custom_call" | custom-call | flops 5368709120 | bytes 12058632 | tf_op jit(solution)/shard_map/pallas_call | solution.py:96
  679.9 34.6 %reduce-scatter.7.cloned.1.call-done = f32[128,4]{1,0:T(8,128)} async-done(((f32[1024,4]{1,0:T(8,128)}), f32[128,4]{1,0:T(8,128)}) %reduce-scatter.7.cloned.1.call-update) | async-done | bytes 2064
  754.9 9.9 %collective-permute-done.80 = bf16[128,768]{1,0:T(8,128)(2,1)S(1)} collective-permute-done((bf16[128,768]{1,0:T(8,128)(2,1)S(1)}, bf16[128,768]{1,0:T(8,128)(2,1)S(1)}, u32[]{:S(2)}, u32[]{:S(2)}) %collective-permute-start.80) | collective-permute-done | bytes 196640 | tf_op jit(solution)/shard_map/ppermute | solution.py:26
  768.1 26.7 %reduce-scatter.5.cloned.1.call-done = f32[256,128]{1,0:T(8,128)} async-done(((f32[256,1024]{1,0:T(8,128)}), f32[256,128]{1,0:T(8,128)}) %reduce-scatter.5.cloned.1.call-update) | async-done | bytes 131088 | tf_op jit(solution)/shard_map/reduce_scatter | solution.py:738
  798.2 19.4 %all-reduce.2.cloned.1.call-done = f32[256,128]{1,0:T(8,128)} async-done(((f32[256,128]{1,0:T(8,128)}), f32[256,128]{1,0:T(8,128)}) %all-reduce.2.cloned.1.call-update) | async-done | bytes 131088 | tf_op jit(solution)/shard_map/psum | solution.py:739
  (661 shorter events, 469.5 us)
Async XLA Ops:
  7.2 707.3 %reduce-scatter.7.cloned.1.call-start = ((), (), s32[]{:S(2)}) async-start(), calls=%async_computation.4 | async-start | bytes 589824
  30.5 42.4 %collective-permute-start.16 = (bf16[128,1280]{1,0:T(8,128)(2,1)S(1)}, bf16[128,1280]{1,0:T(8,128)(2,1)S(1)}, u32[]{:S(2)}, u32[]{:S(2)}) collective-permute-start(bf16[128,1280]{1,0:T(8,128)(2,1)S(1)} %pad_maximum_fusion.3.refs_0_), channel_id=1, source_target_pairs={{0,8},{8,16},{16,24},{24,0},{1,9},{9,17},{17,25},{25,1},{2,10},{10... | collective-permute-start | bytes 983048 | tf_op jit(solution)/shard_map/ppermute | solution.py:26
  74.9 44.3 %collective-permute-start.5 = (bf16[512,1024]{1,0:T(8,128)(2,1)}, bf16[512,1024]{1,0:T(8,128)(2,1)}, u32[]{:S(2)}, u32[]{:S(2)}) collective-permute-start(bf16[512,1024]{1,0:T(8,128)(2,1)} %fusion.4.args_0_), channel_id=1, source_target_pairs={{0,1},{1,0},{2,3},{3,2},{4,5},{5,4},{6,7},{7,6},{8,9},{9,8},{10,11... | collective-permute-start | bytes 3145736 | tf_op jit(solution)/shard_map/ppermute | solution.py:22
  129.2 85.5 %collective-permute-start.38 = (bf16[128,1024]{1,0:T(8,128)(2,1)}, bf16[128,1024]{1,0:T(8,128)(2,1)}, u32[]{:S(2)}, u32[]{:S(2)}) collective-permute-start(bf16[128,1024]{1,0:T(8,128)(2,1)} %refs_0_.3), channel_id=1, source_target_pairs={{0,8},{8,16},{16,24},{24,0},{1,9},{9,17},{17,25},{25,1},{2,10},{10... | collective-permute-start | bytes 786440 | tf_op jit(solution)/shard_map/ppermute | solution.py:26
  136.1 80.2 %collective-permute-start.39 = (bf16[128,1024]{1,0:T(8,128)(2,1)}, bf16[128,1024]{1,0:T(8,128)(2,1)}, u32[]{:S(2)}, u32[]{:S(2)}) collective-permute-start(bf16[128,1024]{1,0:T(8,128)(2,1)} %refs_0_.3), channel_id=1, source_target_pairs={{0,16},{8,24},{16,0},{24,8},{1,17},{9,25},{17,1},{25,9},{2,18},{10... | collective-permute-start | bytes 786440 | tf_op jit(solution)/shard_map/ppermute | solution.py:26
  137.2 41.6 %collective-permute-start.29 = (bf16[128,1024]{1,0:T(8,128)(2,1)S(1)}, bf16[128,1024]{1,0:T(8,128)(2,1)}, u32[]{:S(2)}, u32[]{:S(2)}) collective-permute-start(bf16[128,1024]{1,0:T(8,128)(2,1)S(1)} %copy-done.57), channel_id=1, source_target_pairs={{0,8},{8,16},{16,24},{24,0},{1,9},{9,17},{17,25},{25,1},{2,10},{10... | collective-permute-start | bytes 786440 | tf_op jit(solution)/shard_map/ppermute | solution.py:26
  175.5 76.0 %collective-permute-start.52 = (bf16[256,1024]{0,1:T(8,128)(2,1)}, bf16[256,1024]{0,1:T(8,128)(2,1)}, u32[]{:S(2)}, u32[]{:S(2)}) collective-permute-start(bf16[256,1024]{0,1:T(8,128)(2,1)} %bitcast.194), channel_id=1, source_target_pairs={{0,2},{2,0},{1,3},{3,1},{4,6},{6,4},{5,7},{7,5},{8,10},{10,8},{9,1... | collective-permute-start | bytes 1572872 | tf_op jit(solution)/shard_map/ppermute | solution.py:22
  194.7 69.7 %collective-permute-start.26 = (bf16[256,1024]{1,0:T(8,128)(2,1)}, bf16[256,1024]{1,0:T(8,128)(2,1)}, u32[]{:S(2)}, u32[]{:S(2)}) collective-permute-start(bf16[256,1024]{1,0:T(8,128)(2,1)} %multiply_convert_fusion.2.args_0_), channel_id=1, source_target_pairs={{0,1},{1,0},{2,3},{3,2},{4,5},{5,4},{6,7},{7,6},{8,9},{9,8},{10,11... | collective-permute-start | bytes 1572872 | tf_op jit(solution)/shard_map/ppermute | solution.py:22
  214.7 94.2 %collective-permute-start.33 = (bf16[256,1024]{1,0:T(8,128)(2,1)}, bf16[256,1024]{1,0:T(8,128)(2,1)}, u32[]{:S(2)}, u32[]{:S(2)}) collective-permute-start(bf16[256,1024]{1,0:T(8,128)(2,1)} %get-tuple-element.115.args_3_.args_2_), channel_id=1, source_target_pairs={{0,4},{4,0},{1,5},{5,1},{2,6},{6,2},{3,7},{7,3},{8,12},{12,8},{9,1... | collective-permute-start | bytes 1572872 | tf_op jit(solution)/shard_map/ppermute | solution.py:22
  216.3 91.6 %collective-permute-start.35 = (bf16[256,1024]{1,0:T(8,128)(2,1)}, bf16[256,1024]{1,0:T(8,128)(2,1)}, u32[]{:S(2)}, u32[]{:S(2)}) collective-permute-start(bf16[256,1024]{1,0:T(8,128)(2,1)} %get-tuple-element.115.args_3_.args_2_), channel_id=1, source_target_pairs={{0,2},{2,0},{1,3},{3,1},{4,6},{6,4},{5,7},{7,5},{8,10},{10,8},{9,1... | collective-permute-start | bytes 1572872 | tf_op jit(solution)/shard_map/ppermute | solution.py:22
  249.7 49.5 %collective-permute-start.41 = (bf16[256,1024]{1,0:T(8,128)(2,1)}, bf16[256,1024]{1,0:T(8,128)(2,1)}, u32[]{:S(2)}, u32[]{:S(2)}) collective-permute-start(bf16[256,1024]{1,0:T(8,128)(2,1)} %get-tuple-element.117.args_1_.args_2_), channel_id=1, source_target_pairs={{0,4},{4,0},{1,5},{5,1},{2,6},{6,2},{3,7},{7,3},{8,12},{12,8},{9,1... | collective-permute-start | bytes 1572872 | tf_op jit(solution)/shard_map/ppermute | solution.py:22
  251.5 51.1 %collective-permute-start.44 = (bf16[256,1024]{1,0:T(8,128)(2,1)}, bf16[256,1024]{1,0:T(8,128)(2,1)}, u32[]{:S(2)}, u32[]{:S(2)}) collective-permute-start(bf16[256,1024]{1,0:T(8,128)(2,1)} %get-tuple-element.118.args_2_.args_3_), channel_id=1, source_target_pairs={{0,2},{2,0},{1,3},{3,1},{4,6},{6,4},{5,7},{7,5},{8,10},{10,8},{9,1... | collective-permute-start | bytes 1572872 | tf_op jit(solution)/shard_map/ppermute | solution.py:22
  308.9 44.1 %collective-permute-start.53 = (bf16[512,1024]{1,0:T(8,128)(2,1)}, bf16[512,1024]{1,0:T(8,128)(2,1)S(1)}, u32[]{:S(2)}, u32[]{:S(2)}) collective-permute-start(bf16[512,1024]{1,0:T(8,128)(2,1)} %bitcast_dynamic-update-slice_fusion.args_0_), channel_id=1, source_target_pairs={{0,1},{1,0},{2,3},{3,2},{4,5},{5,4},{6,7},{7,6},{8,9},{9,8},{10,11... | collective-permute-start | bytes 3145736 | tf_op jit(solution)/shard_map/ppermute | solution.py:22
  419.2 55.4 %collective-permute-start.97 = (bf16[512,1024]{1,0:T(8,128)(2,1)}, bf16[512,1024]{1,0:T(8,128)(2,1)}, u32[]{:S(2)}, u32[]{:S(2)}) collective-permute-start(bf16[512,1024]{1,0:T(8,128)(2,1)} %shard_map.264), channel_id=1, source_target_pairs={{0,4},{4,0},{1,5},{5,1},{2,6},{6,2},{3,7},{7,3},{8,12},{12,8},{9,1... | collective-permute-start | bytes 3145736 | tf_op jit(solution)/shard_map/ppermute | solution.py:22
  422.3 53.7 %collective-permute-start.99 = (bf16[512,1024]{1,0:T(8,128)(2,1)}, bf16[512,1024]{1,0:T(8,128)(2,1)}, u32[]{:S(2)}, u32[]{:S(2)}) collective-permute-start(bf16[512,1024]{1,0:T(8,128)(2,1)} %shard_map.265), channel_id=1, source_target_pairs={{0,2},{2,0},{1,3},{3,1},{4,6},{6,4},{5,7},{7,5},{8,10},{10,8},{9,1... | collective-permute-start | bytes 3145736 | tf_op jit(solution)/shard_map/ppermute | solution.py:22
  454.1 60.6 %collective-permute-start.95 = (bf16[128,1024]{1,0:T(8,128)(2,1)S(1)}, bf16[128,1024]{1,0:T(8,128)(2,1)S(1)}, u32[]{:S(2)}, u32[]{:S(2)}) collective-permute-start(bf16[128,1024]{1,0:T(8,128)(2,1)S(1)} %get-tuple-element.182), channel_id=1, source_target_pairs={{0,8},{8,16},{16,24},{24,0},{1,9},{9,17},{17,25},{25,1},{2,10},{10... | collective-permute-start | bytes 786440 | tf_op jit(solution)/shard_map/ppermute | solution.py:26
  560.6 59.2 %collective-permute-start.50 = (bf16[256,1024]{1,0:T(8,128)(2,1)}, bf16[256,1024]{1,0:T(8,128)(2,1)}, u32[]{:S(2)}, u32[]{:S(2)}) collective-permute-start(bf16[256,1024]{1,0:T(8,128)(2,1)} %bitcast.154), channel_id=1, source_target_pairs={{0,2},{2,0},{1,3},{3,1},{4,6},{6,4},{5,7},{7,5},{8,10},{10,8},{9,1... | collective-permute-start | bytes 1572872 | tf_op jit(solution)/shard_map/ppermute | solution.py:22
  642.7 78.4 %collective-permute-start.62 = (bf16[512,768]{1,0:T(8,128)(2,1)}, bf16[512,768]{1,0:T(8,128)(2,1)S(1)}, u32[]{:S(2)}, u32[]{:S(2)}) collective-permute-start(bf16[512,768]{1,0:T(8,128)(2,1)} %shard_map.244), channel_id=1, source_target_pairs={{0,4},{4,0},{1,5},{5,1},{2,6},{6,2},{3,7},{7,3},{8,12},{12,8},{9,1... | collective-permute-start | bytes 2359304 | tf_op jit(solution)/shard_map/ppermute | solution.py:22
  644.1 76.9 %collective-permute-start.64 = (bf16[512,768]{1,0:T(8,128)(2,1)}, bf16[512,768]{1,0:T(8,128)(2,1)}, u32[]{:S(2)}, u32[]{:S(2)}) collective-permute-start(bf16[512,768]{1,0:T(8,128)(2,1)} %shard_map.245), channel_id=1, source_target_pairs={{0,2},{2,0},{1,3},{3,1},{4,6},{6,4},{5,7},{7,5},{8,10},{10,8},{9,1... | collective-permute-start | bytes 2359304 | tf_op jit(solution)/shard_map/ppermute | solution.py:22
  645.5 79.8 %collective-permute-start.76 = (bf16[512,768]{1,0:T(8,128)(2,1)}, bf16[512,768]{1,0:T(8,128)(2,1)S(1)}, u32[]{:S(2)}, u32[]{:S(2)}) collective-permute-start(bf16[512,768]{1,0:T(8,128)(2,1)} %shard_map.252), channel_id=1, source_target_pairs={{0,4},{4,0},{1,5},{5,1},{2,6},{6,2},{3,7},{7,3},{8,12},{12,8},{9,1... | collective-permute-start | bytes 2359304 | tf_op jit(solution)/shard_map/ppermute | solution.py:22
  651.1 76.3 %collective-permute-start.78 = (bf16[512,768]{1,0:T(8,128)(2,1)}, bf16[512,768]{1,0:T(8,128)(2,1)}, u32[]{:S(2)}, u32[]{:S(2)}) collective-permute-start(bf16[512,768]{1,0:T(8,128)(2,1)} %shard_map.253), channel_id=1, source_target_pairs={{0,2},{2,0},{1,3},{3,1},{4,6},{6,4},{5,7},{7,5},{8,10},{10,8},{9,1... | collective-permute-start | bytes 2359304 | tf_op jit(solution)/shard_map/ppermute | solution.py:22
  654.9 139.8 %reduce-scatter.5.cloned.1.call-start = ((), (), s32[]{:S(2)}) async-start(), calls=%async_computation.2 | async-start | bytes 1179648 | tf_op jit(solution)/shard_map/reduce_scatter | solution.py:738
  660.0 157.5 %all-reduce.2.cloned.1.call-start = ((), (), s32[]{:S(2)}) async-start(), calls=%async_computation.3 | async-start | bytes 262144 | tf_op jit(solution)/shard_map/psum | solution.py:739
  675.1 90.8 %collective-permute-start.60 = (bf16[256,1024]{1,0:T(8,128)(2,1)}, bf16[256,1024]{1,0:T(8,128)(2,1)}, u32[]{:S(2)}, u32[]{:S(2)}) collective-permute-start(bf16[256,1024]{1,0:T(8,128)(2,1)} %fusion.32), channel_id=1, source_target_pairs={{0,2},{2,0},{1,3},{3,1},{4,6},{6,4},{5,7},{7,5},{8,10},{10,8},{9,1... | collective-permute-start | bytes 1572872 | tf_op jit(solution)/shard_map/ppermute | solution.py:22
  (203 other events, 2960.6 us)
Sparse Core Ops, SparseCore 0:
  655.0 59.3 reduce-scatter.6
  718.3 76.4 reduce-scatter.4
  797.0 20.4 all-reduce.1

commit v3 on v2

--- a/solution.py
+++ b/solution.py
@@ -120,27 +120,17 @@
     rows, width = pieces[0].shape
 
     def kernel(*refs):
-        ins, outs, sem = refs[: len(pieces)], refs[len(pieces) : -1], refs[-1]
-        copies = [
-            pltpu.make_async_copy(
-                piece, outs[i // half].at[pl.ds((i % half) * rows, rows)], sem.at[i]
-            )
-            for i, piece in enumerate(ins)
-        ]
-        for copy in copies:
-            copy.start()
-        for copy in copies:
-            copy.wait()
-
-    anywhere = pl.BlockSpec(memory_space=pl.ANY)
+        ins, outs = refs[: len(pieces)], refs[len(pieces) :]
+        for i, piece in enumerate(ins):
+            outs[i // half][(i % half) * rows : (i % half + 1) * rows] = piece[...]
+
     return call(
         kernel,
-        (),
+        (1,),
         pieces,
-        [anywhere] * len(pieces),
+        [whole(piece) for piece in pieces],
         [((half * rows, width), BF)] * 2,
-        [anywhere] * 2,
-        scratch_shapes=[pltpu.SemaphoreType.DMA((len(pieces),))],
+        [whole_out((half * rows, width))] * 2,
     )
 
 
@@ -340,29 +330,246 @@
     return scatter_groups(total, 0)
 
 
-def rms_inverse(values):
+def pair(own):
+    return own, swap(own, "c")
+
+
+INFO = 3
+PIECES = 2 * RING
+
+
+def smem():
+    return pl.BlockSpec(memory_space=pltpu.SMEM)
+
+
+def lanes_at(info_ref, index, width):
+    size = width // PIECES
+    return pl.ds(pl.multiple_of(info_ref[index] * size, size), size)
+
+
+def reorder_in(info_ref, source, target, rows=slice(None)):
+    width = source.shape[-1]
+    size = width // PIECES
+    for k in range(PIECES):
+        target[rows, k * size : (k + 1) * size] = source[:, lanes_at(info_ref, INFO + k, width)].astype(target.dtype)
+
+
+def reorder_out(info_ref, source, target, rows=slice(None)):
+    width = source.shape[-1]
+    size = width // PIECES
+    for k in range(PIECES):
+        part = source[rows, lanes_at(info_ref, INFO + PIECES + k, width)]
+        target[:, k * size : (k + 1) * size] = part.astype(target.dtype)
+
+
+def inverse_rms(values):
     return lax.rsqrt(jnp.mean(values * values, axis=-1, keepdims=True) + EPSILON)
 
 
-def rms_forward(values, gain):
-    return (values * rms_inverse(values) * gain).astype(BF)
-
-
-def rms_backward(values, gain, grad):
-    inverse = rms_inverse(values)
+def rms_back(values, gain, grad):
+    inverse = inverse_rms(values)
     scaled = values * inverse
     weighted = grad * gain
-    grad_values = inverse * (weighted - scaled * jnp.mean(scaled * weighted, axis=-1, keepdims=True))
-    return grad_values, jnp.sum(grad * scaled, axis=0)
-
-
-def pair(own):
-    return own, swap(own, "c")
-
-
-def fold(both):
+    back = inverse * (weighted - scaled * jnp.mean(scaled * weighted, axis=-1, keepdims=True))
+    return back, jnp.sum(grad * scaled, axis=0, keepdims=True)
+
+
+def rowwise(kernel, inputs, outputs, scratch=()):
+    return call(
+        kernel,
+        (1,),
+        inputs,
+        [smem()] + [whole(array) for array in inputs[1:]],
+        outputs,
+        [whole_out(shape) for shape, _ in outputs],
+        scratch_shapes=[pltpu.VMEM(shape, dtype) for shape, dtype in scratch],
+    )
+
+
+def own_rows(info, keep, got):
+    rows, width = keep.shape
+
+    def kernel(info_ref, keep_ref, got_ref, out_ref):
+        y = info_ref[2]
+        reorder_in(info_ref, keep_ref, out_ref, pl.ds(pl.multiple_of(y * rows, rows), rows))
+        reorder_in(info_ref, got_ref, out_ref, pl.ds(pl.multiple_of((1 - y) * rows, rows), rows))
+
+    return rowwise(kernel, [info, keep, got], [((2 * rows, width), BF)])[0]
+
+
+def local_rows(info, array):
+    def kernel(info_ref, in_ref, out_ref):
+        reorder_in(info_ref, in_ref, out_ref)
+
+    return rowwise(kernel, [info, array], [(array.shape, array.dtype)])[0]
+
+
+def norm_rows(info, values, gain):
+    def kernel(info_ref, in_ref, gain_ref, out_ref):
+        rows = in_ref[...].astype(F32)
+        out_ref[...] = (rows * inverse_rms(rows) * gain_ref[...]).astype(BF)
+
+    return rowwise(kernel, [info, values, gain], [(values.shape, BF)])[0]
+
+
+def add_norm(info, rows, both, gain):
     own, other = both
-    return own + swap(other, "c").astype(F32)
+
+    def kernel(info_ref, row_ref, own_ref, got_ref, gain_ref, hidden_ref, norm_ref):
+        hidden = row_ref[...].astype(F32) + (own_ref[...] + got_ref[...].astype(F32))
+        hidden_ref[...] = hidden
+        norm_ref[...] = (hidden * inverse_rms(hidden) * gain_ref[...]).astype(BF)
+
+    return rowwise(kernel, [info, rows, own, swap(other, "c"), gain], [(rows.shape, F32), (rows.shape, BF)])
+
+
+def add_out(info, hidden, both):
+    own, other = both
+    rows, width = hidden.shape
+    half = rows // 2
+
+    def kernel(info_ref, hidden_ref, own_ref, got_ref, keep_ref, send_ref, scratch):
+        y = info_ref[2]
+        scratch[...] = hidden_ref[...] + (own_ref[...] + got_ref[...].astype(F32))
+        reorder_out(info_ref, scratch, keep_ref, pl.ds(pl.multiple_of(y * half, half), half))
+        reorder_out(info_ref, scratch, send_ref, pl.ds(pl.multiple_of((1 - y) * half, half), half))
+
+    return rowwise(
+        kernel,
+        [info, hidden, own, swap(other, "c")],
+        [((half, width), BF)] * 2,
+        [((rows, width), F32)],
+    )
+
+
+def step_state(info, state, both, gate, gain):
+    own, other = both
+
+    def kernel(info_ref, state_ref, own_ref, got_ref, gate_ref, gain_ref, next_ref, norm_ref, update_ref):
+        update = own_ref[...] + got_ref[...].astype(F32)
+        update_ref[...] = update
+        after = gate_ref[...] * state_ref[...] + (1.0 - gate_ref[...]) * update
+        next_ref[...] = after
+        norm_ref[...] = (after * inverse_rms(after) * gain_ref[...]).astype(BF)
+
+    return rowwise(
+        kernel,
+        [info, state, own, swap(other, "c"), gate, gain],
+        [(state.shape, F32), (state.shape, BF), (state.shape, F32)],
+    )
+
+
+def last_state(info, state, both, gate):
+    own, other = both
+
+    def kernel(info_ref, state_ref, own_ref, got_ref, gate_ref, final_ref, update_ref, scratch):
+        update = own_ref[...] + got_ref[...].astype(F32)
+        update_ref[...] = update
+        scratch[...] = gate_ref[...] * state_ref[...] + (1.0 - gate_ref[...]) * update
+        reorder_out(info_ref, scratch, final_ref)
+
+    return rowwise(
+        kernel,
+        [info, state, own, swap(other, "c"), gate],
+        [(state.shape, BF), (state.shape, F32)],
+        [(state.shape, F32)],
+    )
+
+
+def back_hidden(info, hidden, both, gain, dy):
+    own, other = both
+
+    def kernel(info_ref, hidden_ref, own_ref, got_ref, gain_ref, dy_ref, grad_ref, branch_ref, gain_grad_ref):
+        grad = own_ref[...] + got_ref[...].astype(F32)
+        back, gain_grad_ref[...] = rms_back(hidden_ref[...], gain_ref[...], grad)
+        total = dy_ref[...].astype(F32) + back
+        grad_ref[...] = total
+        branch_ref[...] = total.astype(BF)
+
+    return rowwise(
+        kernel,
+        [info, hidden, own, swap(other, "c"), gain, dy],
+        [(hidden.shape, F32), (hidden.shape, BF), ((1, hidden.shape[1]), F32)],
+    )
+
+
+def back_update(info, grad, gate):
+    def kernel(info_ref, grad_ref, gate_ref, out_ref):
+        out_ref[...] = ((1.0 - gate_ref[...]) * grad_ref[...].astype(F32)).astype(BF)
+
+    return rowwise(kernel, [info, grad, gate], [(grad.shape, BF)])[0]
+
+
+def back_state(info, grad, state, update, both, gate, gain):
+    own, other = both
+    width = state.shape[1]
+
+    def kernel(
+        info_ref, grad_ref, state_ref, update_ref, own_ref, got_ref, gate_ref, gain_ref, out_ref, low_ref, gain_grad_ref, gate_grad_ref
+    ):
+        gate_open = gate_ref[...]
+        grad_now = grad_ref[...].astype(F32)
+        values = state_ref[...]
+        gate_grad_ref[...] = jnp.sum(grad_now * (values - update_ref[...]), axis=0, keepdims=True) * (
+            gate_open * (1.0 - gate_open)
+        )
+        back, gain_grad_ref[...] = rms_back(values, gain_ref[...], own_ref[...] + got_ref[...].astype(F32))
+        total = gate_open * grad_now + back
+        out_ref[...] = total
+        low_ref[...] = ((1.0 - gate_open) * total).astype(BF)
+
+    return rowwise(
+        kernel,
+        [info, grad, state, update, own, swap(other, "c"), gate, gain],
+        [(state.shape, F32), (state.shape, BF), ((1, width), F32), ((1, width), F32)],
+    )
+
+
+def back_input(info, values, both, gain, grad_hidden):
+    own, other = both
+    rows, width = values.shape
+    half = rows // 2
+
+    def kernel(info_ref, value_ref, own_ref, got_ref, gain_ref, grad_ref, keep_ref, send_ref, gain_grad_ref, scratch):
+        y = info_ref[2]
+        grad = own_ref[...] + got_ref[...].astype(F32)
+        back, gain_grad_ref[...] = rms_back(value_ref[...].astype(F32), gain_ref[...], grad)
+        scratch[...] = grad_ref[...] + back
+        reorder_out(info_ref, scratch, keep_ref, pl.ds(pl.multiple_of(y * half, half), half))
+        reorder_out(info_ref, scratch, send_ref, pl.ds(pl.multiple_of((1 - y) * half, half), half))
+
+    return rowwise(
+        kernel,
+        [info, values, own, swap(other, "c"), gain, grad_hidden],
+        [((half, width), F32), ((half, width), BF), ((1, width), F32)],
+        [((rows, width), F32)],
+    )
+
+
+def place_rows(info, keep, got):
+    shape = (2,) + keep.shape
+
+    def kernel(info_ref, keep_ref, got_ref, out_ref):
+        y = info_ref[2]
+        out_ref[y] = keep_ref[...]
+        out_ref[1 - y] = got_ref[...].astype(keep.dtype)
+
+    return rowwise(kernel, [info, keep, got], [(shape, keep.dtype)])[0]
+
+
+def place_state(info, near, near_c, far, far_c):
+    rows, width = near.shape
+
+    def kernel(info_ref, near_ref, near_c_ref, far_ref, far_c_ref, out_ref):
+        c, y = info_ref[0], info_ref[2]
+        here = pl.ds(pl.multiple_of(c * rows, rows), rows)
+        there = pl.ds(pl.multiple_of((1 - c) * rows, rows), rows)
+        out_ref[y, here] = near_ref[...]
+        out_ref[y, there] = near_c_ref[...]
+        out_ref[1 - y, here] = far_ref[...]
+        out_ref[1 - y, there] = far_c_ref[...]
+
+    return rowwise(kernel, [info, near, near_c, far, far_c], [((2, 2 * rows, width), near.dtype)])[0]
 
 
 SCALE = HEAD_DIM ** (-0.5)
@@ -603,27 +810,28 @@
     state_cotangent,
 ):
     y, c = lax.axis_index("y"), lax.axis_index("c")
-    micro, rows_local, width = tokens.shape[0], tokens.shape[2], tokens.shape[3]
-    state_rows = init_state.shape[0]
-    state_half = state_rows // 2
-
-    def own_rows(array):
-        keep = lax.dynamic_index_in_dim(array[:, 0], y, 0, keepdims=False)
-        send = lax.dynamic_index_in_dim(array[:, 0], 1 - y, 0, keepdims=False)
-        got = swap(send, "y")
-        return jnp.where(y == 0, jnp.concatenate([keep, got]), jnp.concatenate([got, keep]))
-
-    def to_owner(rows, wide):
-        split = rows.reshape(2, rows_local, width)
-        keep = lax.dynamic_index_in_dim(split, y, 0, keepdims=False)
-        send = lax.dynamic_index_in_dim(split, 1 - y, 0, keepdims=False)
-        got = swap(send.astype(BF), "y").astype(wide)
-        keep = keep.astype(wide)
-        return jnp.where(y == 0, jnp.stack([keep, got]), jnp.stack([got, keep]))[:, None]
-
-    x_rows = to_local(own_rows(tokens))
+    width = tokens.shape[3]
+    state_half = init_state.shape[0] // 2
+    blocks = 4 * tokens.shape[2] // BLOCK
     valid_count = lax.dynamic_index_in_dim(counts[:, 0], y, 0, keepdims=False)
-
+    if lax.axis_size("r") == 1:
+        z, x = lax.axis_index("z"), lax.axis_index("x")
+        places = width_places()
+        back = [
+            jnp.bitwise_xor(x, x_to) * RING + lax.rem(z - z_to + RING, RING) for z_to in range(RING) for x_to in range(2)
+        ]
+        before, after = (lambda array: array), (lambda array: array)
+    else:
+        places = back = list(range(PIECES))
+        before, after = to_local, from_local
+    info = jnp.stack([jnp.asarray(v, jnp.int32) for v in [c, valid_count, y] + places + back])
+
+    def micro(array, index):
+        return lax.dynamic_index_in_dim(array[:, 0], index, 0, keepdims=False)
+
+    shard_rows = token_output.shape[0]
+    flat = lambda array: array.reshape(shard_rows, -1)
+    token_got = swap(micro(tokens, 1 - y), "y")
     small = jnp.concatenate(
         [
             lax.dynamic_slice_in_dim(init_state, c * state_half, state_half, 0),
@@ -633,82 +841,73 @@
         ],
         axis=0,
     )
-    shard_rows = token_output.shape[0]
-    flat = lambda array: array.reshape(shard_rows, -1)
     small = gather_rows(small)
     w_token = gather_weight(flat(token_weights))
     w_mid = gather_weight(jnp.concatenate([flat(state_weights), state_output, token_output], axis=1))
+    dy_got = swap(micro(cotangent, 1 - y), "y")
     w_up = gather_weight(hidden_up)
     w_down = gather_weight(hidden_down)
     head = token_output.shape[1]
     at_state, at_state_out, at_token_out = 0, 3 * head, 4 * head
-    gains = small[state_half : state_half + 3].astype(F32)
-    gate_open = jax.nn.sigmoid(small[state_half + 3].astype(F32))
+    gains = [small[state_half + i : state_half + i + 1].astype(F32) for i in range(3)]
+    gate_open = jax.nn.sigmoid(small[state_half + 3 : state_half + 4].astype(F32))
     state_now = small[:state_half].astype(F32)
 
-    dy_rows = to_local(own_rows(cotangent))
+    x_rows = own_rows(info, before(micro(tokens, y)), before(token_got))
+    normed = pair(norm_rows(info, x_rows, gains[0]))
+    state_norm = pair(norm_rows(info, state_now, gains[1]))
+    dy_rows = own_rows(info, before(micro(cotangent, y)), before(dy_got))
     dy_pair = pair(dy_rows)
     grad_final = lax.dynamic_slice(
         state_cotangent, (y, 0, c * state_half, 0), (1, 1, state_half, width)
     )[0, 0]
-    grad_final = to_local(grad_final)
-
-    seq_length = 4 * rows_local
-    blocks = seq_length // BLOCK
-    info = jnp.stack([c, valid_count]).astype(jnp.int32)
-    x_values = x_rows.astype(F32)
-    normed = pair(rms_forward(x_values, gains[0]))
+    grad_final = local_rows(info, before(grad_final))
+
     token_proj = project(*normed, w_token, 0, 3 * head, 3 * head // 2, blocks=blocks)
-
     kept = []
     mixed = []
     for b in range(blocks):
-        state_norm = pair(rms_forward(state_now, gains[1]))
         state_proj = project(*state_norm, w_mid, at_state, 3 * head, 3 * head)
         mixed_b, state_flat, logs = attend_forward(b, blocks, info, token_proj, state_proj)
         mixed.append(mixed_b)
-        update = fold(merge([state_flat], w_mid, at_state_out))
+        both = merge([state_flat], w_mid, at_state_out)
+        if b < blocks - 1:
+            state_next, next_norm, update = step_state(info, state_now, both, gate_open, gains[1])
+        else:
+            final_rows, update = last_state(info, state_now, both, gate_open)
+            state_next, next_norm = None, None
         kept.append((state_now, state_norm, state_proj, logs, state_flat, update))
-        state_now = gate_open * state_now + (1.0 - gate_open) * update
-    hidden = x_values + fold(merge(mixed, w_mid, at_token_out, blocks=blocks))
-    hidden_norm = pair(rms_forward(hidden, gains[2]))
+        state_now = state_next
+        state_norm = None if next_norm is None else pair(next_norm)
+    hidden, hidden_own = add_norm(info, x_rows, merge(mixed, w_mid, at_token_out, blocks=blocks), gains[2])
+    hidden_norm = pair(hidden_own)
     ff = hidden_up.shape[1]
     activated, slope = project(*hidden_norm, w_up, 0, ff, ff // 2, activate=True)
-    result = (hidden + fold(merge([activated], w_down, 0))).astype(BF)
-    output = to_owner(from_local(result), BF)
-
-    final_half = from_local(state_now.astype(BF))
-    final_pair = jnp.stack([final_half, swap(final_half, "y")])
-    final_pair = jnp.where(y == 0, final_pair, final_pair[::-1])
-    final_other = swap(final_pair, "c")
-    final_state = jnp.where(
-        c == 0,
-        jnp.concatenate([final_pair, final_other], axis=1),
-        jnp.concatenate([final_other, final_pair], axis=1),
-    )[:, None]
-
+    keep, send = add_out(info, hidden, merge([activated], w_down, 0))
+    output = place_rows(info, after(keep), swap(after(send), "y"))[:, None]
+    final_rows = after(final_rows)
+    final_far = swap(final_rows, "y")
+    final_state = place_state(info, final_rows, swap(final_rows, "c"), final_far, swap(final_far, "c"))[:, None]
+
+    grad_up = project(*dy_pair, w_down, 0, ff, ff // 2, gate=slope)
     grad_hidden_down = reduce_weight(outer([dy_pair], [activated], ff // 2))
-    grad_up = project(*dy_pair, w_down, 0, ff, ff // 2, gate=slope)
-    grad_hidden_norm = fold(merge([grad_up], w_up, 0))
+    both = merge([grad_up], w_up, 0)
     grad_hidden_up = reduce_weight(outer([hidden_norm], [grad_up], ff // 2))
-    through, gain_hidden = rms_backward(hidden, gains[2], grad_hidden_norm)
-    grad_hidden = dy_rows.astype(F32) + through
-    branch = pair(grad_hidden.astype(BF))
+    grad_hidden, branch, gain_hidden = back_hidden(info, hidden, both, gains[2], dy_rows)
+    branch = pair(branch)
     grad_mixed = project(*branch, w_mid, at_token_out, head, head, blocks=blocks)
     grad_token_output = reduce_weight(
         outer([branch], [jnp.concatenate(mixed, axis=1)], head, blocks=blocks)
     )
 
-    grad_state = grad_final.astype(F32)
-    grad_gate = jnp.zeros((width,), F32)
-    gain_state = jnp.zeros((width,), F32)
+    grad_state = grad_final
+    grad_update = pair(back_update(info, grad_final, gate_open))
+    gate_sums, gain_sums = [], []
     proj_grads = [None] * blocks
     update_all, flat_all, norm_all, state_grads = [], [], [], []
     later = None
     for b in reversed(range(blocks)):
         state_before, state_norm, state_proj, logs, state_flat, update = kept[b]
-        grad_update = pair(((1.0 - gate_open) * grad_state).astype(BF))
-        grad_gate = grad_gate + jnp.sum(grad_state * (state_before - update), axis=0)
         grad_state_mixed = project(*grad_update, w_mid, at_state_out, head, head)
         proj_grads[b], state_grad, later = attend_backward(
             b, blocks, info, token_proj, state_proj, logs, grad_mixed, grad_state_mixed, later
@@ -717,27 +916,39 @@
         flat_all.append(state_flat)
         norm_all.append(state_norm)
         state_grads.append(state_grad)
-        partial = merge([state_grad], w_mid, at_state)
-        previous, gain_piece = rms_backward(state_before, gains[1], fold(partial))
-        gain_state = gain_state + gain_piece
-        grad_state = gate_open * grad_state + previous
-    grad_gate = grad_gate * gate_open * (1.0 - gate_open)
-    grad_state_output = reduce_weight(outer(update_all, flat_all, head))
-    grad_state_weights = reduce_weight(outer(norm_all, state_grads, 3 * head)).reshape(-1, 3, head)
-    grad_normed = fold(merge(proj_grads, w_token, 0, blocks=blocks))
+        both = merge([state_grad], w_mid, at_state)
+        grad_state, low, gain_sum, gate_sum = back_state(
+            info, grad_state, state_before, update, both, gate_open, gains[1]
+        )
+        grad_update = pair(low) if b > 0 else None
+        gain_sums.append(gain_sum)
+        gate_sums.append(gate_sum)
+    both = merge(proj_grads, w_token, 0, blocks=blocks)
     grad_token_weights = reduce_weight(
         outer([normed], [jnp.concatenate(proj_grads, axis=1)], 3 * head, blocks=blocks)
     ).reshape(-1, 3, head)
-    through, gain_token = rms_backward(x_values, gains[0], grad_normed)
-    input_grad = to_owner(from_local(grad_hidden + through), F32)
-
-    vectors = from_local(jnp.stack([gain_token, gain_state, gain_hidden, grad_gate]))
-    vectors = lax.psum_scatter(vectors, ("r", "z", "x"), scatter_dimension=1, tiled=True)
-    vectors = lax.psum(vectors, ("y", "c"))
-    init_grad = from_local(grad_state)
-    init_grad = lax.psum_scatter(init_grad, ("r", "z", "x"), scatter_dimension=1, tiled=True)
-    init_grad = lax.psum(init_grad, "y")
-    init_grad = lax.all_gather(init_grad, "c", axis=0, tiled=True)
+    keep, send, gain_token = back_input(info, x_rows, both, gains[0], grad_hidden)
+    input_grad = place_rows(info, after(keep), swap(after(send), "y"))[:, None]
+    grad_state_weights = reduce_weight(outer(norm_all, state_grads, 3 * head)).reshape(-1, 3, head)
+    grad_state_output = reduce_weight(outer(update_all, flat_all, head))
+
+    vectors = jnp.concatenate(
+        [gain_token, sum(gain_sums), gain_hidden, sum(gate_sums), jnp.zeros((12, width), F32)], axis=0
+    )
+    rows = jnp.concatenate([grad_state, vectors], axis=0).astype(BF)
+    half = width // 2
+    total = (rows[:, :half].astype(F32) + swap(rows[:, half:], "x").astype(F32)).astype(BF)
+    size = half // RING
+    near = total[:, :size].astype(F32)
+    for k in range(1, RING):
+        near = near + turn(total[:, k * size : (k + 1) * size], RING - k).astype(F32)
+    if lax.axis_size("r") > 1:
+        near = lax.psum_scatter(near, "r", scatter_dimension=1, tiled=True)
+    near = near + swap(near, "y")
+    far = swap(near, "c")
+    states, others = near[:state_half], far[:state_half]
+    init_grad = jnp.where(c == 0, jnp.concatenate([states, others]), jnp.concatenate([others, states]))
+    vectors = near[state_half:] + far[state_half:]
     return (
         output,
         final_state,

time: 837 us -> 672 us (0.80)
  local copies, waits for them, and re-layouts: 125 us -> 71.3 us
  other arithmetic: 64.5 us -> 18.2 us
  waiting for transfers between devices: 211 us -> 184 us
  Pallas kernels: 257 us -> 234 us
  between operations: 15.6 us -> 2.41 us
  starting transfers between devices: 147 us -> 157 us
    ppermute x71 -> x75, waiting for transfers between devices: 87.4 us -> 123 us  [swap(): return lax.ppermute(array, axis, [(0, 1), (1, 0)])]
    unnamed x4 -> x0, waiting for transfers between devices: 34.6 us -> none
    reduce_scatter x1 -> x0, waiting for transfers between devices: 26.7 us -> none  [body(): lax.psum_scatter(init_grad, ('r', 'z', 'x'), scatter_dimension=1, tiled=T...]
    dynamic_slice x31 -> x0, local copies, waits for them, and re-layouts: 26.6 us -> none  [the longest x27 21.6 us: take_pieces(): lax.dynamic_index_in_dim(split, place, axis, keepdims=False)]
    another operation x13 -> x1, local copies, waits for them, and re-layouts: 26.2 us -> 0.74 us  [body(): jnp.stack([jnp.asarray(v, jnp.int32) for v in [c, valid_count, y] + place...]
    pallas_call x48 -> x65, Pallas kernels: 257 us -> 234 us  [call(): pl.pallas_call(kernel, grid=grid, in_specs=in_specs, out_specs=out_specs,...]
    psum x1 -> x0, waiting for transfers between devices: 19.4 us -> none  [body(): init_grad = lax.psum(init_grad, 'y')]
    ppermute x33 -> x36, waiting for transfers between devices: 42.4 us -> 60.5 us  [turn(): lax.ppermute(array, 'z', [(i, (i + steps) % RING) for i in range(RING)])]
  transfers between devices with their start and end apart: 107 -> 111, of which waited for: 23 -> 31; matrix products, arithmetic and copies ran while one was open for 19% -> 5% of each run, Pallas kernels for 29% -> 27%
where the time goes in v3:
time: 672 us; the launch traced here: 666 us
  Pallas kernels  234 us (35%)
  waiting for transfers between devices  184 us (27%)
  starting transfers between devices  157 us (23%)
  local copies, waits for them, and re-layouts  71.3 us (11%)
  other arithmetic  18.2 us (3%)
    pallas_call x65, Pallas kernels, call(): pl.pallas_call(kernel, grid=grid, in_specs=in_specs, out_specs=out_specs,...  234 us
    ppermute x75, waiting for transfers between devices, swap(): return lax.ppermute(array, axis, [(0, 1), (1, 0)])  123 us
    ppermute x36, starting transfers between devices, turn(): lax.ppermute(array, 'z', [(i, (i + steps) % RING) for i in range(RING)])  88.4 us
    ppermute x75, starting transfers between devices, swap(): return lax.ppermute(array, axis, [(0, 1), (1, 0)])  68.1 us
    ppermute x36, waiting for transfers between devices, turn(): lax.ppermute(array, 'z', [(i, (i + steps) % RING) for i in range(RING)])  60.5 us
    unnamed x363, local copies, waits for them, and re-layouts  60.3 us
  transfers between devices with their start and end apart: 111, of which 31 were waited for; matrix products, arithmetic and copies ran while one was open for 5% of the time, Pallas kernels for 27%

profile of v3, /device:TPU:0, one launch (start us, length us, event | category | flops | bytes accessed | tf_op | source)
XLA Modules:
  0.0 665.6 jit_solution(16857128546865008705)
XLA Ops:
  26.8 8.0 %collective-permute-done.7.refs_2_ = bf16[128,768]{1,0:T(8,128)(2,1)S(1)} collective-permute-done((bf16[128,768]{1,0:T(8,128)(2,1)S(1)}, bf16[128,768]{1,0:T(8,128)(2,1)S(1)}, u32[]{:S(2)}, u32[]{:S(2)}) %collective-permute-start.7) | collective-permute-done | bytes 196640 | tf_op jit(solution)/shard_map/ppermute | solution.py:26
  44.1 10.3 %collective-permute-done.17.refs_2_ = bf16[128,1280]{1,0:T(8,128)(2,1)S(1)} collective-permute-done((bf16[128,1280]{1,0:T(8,128)(2,1)S(1)}, bf16[128,1280]{1,0:T(8,128)(2,1)S(1)}, u32[]{:S(2)}, u32[]{:S(2)}) %collective-permute-start.17) | collective-permute-done | bytes 327712 | tf_op jit(solution)/shard_map/ppermute | solution.py:26
  75.8 17.8 %collective-permute-done.13.args_8_ = bf16[256,768]{1,0:T(8,128)(2,1)S(1)} collective-permute-done((bf16[256,768]{1,0:T(8,128)(2,1)S(1)}, bf16[256,768]{1,0:T(8,128)(2,1)S(1)}, u32[]{:S(2)}, u32[]{:S(2)}) %collective-permute-start.13) | collective-permute-done | bytes 393248 | tf_op jit(solution)/shard_map/ppermute | solution.py:22
  113.3 10.2 %collective-permute-done.23.args_8_.args_7_ = bf16[256,1280]{1,0:T(8,128)(2,1)S(1)} collective-permute-done((bf16[256,1280]{1,0:T(8,128)(2,1)S(1)}, bf16[256,1280]{1,0:T(8,128)(2,1)S(1)}, u32[]{:S(2)}, u32[]{:S(2)}) %collective-permute-start.23) | collective-permute-done | bytes 655392 | tf_op jit(solution)/shard_map/ppermute | solution.py:22
  130.7 9.5 %shard_map.227 = (bf16[2,512,256]{2,1,0:T(8,128)(2,1)S(1)}, bf16[2,512,256]{2,1,0:T(8,128)(2,1)S(1)}, f32[2,512,128]{2,1,0:T(8,128)S(1)}) custom-call(s32[19]{0:T(128)S(1)} %stack.76.info_ref.args_0_, bf16[2,1024,768]{2,1,0:T(8,128)(2,1)} %shard_map.223.token_ref.args_1_, bf16[2,512,768]{2,1,0:T(8,128)(2,1)S(1)} %copy-done.23), custom_call_target="tpu_custom_call" | custom-call | flops 2147483648 | bytes 6291532 | tf_op jit(solution)/shard_map/pallas_call | solution.py:96
  157.4 10.9 %shard_map.231 = (bf16[2,512,256]{2,1,0:T(8,128)(2,1)S(1)}, bf16[2,512,256]{2,1,0:T(8,128)(2,1)S(1)}, f32[2,512,128]{2,1,0:T(8,128)S(1)}) custom-call(s32[19]{0:T(128)S(1)} %stack.76.info_ref.args_0_, bf16[2,1024,768]{2,1,0:T(8,128)(2,1)} %shard_map.223.token_ref.args_1_, bf16[2,512,768]{2,1,0:T(8,128)(2,1)S(1)} %copy-done.25), custom_call_target="tpu_custom_call" | custom-call | flops 2684354560 | bytes 6291532 | tf_op jit(solution)/shard_map/pallas_call | solution.py:96
  173.5 7.3 %collective-permute-start.29 = (bf16[128,1024]{1,0:T(8,128)(2,1)S(1)}, bf16[128,1024]{1,0:T(8,128)(2,1)S(1)}, u32[]{:S(2)}, u32[]{:S(2)}) collective-permute-start(bf16[128,1024]{1,0:T(8,128)(2,1)S(1)} %copy-done.101), channel_id=1, source_target_pairs={{0,8},{8,16},{16,24},{24,0},{1,9},{9,17},{17,25},{25,1},{2,10},{10... | collective-permute-start | bytes 786440 | tf_op jit(solution)/shard_map/ppermute | solution.py:26
  192.5 9.7 %collective-permute-done.30.refs_2_ = bf16[128,1024]{1,0:T(8,128)(2,1)S(1)} collective-permute-done((bf16[128,1024]{1,0:T(8,128)(2,1)S(1)}, bf16[128,1024]{1,0:T(8,128)(2,1)S(1)}, u32[]{:S(2)}, u32[]{:S(2)}) %collective-permute-start.30) | collective-permute-done | bytes 262176 | tf_op jit(solution)/shard_map/ppermute | solution.py:26
  202.9 10.4 %collective-permute-start.39 = (bf16[128,1024]{1,0:T(8,128)(2,1)S(1)}, bf16[128,1024]{1,0:T(8,128)(2,1)S(1)}, u32[]{:S(2)}, u32[]{:S(2)}) collective-permute-start(bf16[128,1024]{1,0:T(8,128)(2,1)S(1)} %copy-done.102), channel_id=1, source_target_pairs={{0,16},{8,24},{16,0},{24,8},{1,17},{9,25},{17,1},{25,9},{2,18},{10... | collective-permute-start | bytes 786440 | tf_op jit(solution)/shard_map/ppermute | solution.py:26
  216.6 9.4 %collective-permute-done.39.refs_2_ = bf16[128,1024]{1,0:T(8,128)(2,1)S(1)} collective-permute-done((bf16[128,1024]{1,0:T(8,128)(2,1)S(1)}, bf16[128,1024]{1,0:T(8,128)(2,1)S(1)}, u32[]{:S(2)}, u32[]{:S(2)}) %collective-permute-start.39) | collective-permute-done | bytes 262176 | tf_op jit(solution)/shard_map/ppermute | solution.py:26
  243.7 8.4 %collective-permute-done.35.args_7_.args_6_ = bf16[256,1024]{1,0:T(8,128)(2,1)S(1)} collective-permute-done((bf16[256,1024]{1,0:T(8,128)(2,1)S(1)}, bf16[256,1024]{1,0:T(8,128)(2,1)S(1)}, u32[]{:S(2)}, u32[]{:S(2)}) %collective-permute-start.35) | collective-permute-done | bytes 524320 | tf_op jit(solution)/shard_map/ppermute | solution.py:22
  254.6 8.8 %collective-permute-done.44.args_6_.args_7_ = bf16[256,1024]{1,0:T(8,128)(2,1)S(1)} collective-permute-done((bf16[256,1024]{1,0:T(8,128)(2,1)}, bf16[256,1024]{1,0:T(8,128)(2,1)S(1)}, u32[]{:S(2)}, u32[]{:S(2)}) %collective-permute-start.44) | collective-permute-done | bytes 524320 | tf_op jit(solution)/shard_map/ppermute | solution.py:22
  281.2 12.4 %shard_map.235 = (bf16[2,1024,1024]{2,1,0:T(8,128)(2,1)}, bf16[2,1024,1024]{2,1,0:T(8,128)(2,1)}) custom-call(bf16[512,1024]{1,0:T(8,128)(2,1)S(1)} %get-tuple-element.138.args_0_, bf16[512,1024]{1,0:T(8,128)(2,1)} %collective-permute-done.28.args_1_, bf16[256,1024]{1,0:T(8,128)(2,1)S(1)} %copy-done.131, bf16[256,1024]{1,0:T(8,128)(2,1)S(1)} %copy-done.134, ...), custom_call_target="tpu_custom_call" | custom-call | flops 4294967296 | bytes 14680064 | tf_op jit(solution)/shard_map/pallas_call | solution.py:96
  296.4 8.6 %shard_map.244.args_0_.args_2_ = bf16[2,1024,1024]{2,1,0:T(8,128)(2,1)} custom-call(bf16[512,1024]{1,0:T(8,128)(2,1)S(1)} %shard_map.243.args_0_.dy_ref, bf16[512,1024]{1,0:T(8,128)(2,1)} %collective-permute-done.54.args_1_, bf16[256,1024]{1,0:T(8,128)(2,1)S(1)} %get-tuple-element.142.args_1_.args_2_, bf16[256,1024]{1,0:T(8,128)(2,1)} %get-tuple-element.143.args_2_.args_3_, ...), custom_call_target="tpu_custom_call" | custom-call | flops 4294967296 | bytes 14680064 | tf_op jit(solution)/shard_map/pallas_call | solution.py:96
  308.1 8.5 %shard_map.245 = (f32[512,1024]{1,0:T(8,128)}, bf16[512,1024]{1,0:T(8,128)(2,1)S(1)}) custom-call(bf16[2,1024,1024]{2,1,0:T(8,128)(2,1)} %shard_map.244.args_0_.args_2_, bf16[256,1024]{1,0:T(8,128)(2,1)S(1)} %copy-done.132, bf16[256,1024]{1,0:T(8,128)(2,1)S(1)} %copy-done.135, bf16[256,1024]{1,0:T(8,128)(2,1)} %collective-permute-done.32.args_4_.args_3_, ...), custom_call_target="tpu_custom_call" | custom-call | flops 4294967296 | bytes 11534336 | tf_op jit(solution)/shard_map/pallas_call | solution.py:96
  334.4 7.5 %shard_map.275 = (bf16[256,1024]{1,0:T(8,128)(2,1)}, bf16[256,1024]{1,0:T(8,128)(2,1)}, bf16[512,1024]{1,0:T(8,128)(2,1)S(1)}, bf16[512,1024]{1,0:T(8,128)(2,1)}, bf16[512,1024]{1,0:T(8,128)(2,1)S(1)}) custom-call(bf16[512,1024]{1,0:T(8,128)(2,1)S(1)} %get-tuple-element.138.args_0_, bf16[512,1024]{1,0:T(8,128)(2,1)} %collective-permute-done.28.args_1_, ...), custom_call_target="tpu_custom_call" | custom-call | flops 4294967296 | bytes 10485760 | tf_op jit(solution)/shard_map/pallas_call | solution.py:96
  358.1 20.4 %shard_map.251 = (bf16[2,512,768]{2,1,0:T(8,128)(2,1)S(1)}, bf16[2,512,768]{2,1,0:T(8,128)(2,1)S(1)}, f32[2,512,512]{2,1,0:T(8,128)}) custom-call(s32[19]{0:T(128)S(1)} %stack.76.info_ref.args_0_, bf16[2,1024,768]{2,1,0:T(8,128)(2,1)} %shard_map.223.token_ref.args_1_, bf16[2,512,768]{2,1,0:T(8,128)(2,1)} %shard_map.230.state_ref.args_2_, ...), custom_call_target="tpu_custom_call" | custom-call | flops 6710886400 | bytes 12058700 | tf_op jit(solution)/shard_map/pallas_call | solution.py:96
  384.6 8.8 %shard_map.237 = (f32[512,1024]{1,0:T(8,128)}, bf16[512,1024]{1,0:T(8,128)(2,1)}) custom-call(bf16[2,1024,1024]{2,1,0:T(8,128)(2,1)} %get-tuple-element.141.args_0_.args_2_, bf16[256,1024]{1,0:T(8,128)(2,1)S(1)} %copy-done.124, bf16[256,1024]{1,0:T(8,128)(2,1)} %get-tuple-element.143.args_2_.args_3_, bf16[256,1024]{1,0:T(8,128)(2,1)S(1)} %copy-done.127, ...), custom_call_target="tpu_custom_call" | custom-call | flops 4294967296 | bytes 11534336 | tf_op jit(solution)/shard_map/pallas_call | solution.py:96
  433.4 10.6 %collective-permute-done.98.b_ref = bf16[512,1024]{1,0:T(8,128)(2,1)} collective-permute-done((bf16[512,1024]{1,0:T(8,128)(2,1)}, bf16[512,1024]{1,0:T(8,128)(2,1)}, u32[]{:S(2)}, u32[]{:S(2)}) %collective-permute-start.98) | collective-permute-done | bytes 1048608 | tf_op jit(solution)/shard_map/ppermute | solution.py:22
  450.9 8.5 %collective-permute-start.96 = (bf16[128,1024]{1,0:T(8,128)(2,1)}, bf16[128,1024]{1,0:T(8,128)(2,1)}, u32[]{:S(2)}, u32[]{:S(2)}) collective-permute-start(bf16[128,1024]{1,0:T(8,128)(2,1)} %get-tuple-element.217), channel_id=1, source_target_pairs={{0,8},{8,16},{16,24},{24,0},{1,9},{9,17},{17,25},{25,1},{2,10},{10... | collective-permute-start | bytes 786440 | tf_op jit(solution)/shard_map/ppermute | solution.py:26
  467.3 17.8 %shard_map.255 = (bf16[2,512,768]{2,1,0:T(8,128)(2,1)S(1)}, bf16[2,512,768]{2,1,0:T(8,128)(2,1)S(1)}) custom-call(s32[19]{0:T(128)S(1)} %stack.76.info_ref.args_0_, bf16[2,1024,768]{2,1,0:T(8,128)(2,1)} %shard_map.223.token_ref.args_1_, bf16[2,512,768]{2,1,0:T(8,128)(2,1)} %shard_map.226.state_ref.args_2_, f32[2,512,128]{2,1,0:T(8,128)S(1)} %copy-done.162, ...), custom_call_target="tpu_custom_call" | custom-call | flops 5368709120 | bytes 12058700 | tf_op jit(solution)/shard_map/pallas_call | solution.py:96
  521.4 7.6 %collective-permute-done.83.piece_ref = bf16[256,256]{1,0:T(8,128)(2,1)S(1)} collective-permute-done((bf16[256,256]{1,0:T(8,128)(2,1)S(1)}, bf16[256,256]{1,0:T(8,128)(2,1)S(1)}, u32[]{:S(2)}, u32[]{:S(2)}) %collective-permute-start.83) | collective-permute-done | bytes 131104 | tf_op jit(solution)/shard_map/ppermute | solution.py:22
  592.0 12.1 %collective-permute-done.105 = bf16[272,512]{1,0:T(8,128)(2,1)S(1)} collective-permute-done((bf16[272,512]{1,0:T(8,128)(2,1)S(1)}, bf16[272,512]{1,0:T(8,128)(2,1)S(1)}, u32[]{:S(2)}, u32[]{:S(2)}) %collective-permute-start.105) | collective-permute-done | bytes 278560 | tf_op jit(solution)/shard_map/ppermute | solution.py:22
  630.1 7.3 %collective-permute-start.81 = (bf16[128,768]{1,0:T(8,128)(2,1)S(1)}, bf16[128,768]{1,0:T(8,128)(2,1)S(1)}, u32[]{:S(2)}, u32[]{:S(2)}) collective-permute-start(bf16[128,768]{1,0:T(8,128)(2,1)S(1)} %get-tuple-element.198), channel_id=1, source_target_pairs={{0,16},{8,24},{16,0},{24,8},{1,17},{9,25},{17,1},{25,9},{2,18},{10... | collective-permute-start | bytes 589832 | tf_op jit(solution)/shard_map/ppermute | solution.py:26
  (669 shorter events, 412.3 us)
Async XLA Ops:
  17.8 38.0 %collective-permute-start = (bf16[256,1024]{1,0:T(8,128)(2,1)S(1)}, bf16[256,1024]{1,0:T(8,128)(2,1)S(1)}, u32[]{:S(2)}, u32[]{:S(2)}) collective-permute-start(bf16[256,1024]{1,0:T(8,128)(2,1)S(1)} %get-tuple-element.264), channel_id=1, source_target_pairs={{0,2},{2,0},{1,3},{3,1},{4,6},{6,4},{5,7},{7,5},{8,10},{10,8},{9,1... | collective-permute-start | bytes 1572872 | tf_op jit(solution)/shard_map/ppermute | solution.py:22
  58.2 40.4 %collective-permute-start.5 = (bf16[512,1024]{1,0:T(8,128)(2,1)S(1)}, bf16[512,1024]{1,0:T(8,128)(2,1)S(1)}, u32[]{:S(2)}, u32[]{:S(2)}) collective-permute-start(bf16[512,1024]{1,0:T(8,128)(2,1)S(1)} %shard_map.221.args_0_), channel_id=1, source_target_pairs={{0,1},{1,0},{2,3},{3,2},{4,5},{5,4},{6,7},{7,6},{8,9},{9,8},{10,11... | collective-permute-start | bytes 3145736 | tf_op jit(solution)/shard_map/ppermute | solution.py:22
  58.4 38.8 %collective-permute-start.19 = (bf16[256,1280]{1,0:T(8,128)(2,1)S(1)}, bf16[256,1280]{1,0:T(8,128)(2,1)S(1)}, u32[]{:S(2)}, u32[]{:S(2)}) collective-permute-start(bf16[256,1280]{1,0:T(8,128)(2,1)S(1)} %get-tuple-element.127.args_2_.args_1_), channel_id=1, source_target_pairs={{0,4},{4,0},{1,5},{5,1},{2,6},{6,2},{3,7},{7,3},{8,12},{12,8},{9,1... | collective-permute-start | bytes 1966088 | tf_op jit(solution)/shard_map/ppermute | solution.py:22
  173.4 56.6 %collective-permute-start.27 = (bf16[512,1024]{1,0:T(8,128)(2,1)}, bf16[512,1024]{1,0:T(8,128)(2,1)S(1)}, u32[]{:S(2)}, u32[]{:S(2)}) collective-permute-start(bf16[512,1024]{1,0:T(8,128)(2,1)} %get-tuple-element.136), channel_id=1, source_target_pairs={{0,1},{1,0},{2,3},{3,2},{4,5},{5,4},{6,7},{7,6},{8,9},{9,8},{10,11... | collective-permute-start | bytes 3145736 | tf_op jit(solution)/shard_map/ppermute | solution.py:22
  190.9 43.1 %collective-permute-start.53 = (bf16[256,1024]{1,0:T(8,128)(2,1)}, bf16[256,1024]{1,0:T(8,128)(2,1)S(1)}, u32[]{:S(2)}, u32[]{:S(2)}) collective-permute-start(bf16[256,1024]{1,0:T(8,128)(2,1)} %get-tuple-element.262), channel_id=1, source_target_pairs={{0,2},{2,0},{1,3},{3,1},{4,6},{6,4},{5,7},{7,5},{8,10},{10,8},{9,1... | collective-permute-start | bytes 1572872 | tf_op jit(solution)/shard_map/ppermute | solution.py:22
  234.0 41.5 %collective-permute-start.28 = (bf16[512,1024]{1,0:T(8,128)(2,1)S(1)}, bf16[512,1024]{1,0:T(8,128)(2,1)}, u32[]{:S(2)}, u32[]{:S(2)}) collective-permute-start(bf16[512,1024]{1,0:T(8,128)(2,1)S(1)} %get-tuple-element.138.args_0_), channel_id=1, source_target_pairs={{0,1},{1,0},{2,3},{3,2},{4,5},{5,4},{6,7},{7,6},{8,9},{9,8},{10,11... | collective-permute-start | bytes 3145736 | tf_op jit(solution)/shard_map/ppermute | solution.py:22
  254.5 40.8 %collective-permute-start.54 = (bf16[512,1024]{1,0:T(8,128)(2,1)S(1)}, bf16[512,1024]{1,0:T(8,128)(2,1)}, u32[]{:S(2)}, u32[]{:S(2)}) collective-permute-start(bf16[512,1024]{1,0:T(8,128)(2,1)S(1)} %shard_map.243.args_0_.dy_ref), channel_id=1, source_target_pairs={{0,1},{1,0},{2,3},{3,2},{4,5},{5,4},{6,7},{7,6},{8,9},{9,8},{10,11... | collective-permute-start | bytes 3145736 | tf_op jit(solution)/shard_map/ppermute | solution.py:22
  332.9 70.9 %collective-permute-start.51 = (bf16[256,1024]{1,0:T(8,128)(2,1)S(1)}, bf16[256,1024]{1,0:T(8,128)(2,1)}, u32[]{:S(2)}, u32[]{:S(2)}) collective-permute-start(bf16[256,1024]{1,0:T(8,128)(2,1)S(1)} %get-tuple-element.152.near_ref), channel_id=1, source_target_pairs={{0,2},{2,0},{1,3},{3,1},{4,6},{6,4},{5,7},{7,5},{8,10},{10,8},{9,1... | collective-permute-start | bytes 1572872 | tf_op jit(solution)/shard_map/ppermute | solution.py:22
  341.9 42.5 %collective-permute-start.90 = (bf16[256,1024]{1,0:T(8,128)(2,1)}, bf16[256,1024]{1,0:T(8,128)(2,1)}, u32[]{:S(2)}, u32[]{:S(2)}) collective-permute-start(bf16[256,1024]{1,0:T(8,128)(2,1)} %get-tuple-element.211), channel_id=1, source_target_pairs={{0,2},{2,0},{1,3},{3,1},{4,6},{6,4},{5,7},{7,5},{8,10},{10,8},{9,1... | collective-permute-start | bytes 1572872 | tf_op jit(solution)/shard_map/ppermute | solution.py:22
  342.4 50.9 %collective-permute-start.92 = (bf16[256,1024]{1,0:T(8,128)(2,1)}, bf16[256,1024]{1,0:T(8,128)(2,1)}, u32[]{:S(2)}, u32[]{:S(2)}) collective-permute-start(bf16[256,1024]{1,0:T(8,128)(2,1)} %get-tuple-element.213), channel_id=1, source_target_pairs={{0,4},{4,0},{1,5},{5,1},{2,6},{6,2},{3,7},{7,3},{8,12},{12,8},{9,1... | collective-permute-start | bytes 1572872 | tf_op jit(solution)/shard_map/ppermute | solution.py:22
  351.0 44.3 %collective-permute-start.97 = (bf16[256,1024]{1,0:T(8,128)(2,1)}, bf16[256,1024]{1,0:T(8,128)(2,1)}, u32[]{:S(2)}, u32[]{:S(2)}) collective-permute-start(bf16[256,1024]{1,0:T(8,128)(2,1)} %get-tuple-element.220), channel_id=1, source_target_pairs={{0,2},{2,0},{1,3},{3,1},{4,6},{6,4},{5,7},{7,5},{8,10},{10,8},{9,1... | collective-permute-start | bytes 1572872 | tf_op jit(solution)/shard_map/ppermute | solution.py:22
  352.6 46.3 %collective-permute-start.99 = (bf16[256,1024]{1,0:T(8,128)(2,1)}, bf16[256,1024]{1,0:T(8,128)(2,1)}, u32[]{:S(2)}, u32[]{:S(2)}) collective-permute-start(bf16[256,1024]{1,0:T(8,128)(2,1)} %get-tuple-element.222), channel_id=1, source_target_pairs={{0,4},{4,0},{1,5},{5,1},{2,6},{6,2},{3,7},{7,3},{8,12},{12,8},{9,1... | collective-permute-start | bytes 1572872 | tf_op jit(solution)/shard_map/ppermute | solution.py:22
  403.8 40.1 %collective-permute-start.98 = (bf16[512,1024]{1,0:T(8,128)(2,1)}, bf16[512,1024]{1,0:T(8,128)(2,1)}, u32[]{:S(2)}, u32[]{:S(2)}) collective-permute-start(bf16[512,1024]{1,0:T(8,128)(2,1)} %shard_map.280), channel_id=1, source_target_pairs={{0,4},{4,0},{1,5},{5,1},{2,6},{6,2},{3,7},{7,3},{8,12},{12,8},{9,1... | collective-permute-start | bytes 3145736 | tf_op jit(solution)/shard_map/ppermute | solution.py:22
  404.4 43.4 %collective-permute-start.100 = (bf16[512,1024]{1,0:T(8,128)(2,1)}, bf16[512,1024]{1,0:T(8,128)(2,1)}, u32[]{:S(2)}, u32[]{:S(2)}) collective-permute-start(bf16[512,1024]{1,0:T(8,128)(2,1)} %shard_map.281), channel_id=1, source_target_pairs={{0,2},{2,0},{1,3},{3,1},{4,6},{6,4},{5,7},{7,5},{8,10},{10,8},{9,1... | collective-permute-start | bytes 3145736 | tf_op jit(solution)/shard_map/ppermute | solution.py:22
  410.3 50.7 %collective-permute-start.59 = (bf16[256,1024]{1,0:T(8,128)(2,1)}, bf16[256,1024]{1,0:T(8,128)(2,1)S(1)}, u32[]{:S(2)}, u32[]{:S(2)}) collective-permute-start(bf16[256,1024]{1,0:T(8,128)(2,1)} %get-tuple-element.163.args_0_.args_2_), channel_id=1, source_target_pairs={{0,1},{1,0},{2,3},{3,2},{4,5},{5,4},{6,7},{7,6},{8,9},{9,8},{10,11... | collective-permute-start | bytes 1572872 | tf_op jit(solution)/shard_map/ppermute | solution.py:22
  443.9 52.5 %collective-permute-start.50 = (bf16[256,1024]{1,0:T(8,128)(2,1)S(1)}, bf16[256,1024]{1,0:T(8,128)(2,1)S(1)}, u32[]{:S(2)}, u32[]{:S(2)}) collective-permute-start(bf16[256,1024]{1,0:T(8,128)(2,1)S(1)} %get-tuple-element.152.near_ref), channel_id=1, source_target_pairs={{0,1},{1,0},{2,3},{3,2},{4,5},{5,4},{6,7},{7,6},{8,9},{9,8},{10,11... | collective-permute-start | bytes 1572872 | tf_op jit(solution)/shard_map/ppermute | solution.py:22
  447.7 48.7 %collective-permute-start.52 = (bf16[256,1024]{1,0:T(8,128)(2,1)}, bf16[256,1024]{1,0:T(8,128)(2,1)S(1)}, u32[]{:S(2)}, u32[]{:S(2)}) collective-permute-start(bf16[256,1024]{1,0:T(8,128)(2,1)} %collective-permute-done.51.far_ref), channel_id=1, source_target_pairs={{0,1},{1,0},{2,3},{3,2},{4,5},{5,4},{6,7},{7,6},{8,9},{9,8},{10,11... | collective-permute-start | bytes 1572872 | tf_op jit(solution)/shard_map/ppermute | solution.py:22
  450.2 48.6 %collective-permute-start.48 = (bf16[256,1024]{1,0:T(8,128)(2,1)}, bf16[256,1024]{1,0:T(8,128)(2,1)S(1)}, u32[]{:S(2)}, u32[]{:S(2)}) collective-permute-start(bf16[256,1024]{1,0:T(8,128)(2,1)} %get-tuple-element.147), channel_id=1, source_target_pairs={{0,2},{2,0},{1,3},{3,1},{4,6},{6,4},{5,7},{7,5},{8,10},{10,8},{9,1... | collective-permute-start | bytes 1572872 | tf_op jit(solution)/shard_map/ppermute | solution.py:22
  450.9 48.5 %collective-permute-start.96 = (bf16[128,1024]{1,0:T(8,128)(2,1)}, bf16[128,1024]{1,0:T(8,128)(2,1)}, u32[]{:S(2)}, u32[]{:S(2)}) collective-permute-start(bf16[128,1024]{1,0:T(8,128)(2,1)} %get-tuple-element.217), channel_id=1, source_target_pairs={{0,8},{8,16},{16,24},{24,0},{1,9},{9,17},{17,25},{25,1},{2,10},{10... | collective-permute-start | bytes 786440 | tf_op jit(solution)/shard_map/ppermute | solution.py:26
  461.0 47.9 %collective-permute-start.95 = (bf16[128,1024]{1,0:T(8,128)(2,1)}, bf16[128,1024]{1,0:T(8,128)(2,1)}, u32[]{:S(2)}, u32[]{:S(2)}) collective-permute-start(bf16[128,1024]{1,0:T(8,128)(2,1)} %get-tuple-element.216), channel_id=1, source_target_pairs={{0,16},{8,24},{16,0},{24,8},{1,17},{9,25},{17,1},{25,9},{2,18},{10... | collective-permute-start | bytes 786440 | tf_op jit(solution)/shard_map/ppermute | solution.py:26
  499.4 66.1 %collective-permute-start.60 = (bf16[512,1024]{1,0:T(8,128)(2,1)}, bf16[512,1024]{1,0:T(8,128)(2,1)}, u32[]{:S(2)}, u32[]{:S(2)}) collective-permute-start(bf16[512,1024]{1,0:T(8,128)(2,1)} %get-tuple-element.168), channel_id=1, source_target_pairs={{0,1},{1,0},{2,3},{3,2},{4,5},{5,4},{6,7},{7,6},{8,9},{9,8},{10,11... | collective-permute-start | bytes 3145736 | tf_op jit(solution)/shard_map/ppermute | solution.py:22
  577.3 39.0 %collective-permute-start.63 = (bf16[512,768]{1,0:T(8,128)(2,1)}, bf16[512,768]{1,0:T(8,128)(2,1)S(1)}, u32[]{:S(2)}, u32[]{:S(2)}) collective-permute-start(bf16[512,768]{1,0:T(8,128)(2,1)} %copy-done.62), channel_id=1, source_target_pairs={{0,4},{4,0},{1,5},{5,1},{2,6},{6,2},{3,7},{7,3},{8,12},{12,8},{9,1... | collective-permute-start | bytes 2359304 | tf_op jit(solution)/shard_map/ppermute | solution.py:22
  578.9 38.5 %collective-permute-start.65 = (bf16[512,768]{1,0:T(8,128)(2,1)}, bf16[512,768]{1,0:T(8,128)(2,1)S(1)}, u32[]{:S(2)}, u32[]{:S(2)}) collective-permute-start(bf16[512,768]{1,0:T(8,128)(2,1)} %copy-done.59), channel_id=1, source_target_pairs={{0,2},{2,0},{1,3},{3,1},{4,6},{6,4},{5,7},{7,5},{8,10},{10,8},{9,1... | collective-permute-start | bytes 2359304 | tf_op jit(solution)/shard_map/ppermute | solution.py:22
  619.8 39.5 %collective-permute-start.61 = (bf16[256,1024]{1,0:T(8,128)(2,1)}, bf16[256,1024]{1,0:T(8,128)(2,1)}, u32[]{:S(2)}, u32[]{:S(2)}) collective-permute-start(bf16[256,1024]{1,0:T(8,128)(2,1)} %get-tuple-element.171), channel_id=1, source_target_pairs={{0,2},{2,0},{1,3},{3,1},{4,6},{6,4},{5,7},{7,5},{8,10},{10,8},{9,1... | collective-permute-start | bytes 1572872 | tf_op jit(solution)/shard_map/ppermute | solution.py:22
  (265 other events, 3858.3 us)

commit v4 on v3

v4 whole, which is shorter than its diff:
```python
import functools

import jax
import jax.numpy as jnp
from jax import lax
from jax.experimental import pallas as pl
from jax.experimental.pallas import tpu as pltpu
from jax.sharding import Mesh
from jax.sharding import PartitionSpec as P

HEAD_DIM = 128
BLOCK = 512
EPSILON = 1e-06
MASKED = -1e30
COST = 1
GELU = 0.7978845608028654
RING = 4
BF = jnp.bfloat16
F32 = jnp.float32


def swap(array, axis):
    return lax.ppermute(array, axis, [(0, 1), (1, 0)])


def swap_z(array, bit):
    return lax.ppermute(array, "z", [(i, i ^ bit) for i in range(RING)])


def matmul(left, right, contract):
    return lax.dot_general(
        left, right, (contract, ((), ())), preferred_element_type=jnp.float32
    )


def mm(left, right):
    return matmul(left, right, ((1,), (0,)))


def mm_nt(left, right):
    return matmul(left, right, ((1,), (1,)))


def mm_tn(left, right):
    return matmul(left, right, ((0,), (0,)))


RING_BITS = (0, 2, 1, 3)


def width_places():
    z, x = lax.axis_index("z"), lax.axis_index("x")
    return [jnp.bitwise_xor(z, RING_BITS[k]) * 2 + jnp.bitwise_xor(x, dx) for dx in range(2) for k in range(RING)]


def width_places_back():
    z, x = lax.axis_index("z"), lax.axis_index("x")
    places = []
    for z_to in range(RING):
        apart = jnp.bitwise_xor(z, z_to)
        k = lax.rem(apart, 2) * 2 + lax.div(apart, 2)
        places += [jnp.bitwise_xor(x, x_to) * RING + k for x_to in range(2)]
    return places


def take_pieces(array, places):
    groups = lax.axis_size("r")
    lead, width = array.shape[:-1], array.shape[-1]
    split = array.reshape(lead + (groups, len(places), width // (groups * len(places))))
    axis = len(lead) + 1
    return [lax.dynamic_index_in_dim(split, place, axis, keepdims=False) for place in places]


def to_local(array):
    pieces = take_pieces(array, width_places())
    lead = array.shape[:-1]
    return jnp.concatenate([p.reshape(lead + (-1,)) for p in pieces], axis=-1)


def from_local(array):
    groups = lax.axis_size("r")
    lead, width = array.shape[:-1], array.shape[-1]
    split = array.reshape(lead + (2 * RING, groups, width // (groups * 2 * RING)))
    axis = len(lead)
    pieces = [lax.dynamic_index_in_dim(split, place, axis, keepdims=False) for place in width_places_back()]
    return jnp.stack(pieces, axis=axis + 1).reshape(array.shape)


def gather_groups(array, axis):
    if lax.axis_size("r") == 1:
        return array
    return lax.all_gather(array, "r", axis=axis, tiled=True)


def scatter_groups(array, axis):
    if lax.axis_size("r") == 1:
        return array
    return lax.psum_scatter(array, "r", scatter_dimension=axis, tiled=True)


class Order:
    def __init__(self):
        self.last = []


ORDER = Order()


def call(kernel, grid, inputs, in_specs, outputs, out_specs, flops=0, exps=0, deps=(), vmem=16, **more):
    block_bytes = sum(a.size * a.dtype.itemsize for a in inputs)
    shapes = [jax.ShapeDtypeStruct(shape, dtype) for shape, dtype in outputs]
    out_bytes = sum(s.size * s.dtype.itemsize for s in shapes)
    given = len(inputs)
    deps = [array for array in list(deps) + ORDER.last if all(array is not other for other in inputs)]

    def run(*refs):
        kernel(*refs[:given], *refs[given + len(deps) :])

    out = pl.pallas_call(
        run,
        grid=grid,
        in_specs=list(in_specs) + [pl.BlockSpec(memory_space=pl.ANY)] * len(deps),
        out_specs=out_specs,
        out_shape=shapes,
        compiler_params=pltpu.CompilerParams(vmem_limit_bytes=vmem * 2**20),
        cost_estimate=pl.CostEstimate(
            flops=int(flops * COST), bytes_accessed=int((block_bytes + out_bytes) * COST), transcendentals=int(exps * COST)
        ),
        **more,
    )(*inputs, *deps)
    ORDER.last = [min(out, key=lambda array: array.size)]
    return out


def whole(array):
    return pl.BlockSpec(array.shape, lambda *_: (0,) * array.ndim)


def whole_out(shape):
    return pl.BlockSpec(shape, lambda *_: (0,) * len(shape))


def stack_rows(first, second, deps=()):
    rows, width = first.shape

    def kernel(first_ref, second_ref, out_ref):
        out_ref[:rows] = first_ref[...]
        out_ref[rows:] = second_ref[...]

    return call(
        kernel,
        (1,),
        [first, second],
        [whole(first)] * 2,
        [((2 * rows, width), BF)],
        [whole_out((2 * rows, width))],
        deps=deps,
    )[0]


def join_columns(arrays, deps):
    rows = arrays[0].shape[0]
    width = sum(array.shape[1] for array in arrays)

    def kernel(*refs):
        place = 0
        for ref in refs[:-1]:
            refs[-1][:, place : place + ref.shape[1]] = ref[...]
            place += ref.shape[1]

    return call(
        kernel,
        (1,),
        arrays,
        [whole(array) for array in arrays],
        [((rows, width), BF)],
        [whole_out((rows, width))],
        deps=deps,
    )[0]


class Gather:
    def __init__(self, shard):
        self.shard = gather_groups(shard, 0)
        self.got = swap_z(self.shard, 2)

    def spread(self, deps=(), by_x=False):
        low = stack_rows(self.shard, self.got, deps)
        low_x, low_y = swap(low, "x"), swap(low, "y")
        high = swap_z(low, 1)
        high_y, high_x = swap(high, "y"), swap(high, "x")
        low_xy = swap(low_y, "x") if by_x else swap(low_x, "y")
        high_xy = swap(high_y, "x")
        self.pieces = [[[low, high], [low_x, high_x]], [[low_y, high_y], [low_xy, high_xy]]]
        self.ring, self.low, self.high, self.far = [high], [low_x, low_y], [high_x, high_y], [low_xy, high_xy]
        return self.pieces


def flat_pieces(pieces):
    return [pieces[y][x][half] for y in range(2) for x in range(2) for half in range(2)]


def spread_rows(info, near, far):
    size = near.shape[1]
    rows = near.shape[0] // RING

    def kernel(near_ref, far_ref, out_ref):
        for k in range(RING):
            out_ref[:, k * size : (k + 1) * size] = near_ref[k * rows : (k + 1) * rows]
            out_ref[:, (RING + k) * size : (RING + k + 1) * size] = far_ref[k * rows : (k + 1) * rows]

    return call(
        kernel,
        (1,),
        [near, far],
        [whole(near), whole(far)],
        [((rows, 2 * RING * size), near.dtype)],
        [whole_out((rows, 2 * RING * size))],
    )[0]


def row_order(own, other, blocks):
    per = own.shape[0] // blocks
    parts = []
    for b in range(blocks):
        parts += [own[b * per : (b + 1) * per], other[b * per : (b + 1) * per]]
    return jnp.concatenate(parts, axis=0)


def project(own, other, pieces, column, width, block, blocks=1, gate=None, activate=False, deps=()):
    rows = own.shape[0] * 2
    refs = flat_pieces(pieces)
    first = column // block

    def kernel(*args):
        own_ref, other_ref, weights = args[0], args[1], args[2:10]
        left = row_order(own_ref[...], other_ref[...], blocks)
        for y in range(2):
            weight = jnp.concatenate([ref[...] for ref in weights[4 * y : 4 * y + 4]], axis=0)
            total = mm(left, weight)
            if gate is not None:
                gate_ref, out_ref = args[10], args[11]
                low = total.astype(BF).astype(F32)
                out_ref[y] = (low * gate_ref[y].astype(F32)).astype(BF)
            elif activate:
                act_ref, slope_ref = args[10], args[11]
                square = total * total
                curve = jnp.tanh(total * (GELU * 0.044715 * square + GELU))
                share = 0.5 * curve + 0.5
                act = total * share
                act_ref[y] = act.astype(BF)
                slope = share + act * (1.0 - curve) * (GELU * 0.134145 * square + GELU)
                slope_ref[y] = slope.astype(BF)
            else:
                args[10][y] = total.astype(BF)

    spec = pl.BlockSpec((2, rows, block), lambda j: (0, 0, j))
    weight_spec = [pl.BlockSpec((ref.shape[0], block), lambda j: (0, first + j)) for ref in refs]
    extra = [] if gate is None else [gate]
    count = 2 if activate else 1
    out = call(
        kernel,
        (width // block,),
        [own, other] + refs + extra,
        [whole(own), whole(other)] + weight_spec + [spec] * len(extra),
        [((2, rows, width), BF)] * count,
        [spec] * count,
        flops=4 * rows * own.shape[1] * width,
        deps=deps,
    )
    return out if activate else out[0]


def merge(lefts, pieces, column, blocks=1, deps=()):
    refs = flat_pieces(pieces)
    columns = sum(part.shape[2] for part in lefts[0])
    per = lefts[0][0].shape[1] // 2
    rows = per * len(lefts)
    width = 8 * refs[0].shape[0] // 2
    first = column // columns
    parts_count = len(lefts[0])
    flat = [part for left in lefts for part in left]

    def kernel(*args):
        left_refs, weights = args[: len(flat)], args[len(flat) : len(flat) + 8]
        own_ref, other_ref = args[len(flat) + 8 :]
        sides = [
            jnp.concatenate([ref[...] for ref in weights[4 * y : 4 * y + 4]], axis=0) for y in range(2)
        ]
        for core, out_ref in ((1, other_ref), (0, own_ref)):
            total = None
            for y in range(2):
                left = []
                for b in range(len(lefts)):
                    here = left_refs[b * parts_count : (b + 1) * parts_count]
                    left.append(jnp.concatenate([ref[y, core * per : (core + 1) * per] for ref in here], axis=1))
                piece = mm_nt(jnp.concatenate(left, axis=0), sides[y])
                total = piece if total is None else total + piece
            out_ref[...] = total.astype(out_ref.dtype)

    weight_spec = [pl.BlockSpec((ref.shape[0], columns), lambda i: (0, first)) for ref in refs]
    return call(
        kernel,
        (1,),
        flat + refs,
        [whole(left) for left in flat] + weight_spec,
        [((rows, width), F32), ((rows, width), BF)],
        [whole_out((rows, width))] * 2,
        flops=8 * rows * width * columns,
        deps=deps,
    )


def outer(segments, block=None, vmem=16, deps=(), into=None, share=1):
    width = segments[0][0][0][0].shape[1]
    sizes = [rights[0].shape[2] for lefts, rights, blocks in segments]
    columns = sum(sizes)
    block = columns if block is None else block
    half = width // 2
    inputs, in_specs, flops = [], [], 0
    for lefts, rights, blocks in segments:
        flat = [array for pair_ in lefts for array in pair_]
        inputs += flat + list(rights)
        in_specs += [whole(array) for array in flat]
        wide = min(block, rights[0].shape[2])
        in_specs += [pl.BlockSpec((2, right.shape[1], wide), lambda j: (0, 0, j)) for right in rights]
        flops += 4 * width * rights[0].shape[2] * sum(right.shape[1] for right in rights)

    def kernel(*args):
        low11, high11, out10, out01, out00 = args[-5:]
        place, column = 0, 0
        for lefts, rights, blocks in segments:
            left_refs = args[place : place + 2 * len(lefts)]
            right_refs = args[place + 2 * len(lefts) : place + 2 * len(lefts) + len(rights)]
            place += 2 * len(lefts) + len(rights)
            left = jnp.concatenate(
                [row_order(left_refs[2 * i][...], left_refs[2 * i + 1][...], blocks) for i in range(len(lefts))], axis=0
            )
            here = slice(column, column + right_refs[0].shape[2])
            column += right_refs[0].shape[2]
            for y in (1, 0):
                right = jnp.concatenate([ref[y] for ref in right_refs], axis=0)
                for x in (1, 0):
                    total = mm_tn(left[:, x * half : (x + 1) * half], right).astype(BF)
                    if x and y:
                        low11[:, here] = total[: half // 2]
                        high11[:, here] = total[half // 2 :]
                    else:
                        {(1, 0): out10, (0, 1): out01, (0, 0): out00}[(x, y)][:, here] = total

    first = 0 if into is None else columns // block
    aliases = {}
    if into is not None:
        aliases = {len(inputs) + i: i for i in range(5)}
        inputs += list(into)
        in_specs += [pl.BlockSpec(memory_space=pl.ANY)] * 5
    return call(
        kernel,
        (columns // block,),
        inputs,
        in_specs,
        [((half // 2, share * columns), BF)] * 2 + [((half, share * columns), BF)] * 3,
        [pl.BlockSpec((half // 2, block), lambda j: (0, first + j))] * 2
        + [pl.BlockSpec((half, block), lambda j: (0, first + j))] * 3,
        flops=flops,
        vmem=vmem,
        deps=deps,
        input_output_aliases=aliases,
    )


def add_into(array, piece, half, deps=()):
    rows, columns = piece.shape

    def kernel(array_ref, piece_ref, out_ref):
        out_ref[...] = (array_ref[...].astype(F32) + piece_ref[...].astype(F32)).astype(BF)

    return call(
        kernel,
        (1,),
        [array, piece],
        [pl.BlockSpec((rows, columns), lambda i: (half, 0)), pl.BlockSpec((rows, columns), lambda i: (0, 0))],
        [(array.shape, BF)],
        [pl.BlockSpec((rows, columns), lambda i: (half, 0))],
        input_output_aliases={0: 0},
        deps=deps,
        vmem=28,
    )[0]


def add_split(arrays, deps=()):
    rows, columns = arrays[0].shape
    part = rows // 2

    def kernel(*refs):
        for half, out_ref in enumerate(refs[len(arrays) :]):
            piece = slice(half * part, (half + 1) * part)
            total = refs[0][piece].astype(F32)
            for ref in refs[1 : len(arrays)]:
                total = total + ref[piece].astype(F32)
            out_ref[...] = total.astype(out_ref.dtype)

    return call(
        kernel,
        (1,),
        arrays,
        [whole(array) for array in arrays],
        [((part, columns), F32), ((part, columns), BF)],
        [whole_out((part, columns))] * 2,
        deps=deps,
        vmem=28,
    )


class Reduce:
    def __init__(self, quarters, by_x=False):
        low11, high11, self.out10, self.out01, self.out00 = quarters
        self.by_x = by_x
        self.low_got, self.high_got = swap(low11, "x" if by_x else "y"), swap(high11, "x")
        self.first = [self.low_got, self.high_got]

    def second(self, deps=()):
        if self.by_x:
            self.out01 = add_into(self.out01, self.low_got, 0, deps)
        else:
            self.out10 = add_into(self.out10, self.low_got, 0, deps)
        self.x_got = swap(self.out10, "x")
        self.y_got = swap(add_into(self.out01, self.high_got, 1, deps), "y")
        self.next = [self.x_got, self.y_got]

    def third(self, deps=()):
        self.near, far = add_split([self.out00, self.x_got, self.y_got], deps)
        self.got = swap_z(far, 1)

    def fourth(self, deps=()):
        self.near, far = add_split([self.near, self.got], deps)
        self.got = swap_z(far, 2)

    def total(self):
        return scatter_groups(self.near + self.got.astype(F32), 0)


def pair(own):
    return own, swap(own, "c")


INFO = 3
PIECES = 2 * RING
SMALL = 16


def smem():
    return pl.BlockSpec(memory_space=pltpu.SMEM)


def lanes_at(info_ref, index, width):
    size = width // PIECES
    return pl.ds(pl.multiple_of(info_ref[index] * size, size), size)


def reorder_in(info_ref, source, target, rows=slice(None)):
    width = source.shape[-1]
    size = width // PIECES
    for k in range(PIECES):
        target[rows, k * size : (k + 1) * size] = source[:, lanes_at(info_ref, INFO + k, width)].astype(target.dtype)


def reorder_out(info_ref, source, target, rows=slice(None)):
    width = source.shape[-1]
    size = width // PIECES
    for k in range(PIECES):
        part = source[rows, lanes_at(info_ref, INFO + PIECES + k, width)]
        target[:, k * size : (k + 1) * size] = part.astype(target.dtype)


def inverse_rms(values):
    return lax.rsqrt(jnp.mean(values * values, axis=-1, keepdims=True) + EPSILON)


def rms_back(values, gain, grad):
    inverse = inverse_rms(values)
    scaled = values * inverse
    weighted = grad * gain
    back = inverse * (weighted - scaled * jnp.mean(scaled * weighted, axis=-1, keepdims=True))
    return back, jnp.sum(grad * scaled, axis=0, keepdims=True)


def rowwise(kernel, inputs, outputs, scratch=(), deps=()):
    return call(
        kernel,
        (1,),
        inputs,
        [smem()] + [whole(array) for array in inputs[1:]],
        outputs,
        [whole_out(shape) for shape, _ in outputs],
        scratch_shapes=[pltpu.VMEM(shape, dtype) for shape, dtype in scratch],
        deps=deps,
    )


def own_rows(info, keep, got):
    rows, width = keep.shape

    def kernel(info_ref, keep_ref, got_ref, out_ref):
        y = info_ref[2]
        reorder_in(info_ref, keep_ref, out_ref, pl.ds(pl.multiple_of(y * rows, rows), rows))
        reorder_in(info_ref, got_ref, out_ref, pl.ds(pl.multiple_of((1 - y) * rows, rows), rows))

    return rowwise(kernel, [info, keep, got], [((2 * rows, width), BF)])[0]


def local_rows(info, array):
    def kernel(info_ref, in_ref, out_ref):
        reorder_in(info_ref, in_ref, out_ref)

    return rowwise(kernel, [info, array], [(array.shape, array.dtype)])[0]


def norm_rows(info, values, gain, deps=()):
    def kernel(info_ref, in_ref, gain_ref, out_ref):
        rows = in_ref[...].astype(F32)
        out_ref[...] = (rows * inverse_rms(rows) * gain_ref[...]).astype(BF)

    return rowwise(kernel, [info, values, gain], [(values.shape, BF)], deps=deps)[0]


def add_norm(info, rows, both, gain):
    own, other = both

    def kernel(info_ref, row_ref, own_ref, got_ref, gain_ref, hidden_ref, norm_ref):
        hidden = row_ref[...].astype(F32) + (own_ref[...] + got_ref[...].astype(F32))
        hidden_ref[...] = hidden
        norm_ref[...] = (hidden * inverse_rms(hidden) * gain_ref[...]).astype(BF)

    return rowwise(kernel, [info, rows, own, swap(other, "c"), gain], [(rows.shape, F32), (rows.shape, BF)])


def add_out(info, hidden, both):
    own, other = both
    rows, width = hidden.shape
    half = rows // 2

    def kernel(info_ref, hidden_ref, own_ref, got_ref, keep_ref, send_ref, scratch):
        y = info_ref[2]
        scratch[...] = hidden_ref[...] + (own_ref[...] + got_ref[...].astype(F32))
        reorder_out(info_ref, scratch, keep_ref, pl.ds(pl.multiple_of(y * half, half), half))
        reorder_out(info_ref, scratch, send_ref, pl.ds(pl.multiple_of((1 - y) * half, half), half))

    return rowwise(
        kernel,
        [info, hidden, own, swap(other, "c")],
        [((half, width), BF)] * 2,
        [((rows, width), F32)],
    )


def step_state(info, state, both, gate, gain):
    own, other = both

    def kernel(info_ref, state_ref, own_ref, got_ref, gate_ref, gain_ref, next_ref, norm_ref, update_ref):
        update = own_ref[...] + got_ref[...].astype(F32)
        update_ref[...] = update
        after = gate_ref[...] * state_ref[...] + (1.0 - gate_ref[...]) * update
        next_ref[...] = after
        norm_ref[...] = (after * inverse_rms(after) * gain_ref[...]).astype(BF)

    return rowwise(
        kernel,
        [info, state, own, swap(other, "c"), gate, gain],
        [(state.shape, F32), (state.shape, BF), (state.shape, F32)],
    )


def last_state(info, state, both, gate):
    own, other = both

    def kernel(info_ref, state_ref, own_ref, got_ref, gate_ref, final_ref, update_ref, scratch):
        update = own_ref[...] + got_ref[...].astype(F32)
        update_ref[...] = update
        scratch[...] = gate_ref[...] * state_ref[...] + (1.0 - gate_ref[...]) * update
        reorder_out(info_ref, scratch, final_ref)

    return rowwise(
        kernel,
        [info, state, own, swap(other, "c"), gate],
        [(state.shape, BF), (state.shape, F32)],
        [(state.shape, F32)],
    )


def back_hidden(info, hidden, both, gain, dy):
    own, other = both

    def kernel(info_ref, hidden_ref, own_ref, got_ref, gain_ref, dy_ref, grad_ref, branch_ref, gain_grad_ref):
        grad = own_ref[...] + got_ref[...].astype(F32)
        back, gain_grad_ref[...] = rms_back(hidden_ref[...], gain_ref[...], grad)
        total = dy_ref[...].astype(F32) + back
        grad_ref[...] = total
        branch_ref[...] = total.astype(BF)

    return rowwise(
        kernel,
        [info, hidden, own, swap(other, "c"), gain, dy],
        [(hidden.shape, F32), (hidden.shape, BF), ((1, hidden.shape[1]), F32)],
    )


def back_update(info, grad, gate):
    def kernel(info_ref, grad_ref, gate_ref, out_ref):
        out_ref[...] = ((1.0 - gate_ref[...]) * grad_ref[...].astype(F32)).astype(BF)

    return rowwise(kernel, [info, grad, gate], [(grad.shape, BF)])[0]


def back_state(info, grad, state, update, both, gate, gain):
    own, other = both
    width = state.shape[1]

    def kernel(
        info_ref, grad_ref, state_ref, update_ref, own_ref, got_ref, gate_ref, gain_ref, out_ref, low_ref, gain_grad_ref, gate_grad_ref
    ):
        gate_open = gate_ref[...]
        grad_now = grad_ref[...].astype(F32)
        values = state_ref[...]
        gate_grad_ref[...] = jnp.sum(grad_now * (values - update_ref[...]), axis=0, keepdims=True) * (
            gate_open * (1.0 - gate_open)
        )
        back, gain_grad_ref[...] = rms_back(values, gain_ref[...], own_ref[...] + got_ref[...].astype(F32))
        total = gate_open * grad_now + back
        out_ref[...] = total
        low_ref[...] = ((1.0 - gate_open) * total).astype(BF)

    return rowwise(
        kernel,
        [info, grad, state, update, own, swap(other, "c"), gate, gain],
        [(state.shape, F32), (state.shape, BF), ((1, width), F32), ((1, width), F32)],
    )


def back_input(info, values, both, gain, grad_hidden):
    own, other = both
    rows, width = values.shape
    half = rows // 2

    def kernel(info_ref, value_ref, own_ref, got_ref, gain_ref, grad_ref, keep_ref, send_ref, gain_grad_ref, scratch):
        y = info_ref[2]
        grad = own_ref[...] + got_ref[...].astype(F32)
        back, gain_grad_ref[...] = rms_back(value_ref[...].astype(F32), gain_ref[...], grad)
        scratch[...] = grad_ref[...] + back
        reorder_out(info_ref, scratch, keep_ref, pl.ds(pl.multiple_of(y * half, half), half))
        reorder_out(info_ref, scratch, send_ref, pl.ds(pl.multiple_of((1 - y) * half, half), half))

    return rowwise(
        kernel,
        [info, values, own, swap(other, "c"), gain, grad_hidden],
        [((half, width), F32), ((half, width), BF), ((1, width), F32)],
        [((rows, width), F32)],
    )


def pack_small(info, states, vectors):
    rows, width = states.shape
    half = width // 2
    counts = [len(group) for group in vectors]
    flat = [vector for group in vectors for vector in group]
    pad = SMALL - len(vectors)

    def kernel(info_ref, state_ref, *refs):
        near_ref, far_ref = refs[len(flat) :]
        parts, place = [], 0
        for count in counts:
            parts.append(sum(ref[...] for ref in refs[place : place + count]))
            place += count
        tail = jnp.concatenate(parts + [jnp.zeros((pad, width), F32)], axis=0)
        near_ref[:rows] = state_ref[:, :half]
        near_ref[rows:] = tail[:, :half]
        far_ref[:rows] = state_ref[:, half:].astype(BF)
        far_ref[rows:] = tail[:, half:].astype(BF)

    shape = (rows + SMALL, half)
    return rowwise(kernel, [info, states] + flat, [(shape, F32), (shape, BF)])


def add_small(info, near, got):
    rows, width = near.shape
    half = width // 2

    def kernel(info_ref, near_ref, got_ref, near_out, far_out):
        total = near_ref[...] + got_ref[...].astype(F32)
        near_out[...] = total[:, :half]
        far_out[...] = total[:, half:].astype(BF)

    return rowwise(kernel, [info, near, got], [((rows, half), F32), ((rows, half), BF)])


def add_pair(info, near, got):
    def kernel(info_ref, near_ref, got_ref, out_ref):
        out_ref[...] = near_ref[...] + got_ref[...].astype(F32)

    return rowwise(kernel, [info, near, got], [(near.shape, F32)])[0]


def place_small(info, near, far, states):
    size = near.shape[1]

    def kernel(info_ref, near_ref, far_ref, state_ref, gain_ref, gate_ref):
        c = info_ref[0]
        state_ref[pl.ds(pl.multiple_of(c * states, states), states)] = near_ref[:states]
        state_ref[pl.ds(pl.multiple_of((1 - c) * states, states), states)] = far_ref[:states]
        total = near_ref[states:] + far_ref[states:]
        gain_ref[...] = total[:3]
        gate_ref[...] = total[3:4]

    return rowwise(kernel, [info, near, far], [((2 * states, size), F32), ((3, size), F32), ((1, size), F32)])


def place_rows(info, keep, got):
    shape = (2,) + keep.shape

    def kernel(info_ref, keep_ref, got_ref, out_ref):
        y = info_ref[2]
        out_ref[y] = keep_ref[...]
        out_ref[1 - y] = got_ref[...].astype(keep.dtype)

    return rowwise(kernel, [info, keep, got], [(shape, keep.dtype)])[0]


def place_state(info, near, near_c, far, far_c):
    rows, width = near.shape

    def kernel(info_ref, near_ref, near_c_ref, far_ref, far_c_ref, out_ref):
        c, y = info_ref[0], info_ref[2]
        here = pl.ds(pl.multiple_of(c * rows, rows), rows)
        there = pl.ds(pl.multiple_of((1 - c) * rows, rows), rows)
        out_ref[y, here] = near_ref[...]
        out_ref[y, there] = near_c_ref[...]
        out_ref[1 - y, here] = far_ref[...]
        out_ref[1 - y, there] = far_c_ref[...]

    return rowwise(kernel, [info, near, near_c, far, far_c], [((2, 2 * rows, width), near.dtype)])[0]


SCALE = HEAD_DIM ** (-0.5)


def key_tiles(b, j):
    tiles = []
    if b > 0:
        tiles += [(b - 1, jj, "after" if jj == j else "all") for jj in range(j, 2)]
    tiles += [(b, jj, "until" if jj == j else "all") for jj in range(j + 1)]
    return tiles


def tile_mask(kind, size, limit):
    rows = lax.broadcasted_iota(jnp.int32, (size, size), 0)
    columns = lax.broadcasted_iota(jnp.int32, (size, size), 1)
    mask = None
    if kind == "after":
        mask = columns > rows
    if kind == "until":
        mask = columns <= rows
    if limit is not None:
        inside = columns < limit
        mask = inside if mask is None else mask & inside
    return mask


def masked_scores(queries, keys, masks):
    scores = mm_nt(queries, keys) * SCALE
    parts, place = [], 0
    for size, mask in masks:
        part = scores[:, place : place + size]
        parts.append(part if mask is None else jnp.where(mask, part, MASKED))
        place += size
    return jnp.concatenate(parts, axis=1)


def attention_plan(b, last, size, core, count, states):
    def start(block, j):
        return pl.multiple_of(block * 2 * size + jnp.bitwise_xor(core, j) * size, size)

    plan = []
    for j in range(2):
        tiles, masks = [], []
        for block, jj, kind in key_tiles(b, j):
            limit = count - jj * size if block == b and last else None
            tiles.append((block, jj))
            masks.append((size, tile_mask(kind, size, limit)))
        plan.append((tiles, masks + [(states, None)]))
    state_masks = [(states, None)]
    for jj in range(2):
        state_masks.append((size, tile_mask("all", size, count - jj * size if last else None)))
    return start, plan, state_masks


def block_spec(rows, width):
    return pl.BlockSpec((1, rows, width), lambda y: (y, 0, 0))


def head_slices(lanes, h):
    return [slice(p * lanes + h * HEAD_DIM, p * lanes + (h + 1) * HEAD_DIM) for p in range(3)]


def attend_rows(queries, keys, values, masks):
    scores = masked_scores(queries, keys, masks)
    top = jnp.max(scores, axis=1, keepdims=True)
    weights = jnp.exp(scores - top)
    total = jnp.sum(weights, axis=1, keepdims=True)
    mixed = mm(weights.astype(BF), values) / total
    return mixed.astype(BF), top + jnp.log(total)


def attend_rows_back(queries, keys, values, masks, log_total, grad):
    scores = masked_scores(queries, keys, masks)
    probs = jnp.exp(scores - log_total)
    grad_probs = mm_nt(grad, values)
    row_sum = jnp.sum(grad_probs * probs, axis=1, keepdims=True)
    low = (probs * (grad_probs - row_sum)).astype(BF)
    return mm(low, keys) * SCALE, mm_tn(low, queries) * SCALE, mm_tn(probs.astype(BF), grad)


def token_pairs(b, heads, states):
    return 2 * heads * BLOCK * (BLOCK * (1.25 if b else 0.75) + states)


def forward_tokens(b, blocks, info, tokens, states, deps=()):
    lanes = tokens.shape[2] // 3
    heads = lanes // HEAD_DIM
    size = BLOCK // 2
    count_states = states.shape[1]

    def kernel(info_ref, token_ref, state_ref, mixed_ref, log_ref):
        start, plan, state_masks = attention_plan(
            b, b == blocks - 1, size, info_ref[0], info_ref[1], count_states
        )
        for h in range(heads):
            query, key, value = head_slices(lanes, h)
            for j, (tiles, masks) in enumerate(plan):
                rows = [pl.ds(start(*place), size) for place in tiles]
                keys = jnp.concatenate([token_ref[0, at, key] for at in rows] + [state_ref[0, :, key]], axis=0)
                values = jnp.concatenate([token_ref[0, at, value] for at in rows] + [state_ref[0, :, value]], axis=0)
                here = pl.ds(start(0, j), size)
                mixed_ref[0, here, query], log_ref[0, here, h : h + 1] = attend_rows(
                    token_ref[0, pl.ds(start(b, j), size), query], keys, values, masks
                )

    pairs = int(token_pairs(b, heads, count_states))
    return call(
        kernel,
        (2,),
        [info, tokens, states],
        [smem(), block_spec((b + 1) * BLOCK, 3 * lanes), block_spec(count_states, 3 * lanes)],
        [((2, BLOCK, lanes), BF), ((2, BLOCK, 128), F32)],
        [block_spec(BLOCK, lanes), block_spec(BLOCK, 128)],
        flops=4 * pairs * HEAD_DIM,
        exps=pairs,
        deps=deps,
    )


def forward_states(b, blocks, info, tokens, states, deps=()):
    lanes = tokens.shape[2] // 3
    heads = lanes // HEAD_DIM
    size = BLOCK // 2
    count_states = states.shape[1]

    def kernel(info_ref, token_ref, state_ref, mixed_ref, log_ref):
        start, plan, state_masks = attention_plan(
            0, b == blocks - 1, size, info_ref[0], info_ref[1], count_states
        )
        for h in range(heads):
            query, key, value = head_slices(lanes, h)
            rows = [pl.ds(start(0, j), size) for j in range(2)]
            keys = jnp.concatenate([state_ref[0, :, key]] + [token_ref[0, at, key] for at in rows], axis=0)
            values = jnp.concatenate([state_ref[0, :, value]] + [token_ref[0, at, value] for at in rows], axis=0)
            for begin in range(0, count_states, size):
                here = slice(begin, begin + size)
                mixed_ref[0, here, query], log_ref[0, here, h : h + 1] = attend_rows(
                    state_ref[0, here, query], keys, values, state_masks
                )

    pairs = 2 * heads * count_states * (count_states + BLOCK)
    return call(
        kernel,
        (2,),
        [info, tokens, states],
        [smem(), pl.BlockSpec((1, BLOCK, 3 * lanes), lambda y: (y, b, 0)), block_spec(count_states, 3 * lanes)],
        [((2, count_states, lanes), BF), ((2, count_states, 128), F32)],
        [block_spec(count_states, lanes), block_spec(count_states, 128)],
        flops=4 * pairs * HEAD_DIM,
        exps=pairs,
        deps=deps,
    )


def add_part(sums, place, part):
    sums[place] = part if place not in sums else sums[place] + part


def backward_tokens(b, blocks, info, tokens, states, logs, grad_mixed, deps=()):
    lanes = tokens.shape[2] // 3
    heads = lanes // HEAD_DIM
    size = BLOCK // 2
    count_states = states.shape[1]

    def kernel(info_ref, token_ref, state_ref, log_ref, grad_ref, query_ref, own_ref, state_out_ref, *before_ref):
        start, plan, state_masks = attention_plan(
            b, b == blocks - 1, size, info_ref[0], info_ref[1], count_states
        )
        for h in range(heads):
            query, key, value = head_slices(lanes, h)
            sums = ({}, {})
            for j, (tiles, masks) in enumerate(plan):
                rows = [pl.ds(start(*place), size) for place in tiles]
                keys = jnp.concatenate([token_ref[0, at, key] for at in rows] + [state_ref[0, :, key]], axis=0)
                values = jnp.concatenate([token_ref[0, at, value] for at in rows] + [state_ref[0, :, value]], axis=0)
                here = pl.ds(start(0, j), size)
                dq, dk, dv = attend_rows_back(
                    token_ref[0, pl.ds(start(b, j), size), query],
                    keys,
                    values,
                    masks,
                    log_ref[0, here, h : h + 1],
                    grad_ref[0, here, query],
                )
                query_ref[0, here, query] = dq.astype(BF)
                for which, grads in enumerate((dk, dv)):
                    for i, place in enumerate(tiles):
                        add_part(sums[which], place, grads[i * size : (i + 1) * size])
                    add_part(sums[which], "state", grads[len(tiles) * size :])
            for which in range(2):
                columns = slice(which * lanes + h * HEAD_DIM, which * lanes + (h + 1) * HEAD_DIM)
                state_out_ref[0, :, columns] = sums[which]["state"]
                for j in range(2):
                    here = pl.ds(start(0, j), size)
                    own_ref[0, here, columns] = sums[which][(b, j)]
                    if b > 0:
                        before_ref[0][0, here, columns] = sums[which][(b - 1, j)]

    pairs = int(token_pairs(b, heads, count_states))
    outputs = [((2, BLOCK, lanes), BF), ((2, BLOCK, 2 * lanes), F32), ((2, count_states, 2 * lanes), F32)]
    out_specs = [block_spec(BLOCK, lanes), block_spec(BLOCK, 2 * lanes), block_spec(count_states, 2 * lanes)]
    if b > 0:
        outputs.append(((2, BLOCK, 2 * lanes), F32))
        out_specs.append(block_spec(BLOCK, 2 * lanes))
    return call(
        kernel,
        (2,),
        [info, tokens, states, logs, grad_mixed],
        [
            smem(),
            block_spec((b + 1) * BLOCK, 3 * lanes),
            block_spec(count_states, 3 * lanes),
            block_spec(BLOCK, 128),
            pl.BlockSpec((1, BLOCK, lanes), lambda y: (y, b, 0)),
        ],
        outputs,
        out_specs,
        flops=10 * pairs * HEAD_DIM,
        exps=pairs,
        deps=deps,
    )


def backward_states(b, blocks, info, tokens, states, logs, grad_mixed, token_sums, state_sums, deps=()):
    lanes = tokens.shape[2] // 3
    heads = lanes // HEAD_DIM
    size = BLOCK // 2
    count_states = states.shape[1]
    count = len(token_sums)

    def kernel(info_ref, token_ref, state_ref, log_ref, grad_ref, sum_ref, *rest):
        token_sum_refs, (state_out_ref, token_out_ref) = rest[:count], rest[count:]
        start, plan, state_masks = attention_plan(
            0, b == blocks - 1, size, info_ref[0], info_ref[1], count_states
        )
        for h in range(heads):
            query, key, value = head_slices(lanes, h)
            rows = [pl.ds(start(0, j), size) for j in range(2)]
            keys = jnp.concatenate([state_ref[0, :, key]] + [token_ref[0, at, key] for at in rows], axis=0)
            values = jnp.concatenate([state_ref[0, :, value]] + [token_ref[0, at, value] for at in rows], axis=0)
            sums = [None, None]
            for begin in range(0, count_states, size):
                here = slice(begin, begin + size)
                dq, dk, dv = attend_rows_back(
                    state_ref[0, here, query],
                    keys,
                    values,
                    state_masks,
                    log_ref[0, here, h : h + 1],
                    grad_ref[0, here, query],
                )
                state_out_ref[0, here, query] = dq.astype(BF)
                sums = [part if old is None else old + part for old, part in zip(sums, (dk, dv))]
            for which, to in ((0, key), (1, value)):
                columns = slice(which * lanes + h * HEAD_DIM, which * lanes + (h + 1) * HEAD_DIM)
                state_out_ref[0, :, to] = (sums[which][:count_states] + sum_ref[0, :, columns]).astype(BF)
                for j in range(2):
                    total = sums[which][count_states + j * size : count_states + (j + 1) * size]
                    for ref in token_sum_refs:
                        total = total + ref[0, rows[j], columns]
                    token_out_ref[0, rows[j], columns] = total.astype(BF)

    pairs = 2 * heads * count_states * (count_states + BLOCK)
    return call(
        kernel,
        (2,),
        [info, tokens, states, logs, grad_mixed, state_sums] + list(token_sums),
        [
            smem(),
            pl.BlockSpec((1, BLOCK, 3 * lanes), lambda y: (y, b, 0)),
            block_spec(count_states, 3 * lanes),
            block_spec(count_states, 128),
            block_spec(count_states, lanes),
            block_spec(count_states, 2 * lanes),
        ]
        + [block_spec(BLOCK, 2 * lanes)] * count,
        [((2, count_states, 3 * lanes), BF), ((2, BLOCK, 2 * lanes), BF)],
        [block_spec(count_states, 3 * lanes), block_spec(BLOCK, 2 * lanes)],
        flops=10 * pairs * HEAD_DIM,
        exps=pairs,
        deps=deps,
    )


def body(
    tokens,
    counts,
    token_weights,
    token_output,
    state_weights,
    state_output,
    hidden_up,
    hidden_down,
    norm_gains,
    gate_bias,
    init_state,
    cotangent,
    state_cotangent,
):
    y, c = lax.axis_index("y"), lax.axis_index("c")
    width = tokens.shape[3]
    state_half = init_state.shape[0] // 2
    blocks = 4 * tokens.shape[2] // BLOCK
    valid_count = lax.dynamic_index_in_dim(counts[:, 0], y, 0, keepdims=False)
    if lax.axis_size("r") == 1:
        places, back = width_places(), width_places_back()
        before, after = (lambda array: array), (lambda array: array)
    else:
        places = back = list(range(PIECES))
        before, after = to_local, from_local
    info = jnp.stack([jnp.asarray(v, jnp.int32) for v in [c, valid_count, y] + places + back])

    def micro(array, index):
        return lax.dynamic_index_in_dim(array[:, 0], index, 0, keepdims=False)

    ORDER.last = []
    shard_rows = token_output.shape[0]
    head, ff = token_output.shape[1], hidden_up.shape[1]
    at_state, at_state_out, at_token_out = 0, 3 * head, ff
    flat = lambda array: array.reshape(shard_rows, -1)
    token = Gather(flat(token_weights))
    token_got = swap(micro(tokens, 1 - y), "y")
    small = jnp.concatenate(
        [
            lax.dynamic_slice_in_dim(init_state, c * state_half, state_half, 0),
            norm_gains,
            gate_bias[None],
            jnp.zeros((12, init_state.shape[1]), BF),
        ],
        axis=0,
    )
    if lax.axis_size("r") > 1:
        small = lax.all_gather(small, "r", axis=1, tiled=True)
    small_got = swap_z(small, 2)
    w_token = token.spread(by_x=True)
    mid = Gather(join_columns([flat(state_weights), state_output], ()))
    small = stack_rows(small, small_got)
    small = stack_rows(small, swap_z(small, 1))
    small_got = swap(small, "x")
    x_rows = own_rows(info, before(micro(tokens, y)), before(token_got))
    small = spread_rows(info, small, small_got)
    gains = [small[state_half + i : state_half + i + 1].astype(F32) for i in range(3)]
    gate_open = jax.nn.sigmoid(small[state_half + 3 : state_half + 4].astype(F32))
    state_now = small[:state_half].astype(F32)
    normed = pair(norm_rows(info, x_rows, gains[0], token.low))
    state_norm = pair(norm_rows(info, state_now, gains[1]))
    w_mid = mid.spread(token.low)
    up = Gather(join_columns([hidden_up, token_output], ()))

    token_proj = project(*normed, w_token, 0, 3 * head, 3 * head // 2, blocks=blocks)
    w_up = up.spread(mid.low)
    down = Gather(join_columns([hidden_down], ()))
    dy_got = swap(micro(cotangent, 1 - y), "y")
    grad_final = lax.dynamic_slice(
        state_cotangent, (y, 0, c * state_half, 0), (1, 1, state_half, width)
    )[0, 0]
    grad_final = local_rows(info, before(grad_final))
    grad_update = pair(back_update(info, grad_final, gate_open))
    kept = []
    mixed = []
    for b in range(blocks):
        proj_wait, state_wait, merge_wait, token_wait = (
            (up.ring, [], up.low + [down.got], up.high) if b == 0 else (up.far, [], down.ring, down.low)
        )
        state_proj = project(*state_norm, w_mid, at_state, 3 * head, 3 * head, deps=proj_wait)
        state_flat, state_logs = forward_states(b, blocks, info, token_proj, state_proj, deps=state_wait)
        both = merge([[state_flat]], w_mid, at_state_out, deps=merge_wait)
        mixed_b, logs = forward_tokens(b, blocks, info, token_proj, state_proj, deps=token_wait)
        mixed.append(mixed_b)
        if b < blocks - 1:
            state_next, next_norm, update = step_state(info, state_now, both, gate_open, gains[1])
        else:
            final_rows, update = last_state(info, state_now, both, gate_open)
            state_next, next_norm = None, None
        kept.append((state_now, state_norm, state_proj, logs, state_logs, state_flat, update))
        state_now = state_next
        state_norm = None if next_norm is None else pair(next_norm)
        if b == 0:
            dy_rows = own_rows(info, before(micro(cotangent, y)), before(dy_got))
            dy_pair = pair(dy_rows)
            grad_state_mixed = project(*grad_update, w_mid, at_state_out, head, head)
            w_down = down.spread()
    hidden, hidden_own = add_norm(
        info, x_rows, merge([[part] for part in mixed], w_up, at_token_out, blocks=blocks, deps=down.high), gains[2]
    )
    hidden_norm = pair(hidden_own)
    activated, slope = project(*hidden_norm, w_up, 0, ff, ff // 2, activate=True)

    quarters = outer([([dy_pair], [activated], 1)], ff // 2, share=2)
    grad_up = project(*dy_pair, w_down, 0, ff, ff // 2, gate=slope)
    both = merge([[grad_up]], w_up, 0)
    ff_grad = Reduce(outer([([hidden_norm], [grad_up], 1)], ff // 2, share=2, into=quarters))
    grad_hidden, branch, gain_hidden = back_hidden(info, hidden, both, gains[2], dy_rows)
    branch = pair(branch)

    grad_mixed = project(*branch, w_up, at_token_out, head, head, blocks=blocks)
    grad_state = grad_final
    gate_sums, gain_sums = [], []
    query_grads, pair_grads = [None] * blocks, [None] * blocks
    update_all, flat_all, norm_all, state_grads = [], [], [], []
    sums = [None] * blocks

    def tokens_back(b, deps=()):
        state_proj, logs = kept[b][2], kept[b][3]
        query_grads[b], *sums[b] = backward_tokens(b, blocks, info, token_proj, state_proj, logs, grad_mixed, deps)

    def states_back(b, later, deps=()):
        state_before, state_norm, state_proj, logs, state_logs, state_flat, update = kept[b]
        own_sums, state_sums, *before_sums = sums[b]
        state_grad, pair_grads[b] = backward_states(
            b, blocks, info, token_proj, state_proj, state_logs, grad_state_mixed, [own_sums] + later, state_sums, deps
        )
        update_all.append(grad_update)
        flat_all.append(state_flat)
        norm_all.append(state_norm)
        state_grads.append(state_grad)
        return merge([[state_grad]], w_mid, at_state), before_sums

    def state_step(b, both, grad_state):
        state_before, update = kept[b][0], kept[b][-1]
        grad_state, low, gain_sum, gate_sum = back_state(
            info, grad_state, state_before, update, both, gate_open, gains[1]
        )
        gain_sums.append(gain_sum)
        gate_sums.append(gate_sum)
        return grad_state, low

    last = blocks - 1
    tokens_back(last)
    both, later = states_back(last, [])
    ff_grad.second()
    for b in range(last - 1, -1, -1):
        tokens_back(b)
        grad_state, low = state_step(b + 1, both, grad_state)
        grad_update = pair(low)
        if b == 0:
            final_rows = after(final_rows)
            final_far = swap(final_rows, "y")
        grad_state_mixed = project(*grad_update, w_mid, at_state_out, head, head)
        if b == 0:
            early_grad = Reduce(
                outer(
                    [
                        ([branch], mixed, blocks),
                        ([normed], query_grads, blocks),
                        ([grad_update] + update_all, [kept[0][5]] + flat_all, 1),
                    ],
                    vmem=28,
                ),
                by_x=True,
            )
        both, later = states_back(b, later)

    late_grad = Reduce(outer([([normed], pair_grads, blocks), (norm_all, state_grads, 1)], vmem=28), by_x=True)
    token_both = merge([[query_grads[i], pair_grads[i]] for i in range(blocks)], w_token, 0, blocks=blocks)
    grad_state, low = state_step(0, both, grad_state)
    out_both = merge([[activated]], w_down, 0)
    early_grad.second()
    keep, send, gain_token = back_input(info, x_rows, token_both, gains[0], grad_hidden)
    input_keep, input_got = after(keep), swap(after(send), "y")
    near, far = pack_small(info, grad_state, [[gain_token], gain_sums, [gain_hidden], gate_sums])
    far = swap(far, "x")
    ff_grad.third()
    keep, send = add_out(info, hidden, out_both)
    output_got = swap(after(send), "y")
    output_keep = after(keep)
    late_grad.second()
    near, far = add_small(info, near, far)
    far = swap_z(far, 1)
    early_grad.third()
    ff_grad.fourth()
    near, far = add_small(info, near, far)
    far = swap_z(far, 2)
    final_state = place_state(info, final_rows, swap(final_rows, "c"), final_far, swap(final_far, "c"))[:, None]
    early_grad.fourth()
    near = add_pair(info, near, far)
    if lax.axis_size("r") > 1:
        near = lax.psum_scatter(near, "r", scatter_dimension=1, tiled=True)
    far = swap(near, "y")
    late_grad.third()
    near = add_pair(info, near, far)
    far = swap(near, "c")
    output = place_rows(info, output_keep, output_got)[:, None]
    init_grad, grad_gains, grad_gate = place_small(info, near, far, state_half)
    late_grad.fourth()
    input_grad = place_rows(info, input_keep, input_got)[:, None]
    both = ff_grad.total()
    grad_hidden_down, grad_hidden_up = both[:, :ff], both[:, ff:]
    early = early_grad.total()
    grad_token_output, grad_query, grad_state_output = [early[:, i * head : (i + 1) * head] for i in range(3)]
    late = late_grad.total()
    grad_token_weights = jnp.stack([grad_query, late[:, :head], late[:, head : 2 * head]], axis=1)
    grad_state_weights = late[:, 2 * head :].reshape(-1, 3, head)
    return (
        output,
        final_state,
        input_grad,
        grad_token_weights,
        grad_token_output,
        grad_state_weights,
        grad_state_output,
        grad_hidden_up,
        grad_hidden_down,
        grad_gains,
        grad_gate[0],
        init_grad,
    )


def solution(mesh):
    dp, heads = mesh.devices.shape
    fine = Mesh(mesh.devices.reshape(dp // (2 * RING), RING, 2, heads // 2, 2), ("r", "z", "x", "y", "c"))
    d, h = ("r", "z", "x"), ("y", "c")
    return jax.shard_map(
        body,
        mesh=fine,
        in_specs=(
            P(None, d, h, None),
            P(None, d),
            P(d, None, h),
            P(d, h),
            P(d, None, h),
            P(d, h),
            P(d, h),
            P(d, h),
            P(None, d),
            P(d),
            P(None, d),
            P(None, d, h, None),
            P(None, d, None, None),
        ),
        out_specs=(
            P(None, d, h, None),
            P(None, d, None, None),
            P(None, d, h, None),
            P(d, None, h),
            P(d, h),
            P(d, None, h),
            P(d, h),
            P(d, h),
            P(d, h),
            P(None, d),
            P(d),
            P(None, d),
        ),
        check_vma=False,
    )
```

time: 672 us -> 489 us (0.73)
  starting transfers between devices: 157 us -> 71.2 us
  Pallas kernels: 234 us -> 170 us
  local copies, waits for them, and re-layouts: 71.3 us -> 42.8 us
  other arithmetic: 18.2 us -> 1.25 us
  waiting for transfers between devices: 184 us -> 198 us
    pallas_call x65 -> x73, Pallas kernels: 234 us -> 170 us  [call(): pl.pallas_call(run, grid=grid, in_specs=list(in_specs) + [pl.BlockSpec(me...]
    ppermute x36 -> x18, starting transfers between devices: 88.4 us -> 25.4 us  [swap_z(): return lax.ppermute(array, 'z', [(i, i ^ bit) for i in range(RING)])]
    unnamed x363 -> x245, local copies, waits for them, and re-layouts: 60.3 us -> 35.9 us
    ppermute x75 -> x63, starting transfers between devices: 68.1 us -> 45.8 us  [swap(): return lax.ppermute(array, axis, [(0, 1), (1, 0)])]
    add x9 -> x3, other arithmetic: 9.8 us -> 0.24 us  [total(): return scatter_groups(self.near + self.got.astype(F32), 0)]
    ppermute x36 -> x18, waiting for transfers between devices: 60.5 us -> 68.3 us  [swap_z(): return lax.ppermute(array, 'z', [(i, i ^ bit) for i in range(RING)])]
    ppermute x75 -> x63, waiting for transfers between devices: 123 us -> 129 us  [swap(): return lax.ppermute(array, axis, [(0, 1), (1, 0)])]
  transfers between devices with their start and end apart: 111 -> 81, of which waited for: 31 -> 30; matrix products, arithmetic and copies ran while one was open for 5% -> 1% of each run, Pallas kernels for 27% -> 32%
where the time goes in v4:
time: 489 us; the launch traced here: 485 us
  waiting for transfers between devices  198 us (40%)
  Pallas kernels  170 us (35%)
  starting transfers between devices  71.2 us (15%)
  local copies, waits for them, and re-layouts  42.8 us (9%)
    pallas_call x73, Pallas kernels, call(): pl.pallas_call(run, grid=grid, in_specs=list(in_specs) + [pl.BlockSpec(me...  170 us
    ppermute x63, waiting for transfers between devices, swap(): return lax.ppermute(array, axis, [(0, 1), (1, 0)])  129 us
    ppermute x18, waiting for transfers between devices, swap_z(): return lax.ppermute(array, 'z', [(i, i ^ bit) for i in range(RING)])  68.3 us
    ppermute x63, starting transfers between devices, swap(): return lax.ppermute(array, axis, [(0, 1), (1, 0)])  45.8 us
    unnamed x245, local copies, waits for them, and re-layouts  35.9 us
    ppermute x18, starting transfers between devices, swap_z(): return lax.ppermute(array, 'z', [(i, i ^ bit) for i in range(RING)])  25.4 us
  transfers between devices with their start and end apart: 81, of which 30 were waited for; matrix products, arithmetic and copies ran while one was open for 1% of the time, Pallas kernels for 32%

profile of v4, /device:TPU:0, one launch (start us, length us, event | category | flops | bytes accessed | tf_op | source)
XLA Modules:
  0.0 485.1 jit_solution(14684873043653442791)
XLA Ops:
  11.4 8.6 %collective-permute-done.2.refs_1_ = bf16[128,768]{1,0:T(8,128)(2,1)S(1)} collective-permute-done((bf16[128,768]{1,0:T(8,128)(2,1)S(1)}, bf16[128,768]{1,0:T(8,128)(2,1)S(1)}, u32[]{:S(2)}, u32[]{:S(2)}) %collective-permute-start.2) | collective-permute-done | bytes 196640 | tf_op jit(solution)/shard_map/ppermute | solution.py:27
  50.9 12.1 %collective-permute-done.22.refs_1_ = bf16[128,1280]{1,0:T(8,128)(2,1)S(1)} collective-permute-done((bf16[128,1280]{1,0:T(8,128)(2,1)S(1)}, bf16[128,1280]{1,0:T(8,128)(2,1)S(1)}, u32[]{:S(2)}, u32[]{:S(2)}) %collective-permute-start.22) | collective-permute-done | bytes 327712 | tf_op jit(solution)/shard_map/ppermute | solution.py:27
  69.0 7.6 %collective-permute-done.15.refs_3_.refs_2_ = bf16[256,1024]{1,0:T(8,128)(2,1)S(1)} collective-permute-done((bf16[256,1024]{1,0:T(8,128)(2,1)S(1)}, bf16[256,1024]{1,0:T(8,128)(2,1)S(1)}, u32[]{:S(2)}, u32[]{:S(2)}) %collective-permute-start.15) | collective-permute-done | bytes 524320 | tf_op jit(solution)/shard_map/ppermute | solution.py:27
  79.5 7.5 %collective-permute-done.12.refs_9_.refs_11_ = bf16[256,768]{1,0:T(8,128)(2,1)S(1)} collective-permute-done((bf16[256,768]{1,0:T(8,128)(2,1)S(1)}, bf16[256,768]{1,0:T(8,128)(2,1)S(1)}, u32[]{:S(2)}, u32[]{:S(2)}) %collective-permute-start.12) | collective-permute-done | bytes 393248 | tf_op jit(solution)/shard_map/ppermute | solution.py:23
  89.0 6.3 %shard_map.230.refs_4_.refs_1_ = bf16[2,1024,768]{2,1,0:T(8,128)(2,1)S(1)} custom-call(bf16[512,1024]{1,0:T(8,128)(2,1)S(1)} %shard_map.226.refs_3_.refs_0_.refs_4_, bf16[512,1024]{1,0:T(8,128)(2,1)S(1)} %collective-permute-done.7.refs_1_.refs_5_, bf16[256,768]{1,0:T(8,128)(2,1)} %shard_map.220.refs_2_.refs_4_, ...), custom_call_target="tpu_custom_call" | custom-call | flops 3221225472 | bytes 8388608 | tf_op jit(solution)/shard_map/pallas_call | solution.py:119
  106.8 9.5 %collective-permute-done.23.refs_10_.refs_3_.refs_2_ = bf16[256,1280]{1,0:T(8,128)(2,1)S(1)} collective-permute-done((bf16[256,1280]{1,0:T(8,128)(2,1)S(1)}, bf16[256,1280]{1,0:T(8,128)(2,1)S(1)}, u32[]{:S(2)}, u32[]{:S(2)}) %collective-permute-start.23) | collective-permute-done | bytes 655392 | tf_op jit(solution)/shard_map/ppermute | solution.py:27
  128.7 10.6 %collective-permute-done.24.refs_3_.refs_5_.refs_4_ = bf16[256,1280]{1,0:T(8,128)(2,1)S(1)} collective-permute-done((bf16[256,1280]{1,0:T(8,128)(2,1)S(1)}, bf16[256,1280]{1,0:T(8,128)(2,1)S(1)}, u32[]{:S(2)}, u32[]{:S(2)}) %collective-permute-start.24) | collective-permute-done | bytes 655392 | tf_op jit(solution)/shard_map/ppermute | solution.py:23
  189.5 9.2 %shard_map.250 = (bf16[2,1024,1024]{2,1,0:T(8,128)(2,1)S(1)}, bf16[2,1024,1024]{2,1,0:T(8,128)(2,1)S(1)}) custom-call(bf16[512,1024]{1,0:T(8,128)(2,1)S(1)} %get-tuple-element.130.refs_0_, bf16[512,1024]{1,0:T(8,128)(2,1)S(1)} %collective-permute-done.42.refs_1_, bf16[256,1280]{1,0:T(8,128)(2,1)S(1)} %shard_map.231.refs_1_.refs_2_, ...), custom_call_target="tpu_custom_call" | custom-call | flops 4294967296 | bytes 15728640 | tf_op jit(solution)/shard_map/pallas_call | solution.py:119
  200.7 5.9 %shard_map.251 = (bf16[256,2048]{1,0:T(8,128)(2,1)S(1)}, bf16[256,2048]{1,0:T(8,128)(2,1)}, bf16[512,2048]{1,0:T(8,128)(2,1)S(1)}, bf16[512,2048]{1,0:T(8,128)(2,1)S(1)}, bf16[512,2048]{1,0:T(8,128)(2,1)S(1)}) custom-call(bf16[512,1024]{1,0:T(8,128)(2,1)S(1)} %shard_map.240.refs_10_.refs_0_.refs_5_, bf16[512,1024]{1,0:T(8,128)(2,1)S(1)} %collective-permute-done.45.refs_1_, ...), custom_call_target="tpu_custom_call" | custom-call | flops 4294967296 | bytes 14680064 | tf_op jit(solution)/shard_map/pallas_call | solution.py:119
  212.6 6.0 %shard_map.252.refs_0_.refs_2_ = bf16[2,1024,1024]{2,1,0:T(8,128)(2,1)S(1)} custom-call(bf16[512,1024]{1,0:T(8,128)(2,1)S(1)} %shard_map.240.refs_10_.refs_0_.refs_5_, bf16[512,1024]{1,0:T(8,128)(2,1)S(1)} %collective-permute-done.45.refs_1_, bf16[256,1024]{1,0:T(8,128)(2,1)S(1)} %shard_map.242.refs_12_.refs_2_.refs_1_, bf16[256,1024]{1,0:T(8,128)(2,1)S(1)} %copy-done.54, ...), custom_call_target="tpu_custom_call" | custom-call | flops 4294967296 | bytes 14680064 | tf_op jit(solution)/shard_map/pallas_call | solution.py:119
  229.8 6.1 %shard_map.254 = (bf16[256,2048]{1,0:T(8,128)(2,1)S(1)}, bf16[256,2048]{1,0:T(8,128)(2,1)}, bf16[512,2048]{1,0:T(8,128)(2,1)S(1)}, bf16[512,2048]{1,0:T(8,128)(2,1)S(1)}, bf16[512,2048]{1,0:T(8,128)(2,1)S(1)}) custom-call(bf16[512,1024]{1,0:T(8,128)(2,1)S(1)} %copy-done.26, ...), custom_call_target="tpu_custom_call", output_to_operand_aliasing={{0}: (3, {}), {1}: (4, {}), {2}: (5, {}), {3}: (6, {}), {4}... | custom-call | flops 4294967296 | bytes 23068672 | tf_op jit(solution)/shard_map/pallas_call | solution.py:119
  244.0 11.6 %shard_map.257 = (bf16[2,512,256]{2,1,0:T(8,128)(2,1)S(1)}, f32[2,512,512]{2,1,0:T(8,128)S(1)}, f32[2,512,512]{2,1,0:T(8,128)S(1)}, f32[2,512,512]{2,1,0:T(8,128)S(1)}) custom-call(s32[19]{0:T(128)S(1)} %stack.88.refs_0_, bf16[2,1024,768]{2,1,0:T(8,128)(2,1)S(1)} %shard_map.230.refs_4_.refs_1_, bf16[2,512,768]{2,1,0:T(8,128)(2,1)S(1)} %shard_map.243.refs_2_, ...), custom_call_target="tpu_custom_call" | custom-call | flops 3019898880 | bytes 13107276 | tf_op jit(solution)/shard_map/pallas_call | solution.py:119
  255.6 9.5 %shard_map.258 = (bf16[2,512,768]{2,1,0:T(8,128)(2,1)S(1)}, bf16[2,512,512]{2,1,0:T(8,128)(2,1)S(1)}) custom-call(s32[19]{0:T(128)S(1)} %stack.88.refs_0_, bf16[2,1024,768]{2,1,0:T(8,128)(2,1)S(1)} %shard_map.230.refs_4_.refs_1_, bf16[2,512,768]{2,1,0:T(8,128)(2,1)S(1)} %shard_map.243.refs_2_, f32[2,512,128]{2,1,0:T(8,128)S(1)} %copy-done.20, ...), custom_call_target="tpu_custom_call" | custom-call | flops 2684354560 | bytes 12582988 | tf_op jit(solution)/shard_map/pallas_call | solution.py:119
  270.5 8.4 %shard_map.262 = (bf16[2,512,256]{2,1,0:T(8,128)(2,1)S(1)}, f32[2,512,512]{2,1,0:T(8,128)S(1)}, f32[2,512,512]{2,1,0:T(8,128)S(1)}) custom-call(s32[19]{0:T(128)S(1)} %stack.88.refs_0_, bf16[2,1024,768]{2,1,0:T(8,128)(2,1)S(1)} %shard_map.230.refs_4_.refs_1_, bf16[2,512,768]{2,1,0:T(8,128)(2,1)S(1)} %shard_map.235.refs_2_, f32[2,512,128]{2,1,0:T(8,128)S(1)} %copy-done.50, ...), custom_call_target="tpu_custom_call" | custom-call | flops 2348810240 | bytes 11010124 | tf_op jit(solution)/shard_map/pallas_call | solution.py:119
  298.4 9.4 %shard_map.266 = (bf16[2,512,768]{2,1,0:T(8,128)(2,1)S(1)}, bf16[2,512,512]{2,1,0:T(8,128)(2,1)S(1)}) custom-call(s32[19]{0:T(128)S(1)} %stack.88.refs_0_, bf16[2,1024,768]{2,1,0:T(8,128)(2,1)S(1)} %shard_map.230.refs_4_.refs_1_, bf16[2,512,768]{2,1,0:T(8,128)(2,1)S(1)} %shard_map.235.refs_2_, f32[2,512,128]{2,1,0:T(8,128)S(1)} %get-tuple-element.113.refs_12_.refs_3_, ...), custom_call_target="tpu_custom_call" | custom-call | flops 2684354560 | bytes 14680140 | tf_op jit(solution)/shard_map/pallas_call | solution.py:119
  324.8 14.9 %collective-permute-done.57.refs_1_ = bf16[256,768]{1,0:T(8,128)(2,1)} collective-permute-done((bf16[256,768]{1,0:T(8,128)(2,1)}, bf16[256,768]{1,0:T(8,128)(2,1)}, u32[]{:S(2)}, u32[]{:S(2)}) %collective-permute-start.57) | collective-permute-done | bytes 393248 | tf_op jit(solution)/shard_map/ppermute | solution.py:23
  340.7 5.9 %shard_map.271 = (f32[512,1024]{1,0:T(8,128)S(1)}, bf16[512,1024]{1,0:T(8,128)(2,1)S(1)}) custom-call(bf16[2,1024,1024]{2,1,0:T(8,128)(2,1)S(1)} %copy-done.113, bf16[256,1024]{1,0:T(8,128)(2,1)S(1)} %shard_map.242.refs_12_.refs_2_.refs_1_, bf16[256,1024]{1,0:T(8,128)(2,1)S(1)} %copy-done.55, bf16[256,1024]{1,0:T(8,128)(2,1)} %collective-permute-done.35.refs_3_.refs_4_, ...), custom_call_target="tpu_custom_call" | custom-call | flops 4294967296 | bytes 11534336 | tf_op jit(solution)/shard_map/pallas_call | solution.py:119
  346.6 14.9 %collective-permute-done.58.refs_1_ = bf16[256,768]{1,0:T(8,128)(2,1)S(1)} collective-permute-done((bf16[256,768]{1,0:T(8,128)(2,1)S(1)}, bf16[256,768]{1,0:T(8,128)(2,1)S(1)}, u32[]{:S(2)}, u32[]{:S(2)}) %collective-permute-start.58) | collective-permute-done | bytes 393248 | tf_op jit(solution)/shard_map/ppermute | solution.py:23
  373.1 6.2 %collective-permute-done.62.refs_1_ = bf16[256,1280]{1,0:T(8,128)(2,1)S(1)} collective-permute-done((bf16[256,1280]{1,0:T(8,128)(2,1)}, bf16[256,1280]{1,0:T(8,128)(2,1)S(1)}, u32[]{:S(2)}, u32[]{:S(2)}) %collective-permute-start.62) | collective-permute-done | bytes 655392 | tf_op jit(solution)/shard_map/ppermute | solution.py:23
  387.3 14.7 %collective-permute-done.65.refs_1_ = bf16[512,768]{1,0:T(8,128)(2,1)S(1)} collective-permute-done((bf16[512,768]{1,0:T(8,128)(2,1)S(1)}, bf16[512,768]{1,0:T(8,128)(2,1)S(1)}, u32[]{:S(2)}, u32[]{:S(2)}) %collective-permute-start.65) | collective-permute-done | bytes 786464 | tf_op jit(solution)/shard_map/ppermute | solution.py:23
  412.8 7.7 %collective-permute-done.68.refs_1_ = bf16[256,768]{1,0:T(8,128)(2,1)S(1)} collective-permute-done((bf16[256,768]{1,0:T(8,128)(2,1)S(1)}, bf16[256,768]{1,0:T(8,128)(2,1)S(1)}, u32[]{:S(2)}, u32[]{:S(2)}) %collective-permute-start.68) | collective-permute-done | bytes 393248 | tf_op jit(solution)/shard_map/ppermute | solution.py:27
  423.2 6.6 %collective-permute-done.73.refs_1_ = bf16[512,1280]{1,0:T(8,128)(2,1)S(1)} collective-permute-done((bf16[512,1280]{1,0:T(8,128)(2,1)S(1)}, bf16[512,1280]{1,0:T(8,128)(2,1)S(1)}, u32[]{:S(2)}, u32[]{:S(2)}) %collective-permute-start.73) | collective-permute-done | bytes 1310752 | tf_op jit(solution)/shard_map/ppermute | solution.py:23
  435.6 22.9 %collective-permute-done.72.refs_2_ = f32[272,128]{1,0:T(8,128)S(1)} collective-permute-done((f32[272,128]{1,0:T(8,128)S(1)}, f32[272,128]{1,0:T(8,128)S(1)}, u32[]{:S(2)}, u32[]{:S(2)}) %collective-permute-start.72) | collective-permute-done | bytes 139296 | tf_op jit(solution)/shard_map/ppermute | solution.py:23
  469.8 13.1 %collective-permute-done.79 = bf16[128,1280]{1,0:T(8,128)(2,1)S(1)} collective-permute-done((bf16[128,1280]{1,0:T(8,128)(2,1)S(1)}, bf16[128,1280]{1,0:T(8,128)(2,1)S(1)}, u32[]{:S(2)}, u32[]{:S(2)}) %collective-permute-start.79) | collective-permute-done | bytes 327712 | tf_op jit(solution)/shard_map/ppermute | solution.py:27
  (479 shorter events, 247.2 us)
Async XLA Ops:
  2.9 28.2 %collective-permute-start = (bf16[256,1024]{1,0:T(8,128)(2,1)}, bf16[256,1024]{1,0:T(8,128)(2,1)}, u32[]{:S(2)}, u32[]{:S(2)}) collective-permute-start(bf16[256,1024]{1,0:T(8,128)(2,1)} %get-tuple-element.240), channel_id=1, source_target_pairs={{0,2},{2,0},{1,3},{3,1},{4,6},{6,4},{5,7},{7,5},{8,10},{10,8},{9,1... | collective-permute-start | bytes 1572872 | tf_op jit(solution)/shard_map/ppermute | solution.py:23
  41.9 46.5 %collective-permute-start.7 = (bf16[512,1024]{1,0:T(8,128)(2,1)S(1)}, bf16[512,1024]{1,0:T(8,128)(2,1)S(1)}, u32[]{:S(2)}, u32[]{:S(2)}) collective-permute-start(bf16[512,1024]{1,0:T(8,128)(2,1)S(1)} %shard_map.226.refs_3_.refs_0_.refs_4_), channel_id=1, source_target_pairs={{0,1},{1,0},{2,3},{3,2},{4,5},{5,4},{6,7},{7,6},{8,9},{9,8},{10,11... | collective-permute-start | bytes 3145736 | tf_op jit(solution)/shard_map/ppermute | solution.py:23
  68.2 27.1 %collective-permute-start.18 = (bf16[256,1024]{1,0:T(8,128)(2,1)S(1)}, bf16[256,1024]{1,0:T(8,128)(2,1)S(1)}, u32[]{:S(2)}, u32[]{:S(2)}) collective-permute-start(bf16[256,1024]{1,0:T(8,128)(2,1)S(1)} %shard_map.228.refs_2_.refs_1_), channel_id=1, source_target_pairs={{0,2},{2,0},{1,3},{3,1},{4,6},{6,4},{5,7},{7,5},{8,10},{10,8},{9,1... | collective-permute-start | bytes 1572872 | tf_op jit(solution)/shard_map/ppermute | solution.py:23
  97.4 29.7 %collective-permute-start.26 = (bf16[256,1280]{1,0:T(8,128)(2,1)S(1)}, bf16[256,1280]{1,0:T(8,128)(2,1)S(1)}, u32[]{:S(2)}, u32[]{:S(2)}) collective-permute-start(bf16[256,1280]{1,0:T(8,128)(2,1)S(1)} %shard_map.231.refs_1_.refs_2_), channel_id=1, source_target_pairs={{0,4},{4,0},{1,5},{5,1},{2,6},{6,2},{3,7},{7,3},{8,12},{12,8},{9,1... | collective-permute-start | bytes 1966088 | tf_op jit(solution)/shard_map/ppermute | solution.py:23
  101.8 25.3 %collective-permute-start.27 = (bf16[256,1280]{1,0:T(8,128)(2,1)S(1)}, bf16[256,1280]{1,0:T(8,128)(2,1)S(1)}, u32[]{:S(2)}, u32[]{:S(2)}) collective-permute-start(bf16[256,1280]{1,0:T(8,128)(2,1)S(1)} %shard_map.231.refs_1_.refs_2_), channel_id=1, source_target_pairs={{0,2},{2,0},{1,3},{3,1},{4,6},{6,4},{5,7},{7,5},{8,10},{10,8},{9,1... | collective-permute-start | bytes 1966088 | tf_op jit(solution)/shard_map/ppermute | solution.py:23
  116.3 23.0 %collective-permute-start.24 = (bf16[256,1280]{1,0:T(8,128)(2,1)S(1)}, bf16[256,1280]{1,0:T(8,128)(2,1)S(1)}, u32[]{:S(2)}, u32[]{:S(2)}) collective-permute-start(bf16[256,1280]{1,0:T(8,128)(2,1)S(1)} %collective-permute-done.23.refs_10_.refs_3_.refs_2_), channel_id=1, source_target_pairs={{0,4},{4,0},{1,5},{5,1},{2,6},{6,2},{3,7},{7,3},{8,12},{12,8},{9,1... | collective-permute-start | bytes 1966088 | tf_op jit(solution)/shard_map/ppermute | solution.py:23
  116.4 23.1 %collective-permute-start.25 = (bf16[256,1280]{1,0:T(8,128)(2,1)S(1)}, bf16[256,1280]{1,0:T(8,128)(2,1)S(1)}, u32[]{:S(2)}, u32[]{:S(2)}) collective-permute-start(bf16[256,1280]{1,0:T(8,128)(2,1)S(1)} %collective-permute-done.23.refs_10_.refs_3_.refs_2_), channel_id=1, source_target_pairs={{0,2},{2,0},{1,3},{3,1},{4,6},{6,4},{5,7},{7,5},{8,10},{10,8},{9,1... | collective-permute-start | bytes 1966088 | tf_op jit(solution)/shard_map/ppermute | solution.py:23
  239.4 28.0 %collective-permute-start.50 = (bf16[256,2048]{1,0:T(8,128)(2,1)S(1)}, bf16[256,2048]{1,0:T(8,128)(2,1)S(1)}, u32[]{:S(2)}, u32[]{:S(2)}) collective-permute-start(bf16[256,2048]{1,0:T(8,128)(2,1)S(1)} %get-tuple-element.141.refs_6_), channel_id=1, source_target_pairs={{0,2},{2,0},{1,3},{3,1},{4,6},{6,4},{5,7},{7,5},{8,10},{10,8},{9,1... | collective-permute-start | bytes 3145736 | tf_op jit(solution)/shard_map/ppermute | solution.py:23
  240.3 28.0 %collective-permute-start.49 = (bf16[256,2048]{1,0:T(8,128)(2,1)}, bf16[256,2048]{1,0:T(8,128)(2,1)}, u32[]{:S(2)}, u32[]{:S(2)}) collective-permute-start(bf16[256,2048]{1,0:T(8,128)(2,1)} %get-tuple-element.152), channel_id=1, source_target_pairs={{0,4},{4,0},{1,5},{5,1},{2,6},{6,2},{3,7},{7,3},{8,12},{12,8},{9,1... | collective-permute-start | bytes 3145736 | tf_op jit(solution)/shard_map/ppermute | solution.py:23
  282.7 85.3 %collective-permute-start.54 = (bf16[512,2048]{1,0:T(8,128)(2,1)S(1)}, bf16[512,2048]{1,0:T(8,128)(2,1)}, u32[]{:S(2)}, u32[]{:S(2)}) collective-permute-start(bf16[512,2048]{1,0:T(8,128)(2,1)S(1)} %shard_map.260.refs_2_), channel_id=1, source_target_pairs={{0,4},{4,0},{1,5},{5,1},{2,6},{6,2},{3,7},{7,3},{8,12},{12,8},{9,1... | collective-permute-start | bytes 6291464 | tf_op jit(solution)/shard_map/ppermute | solution.py:23
  283.6 85.3 %collective-permute-start.55 = (bf16[512,2048]{1,0:T(8,128)(2,1)S(1)}, bf16[512,2048]{1,0:T(8,128)(2,1)}, u32[]{:S(2)}, u32[]{:S(2)}) collective-permute-start(bf16[512,2048]{1,0:T(8,128)(2,1)S(1)} %shard_map.261.refs_5_), channel_id=1, source_target_pairs={{0,2},{2,0},{1,3},{3,1},{4,6},{6,4},{5,7},{7,5},{8,10},{10,8},{9,1... | collective-permute-start | bytes 6291464 | tf_op jit(solution)/shard_map/ppermute | solution.py:23
  292.8 46.9 %collective-permute-start.57 = (bf16[256,768]{1,0:T(8,128)(2,1)}, bf16[256,768]{1,0:T(8,128)(2,1)}, u32[]{:S(2)}, u32[]{:S(2)}) collective-permute-start(bf16[256,768]{1,0:T(8,128)(2,1)} %get-tuple-element.162.refs_8_), channel_id=1, source_target_pairs={{0,4},{4,0},{1,5},{5,1},{2,6},{6,2},{3,7},{7,3},{8,12},{12,8},{9,1... | collective-permute-start | bytes 1179656 | tf_op jit(solution)/shard_map/ppermute | solution.py:23
  321.3 41.2 %collective-permute-start.56 = (bf16[512,1024]{1,0:T(8,128)(2,1)S(1)}, bf16[512,1024]{1,0:T(8,128)(2,1)S(1)}, u32[]{:S(2)}, u32[]{:S(2)}) collective-permute-start(bf16[512,1024]{1,0:T(8,128)(2,1)S(1)} %get-tuple-element.174), channel_id=1, source_target_pairs={{0,1},{1,0},{2,3},{3,2},{4,5},{5,4},{6,7},{7,6},{8,9},{9,8},{10,11... | collective-permute-start | bytes 3145736 | tf_op jit(solution)/shard_map/ppermute | solution.py:23
  321.4 40.1 %collective-permute-start.61 = (bf16[256,1280]{1,0:T(8,128)(2,1)S(1)}, bf16[256,1280]{1,0:T(8,128)(2,1)S(1)}, u32[]{:S(2)}, u32[]{:S(2)}) collective-permute-start(bf16[256,1280]{1,0:T(8,128)(2,1)S(1)} %get-tuple-element.167.refs_12_), channel_id=1, source_target_pairs={{0,4},{4,0},{1,5},{5,1},{2,6},{6,2},{3,7},{7,3},{8,12},{12,8},{9,1... | collective-permute-start | bytes 1966088 | tf_op jit(solution)/shard_map/ppermute | solution.py:23
  369.0 33.1 %collective-permute-start.65 = (bf16[512,768]{1,0:T(8,128)(2,1)S(1)}, bf16[512,768]{1,0:T(8,128)(2,1)S(1)}, u32[]{:S(2)}, u32[]{:S(2)}) collective-permute-start(bf16[512,768]{1,0:T(8,128)(2,1)S(1)} %copy-done.91), channel_id=1, source_target_pairs={{0,4},{4,0},{1,5},{5,1},{2,6},{6,2},{3,7},{7,3},{8,12},{12,8},{9,1... | collective-permute-start | bytes 2359304 | tf_op jit(solution)/shard_map/ppermute | solution.py:23
  379.2 28.2 %collective-permute-start.64 = (bf16[256,2048]{1,0:T(8,128)(2,1)S(1)}, bf16[256,2048]{1,0:T(8,128)(2,1)S(1)}, u32[]{:S(2)}, u32[]{:S(2)}) collective-permute-start(bf16[256,2048]{1,0:T(8,128)(2,1)S(1)} %get-tuple-element.190), channel_id=1, source_target_pairs={{0,8},{8,0},{16,24},{24,16},{1,9},{9,1},{17,25},{25,17},{2,10},{10... | collective-permute-start | bytes 3145736 | tf_op jit(solution)/shard_map/ppermute | solution.py:27
  380.0 22.8 %collective-permute-start.66 = (bf16[512,768]{1,0:T(8,128)(2,1)S(1)}, bf16[512,768]{1,0:T(8,128)(2,1)S(1)}, u32[]{:S(2)}, u32[]{:S(2)}) collective-permute-start(bf16[512,768]{1,0:T(8,128)(2,1)S(1)} %shard_map.273.refs_6_), channel_id=1, source_target_pairs={{0,2},{2,0},{1,3},{3,1},{4,6},{6,4},{5,7},{7,5},{8,10},{10,8},{9,1... | collective-permute-start | bytes 2359304 | tf_op jit(solution)/shard_map/ppermute | solution.py:23
  384.6 45.1 %collective-permute-start.73 = (bf16[512,1280]{1,0:T(8,128)(2,1)S(1)}, bf16[512,1280]{1,0:T(8,128)(2,1)S(1)}, u32[]{:S(2)}, u32[]{:S(2)}) collective-permute-start(bf16[512,1280]{1,0:T(8,128)(2,1)S(1)} %copy-done.86), channel_id=1, source_target_pairs={{0,4},{4,0},{1,5},{5,1},{2,6},{6,2},{3,7},{7,3},{8,12},{12,8},{9,1... | collective-permute-start | bytes 3932168 | tf_op jit(solution)/shard_map/ppermute | solution.py:23
  385.2 44.6 %collective-permute-start.74 = (bf16[512,1280]{1,0:T(8,128)(2,1)S(1)}, bf16[512,1280]{1,0:T(8,128)(2,1)S(1)}, u32[]{:S(2)}, u32[]{:S(2)}) collective-permute-start(bf16[512,1280]{1,0:T(8,128)(2,1)S(1)} %shard_map.279.refs_3_), channel_id=1, source_target_pairs={{0,2},{2,0},{1,3},{3,1},{4,6},{6,4},{5,7},{7,5},{8,10},{10,8},{9,1... | collective-permute-start | bytes 3932168 | tf_op jit(solution)/shard_map/ppermute | solution.py:23
  430.2 33.8 %collective-permute-start.76 = (bf16[256,1280]{1,0:T(8,128)(2,1)S(1)}, bf16[256,1280]{1,0:T(8,128)(2,1)S(1)}, u32[]{:S(2)}, u32[]{:S(2)}) collective-permute-start(bf16[256,1280]{1,0:T(8,128)(2,1)S(1)} %get-tuple-element.204), channel_id=1, source_target_pairs={{0,8},{8,0},{16,24},{24,16},{1,9},{9,1},{17,25},{25,17},{2,10},{10... | collective-permute-start | bytes 1966088 | tf_op jit(solution)/shard_map/ppermute | solution.py:27
  431.1 28.9 %collective-permute-start.59 = (bf16[256,1024]{1,0:T(8,128)(2,1)S(1)}, bf16[256,1024]{1,0:T(8,128)(2,1)S(1)}, u32[]{:S(2)}, u32[]{:S(2)}) collective-permute-start(bf16[256,1024]{1,0:T(8,128)(2,1)S(1)} %get-tuple-element.184), channel_id=1, source_target_pairs={{0,2},{2,0},{1,3},{3,1},{4,6},{6,4},{5,7},{7,5},{8,10},{10,8},{9,1... | collective-permute-start | bytes 1572872 | tf_op jit(solution)/shard_map/ppermute | solution.py:23
  432.5 34.1 %collective-permute-start.80 = (bf16[128,2048]{1,0:T(8,128)(2,1)S(1)}, bf16[128,2048]{1,0:T(8,128)(2,1)S(1)}, u32[]{:S(2)}, u32[]{:S(2)}) collective-permute-start(bf16[128,2048]{1,0:T(8,128)(2,1)S(1)} %get-tuple-element.209), channel_id=1, source_target_pairs={{0,16},{8,24},{16,0},{24,8},{1,17},{9,25},{17,1},{25,9},{2,18},{10... | collective-permute-start | bytes 1572872 | tf_op jit(solution)/shard_map/ppermute | solution.py:27
  433.5 34.2 %collective-permute-start.75 = (bf16[256,1024]{1,0:T(8,128)(2,1)S(1)}, bf16[256,1024]{1,0:T(8,128)(2,1)S(1)}, u32[]{:S(2)}, u32[]{:S(2)}) collective-permute-start(bf16[256,1024]{1,0:T(8,128)(2,1)S(1)} %get-tuple-element.203), channel_id=1, source_target_pairs={{0,2},{2,0},{1,3},{3,1},{4,6},{6,4},{5,7},{7,5},{8,10},{10,8},{9,1... | collective-permute-start | bytes 1572872 | tf_op jit(solution)/shard_map/ppermute | solution.py:23
  434.8 23.7 %collective-permute-start.72 = (f32[272,128]{1,0:T(8,128)S(1)}, f32[272,128]{1,0:T(8,128)S(1)}, u32[]{:S(2)}, u32[]{:S(2)}) collective-permute-start(f32[272,128]{1,0:T(8,128)S(1)} %shard_map.286.refs_3_.refs_1_), channel_id=1, source_target_pairs={{0,2},{2,0},{1,3},{3,1},{4,6},{6,4},{5,7},{7,5},{8,10},{10,8},{9,1... | collective-permute-start | bytes 417800 | tf_op jit(solution)/shard_map/ppermute | solution.py:23
  (178 other events, 1800.6 us)

commit v5 on v4

--- a/solution.py
+++ b/solution.py
@@ -12,7 +12,8 @@
 BLOCK = 512
 EPSILON = 1e-06
 MASKED = -1e30
-COST = 1
+COST = 0.01
+LONG = 1e11
 GELU = 0.7978845608028654
 RING = 4
 BF = jnp.bfloat16
@@ -106,7 +107,7 @@
 ORDER = Order()
 
 
-def call(kernel, grid, inputs, in_specs, outputs, out_specs, flops=0, exps=0, deps=(), vmem=16, **more):
+def call(kernel, grid, inputs, in_specs, outputs, out_specs, flops=0, exps=0, deps=(), vmem=16, long=False, **more):
     block_bytes = sum(a.size * a.dtype.itemsize for a in inputs)
     shapes = [jax.ShapeDtypeStruct(shape, dtype) for shape, dtype in outputs]
     out_bytes = sum(s.size * s.dtype.itemsize for s in shapes)
@@ -124,7 +125,7 @@
         out_shape=shapes,
         compiler_params=pltpu.CompilerParams(vmem_limit_bytes=vmem * 2**20),
         cost_estimate=pl.CostEstimate(
-            flops=int(flops * COST), bytes_accessed=int((block_bytes + out_bytes) * COST), transcendentals=int(exps * COST)
+            flops=int(LONG) if long else int(flops * COST), bytes_accessed=int((block_bytes + out_bytes) * COST), transcendentals=int(exps * COST)
         ),
         **more,
     )(*inputs, *deps)
@@ -227,7 +228,7 @@
     return jnp.concatenate(parts, axis=0)
 
 
-def project(own, other, pieces, column, width, block, blocks=1, gate=None, activate=False, deps=()):
+def project(own, other, pieces, column, width, block, blocks=1, gate=None, activate=False, deps=(), long=False):
     rows = own.shape[0] * 2
     refs = flat_pieces(pieces)
     first = column // block
@@ -266,12 +267,12 @@
         [((2, rows, width), BF)] * count,
         [spec] * count,
         flops=4 * rows * own.shape[1] * width,
-        deps=deps,
+        deps=deps, long=long,
     )
     return out if activate else out[0]
 
 
-def merge(lefts, pieces, column, blocks=1, deps=()):
+def merge(lefts, pieces, column, blocks=1, deps=(), long=False, halves=1):
     refs = flat_pieces(pieces)
     columns = sum(part.shape[2] for part in lefts[0])
     per = lefts[0][0].shape[1] // 2
@@ -283,11 +284,12 @@
 
     def kernel(*args):
         left_refs, weights = args[: len(flat)], args[len(flat) : len(flat) + 8]
-        own_ref, other_ref = args[len(flat) + 8 :]
+        own_ref, *other_refs = args[len(flat) + 8 :]
+        size = rows // halves
         sides = [
             jnp.concatenate([ref[...] for ref in weights[4 * y : 4 * y + 4]], axis=0) for y in range(2)
         ]
-        for core, out_ref in ((1, other_ref), (0, own_ref)):
+        for core in (1, 0):
             total = None
             for y in range(2):
                 left = []
@@ -296,7 +298,11 @@
                     left.append(jnp.concatenate([ref[y, core * per : (core + 1) * per] for ref in here], axis=1))
                 piece = mm_nt(jnp.concatenate(left, axis=0), sides[y])
                 total = piece if total is None else total + piece
-            out_ref[...] = total.astype(out_ref.dtype)
+            if core:
+                for i, ref in enumerate(other_refs):
+                    ref[...] = total[i * size : (i + 1) * size].astype(BF)
+            else:
+                own_ref[...] = total
 
     weight_spec = [pl.BlockSpec((ref.shape[0], columns), lambda i: (0, first)) for ref in refs]
     return call(
@@ -304,14 +310,17 @@
         (1,),
         flat + refs,
         [whole(left) for left in flat] + weight_spec,
-        [((rows, width), F32), ((rows, width), BF)],
-        [whole_out((rows, width))] * 2,
+        [((rows, width), F32)] + [((rows // halves, width), BF)] * halves,
+        [whole_out((rows, width))] + [whole_out((rows // halves, width))] * halves,
         flops=8 * rows * width * columns,
-        deps=deps,
-    )
-
-
-def outer(segments, block=None, vmem=16, deps=(), into=None, share=1):
+        deps=deps, long=long,
+    )
+
+
+QUARTERS = ((1, 1), (1, 0), (0, 1), (0, 0))
+
+
+def outer(segments, block=None, vmem=16, deps=(), long=False, split=False):
     width = segments[0][0][0][0].shape[1]
     sizes = [rights[0].shape[2] for lefts, rights, blocks in segments]
     columns = sum(sizes)
@@ -326,8 +335,10 @@
         in_specs += [pl.BlockSpec((2, right.shape[1], wide), lambda j: (0, 0, j)) for right in rights]
         flops += 4 * width * rights[0].shape[2] * sum(right.shape[1] for right in rights)
 
+    sizes_out = [half // 2, half, half, half, half // 2] if split else [half] * 4
+
     def kernel(*args):
-        low11, high11, out10, out01, out00 = args[-5:]
+        outs = args[len(inputs) :]
         place, column = 0, 0
         for lefts, rights, blocks in segments:
             left_refs = args[place : place + 2 * len(lefts)]
@@ -342,55 +353,40 @@
                 right = jnp.concatenate([ref[y] for ref in right_refs], axis=0)
                 for x in (1, 0):
                     total = mm_tn(left[:, x * half : (x + 1) * half], right).astype(BF)
-                    if x and y:
-                        low11[:, here] = total[: half // 2]
-                        high11[:, here] = total[half // 2 :]
+                    if split and x and y:
+                        outs[0][:, here] = total[: half // 2]
+                        outs[-1][:, here] = total[half // 2 :]
                     else:
-                        {(1, 0): out10, (0, 1): out01, (0, 0): out00}[(x, y)][:, here] = total
-
-    first = 0 if into is None else columns // block
-    aliases = {}
-    if into is not None:
-        aliases = {len(inputs) + i: i for i in range(5)}
-        inputs += list(into)
-        in_specs += [pl.BlockSpec(memory_space=pl.ANY)] * 5
+                        outs[QUARTERS.index((x, y))][:, here] = total
+
     return call(
         kernel,
         (columns // block,),
         inputs,
         in_specs,
-        [((half // 2, share * columns), BF)] * 2 + [((half, share * columns), BF)] * 3,
-        [pl.BlockSpec((half // 2, block), lambda j: (0, first + j))] * 2
-        + [pl.BlockSpec((half, block), lambda j: (0, first + j))] * 3,
+        [((rows, columns), BF) for rows in sizes_out],
+        [pl.BlockSpec((rows, block), lambda j: (0, j)) for rows in sizes_out],
         flops=flops,
         vmem=vmem,
-        deps=deps,
-        input_output_aliases=aliases,
-    )
-
-
-def add_into(array, piece, half, deps=()):
-    rows, columns = piece.shape
-
-    def kernel(array_ref, piece_ref, out_ref):
-        out_ref[...] = (array_ref[...].astype(F32) + piece_ref[...].astype(F32)).astype(BF)
-
-    return call(
-        kernel,
-        (1,),
-        [array, piece],
-        [pl.BlockSpec((rows, columns), lambda i: (half, 0)), pl.BlockSpec((rows, columns), lambda i: (0, 0))],
-        [(array.shape, BF)],
-        [pl.BlockSpec((rows, columns), lambda i: (half, 0))],
-        input_output_aliases={0: 0},
-        deps=deps,
-        vmem=28,
-    )[0]
-
-
-def add_split(arrays, deps=()):
+        deps=deps, long=long,
+    )
+
+
+def add_low(first, second, deps=(), long=False):
+    rows, columns = first.shape
+    half = rows // 2
+
+    def kernel(first_ref, second_ref, out_ref):
+        out_ref[...] = (first_ref[...].astype(F32) + second_ref[...].astype(F32)).astype(BF)
+
+    spec = pl.BlockSpec((half, columns), lambda i: (i, 0))
+    return call(kernel, (2,), [first, second], [spec, spec], [(first.shape, BF)], [spec], deps=deps, long=long)[0]
+
+
+def add_split(arrays, deps=(), long=False, whole_sum=False):
     rows, columns = arrays[0].shape
-    part = rows // 2
+    part = rows if whole_sum else rows // 2
+    types = (F32,) if whole_sum else (F32, BF)
 
     def kernel(*refs):
         for half, out_ref in enumerate(refs[len(arrays) :]):
@@ -405,39 +401,61 @@
         (1,),
         arrays,
         [whole(array) for array in arrays],
-        [((part, columns), F32), ((part, columns), BF)],
-        [whole_out((part, columns))] * 2,
+        [((part, columns), dtype) for dtype in types],
+        [whole_out((part, columns))] * len(types),
+        deps=deps, long=long,
+    )
+
+
+def add_into(array, piece, half, deps=()):
+    rows, columns = piece.shape
+
+    def kernel(array_ref, piece_ref, out_ref):
+        out_ref[...] = (array_ref[...].astype(F32) + piece_ref[...].astype(F32)).astype(BF)
+
+    here, there = pl.BlockSpec((rows, columns), lambda i: (half, 0)), pl.BlockSpec((rows, columns), lambda i: (0, 0))
+    return call(
+        kernel,
+        (1,),
+        [array, piece],
+        [here, there],
+        [(array.shape, BF)],
+        [here],
+        input_output_aliases={0: 0},
         deps=deps,
-        vmem=28,
-    )
+    )[0]
 
 
 class Reduce:
-    def __init__(self, quarters, by_x=False):
-        low11, high11, self.out10, self.out01, self.out00 = quarters
-        self.by_x = by_x
-        self.low_got, self.high_got = swap(low11, "x" if by_x else "y"), swap(high11, "x")
-        self.first = [self.low_got, self.high_got]
-
-    def second(self, deps=()):
-        if self.by_x:
-            self.out01 = add_into(self.out01, self.low_got, 0, deps)
+    def __init__(self, quarters, first_axis=None):
+        self.first_axis = first_axis
+        if first_axis is None:
+            low11, self.out10, self.out01, self.out00, high11 = quarters
+            self.first = [swap(low11, "y"), swap(high11, "x")]
         else:
-            self.out10 = add_into(self.out10, self.low_got, 0, deps)
-        self.x_got = swap(self.out10, "x")
-        self.y_got = swap(add_into(self.out01, self.high_got, 1, deps), "y")
-        self.next = [self.x_got, self.y_got]
-
-    def third(self, deps=()):
-        self.near, far = add_split([self.out00, self.x_got, self.y_got], deps)
+            out11, self.out10, self.out01, self.out00 = quarters
+            self.first = [swap(out11, first_axis)]
+
+    def second(self, deps=(), long=False):
+        if self.first_axis is None:
+            self.out10 = add_into(self.out10, self.first[0], 0, deps)
+            self.out01 = add_into(self.out01, self.first[1], 1, deps)
+        elif self.first_axis == "x":
+            self.out01 = add_low(self.out01, self.first[0], deps, long)
+        else:
+            self.out10 = add_low(self.out10, self.first[0], deps, long)
+        self.next = [swap(self.out10, "x"), swap(self.out01, "y")]
+
+    def third(self, deps=(), long=False):
+        self.near, far = add_split([self.out00] + self.next, deps, long)
         self.got = swap_z(far, 1)
 
-    def fourth(self, deps=()):
-        self.near, far = add_split([self.near, self.got], deps)
+    def fourth(self, deps=(), long=False):
+        self.near, far = add_split([self.near, self.got], deps, long)
         self.got = swap_z(far, 2)
 
-    def total(self):
-        return scatter_groups(self.near + self.got.astype(F32), 0)
+    def finish(self, **how):
+        self.total = scatter_groups(add_split([self.near, self.got], whole_sum=True, **how)[0], 0)
 
 
 def pair(own):
@@ -473,6 +491,14 @@
         target[:, k * size : (k + 1) * size] = part.astype(target.dtype)
 
 
+def swap_all(arrays):
+    return [swap(array, "c") for array in arrays]
+
+
+def both_cores(own_ref, low_ref, high_ref):
+    return own_ref[...] + jnp.concatenate([low_ref[...], high_ref[...]], axis=0).astype(F32)
+
+
 def inverse_rms(values):
     return lax.rsqrt(jnp.mean(values * values, axis=-1, keepdims=True) + EPSILON)
 
@@ -485,7 +511,7 @@
     return back, jnp.sum(grad * scaled, axis=0, keepdims=True)
 
 
-def rowwise(kernel, inputs, outputs, scratch=(), deps=()):
+def rowwise(kernel, inputs, outputs, scratch=(), deps=(), long=False):
     return call(
         kernel,
         (1,),
@@ -494,7 +520,7 @@
         outputs,
         [whole_out(shape) for shape, _ in outputs],
         scratch_shapes=[pltpu.VMEM(shape, dtype) for shape, dtype in scratch],
-        deps=deps,
+        deps=deps, long=long,
     )
 
 
@@ -525,37 +551,37 @@
 
 
 def add_norm(info, rows, both, gain):
-    own, other = both
+    own, *others = both
 
     def kernel(info_ref, row_ref, own_ref, got_ref, gain_ref, hidden_ref, norm_ref):
         hidden = row_ref[...].astype(F32) + (own_ref[...] + got_ref[...].astype(F32))
         hidden_ref[...] = hidden
         norm_ref[...] = (hidden * inverse_rms(hidden) * gain_ref[...]).astype(BF)
 
-    return rowwise(kernel, [info, rows, own, swap(other, "c"), gain], [(rows.shape, F32), (rows.shape, BF)])
+    return rowwise(kernel, [info, rows, own, *swap_all(others), gain], [(rows.shape, F32), (rows.shape, BF)])
 
 
 def add_out(info, hidden, both):
-    own, other = both
+    own, *others = both
     rows, width = hidden.shape
     half = rows // 2
 
-    def kernel(info_ref, hidden_ref, own_ref, got_ref, keep_ref, send_ref, scratch):
+    def kernel(info_ref, hidden_ref, own_ref, low_ref, high_ref, keep_ref, send_ref, scratch):
         y = info_ref[2]
-        scratch[...] = hidden_ref[...] + (own_ref[...] + got_ref[...].astype(F32))
+        scratch[...] = hidden_ref[...] + (both_cores(own_ref, low_ref, high_ref))
         reorder_out(info_ref, scratch, keep_ref, pl.ds(pl.multiple_of(y * half, half), half))
         reorder_out(info_ref, scratch, send_ref, pl.ds(pl.multiple_of((1 - y) * half, half), half))
 
     return rowwise(
         kernel,
-        [info, hidden, own, swap(other, "c")],
+        [info, hidden, own, *swap_all(others)],
         [((half, width), BF)] * 2,
         [((rows, width), F32)],
     )
 
 
 def step_state(info, state, both, gate, gain):
-    own, other = both
+    own, *others = both
 
     def kernel(info_ref, state_ref, own_ref, got_ref, gate_ref, gain_ref, next_ref, norm_ref, update_ref):
         update = own_ref[...] + got_ref[...].astype(F32)
@@ -566,13 +592,13 @@
 
     return rowwise(
         kernel,
-        [info, state, own, swap(other, "c"), gate, gain],
+        [info, state, own, *swap_all(others), gate, gain],
         [(state.shape, F32), (state.shape, BF), (state.shape, F32)],
     )
 
 
 def last_state(info, state, both, gate):
-    own, other = both
+    own, *others = both
 
     def kernel(info_ref, state_ref, own_ref, got_ref, gate_ref, final_ref, update_ref, scratch):
         update = own_ref[...] + got_ref[...].astype(F32)
@@ -582,17 +608,17 @@
 
     return rowwise(
         kernel,
-        [info, state, own, swap(other, "c"), gate],
+        [info, state, own, *swap_all(others), gate],
         [(state.shape, BF), (state.shape, F32)],
         [(state.shape, F32)],
     )
 
 
 def back_hidden(info, hidden, both, gain, dy):
-    own, other = both
-
-    def kernel(info_ref, hidden_ref, own_ref, got_ref, gain_ref, dy_ref, grad_ref, branch_ref, gain_grad_ref):
-        grad = own_ref[...] + got_ref[...].astype(F32)
+    own, *others = both
+
+    def kernel(info_ref, hidden_ref, own_ref, low_ref, high_ref, gain_ref, dy_ref, grad_ref, branch_ref, gain_grad_ref):
+        grad = both_cores(own_ref, low_ref, high_ref)
         back, gain_grad_ref[...] = rms_back(hidden_ref[...], gain_ref[...], grad)
         total = dy_ref[...].astype(F32) + back
         grad_ref[...] = total
@@ -600,7 +626,7 @@
 
     return rowwise(
         kernel,
-        [info, hidden, own, swap(other, "c"), gain, dy],
+        [info, hidden, own, *swap_all(others), gain, dy],
         [(hidden.shape, F32), (hidden.shape, BF), ((1, hidden.shape[1]), F32)],
     )
 
@@ -613,11 +639,11 @@
 
 
 def back_state(info, grad, state, update, both, gate, gain):
-    own, other = both
+    own, *others = both
     width = state.shape[1]
 
     def kernel(
-        info_ref, grad_ref, state_ref, update_ref, own_ref, got_ref, gate_ref, gain_ref, out_ref, low_ref, gain_grad_ref, gate_grad_ref
+        info_ref, grad_ref, state_ref, update_ref, own_ref, low_ref, high_ref, gate_ref, gain_ref, out_ref, next_ref, gain_grad_ref, gate_grad_ref
     ):
         gate_open = gate_ref[...]
         grad_now = grad_ref[...].astype(F32)
@@ -625,26 +651,26 @@
         gate_grad_ref[...] = jnp.sum(grad_now * (values - update_ref[...]), axis=0, keepdims=True) * (
             gate_open * (1.0 - gate_open)
         )
-        back, gain_grad_ref[...] = rms_back(values, gain_ref[...], own_ref[...] + got_ref[...].astype(F32))
+        back, gain_grad_ref[...] = rms_back(values, gain_ref[...], both_cores(own_ref, low_ref, high_ref))
         total = gate_open * grad_now + back
         out_ref[...] = total
-        low_ref[...] = ((1.0 - gate_open) * total).astype(BF)
+        next_ref[...] = ((1.0 - gate_open) * total).astype(BF)
 
     return rowwise(
         kernel,
-        [info, grad, state, update, own, swap(other, "c"), gate, gain],
+        [info, grad, state, update, own, *swap_all(others), gate, gain],
         [(state.shape, F32), (state.shape, BF), ((1, width), F32), ((1, width), F32)],
     )
 
 
 def back_input(info, values, both, gain, grad_hidden):
-    own, other = both
+    own, *others = both
     rows, width = values.shape
     half = rows // 2
 
-    def kernel(info_ref, value_ref, own_ref, got_ref, gain_ref, grad_ref, keep_ref, send_ref, gain_grad_ref, scratch):
+    def kernel(info_ref, value_ref, own_ref, low_ref, high_ref, gain_ref, grad_ref, keep_ref, send_ref, gain_grad_ref, scratch):
         y = info_ref[2]
-        grad = own_ref[...] + got_ref[...].astype(F32)
+        grad = both_cores(own_ref, low_ref, high_ref)
         back, gain_grad_ref[...] = rms_back(value_ref[...].astype(F32), gain_ref[...], grad)
         scratch[...] = grad_ref[...] + back
         reorder_out(info_ref, scratch, keep_ref, pl.ds(pl.multiple_of(y * half, half), half))
@@ -652,7 +678,7 @@
 
     return rowwise(
         kernel,
-        [info, values, own, swap(other, "c"), gain, grad_hidden],
+        [info, values, own, *swap_all(others), gain, grad_hidden],
         [((half, width), F32), ((half, width), BF), ((1, width), F32)],
         [((rows, width), F32)],
     )
@@ -897,7 +923,7 @@
     sums[place] = part if place not in sums else sums[place] + part
 
 
-def backward_tokens(b, blocks, info, tokens, states, logs, grad_mixed, deps=()):
+def backward_tokens(b, blocks, info, tokens, states, logs, grad_mixed, deps=(), long=False):
     lanes = tokens.shape[2] // 3
     heads = lanes // HEAD_DIM
     size = BLOCK // 2
@@ -959,10 +985,11 @@
         flops=10 * pairs * HEAD_DIM,
         exps=pairs,
         deps=deps,
-    )
-
-
-def backward_states(b, blocks, info, tokens, states, logs, grad_mixed, token_sums, state_sums, deps=()):
+        long=long,
+    )
+
+
+def backward_states(b, blocks, info, tokens, states, logs, grad_mixed, token_sums, state_sums, deps=(), long=False):
     lanes = tokens.shape[2] // 3
     heads = lanes // HEAD_DIM
     size = BLOCK // 2
@@ -1020,6 +1047,7 @@
         flops=10 * pairs * HEAD_DIM,
         exps=pairs,
         deps=deps,
+        long=long,
     )
 
 
@@ -1127,10 +1155,11 @@
     hidden_norm = pair(hidden_own)
     activated, slope = project(*hidden_norm, w_up, 0, ff, ff // 2, activate=True)
 
-    quarters = outer([([dy_pair], [activated], 1)], ff // 2, share=2)
-    grad_up = project(*dy_pair, w_down, 0, ff, ff // 2, gate=slope)
-    both = merge([[grad_up]], w_up, 0)
-    ff_grad = Reduce(outer([([hidden_norm], [grad_up], 1)], ff // 2, share=2, into=quarters))
+    down_grad = Reduce(outer([([dy_pair], [activated], 1)], ff // 2, split=True))
+    grad_up = project(*dy_pair, w_down, 0, ff, ff // 2, gate=slope, long=True)
+    both = merge([[grad_up]], w_up, 0, halves=2)
+    up_grad = Reduce(outer([([hidden_norm], [grad_up], 1)], ff // 2, split=True))
+    down_grad.second()
     grad_hidden, branch, gain_hidden = back_hidden(info, hidden, both, gains[2], dy_rows)
     branch = pair(branch)
 
@@ -1141,21 +1170,21 @@
     update_all, flat_all, norm_all, state_grads = [], [], [], []
     sums = [None] * blocks
 
-    def tokens_back(b, deps=()):
+    def tokens_back(b, **how):
         state_proj, logs = kept[b][2], kept[b][3]
-        query_grads[b], *sums[b] = backward_tokens(b, blocks, info, token_proj, state_proj, logs, grad_mixed, deps)
-
-    def states_back(b, later, deps=()):
+        query_grads[b], *sums[b] = backward_tokens(b, blocks, info, token_proj, state_proj, logs, grad_mixed, **how)
+
+    def states_back(b, later, **how):
         state_before, state_norm, state_proj, logs, state_logs, state_flat, update = kept[b]
         own_sums, state_sums, *before_sums = sums[b]
         state_grad, pair_grads[b] = backward_states(
-            b, blocks, info, token_proj, state_proj, state_logs, grad_state_mixed, [own_sums] + later, state_sums, deps
+            b, blocks, info, token_proj, state_proj, state_logs, grad_state_mixed, [own_sums] + later, state_sums, **how
         )
         update_all.append(grad_update)
         flat_all.append(state_flat)
         norm_all.append(state_norm)
         state_grads.append(state_grad)
-        return merge([[state_grad]], w_mid, at_state), before_sums
+        return merge([[state_grad]], w_mid, at_state, halves=2), before_sums
 
     def state_step(b, both, grad_state):
         state_before, update = kept[b][0], kept[b][-1]
@@ -1169,14 +1198,13 @@
     last = blocks - 1
     tokens_back(last)
     both, later = states_back(last, [])
-    ff_grad.second()
     for b in range(last - 1, -1, -1):
         tokens_back(b)
+        if b == last - 1:
+            up_grad.second()
+            down_grad.third()
         grad_state, low = state_step(b + 1, both, grad_state)
         grad_update = pair(low)
-        if b == 0:
-            final_rows = after(final_rows)
-            final_far = swap(final_rows, "y")
         grad_state_mixed = project(*grad_update, w_mid, at_state_out, head, head)
         if b == 0:
             early_grad = Reduce(
@@ -1187,49 +1215,56 @@
                         ([grad_update] + update_all, [kept[0][5]] + flat_all, 1),
                     ],
                     vmem=28,
-                ),
-                by_x=True,
+                    split=True,
+                )
             )
-        both, later = states_back(b, later)
-
-    late_grad = Reduce(outer([([normed], pair_grads, blocks), (norm_all, state_grads, 1)], vmem=28), by_x=True)
-    token_both = merge([[query_grads[i], pair_grads[i]] for i in range(blocks)], w_token, 0, blocks=blocks)
+        both, later = states_back(b, later, long=b == 0)
+
+    down_grad.fourth()
+    token_both = merge([[query_grads[i], pair_grads[i]] for i in range(blocks)], w_token, 0, blocks=blocks, halves=2)
+    late_grad = Reduce(outer([([normed], pair_grads, blocks), (norm_all, state_grads, 1)], vmem=28, split=True))
+    up_grad.third()
+    early_grad.second()
+    down_grad.finish()
     grad_state, low = state_step(0, both, grad_state)
-    out_both = merge([[activated]], w_down, 0)
-    early_grad.second()
     keep, send, gain_token = back_input(info, x_rows, token_both, gains[0], grad_hidden)
     input_keep, input_got = after(keep), swap(after(send), "y")
     near, far = pack_small(info, grad_state, [[gain_token], gain_sums, [gain_hidden], gate_sums])
     far = swap(far, "x")
-    ff_grad.third()
+    up_grad.fourth()
+    late_grad.second()
+    out_both = merge([[activated]], w_down, 0, halves=2)
+    up_grad.finish()
+    early_grad.third()
     keep, send = add_out(info, hidden, out_both)
     output_got = swap(after(send), "y")
     output_keep = after(keep)
-    late_grad.second()
+    final_rows = after(final_rows)
+    final_far = swap(final_rows, "y")
+    early_grad.fourth()
+    late_grad.third()
     near, far = add_small(info, near, far)
     far = swap_z(far, 1)
-    early_grad.third()
-    ff_grad.fourth()
+    early_grad.finish()
+    late_grad.fourth()
     near, far = add_small(info, near, far)
     far = swap_z(far, 2)
-    final_state = place_state(info, final_rows, swap(final_rows, "c"), final_far, swap(final_far, "c"))[:, None]
-    early_grad.fourth()
     near = add_pair(info, near, far)
     if lax.axis_size("r") > 1:
         near = lax.psum_scatter(near, "r", scatter_dimension=1, tiled=True)
     far = swap(near, "y")
-    late_grad.third()
+    output = place_rows(info, output_keep, output_got)[:, None]
     near = add_pair(info, near, far)
     far = swap(near, "c")
-    output = place_rows(info, output_keep, output_got)[:, None]
+    final_state = place_state(info, final_rows, swap(final_rows, "c"), final_far, swap(final_far, "c"))[:, None]
     init_grad, grad_gains, grad_gate = place_small(info, near, far, state_half)
-    late_grad.fourth()
     input_grad = place_rows(info, input_keep, input_got)[:, None]
-    both = ff_grad.total()
-    grad_hidden_down, grad_hidden_up = both[:, :ff], both[:, ff:]
-    early = early_grad.total()
-    grad_token_output, grad_query, grad_state_output = [early[:, i * head : (i + 1) * head] for i in range(3)]
-    late = late_grad.total()
+    late_grad.finish()
+    grad_hidden_down, grad_hidden_up = down_grad.total, up_grad.total
+    grad_token_output, grad_query, grad_state_output = [
+        early_grad.total[:, i * head : (i + 1) * head] for i in range(3)
+    ]
+    late = late_grad.total
     grad_token_weights = jnp.stack([grad_query, late[:, :head], late[:, head : 2 * head]], axis=1)
     grad_state_weights = late[:, 2 * head :].reshape(-1, 3, head)
     return (

time: 489 us -> 458 us (0.937)
  waiting for transfers between devices: 198 us -> 168 us
  starting transfers between devices: 71.2 us -> 79.7 us
  local copies, waits for them, and re-layouts: 42.8 us -> 37.5 us
  Pallas kernels: 170 us -> 165 us
    ppermute x63 -> x72, waiting for transfers between devices: 129 us -> 105 us  [swap(): return lax.ppermute(array, axis, [(0, 1), (1, 0)])]
    ppermute x63 -> x72, starting transfers between devices: 45.8 us -> 54.6 us  [swap(): return lax.ppermute(array, axis, [(0, 1), (1, 0)])]
    ppermute x18 -> x20, waiting for transfers between devices: 68.3 us -> 63 us  [swap_z(): return lax.ppermute(array, 'z', [(i, i ^ bit) for i in range(RING)])]
    pallas_call x73 -> x81, Pallas kernels: 170 us -> 165 us  [call(): pl.pallas_call(run, grid=grid, in_specs=list(in_specs) + [pl.BlockSpec(me...]
    unnamed x245 -> x187, local copies, waits for them, and re-layouts: 35.9 us -> 31.3 us
    ppermute x18 -> x20, starting transfers between devices: 25.4 us -> 25.1 us  [swap_z(): return lax.ppermute(array, 'z', [(i, i ^ bit) for i in range(RING)])]
  transfers between devices with their start and end apart: 81 -> 92, of which waited for: 30 -> 35; matrix products, arithmetic and copies ran while one was open for 1% -> 1% of each run, Pallas kernels for 32% -> 35%
where the time goes in v5:
time: 458 us; the launch traced here: 454 us
  waiting for transfers between devices  168 us (37%)
  Pallas kernels  165 us (36%)
  starting transfers between devices  79.7 us (17%)
  local copies, waits for them, and re-layouts  37.5 us (8%)
    pallas_call x81, Pallas kernels, call(): pl.pallas_call(run, grid=grid, in_specs=list(in_specs) + [pl.BlockSpec(me...  165 us
    ppermute x72, waiting for transfers between devices, swap(): return lax.ppermute(array, axis, [(0, 1), (1, 0)])  105 us
    ppermute x20, waiting for transfers between devices, swap_z(): return lax.ppermute(array, 'z', [(i, i ^ bit) for i in range(RING)])  63 us
    ppermute x72, starting transfers between devices, swap(): return lax.ppermute(array, axis, [(0, 1), (1, 0)])  54.6 us
    unnamed x187, local copies, waits for them, and re-layouts  31.3 us
    ppermute x20, starting transfers between devices, swap_z(): return lax.ppermute(array, 'z', [(i, i ^ bit) for i in range(RING)])  25.1 us
  transfers between devices with their start and end apart: 92, of which 35 were waited for; matrix products, arithmetic and copies ran while one was open for 1% of the time, Pallas kernels for 35%

profile of v5, /device:TPU:0, one launch (start us, length us, event | category | flops | bytes accessed | tf_op | source)
XLA Modules:
  0.0 453.7 jit_solution(6384015359535683859)
XLA Ops:
  10.9 6.7 %collective-permute-done.2.refs_1_ = bf16[128,768]{1,0:T(8,128)(2,1)S(1)} collective-permute-done((bf16[128,768]{1,0:T(8,128)(2,1)S(1)}, bf16[128,768]{1,0:T(8,128)(2,1)S(1)}, u32[]{:S(2)}, u32[]{:S(2)}) %collective-permute-start.2) | collective-permute-done | bytes 196640 | tf_op jit(solution)/shard_map/ppermute | solution.py:28
  49.1 11.6 %collective-permute-done.22.refs_1_ = bf16[128,1280]{1,0:T(8,128)(2,1)S(1)} collective-permute-done((bf16[128,1280]{1,0:T(8,128)(2,1)S(1)}, bf16[128,1280]{1,0:T(8,128)(2,1)S(1)}, u32[]{:S(2)}, u32[]{:S(2)}) %collective-permute-start.22) | collective-permute-done | bytes 327712 | tf_op jit(solution)/shard_map/ppermute | solution.py:28
  68.2 5.3 %collective-permute-done.15.refs_3_.refs_2_ = bf16[256,1024]{1,0:T(8,128)(2,1)S(1)} collective-permute-done((bf16[256,1024]{1,0:T(8,128)(2,1)S(1)}, bf16[256,1024]{1,0:T(8,128)(2,1)S(1)}, u32[]{:S(2)}, u32[]{:S(2)}) %collective-permute-start.15) | collective-permute-done | bytes 524320 | tf_op jit(solution)/shard_map/ppermute | solution.py:28
  77.6 5.6 %shard_map.230.refs_4_.refs_1_ = bf16[2,1024,768]{2,1,0:T(8,128)(2,1)S(1)} custom-call(bf16[512,1024]{1,0:T(8,128)(2,1)S(1)} %shard_map.226.refs_3_.refs_0_.refs_4_, bf16[512,1024]{1,0:T(8,128)(2,1)S(1)} %collective-permute-done.7.refs_1_.refs_5_, bf16[256,768]{1,0:T(8,128)(2,1)S(1)} %shard_map.220.refs_2_.refs_4_, ...), custom_call_target="tpu_custom_call" | custom-call | flops 32212254 | bytes 83886 | tf_op jit(solution)/shard_map/pallas_call | solution.py:120
  118.6 5.1 %collective-permute-done.26.refs_9_.refs_4_.refs_3_ = bf16[256,1280]{1,0:T(8,128)(2,1)S(1)} collective-permute-done((bf16[256,1280]{1,0:T(8,128)(2,1)S(1)}, bf16[256,1280]{1,0:T(8,128)(2,1)S(1)}, u32[]{:S(2)}, u32[]{:S(2)}) %collective-permute-start.26) | collective-permute-done | bytes 655392 | tf_op jit(solution)/shard_map/ppermute | solution.py:24
  125.8 10.7 %collective-permute-done.24.refs_3_.refs_5_.refs_4_ = bf16[256,1280]{1,0:T(8,128)(2,1)S(1)} collective-permute-done((bf16[256,1280]{1,0:T(8,128)(2,1)S(1)}, bf16[256,1280]{1,0:T(8,128)(2,1)S(1)}, u32[]{:S(2)}, u32[]{:S(2)}) %collective-permute-start.24) | collective-permute-done | bytes 655392 | tf_op jit(solution)/shard_map/ppermute | solution.py:24
  138.5 5.3 %shard_map.238 = (bf16[2,512,256]{2,1,0:T(8,128)(2,1)S(1)}, f32[2,512,128]{2,1,0:T(8,128)S(1)}) custom-call(s32[19]{0:T(128)S(1)} %copy-done.71, bf16[2,1024,768]{2,1,0:T(8,128)(2,1)S(1)} %shard_map.230.refs_4_.refs_1_, bf16[2,512,768]{2,1,0:T(8,128)(2,1)S(1)} %shard_map.235.refs_2_, bf16[256,1280]{1,0:T(8,128)(2,1)S(1)} %collective-permute-done.24.refs_3_.refs_5_.refs_4_, ...), custom_call_target="tpu_custom_call" | custom-call | flops 9395240 | bytes 57672 | tf_op jit(solution)/shard_map/pallas_call | solution.py:120
  167.1 5.8 %shard_map.246 = (bf16[2,512,256]{2,1,0:T(8,128)(2,1)S(1)}, f32[2,512,128]{2,1,0:T(8,128)S(1)}) custom-call(s32[19]{0:T(128)S(1)} %copy-done.71, bf16[2,1024,768]{2,1,0:T(8,128)(2,1)S(1)} %shard_map.230.refs_4_.refs_1_, bf16[2,512,768]{2,1,0:T(8,128)(2,1)S(1)} %shard_map.243.refs_2_, bf16[256,1024]{1,0:T(8,128)(2,1)S(1)} %collective-permute-done.35.refs_3_.refs_4_, ...), custom_call_target="tpu_custom_call" | custom-call | flops 12079595 | bytes 57672 | tf_op jit(solution)/shard_map/pallas_call | solution.py:120
  187.2 9.0 %shard_map.250 = (bf16[2,1024,1024]{2,1,0:T(8,128)(2,1)S(1)}, bf16[2,1024,1024]{2,1,0:T(8,128)(2,1)S(1)}) custom-call(bf16[512,1024]{1,0:T(8,128)(2,1)S(1)} %get-tuple-element.139.refs_0_, bf16[512,1024]{1,0:T(8,128)(2,1)S(1)} %collective-permute-done.42.refs_1_, bf16[256,1280]{1,0:T(8,128)(2,1)S(1)} %shard_map.231.refs_1_.refs_2_, ...), custom_call_target="tpu_custom_call" | custom-call | flops 42949672 | bytes 157286 | tf_op jit(solution)/shard_map/pallas_call | solution.py:120
  198.2 5.4 %shard_map.251 = (bf16[256,1024]{1,0:T(8,128)(2,1)S(1)}, bf16[512,1024]{1,0:T(8,128)(2,1)S(1)}, bf16[512,1024]{1,0:T(8,128)(2,1)S(1)}, bf16[512,1024]{1,0:T(8,128)(2,1)S(1)}, bf16[256,1024]{1,0:T(8,128)(2,1)S(1)}) custom-call(bf16[512,1024]{1,0:T(8,128)(2,1)S(1)} %shard_map.240.refs_10_.refs_0_.refs_6_, ...), custom_call_target="tpu_custom_call" | custom-call | flops 42949672 | bytes 104857 | tf_op jit(solution)/shard_map/pallas_call | solution.py:120
  209.3 5.6 %shard_map.252.refs_0_.refs_2_ = bf16[2,1024,1024]{2,1,0:T(8,128)(2,1)S(1)} custom-call(bf16[512,1024]{1,0:T(8,128)(2,1)S(1)} %shard_map.240.refs_10_.refs_0_.refs_6_, bf16[512,1024]{1,0:T(8,128)(2,1)S(1)} %collective-permute-done.45.refs_1_, bf16[256,1024]{1,0:T(8,128)(2,1)S(1)} %shard_map.242.refs_12_.refs_2_.refs_1_, ...), custom_call_target="tpu_custom_call" | custom-call | flops 99999997952 | bytes 146800 | tf_op jit(solution)/shard_map/pallas_call | solution.py:120
  220.1 5.6 %shard_map.254 = (bf16[256,1024]{1,0:T(8,128)(2,1)S(1)}, bf16[512,1024]{1,0:T(8,128)(2,1)S(1)}, bf16[512,1024]{1,0:T(8,128)(2,1)S(1)}, bf16[512,1024]{1,0:T(8,128)(2,1)S(1)}, bf16[256,1024]{1,0:T(8,128)(2,1)S(1)}) custom-call(bf16[512,1024]{1,0:T(8,128)(2,1)S(1)} %get-tuple-element.139.refs_0_, bf16[512,1024]{1,0:T(8,128)(2,1)S(1)} %collective-permute-done.42.refs_1_, ...), custom_call_target="tpu_custom_call" | custom-call | flops 42949672 | bytes 104857 | tf_op jit(solution)/shard_map/pallas_call | solution.py:120
  233.8 11.4 %shard_map.259 = (bf16[2,512,256]{2,1,0:T(8,128)(2,1)S(1)}, f32[2,512,512]{2,1,0:T(8,128)S(1)}, f32[2,512,512]{2,1,0:T(8,128)S(1)}, f32[2,512,512]{2,1,0:T(8,128)S(1)}) custom-call(s32[19]{0:T(128)S(1)} %copy-done.71, bf16[2,1024,768]{2,1,0:T(8,128)(2,1)S(1)} %shard_map.230.refs_4_.refs_1_, bf16[2,512,768]{2,1,0:T(8,128)(2,1)S(1)} %shard_map.243.refs_2_, ...), custom_call_target="tpu_custom_call" | custom-call | flops 30198988 | bytes 131072 | tf_op jit(solution)/shard_map/pallas_call | solution.py:120
  245.2 9.4 %shard_map.260 = (bf16[2,512,768]{2,1,0:T(8,128)(2,1)S(1)}, bf16[2,512,512]{2,1,0:T(8,128)(2,1)S(1)}) custom-call(s32[19]{0:T(128)S(1)} %copy-done.71, bf16[2,1024,768]{2,1,0:T(8,128)(2,1)S(1)} %shard_map.230.refs_4_.refs_1_, bf16[2,512,768]{2,1,0:T(8,128)(2,1)S(1)} %shard_map.243.refs_2_, f32[2,512,128]{2,1,0:T(8,128)S(1)} %get-tuple-element.130.refs_10_.refs_3_, ...), custom_call_target="tpu_custom_call" | custom-call | flops 26843544 | bytes 125829 | tf_op jit(solution)/shard_map/pallas_call | solution.py:120
  256.5 8.7 %collective-permute-done.56.refs_1_ = bf16[256,1024]{1,0:T(8,128)(2,1)S(1)} collective-permute-done((bf16[256,1024]{1,0:T(8,128)(2,1)S(1)}, bf16[256,1024]{1,0:T(8,128)(2,1)S(1)}, u32[]{:S(2)}, u32[]{:S(2)}) %collective-permute-start.56) | collective-permute-done | bytes 524320 | tf_op jit(solution)/shard_map/ppermute | solution.py:24
  265.2 8.1 %shard_map.262 = (bf16[2,512,256]{2,1,0:T(8,128)(2,1)S(1)}, f32[2,512,512]{2,1,0:T(8,128)S(1)}, f32[2,512,512]{2,1,0:T(8,128)S(1)}) custom-call(s32[19]{0:T(128)S(1)} %copy-done.71, bf16[2,1024,768]{2,1,0:T(8,128)(2,1)S(1)} %shard_map.230.refs_4_.refs_1_, bf16[2,512,768]{2,1,0:T(8,128)(2,1)S(1)} %shard_map.235.refs_2_, ...), custom_call_target="tpu_custom_call" | custom-call | flops 23488102 | bytes 110101 | tf_op jit(solution)/shard_map/pallas_call | solution.py:120
  297.2 9.2 %shard_map.269 = (bf16[2,512,768]{2,1,0:T(8,128)(2,1)S(1)}, bf16[2,512,512]{2,1,0:T(8,128)(2,1)S(1)}) custom-call(s32[19]{0:T(128)S(1)} %copy-done.71, bf16[2,1024,768]{2,1,0:T(8,128)(2,1)S(1)} %shard_map.230.refs_4_.refs_1_, bf16[2,512,768]{2,1,0:T(8,128)(2,1)S(1)} %shard_map.235.refs_2_, f32[2,512,128]{2,1,0:T(8,128)S(1)} %copy-done.69, ...), custom_call_target="tpu_custom_call" | custom-call | flops 99999997952 | bytes 146801 | tf_op jit(solution)/shard_map/pallas_call | solution.py:120
  315.3 5.6 %shard_map.273 = (bf16[256,1280]{1,0:T(8,128)(2,1)S(1)}, bf16[512,1280]{1,0:T(8,128)(2,1)S(1)}, bf16[512,1280]{1,0:T(8,128)(2,1)S(1)}, bf16[512,1280]{1,0:T(8,128)(2,1)S(1)}, bf16[256,1280]{1,0:T(8,128)(2,1)S(1)}) custom-call(bf16[512,1024]{1,0:T(8,128)(2,1)S(1)} %copy-done.3, bf16[512,1024]{1,0:T(8,128)(2,1)S(1)} %copy-done.11, ...), custom_call_target="tpu_custom_call" | custom-call | flops 53687092 | bytes 146800 | tf_op jit(solution)/shard_map/pallas_call | solution.py:120
  351.4 8.5 %collective-permute-done.75.refs_1_ = bf16[128,1024]{1,0:T(8,128)(2,1)S(1)} collective-permute-done((bf16[128,1024]{1,0:T(8,128)(2,1)S(1)}, bf16[128,1024]{1,0:T(8,128)(2,1)S(1)}, u32[]{:S(2)}, u32[]{:S(2)}) %collective-permute-start.75) | collective-permute-done | bytes 262176 | tf_op jit(solution)/shard_map/ppermute | solution.py:28
  361.3 30.0 %collective-permute-done.73.refs_1_ = bf16[512,768]{1,0:T(8,128)(2,1)S(1)} collective-permute-done((bf16[512,768]{1,0:T(8,128)(2,1)S(1)}, bf16[512,768]{1,0:T(8,128)(2,1)S(1)}, u32[]{:S(2)}, u32[]{:S(2)}) %collective-permute-start.73) | collective-permute-done | bytes 786464 | tf_op jit(solution)/shard_map/ppermute | solution.py:24
  394.6 7.1 %collective-permute-done.80.refs_1_ = bf16[256,768]{1,0:T(8,128)(2,1)S(1)} collective-permute-done((bf16[256,768]{1,0:T(8,128)(2,1)S(1)}, bf16[256,768]{1,0:T(8,128)(2,1)S(1)}, u32[]{:S(2)}, u32[]{:S(2)}) %collective-permute-start.80) | collective-permute-done | bytes 393248 | tf_op jit(solution)/shard_map/ppermute | solution.py:28
  412.0 6.1 %collective-permute-done.86.refs_3_ = bf16[256,1024]{1,0:T(8,128)(2,1)S(1)} collective-permute-done((bf16[256,1024]{1,0:T(8,128)(2,1)S(1)}, bf16[256,1024]{1,0:T(8,128)(2,1)S(1)}, u32[]{:S(2)}, u32[]{:S(2)}) %collective-permute-start.86) | collective-permute-done | bytes 524320 | tf_op jit(solution)/shard_map/ppermute | solution.py:24
  425.2 5.2 %collective-permute-done.84.refs_2_ = bf16[272,128]{1,0:T(8,128)(2,1)S(1)} collective-permute-done((bf16[272,128]{1,0:T(8,128)(2,1)S(1)}, bf16[272,128]{1,0:T(8,128)(2,1)S(1)}, u32[]{:S(2)}, u32[]{:S(2)}) %collective-permute-start.84) | collective-permute-done | bytes 69664 | tf_op jit(solution)/shard_map/ppermute | solution.py:28
  434.3 5.4 %collective-permute-done.88.refs_2_ = f32[272,128]{1,0:T(8,128)S(1)} collective-permute-done((f32[272,128]{1,0:T(8,128)S(1)}, f32[272,128]{1,0:T(8,128)S(1)}, u32[]{:S(2)}, u32[]{:S(2)}) %collective-permute-start.88) | collective-permute-done | bytes 139296 | tf_op jit(solution)/shard_map/ppermute | solution.py:24
  (447 shorter events, 254.9 us)
Async XLA Ops:
  40.0 36.0 %collective-permute-start.7 = (bf16[512,1024]{1,0:T(8,128)(2,1)S(1)}, bf16[512,1024]{1,0:T(8,128)(2,1)S(1)}, u32[]{:S(2)}, u32[]{:S(2)}) collective-permute-start(bf16[512,1024]{1,0:T(8,128)(2,1)S(1)} %shard_map.226.refs_3_.refs_0_.refs_4_), channel_id=1, source_target_pairs={{0,1},{1,0},{2,3},{3,2},{4,5},{5,4},{6,7},{7,6},{8,9},{9,8},{10,11... | collective-permute-start | bytes 3145736 | tf_op jit(solution)/shard_map/ppermute | solution.py:24
  63.0 24.2 %collective-permute-start.16 = (bf16[256,1024]{1,0:T(8,128)(2,1)S(1)}, bf16[256,1024]{1,0:T(8,128)(2,1)S(1)}, u32[]{:S(2)}, u32[]{:S(2)}) collective-permute-start(bf16[256,1024]{1,0:T(8,128)(2,1)S(1)} %shard_map.228.refs_2_.refs_1_), channel_id=1, source_target_pairs={{0,4},{4,0},{1,5},{5,1},{2,6},{6,2},{3,7},{7,3},{8,12},{12,8},{9,1... | collective-permute-start | bytes 1572872 | tf_op jit(solution)/shard_map/ppermute | solution.py:24
  93.2 30.5 %collective-permute-start.26 = (bf16[256,1280]{1,0:T(8,128)(2,1)S(1)}, bf16[256,1280]{1,0:T(8,128)(2,1)S(1)}, u32[]{:S(2)}, u32[]{:S(2)}) collective-permute-start(bf16[256,1280]{1,0:T(8,128)(2,1)S(1)} %shard_map.231.refs_1_.refs_2_), channel_id=1, source_target_pairs={{0,4},{4,0},{1,5},{5,1},{2,6},{6,2},{3,7},{7,3},{8,12},{12,8},{9,1... | collective-permute-start | bytes 1966088 | tf_op jit(solution)/shard_map/ppermute | solution.py:24
  98.5 25.3 %collective-permute-start.27 = (bf16[256,1280]{1,0:T(8,128)(2,1)S(1)}, bf16[256,1280]{1,0:T(8,128)(2,1)S(1)}, u32[]{:S(2)}, u32[]{:S(2)}) collective-permute-start(bf16[256,1280]{1,0:T(8,128)(2,1)S(1)} %shard_map.231.refs_1_.refs_2_), channel_id=1, source_target_pairs={{0,2},{2,0},{1,3},{3,1},{4,6},{6,4},{5,7},{7,5},{8,10},{10,8},{9,1... | collective-permute-start | bytes 1966088 | tf_op jit(solution)/shard_map/ppermute | solution.py:24
  103.8 32.7 %collective-permute-start.24 = (bf16[256,1280]{1,0:T(8,128)(2,1)S(1)}, bf16[256,1280]{1,0:T(8,128)(2,1)S(1)}, u32[]{:S(2)}, u32[]{:S(2)}) collective-permute-start(bf16[256,1280]{1,0:T(8,128)(2,1)S(1)} %collective-permute-done.23.refs_10_.refs_3_.refs_2_), channel_id=1, source_target_pairs={{0,4},{4,0},{1,5},{5,1},{2,6},{6,2},{3,7},{7,3},{8,12},{12,8},{9,1... | collective-permute-start | bytes 1966088 | tf_op jit(solution)/shard_map/ppermute | solution.py:24
  109.7 27.3 %collective-permute-start.25 = (bf16[256,1280]{1,0:T(8,128)(2,1)S(1)}, bf16[256,1280]{1,0:T(8,128)(2,1)S(1)}, u32[]{:S(2)}, u32[]{:S(2)}) collective-permute-start(bf16[256,1280]{1,0:T(8,128)(2,1)S(1)} %collective-permute-done.23.refs_10_.refs_3_.refs_2_), channel_id=1, source_target_pairs={{0,2},{2,0},{1,3},{3,1},{4,6},{6,4},{5,7},{7,5},{8,10},{10,8},{9,1... | collective-permute-start | bytes 1966088 | tf_op jit(solution)/shard_map/ppermute | solution.py:24
  228.5 46.8 %collective-permute-start.54 = (bf16[512,1024]{1,0:T(8,128)(2,1)S(1)}, bf16[512,1024]{1,0:T(8,128)(2,1)S(1)}, u32[]{:S(2)}, u32[]{:S(2)}) collective-permute-start(bf16[512,1024]{1,0:T(8,128)(2,1)S(1)} %shard_map.256.refs_7_), channel_id=1, source_target_pairs={{0,2},{2,0},{1,3},{3,1},{4,6},{6,4},{5,7},{7,5},{8,10},{10,8},{9,1... | collective-permute-start | bytes 3145736 | tf_op jit(solution)/shard_map/ppermute | solution.py:24
  229.9 45.5 %collective-permute-start.53 = (bf16[512,1024]{1,0:T(8,128)(2,1)S(1)}, bf16[512,1024]{1,0:T(8,128)(2,1)S(1)}, u32[]{:S(2)}, u32[]{:S(2)}) collective-permute-start(bf16[512,1024]{1,0:T(8,128)(2,1)S(1)} %shard_map.255.refs_2_), channel_id=1, source_target_pairs={{0,4},{4,0},{1,5},{5,1},{2,6},{6,2},{3,7},{7,3},{8,12},{12,8},{9,1... | collective-permute-start | bytes 3145736 | tf_op jit(solution)/shard_map/ppermute | solution.py:24
  230.4 34.8 %collective-permute-start.56 = (bf16[256,1024]{1,0:T(8,128)(2,1)S(1)}, bf16[256,1024]{1,0:T(8,128)(2,1)S(1)}, u32[]{:S(2)}, u32[]{:S(2)}) collective-permute-start(bf16[256,1024]{1,0:T(8,128)(2,1)S(1)} %get-tuple-element.150.refs_2_), channel_id=1, source_target_pairs={{0,2},{2,0},{1,3},{3,1},{4,6},{6,4},{5,7},{7,5},{8,10},{10,8},{9,1... | collective-permute-start | bytes 1572872 | tf_op jit(solution)/shard_map/ppermute | solution.py:24
  232.0 41.7 %collective-permute-start.55 = (bf16[256,1024]{1,0:T(8,128)(2,1)S(1)}, bf16[256,1024]{1,0:T(8,128)(2,1)S(1)}, u32[]{:S(2)}, u32[]{:S(2)}) collective-permute-start(bf16[256,1024]{1,0:T(8,128)(2,1)S(1)} %get-tuple-element.163), channel_id=1, source_target_pairs={{0,4},{4,0},{1,5},{5,1},{2,6},{6,2},{3,7},{7,3},{8,12},{12,8},{9,1... | collective-permute-start | bytes 1572872 | tf_op jit(solution)/shard_map/ppermute | solution.py:24
  279.7 31.5 %collective-permute-start.62 = (bf16[512,1024]{1,0:T(8,128)(2,1)S(1)}, bf16[512,1024]{1,0:T(8,128)(2,1)}, u32[]{:S(2)}, u32[]{:S(2)}) collective-permute-start(bf16[512,1024]{1,0:T(8,128)(2,1)S(1)} %shard_map.264.refs_3_), channel_id=1, source_target_pairs={{0,2},{2,0},{1,3},{3,1},{4,6},{6,4},{5,7},{7,5},{8,10},{10,8},{9,1... | collective-permute-start | bytes 3145736 | tf_op jit(solution)/shard_map/ppermute | solution.py:24
  281.1 30.2 %collective-permute-start.61 = (bf16[512,1024]{1,0:T(8,128)(2,1)S(1)}, bf16[512,1024]{1,0:T(8,128)(2,1)}, u32[]{:S(2)}, u32[]{:S(2)}) collective-permute-start(bf16[512,1024]{1,0:T(8,128)(2,1)S(1)} %shard_map.263.refs_2_), channel_id=1, source_target_pairs={{0,4},{4,0},{1,5},{5,1},{2,6},{6,2},{3,7},{7,3},{8,12},{12,8},{9,1... | collective-permute-start | bytes 3145736 | tf_op jit(solution)/shard_map/ppermute | solution.py:24
  281.6 26.7 %collective-permute-start.58 = (bf16[256,1024]{1,0:T(8,128)(2,1)}, bf16[256,1024]{1,0:T(8,128)(2,1)S(1)}, u32[]{:S(2)}, u32[]{:S(2)}) collective-permute-start(bf16[256,1024]{1,0:T(8,128)(2,1)} %get-tuple-element.175), channel_id=1, source_target_pairs={{0,8},{8,0},{16,24},{24,16},{1,9},{9,1},{17,25},{25,17},{2,10},{10... | collective-permute-start | bytes 1572872 | tf_op jit(solution)/shard_map/ppermute | solution.py:28
  289.3 36.3 %collective-permute-start.68 = (bf16[256,768]{1,0:T(8,128)(2,1)}, bf16[256,768]{1,0:T(8,128)(2,1)}, u32[]{:S(2)}, u32[]{:S(2)}) collective-permute-start(bf16[256,768]{1,0:T(8,128)(2,1)} %get-tuple-element.172.refs_8_), channel_id=1, source_target_pairs={{0,2},{2,0},{1,3},{3,1},{4,6},{6,4},{5,7},{7,5},{8,10},{10,8},{9,1... | collective-permute-start | bytes 1179656 | tf_op jit(solution)/shard_map/ppermute | solution.py:24
  290.9 37.1 %collective-permute-start.67 = (bf16[256,768]{1,0:T(8,128)(2,1)}, bf16[256,768]{1,0:T(8,128)(2,1)}, u32[]{:S(2)}, u32[]{:S(2)}) collective-permute-start(bf16[256,768]{1,0:T(8,128)(2,1)} %get-tuple-element.192), channel_id=1, source_target_pairs={{0,4},{4,0},{1,5},{5,1},{2,6},{6,2},{3,7},{7,3},{8,12},{12,8},{9,1... | collective-permute-start | bytes 1179656 | tf_op jit(solution)/shard_map/ppermute | solution.py:24
  334.9 25.1 %collective-permute-start.74 = (bf16[512,768]{1,0:T(8,128)(2,1)S(1)}, bf16[512,768]{1,0:T(8,128)(2,1)S(1)}, u32[]{:S(2)}, u32[]{:S(2)}) collective-permute-start(bf16[512,768]{1,0:T(8,128)(2,1)S(1)} %shard_map.276.refs_2_), channel_id=1, source_target_pairs={{0,2},{2,0},{1,3},{3,1},{4,6},{6,4},{5,7},{7,5},{8,10},{10,8},{9,1... | collective-permute-start | bytes 2359304 | tf_op jit(solution)/shard_map/ppermute | solution.py:24
  343.1 58.7 %collective-permute-start.79 = (bf16[512,1280]{1,0:T(8,128)(2,1)S(1)}, bf16[512,1280]{1,0:T(8,128)(2,1)S(1)}, u32[]{:S(2)}, u32[]{:S(2)}) collective-permute-start(bf16[512,1280]{1,0:T(8,128)(2,1)S(1)} %shard_map.283.refs_9_), channel_id=1, source_target_pairs={{0,2},{2,0},{1,3},{3,1},{4,6},{6,4},{5,7},{7,5},{8,10},{10,8},{9,1... | collective-permute-start | bytes 3932168 | tf_op jit(solution)/shard_map/ppermute | solution.py:24
  344.8 57.0 %collective-permute-start.78 = (bf16[512,1280]{1,0:T(8,128)(2,1)S(1)}, bf16[512,1280]{1,0:T(8,128)(2,1)S(1)}, u32[]{:S(2)}, u32[]{:S(2)}) collective-permute-start(bf16[512,1280]{1,0:T(8,128)(2,1)S(1)} %shard_map.282.refs_2_), channel_id=1, source_target_pairs={{0,4},{4,0},{1,5},{5,1},{2,6},{6,2},{3,7},{7,3},{8,12},{12,8},{9,1... | collective-permute-start | bytes 3932168 | tf_op jit(solution)/shard_map/ppermute | solution.py:24
  345.3 46.0 %collective-permute-start.73 = (bf16[512,768]{1,0:T(8,128)(2,1)S(1)}, bf16[512,768]{1,0:T(8,128)(2,1)S(1)}, u32[]{:S(2)}, u32[]{:S(2)}) collective-permute-start(bf16[512,768]{1,0:T(8,128)(2,1)S(1)} %shard_map.275.refs_2_), channel_id=1, source_target_pairs={{0,4},{4,0},{1,5},{5,1},{2,6},{6,2},{3,7},{7,3},{8,12},{12,8},{9,1... | collective-permute-start | bytes 2359304 | tf_op jit(solution)/shard_map/ppermute | solution.py:24
  360.0 33.3 %collective-permute-start.71 = (bf16[256,1024]{1,0:T(8,128)(2,1)S(1)}, bf16[256,1024]{1,0:T(8,128)(2,1)S(1)}, u32[]{:S(2)}, u32[]{:S(2)}) collective-permute-start(bf16[256,1024]{1,0:T(8,128)(2,1)S(1)} %get-tuple-element.205.refs_2_), channel_id=1, source_target_pairs={{0,1},{1,0},{2,3},{3,2},{4,5},{5,4},{6,7},{7,6},{8,9},{9,8},{10,11... | collective-permute-start | bytes 1572872 | tf_op jit(solution)/shard_map/ppermute | solution.py:24
  360.0 33.3 %collective-permute-start.72 = (bf16[256,1024]{1,0:T(8,128)(2,1)S(1)}, bf16[256,1024]{1,0:T(8,128)(2,1)S(1)}, u32[]{:S(2)}, u32[]{:S(2)}) collective-permute-start(bf16[256,1024]{1,0:T(8,128)(2,1)S(1)} %get-tuple-element.206), channel_id=1, source_target_pairs={{0,1},{1,0},{2,3},{3,2},{4,5},{5,4},{6,7},{7,6},{8,9},{9,8},{10,11... | collective-permute-start | bytes 1572872 | tf_op jit(solution)/shard_map/ppermute | solution.py:24
  405.2 26.4 %collective-permute-start.76 = (bf16[256,1024]{1,0:T(8,128)(2,1)S(1)}, bf16[256,1024]{1,0:T(8,128)(2,1)S(1)}, u32[]{:S(2)}, u32[]{:S(2)}) collective-permute-start(bf16[256,1024]{1,0:T(8,128)(2,1)S(1)} %get-tuple-element.211), channel_id=1, source_target_pairs={{0,2},{2,0},{1,3},{3,1},{4,6},{6,4},{5,7},{7,5},{8,10},{10,8},{9,1... | collective-permute-start | bytes 1572872 | tf_op jit(solution)/shard_map/ppermute | solution.py:24
  418.1 24.2 %collective-permute-start.85 = (bf16[256,1024]{1,0:T(8,128)(2,1)S(1)}, bf16[256,1024]{1,0:T(8,128)(2,1)S(1)}, u32[]{:S(2)}, u32[]{:S(2)}) collective-permute-start(bf16[256,1024]{1,0:T(8,128)(2,1)S(1)} %copy-done.35), channel_id=1, source_target_pairs={{0,1},{1,0},{2,3},{3,2},{4,5},{5,4},{6,7},{7,6},{8,9},{9,8},{10,11... | collective-permute-start | bytes 1572872 | tf_op jit(solution)/shard_map/ppermute | solution.py:24
  421.8 25.4 %collective-permute-start.89 = (bf16[256,1024]{1,0:T(8,128)(2,1)S(1)}, bf16[256,1024]{1,0:T(8,128)(2,1)S(1)}, u32[]{:S(2)}, u32[]{:S(2)}) collective-permute-start(bf16[256,1024]{1,0:T(8,128)(2,1)S(1)} %get-tuple-element.225), channel_id=1, source_target_pairs={{0,2},{2,0},{1,3},{3,1},{4,6},{6,4},{5,7},{7,5},{8,10},{10,8},{9,1... | collective-permute-start | bytes 1572872 | tf_op jit(solution)/shard_map/ppermute | solution.py:24
  (160 other events, 2014.0 us)

commit v6 on v5

--- a/solution.py
+++ b/solution.py
@@ -495,8 +495,8 @@
     return [swap(array, "c") for array in arrays]
 
 
-def both_cores(own_ref, low_ref, high_ref):
-    return own_ref[...] + jnp.concatenate([low_ref[...], high_ref[...]], axis=0).astype(F32)
+def both_cores(own_ref, *got_refs):
+    return own_ref[...] + jnp.concatenate([ref[...] for ref in got_refs], axis=0).astype(F32)
 
 
 def inverse_rms(values):
@@ -643,15 +643,17 @@
     width = state.shape[1]
 
     def kernel(
-        info_ref, grad_ref, state_ref, update_ref, own_ref, low_ref, high_ref, gate_ref, gain_ref, out_ref, next_ref, gain_grad_ref, gate_grad_ref
+        info_ref, grad_ref, state_ref, update_ref, own_ref, *refs
     ):
+        got_refs = refs[: len(others)]
+        gate_ref, gain_ref, out_ref, next_ref, gain_grad_ref, gate_grad_ref = refs[len(others) :]
         gate_open = gate_ref[...]
         grad_now = grad_ref[...].astype(F32)
         values = state_ref[...]
         gate_grad_ref[...] = jnp.sum(grad_now * (values - update_ref[...]), axis=0, keepdims=True) * (
             gate_open * (1.0 - gate_open)
         )
-        back, gain_grad_ref[...] = rms_back(values, gain_ref[...], both_cores(own_ref, low_ref, high_ref))
+        back, gain_grad_ref[...] = rms_back(values, gain_ref[...], both_cores(own_ref, *got_refs))
         total = gate_open * grad_now + back
         out_ref[...] = total
         next_ref[...] = ((1.0 - gate_open) * total).astype(BF)
@@ -698,23 +700,28 @@
             parts.append(sum(ref[...] for ref in refs[place : place + count]))
             place += count
         tail = jnp.concatenate(parts + [jnp.zeros((pad, width), F32)], axis=0)
-        near_ref[:rows] = state_ref[:, :half]
-        near_ref[rows:] = tail[:, :half]
-        far_ref[:rows] = state_ref[:, half:].astype(BF)
-        far_ref[rows:] = tail[:, half:].astype(BF)
+        quarter = half // 2
+        for source, here in ((state_ref[...], slice(0, rows)), (tail, slice(rows, rows + SMALL))):
+            for x in range(2):
+                to = slice(x * quarter, (x + 1) * quarter)
+                near_ref[here, to] = source[:, 2 * x * quarter : (2 * x + 1) * quarter]
+                far_ref[here, to] = source[:, (2 * x + 1) * quarter : (2 * x + 2) * quarter].astype(BF)
 
     shape = (rows + SMALL, half)
     return rowwise(kernel, [info, states] + flat, [(shape, F32), (shape, BF)])
 
 
-def add_small(info, near, got):
+def add_small(info, near, got, groups=1):
     rows, width = near.shape
     half = width // 2
 
     def kernel(info_ref, near_ref, got_ref, near_out, far_out):
         total = near_ref[...] + got_ref[...].astype(F32)
-        near_out[...] = total[:, :half]
-        far_out[...] = total[:, half:].astype(BF)
+        size = half // groups
+        for g in range(groups):
+            to = slice(g * size, (g + 1) * size)
+            near_out[:, to] = total[:, 2 * g * size : (2 * g + 1) * size]
+            far_out[:, to] = total[:, (2 * g + 1) * size : (2 * g + 2) * size].astype(BF)
 
     return rowwise(kernel, [info, near, got], [((rows, half), F32), ((rows, half), BF)])
 
@@ -1184,7 +1191,7 @@
         flat_all.append(state_flat)
         norm_all.append(state_norm)
         state_grads.append(state_grad)
-        return merge([[state_grad]], w_mid, at_state, halves=2), before_sums
+        return merge([[state_grad]], w_mid, at_state, halves=1 if b else 2), before_sums
 
     def state_step(b, both, grad_state):
         state_before, update = kept[b][0], kept[b][-1]
@@ -1221,43 +1228,45 @@
         both, later = states_back(b, later, long=b == 0)
 
     down_grad.fourth()
-    token_both = merge([[query_grads[i], pair_grads[i]] for i in range(blocks)], w_token, 0, blocks=blocks, halves=2)
+    early_grad.second()
+    token_both = merge(
+        [[query_grads[i], pair_grads[i]] for i in range(blocks)], w_token, 0, blocks=blocks, halves=2
+    )
+    grad_state, low = state_step(0, both, grad_state)
     late_grad = Reduce(outer([([normed], pair_grads, blocks), (norm_all, state_grads, 1)], vmem=28, split=True))
-    up_grad.third()
-    early_grad.second()
-    down_grad.finish()
-    grad_state, low = state_step(0, both, grad_state)
     keep, send, gain_token = back_input(info, x_rows, token_both, gains[0], grad_hidden)
     input_keep, input_got = after(keep), swap(after(send), "y")
     near, far = pack_small(info, grad_state, [[gain_token], gain_sums, [gain_hidden], gate_sums])
-    far = swap(far, "x")
+    far = swap_z(far, 1)
+    up_grad.third()
+    down_grad.finish()
+    late_grad.second(early_grad.next)
+    out_both = merge([[activated]], w_down, 0, halves=2)
+    early_grad.third()
     up_grad.fourth()
-    late_grad.second()
-    out_both = merge([[activated]], w_down, 0, halves=2)
-    up_grad.finish()
-    early_grad.third()
+    near, far = add_small(info, near, far, 2)
+    far = swap_z(far, 2)
     keep, send = add_out(info, hidden, out_both)
     output_got = swap(after(send), "y")
     output_keep = after(keep)
     final_rows = after(final_rows)
     final_far = swap(final_rows, "y")
     early_grad.fourth()
+    up_grad.finish()
+    near, far = add_small(info, near, far)
+    far = swap(far, "x")
     late_grad.third()
-    near, far = add_small(info, near, far)
-    far = swap_z(far, 1)
-    early_grad.finish()
-    late_grad.fourth()
-    near, far = add_small(info, near, far)
-    far = swap_z(far, 2)
     near = add_pair(info, near, far)
     if lax.axis_size("r") > 1:
         near = lax.psum_scatter(near, "r", scatter_dimension=1, tiled=True)
     far = swap(near, "y")
-    output = place_rows(info, output_keep, output_got)[:, None]
+    early_grad.finish()
     near = add_pair(info, near, far)
     far = swap(near, "c")
+    late_grad.fourth()
+    init_grad, grad_gains, grad_gate = place_small(info, near, far, state_half)
+    output = place_rows(info, output_keep, output_got)[:, None]
     final_state = place_state(info, final_rows, swap(final_rows, "c"), final_far, swap(final_far, "c"))[:, None]
-    init_grad, grad_gains, grad_gate = place_small(info, near, far, state_half)
     input_grad = place_rows(info, input_keep, input_got)[:, None]
     late_grad.finish()
     grad_hidden_down, grad_hidden_up = down_grad.total, up_grad.total

time: 458 us -> 439 us (0.959)
  waiting for transfers between devices: 168 us -> 146 us
  starting transfers between devices: 79.7 us -> 86.2 us
    ppermute x72 -> x71, waiting for transfers between devices: 105 us -> 82.7 us  [swap(): return lax.ppermute(array, axis, [(0, 1), (1, 0)])]
    ppermute x20, starting transfers between devices: 25.1 us -> 30.4 us  [swap_z(): return lax.ppermute(array, 'z', [(i, i ^ bit) for i in range(RING)])]
    unnamed x187 -> x163, local copies, waits for them, and re-layouts: 31.3 us -> 29.1 us
    ppermute x72 -> x71, starting transfers between devices: 54.6 us -> 55.8 us  [swap(): return lax.ppermute(array, axis, [(0, 1), (1, 0)])]
  transfers between devices with their start and end apart: 92 -> 91, of which waited for: 35 -> 36; matrix products, arithmetic and copies ran while one was open for 1% -> 1% of each run, Pallas kernels for 35% -> 36%
where the time goes in v6:
time: 439 us; the launch traced here: 435 us
  Pallas kernels  163 us (37%)
  waiting for transfers between devices  146 us (33%)
  starting transfers between devices  86.2 us (20%)
  local copies, waits for them, and re-layouts  35.2 us (8%)
    pallas_call x81, Pallas kernels, call(): pl.pallas_call(run, grid=grid, in_specs=list(in_specs) + [pl.BlockSpec(me...  163 us
    ppermute x71, waiting for transfers between devices, swap(): return lax.ppermute(array, axis, [(0, 1), (1, 0)])  82.7 us
    ppermute x20, waiting for transfers between devices, swap_z(): return lax.ppermute(array, 'z', [(i, i ^ bit) for i in range(RING)])  63.6 us
    ppermute x71, starting transfers between devices, swap(): return lax.ppermute(array, axis, [(0, 1), (1, 0)])  55.8 us
    ppermute x20, starting transfers between devices, swap_z(): return lax.ppermute(array, 'z', [(i, i ^ bit) for i in range(RING)])  30.4 us
    unnamed x163, local copies, waits for them, and re-layouts  29.1 us
  transfers between devices with their start and end apart: 91, of which 36 were waited for; matrix products, arithmetic and copies ran while one was open for 1% of the time, Pallas kernels for 36%

profile of v6, /device:TPU:0, one launch (start us, length us, event | category | flops | bytes accessed | tf_op | source)
XLA Modules:
  0.0 434.6 jit_solution(18256973593574122689)
XLA Ops:
  10.9 6.7 %collective-permute-done.2.refs_1_ = bf16[128,768]{1,0:T(8,128)(2,1)S(1)} collective-permute-done((bf16[128,768]{1,0:T(8,128)(2,1)S(1)}, bf16[128,768]{1,0:T(8,128)(2,1)S(1)}, u32[]{:S(2)}, u32[]{:S(2)}) %collective-permute-start.2) | collective-permute-done | bytes 196640 | tf_op jit(solution)/shard_map/ppermute | solution.py:28
  49.1 11.7 %collective-permute-done.22.refs_1_ = bf16[128,1280]{1,0:T(8,128)(2,1)S(1)} collective-permute-done((bf16[128,1280]{1,0:T(8,128)(2,1)S(1)}, bf16[128,1280]{1,0:T(8,128)(2,1)S(1)}, u32[]{:S(2)}, u32[]{:S(2)}) %collective-permute-start.22) | collective-permute-done | bytes 327712 | tf_op jit(solution)/shard_map/ppermute | solution.py:28
  68.3 5.3 %collective-permute-done.15.refs_3_.refs_2_ = bf16[256,1024]{1,0:T(8,128)(2,1)S(1)} collective-permute-done((bf16[256,1024]{1,0:T(8,128)(2,1)S(1)}, bf16[256,1024]{1,0:T(8,128)(2,1)S(1)}, u32[]{:S(2)}, u32[]{:S(2)}) %collective-permute-start.15) | collective-permute-done | bytes 524320 | tf_op jit(solution)/shard_map/ppermute | solution.py:28
  77.5 5.6 %shard_map.230.refs_4_.refs_1_ = bf16[2,1024,768]{2,1,0:T(8,128)(2,1)S(1)} custom-call(bf16[512,1024]{1,0:T(8,128)(2,1)S(1)} %shard_map.226.refs_3_.refs_0_.refs_4_, bf16[512,1024]{1,0:T(8,128)(2,1)S(1)} %collective-permute-done.7.refs_1_.refs_5_, bf16[256,768]{1,0:T(8,128)(2,1)S(1)} %shard_map.220.refs_2_.refs_4_, ...), custom_call_target="tpu_custom_call" | custom-call | flops 32212254 | bytes 83886 | tf_op jit(solution)/shard_map/pallas_call | solution.py:120
  113.6 5.0 %shard_map.236 = (bf16[2,512,256]{2,1,0:T(8,128)(2,1)S(1)}, f32[2,512,128]{2,1,0:T(8,128)S(1)}) custom-call(s32[19]{0:T(128)S(1)} %copy-done.59, bf16[2,1024,768]{2,1,0:T(8,128)(2,1)S(1)} %shard_map.230.refs_4_.refs_1_, bf16[2,512,768]{2,1,0:T(8,128)(2,1)S(1)} %shard_map.235.refs_2_), custom_call_target="tpu_custom_call" | custom-call | flops 10737418 | bytes 57672 | tf_op jit(solution)/shard_map/pallas_call | solution.py:120
  125.8 10.7 %collective-permute-done.24.refs_3_.refs_5_.refs_4_ = bf16[256,1280]{1,0:T(8,128)(2,1)S(1)} collective-permute-done((bf16[256,1280]{1,0:T(8,128)(2,1)S(1)}, bf16[256,1280]{1,0:T(8,128)(2,1)S(1)}, u32[]{:S(2)}, u32[]{:S(2)}) %collective-permute-start.24) | collective-permute-done | bytes 655392 | tf_op jit(solution)/shard_map/ppermute | solution.py:24
  138.5 5.3 %shard_map.238 = (bf16[2,512,256]{2,1,0:T(8,128)(2,1)S(1)}, f32[2,512,128]{2,1,0:T(8,128)S(1)}) custom-call(s32[19]{0:T(128)S(1)} %copy-done.59, bf16[2,1024,768]{2,1,0:T(8,128)(2,1)S(1)} %shard_map.230.refs_4_.refs_1_, bf16[2,512,768]{2,1,0:T(8,128)(2,1)S(1)} %shard_map.235.refs_2_, bf16[256,1280]{1,0:T(8,128)(2,1)S(1)} %collective-permute-done.24.refs_3_.refs_5_.refs_4_, ...), custom_call_target="tpu_custom_call" | custom-call | flops 9395240 | bytes 57672 | tf_op jit(solution)/shard_map/pallas_call | solution.py:120
  149.8 5.2 %collective-permute-done.31.refs_10_.refs_8_.refs_7_ = bf16[256,1280]{1,0:T(8,128)(2,1)S(1)} collective-permute-done((bf16[256,1280]{1,0:T(8,128)(2,1)S(1)}, bf16[256,1280]{1,0:T(8,128)(2,1)S(1)}, u32[]{:S(2)}, u32[]{:S(2)}) %collective-permute-start.31) | collective-permute-done | bytes 655392 | tf_op jit(solution)/shard_map/ppermute | solution.py:24
  157.0 5.1 %shard_map.244 = (bf16[2,512,256]{2,1,0:T(8,128)(2,1)S(1)}, f32[2,512,128]{2,1,0:T(8,128)S(1)}) custom-call(s32[19]{0:T(128)S(1)} %copy-done.59, bf16[2,1024,768]{2,1,0:T(8,128)(2,1)S(1)} %shard_map.230.refs_4_.refs_1_, bf16[2,512,768]{2,1,0:T(8,128)(2,1)S(1)} %shard_map.243.refs_2_), custom_call_target="tpu_custom_call" | custom-call | flops 10737418 | bytes 57672 | tf_op jit(solution)/shard_map/pallas_call | solution.py:120
  167.0 5.8 %shard_map.246 = (bf16[2,512,256]{2,1,0:T(8,128)(2,1)S(1)}, f32[2,512,128]{2,1,0:T(8,128)S(1)}) custom-call(s32[19]{0:T(128)S(1)} %copy-done.59, bf16[2,1024,768]{2,1,0:T(8,128)(2,1)S(1)} %shard_map.230.refs_4_.refs_1_, bf16[2,512,768]{2,1,0:T(8,128)(2,1)S(1)} %shard_map.243.refs_2_, bf16[256,1024]{1,0:T(8,128)(2,1)S(1)} %collective-permute-done.35.refs_3_.refs_4_, ...), custom_call_target="tpu_custom_call" | custom-call | flops 12079595 | bytes 57672 | tf_op jit(solution)/shard_map/pallas_call | solution.py:120
  186.6 9.0 %shard_map.250 = (bf16[2,1024,1024]{2,1,0:T(8,128)(2,1)S(1)}, bf16[2,1024,1024]{2,1,0:T(8,128)(2,1)S(1)}) custom-call(bf16[512,1024]{1,0:T(8,128)(2,1)S(1)} %get-tuple-element.138.refs_0_, bf16[512,1024]{1,0:T(8,128)(2,1)S(1)} %collective-permute-done.42.refs_1_, bf16[256,1280]{1,0:T(8,128)(2,1)S(1)} %shard_map.231.refs_1_.refs_2_, ...), custom_call_target="tpu_custom_call" | custom-call | flops 42949672 | bytes 157286 | tf_op jit(solution)/shard_map/pallas_call | solution.py:120
  197.6 5.4 %shard_map.251 = (bf16[256,1024]{1,0:T(8,128)(2,1)S(1)}, bf16[512,1024]{1,0:T(8,128)(2,1)S(1)}, bf16[512,1024]{1,0:T(8,128)(2,1)S(1)}, bf16[512,1024]{1,0:T(8,128)(2,1)S(1)}, bf16[256,1024]{1,0:T(8,128)(2,1)S(1)}) custom-call(bf16[512,1024]{1,0:T(8,128)(2,1)S(1)} %shard_map.240.refs_10_.refs_0_.refs_6_, ...), custom_call_target="tpu_custom_call" | custom-call | flops 42949672 | bytes 104857 | tf_op jit(solution)/shard_map/pallas_call | solution.py:120
  207.4 5.6 %shard_map.252.refs_0_.refs_2_ = bf16[2,1024,1024]{2,1,0:T(8,128)(2,1)S(1)} custom-call(bf16[512,1024]{1,0:T(8,128)(2,1)S(1)} %shard_map.240.refs_10_.refs_0_.refs_6_, bf16[512,1024]{1,0:T(8,128)(2,1)S(1)} %collective-permute-done.45.refs_1_, bf16[256,1024]{1,0:T(8,128)(2,1)S(1)} %shard_map.242.refs_12_.refs_2_.refs_1_, ...), custom_call_target="tpu_custom_call" | custom-call | flops 99999997952 | bytes 146800 | tf_op jit(solution)/shard_map/pallas_call | solution.py:120
  219.8 6.2 %shard_map.254 = (bf16[256,1024]{1,0:T(8,128)(2,1)}, bf16[512,1024]{1,0:T(8,128)(2,1)S(1)}, bf16[512,1024]{1,0:T(8,128)(2,1)S(1)}, bf16[512,1024]{1,0:T(8,128)(2,1)S(1)}, bf16[256,1024]{1,0:T(8,128)(2,1)}) custom-call(bf16[512,1024]{1,0:T(8,128)(2,1)S(1)} %get-tuple-element.138.refs_0_, bf16[512,1024]{1,0:T(8,128)(2,1)S(1)} %collective-permute-done.42.refs_1_, ...), custom_call_target="tpu_custom_call" | custom-call | flops 42949672 | bytes 104857 | tf_op jit(solution)/shard_map/pallas_call | solution.py:120
  234.1 11.4 %shard_map.259 = (bf16[2,512,256]{2,1,0:T(8,128)(2,1)S(1)}, f32[2,512,512]{2,1,0:T(8,128)S(1)}, f32[2,512,512]{2,1,0:T(8,128)S(1)}, f32[2,512,512]{2,1,0:T(8,128)S(1)}) custom-call(s32[19]{0:T(128)S(1)} %copy-done.59, bf16[2,1024,768]{2,1,0:T(8,128)(2,1)S(1)} %shard_map.230.refs_4_.refs_1_, bf16[2,512,768]{2,1,0:T(8,128)(2,1)S(1)} %shard_map.243.refs_2_, ...), custom_call_target="tpu_custom_call" | custom-call | flops 30198988 | bytes 131072 | tf_op jit(solution)/shard_map/pallas_call | solution.py:120
  246.9 9.4 %shard_map.260 = (bf16[2,512,768]{2,1,0:T(8,128)(2,1)S(1)}, bf16[2,512,512]{2,1,0:T(8,128)(2,1)S(1)}) custom-call(s32[19]{0:T(128)S(1)} %copy-done.59, bf16[2,1024,768]{2,1,0:T(8,128)(2,1)S(1)} %shard_map.230.refs_4_.refs_1_, bf16[2,512,768]{2,1,0:T(8,128)(2,1)S(1)} %shard_map.243.refs_2_, f32[2,512,128]{2,1,0:T(8,128)S(1)} %get-tuple-element.129.refs_10_.refs_3_, ...), custom_call_target="tpu_custom_call" | custom-call | flops 26843544 | bytes 125829 | tf_op jit(solution)/shard_map/pallas_call | solution.py:120
  258.2 8.1 %shard_map.262 = (bf16[2,512,256]{2,1,0:T(8,128)(2,1)S(1)}, f32[2,512,512]{2,1,0:T(8,128)S(1)}, f32[2,512,512]{2,1,0:T(8,128)S(1)}) custom-call(s32[19]{0:T(128)S(1)} %copy-done.59, bf16[2,1024,768]{2,1,0:T(8,128)(2,1)S(1)} %shard_map.230.refs_4_.refs_1_, bf16[2,512,768]{2,1,0:T(8,128)(2,1)S(1)} %shard_map.235.refs_2_, ...), custom_call_target="tpu_custom_call" | custom-call | flops 23488102 | bytes 110101 | tf_op jit(solution)/shard_map/pallas_call | solution.py:120
  289.1 9.2 %shard_map.269 = (bf16[2,512,768]{2,1,0:T(8,128)(2,1)S(1)}, bf16[2,512,512]{2,1,0:T(8,128)(2,1)S(1)}) custom-call(s32[19]{0:T(128)S(1)} %copy-done.59, bf16[2,1024,768]{2,1,0:T(8,128)(2,1)S(1)} %shard_map.230.refs_4_.refs_1_, bf16[2,512,768]{2,1,0:T(8,128)(2,1)S(1)} %shard_map.235.refs_2_, f32[2,512,128]{2,1,0:T(8,128)S(1)} %copy-done.57, ...), custom_call_target="tpu_custom_call" | custom-call | flops 99999997952 | bytes 146801 | tf_op jit(solution)/shard_map/pallas_call | solution.py:120
  317.4 5.6 %shard_map.276 = (bf16[256,1280]{1,0:T(8,128)(2,1)S(1)}, bf16[512,1280]{1,0:T(8,128)(2,1)S(1)}, bf16[512,1280]{1,0:T(8,128)(2,1)S(1)}, bf16[512,1280]{1,0:T(8,128)(2,1)S(1)}, bf16[256,1280]{1,0:T(8,128)(2,1)}) custom-call(bf16[512,1024]{1,0:T(8,128)(2,1)S(1)} %copy-done.3, bf16[512,1024]{1,0:T(8,128)(2,1)S(1)} %copy-done.11, ...), custom_call_target="tpu_custom_call" | custom-call | flops 53687092 | bytes 146800 | tf_op jit(solution)/shard_map/pallas_call | solution.py:120
  331.9 7.0 %collective-permute-done.66.refs_1_ = bf16[128,1024]{1,0:T(8,128)(2,1)S(1)} collective-permute-done((bf16[128,1024]{1,0:T(8,128)(2,1)}, bf16[128,1024]{1,0:T(8,128)(2,1)S(1)}, u32[]{:S(2)}, u32[]{:S(2)}) %collective-permute-start.66) | collective-permute-done | bytes 262176 | tf_op jit(solution)/shard_map/ppermute | solution.py:28
  339.8 6.9 %collective-permute-done.65.refs_1_ = bf16[256,1280]{1,0:T(8,128)(2,1)S(1)} collective-permute-done((bf16[256,1280]{1,0:T(8,128)(2,1)S(1)}, bf16[256,1280]{1,0:T(8,128)(2,1)S(1)}, u32[]{:S(2)}, u32[]{:S(2)}) %collective-permute-start.65) | collective-permute-done | bytes 655392 | tf_op jit(solution)/shard_map/ppermute | solution.py:24
  360.9 8.7 %collective-permute-done.74.refs_1_ = bf16[256,1024]{1,0:T(8,128)(2,1)S(1)} collective-permute-done((bf16[256,1024]{1,0:T(8,128)(2,1)S(1)}, bf16[256,1024]{1,0:T(8,128)(2,1)S(1)}, u32[]{:S(2)}, u32[]{:S(2)}) %collective-permute-start.74) | collective-permute-done | bytes 524320 | tf_op jit(solution)/shard_map/ppermute | solution.py:28
  376.5 9.4 %collective-permute-done.78.refs_1_ = bf16[256,768]{1,0:T(8,128)(2,1)S(1)} collective-permute-done((bf16[256,768]{1,0:T(8,128)(2,1)S(1)}, bf16[256,768]{1,0:T(8,128)(2,1)S(1)}, u32[]{:S(2)}, u32[]{:S(2)}) %collective-permute-start.78) | collective-permute-done | bytes 393248 | tf_op jit(solution)/shard_map/ppermute | solution.py:28
  400.4 7.0 %collective-permute-done.87.refs_3_ = bf16[256,1024]{1,0:T(8,128)(2,1)S(1)} collective-permute-done((bf16[256,1024]{1,0:T(8,128)(2,1)S(1)}, bf16[256,1024]{1,0:T(8,128)(2,1)S(1)}, u32[]{:S(2)}, u32[]{:S(2)}) %collective-permute-start.87) | collective-permute-done | bytes 524320 | tf_op jit(solution)/shard_map/ppermute | solution.py:24
  (421 shorter events, 256.9 us)
Async XLA Ops:
  8.4 24.0 %collective-permute-start = (bf16[256,1024]{1,0:T(8,128)(2,1)}, bf16[256,1024]{1,0:T(8,128)(2,1)}, u32[]{:S(2)}, u32[]{:S(2)}) collective-permute-start(bf16[256,1024]{1,0:T(8,128)(2,1)} %get-tuple-element.254), channel_id=1, source_target_pairs={{0,2},{2,0},{1,3},{3,1},{4,6},{6,4},{5,7},{7,5},{8,10},{10,8},{9,1... | collective-permute-start | bytes 1572872 | tf_op jit(solution)/shard_map/ppermute | solution.py:24
  40.0 36.0 %collective-permute-start.7 = (bf16[512,1024]{1,0:T(8,128)(2,1)S(1)}, bf16[512,1024]{1,0:T(8,128)(2,1)S(1)}, u32[]{:S(2)}, u32[]{:S(2)}) collective-permute-start(bf16[512,1024]{1,0:T(8,128)(2,1)S(1)} %shard_map.226.refs_3_.refs_0_.refs_4_), channel_id=1, source_target_pairs={{0,1},{1,0},{2,3},{3,2},{4,5},{5,4},{6,7},{7,6},{8,9},{9,8},{10,11... | collective-permute-start | bytes 3145736 | tf_op jit(solution)/shard_map/ppermute | solution.py:24
  63.0 24.1 %collective-permute-start.16 = (bf16[256,1024]{1,0:T(8,128)(2,1)S(1)}, bf16[256,1024]{1,0:T(8,128)(2,1)S(1)}, u32[]{:S(2)}, u32[]{:S(2)}) collective-permute-start(bf16[256,1024]{1,0:T(8,128)(2,1)S(1)} %shard_map.228.refs_2_.refs_1_), channel_id=1, source_target_pairs={{0,4},{4,0},{1,5},{5,1},{2,6},{6,2},{3,7},{7,3},{8,12},{12,8},{9,1... | collective-permute-start | bytes 1572872 | tf_op jit(solution)/shard_map/ppermute | solution.py:24
  76.0 22.4 %collective-permute-start.17 = (bf16[256,1024]{1,0:T(8,128)(2,1)S(1)}, bf16[256,1024]{1,0:T(8,128)(2,1)S(1)}, u32[]{:S(2)}, u32[]{:S(2)}) collective-permute-start(bf16[256,1024]{1,0:T(8,128)(2,1)S(1)} %collective-permute-done.15.refs_3_.refs_2_), channel_id=1, source_target_pairs={{0,4},{4,0},{1,5},{5,1},{2,6},{6,2},{3,7},{7,3},{8,12},{12,8},{9,1... | collective-permute-start | bytes 1572872 | tf_op jit(solution)/shard_map/ppermute | solution.py:24
  93.4 30.2 %collective-permute-start.26 = (bf16[256,1280]{1,0:T(8,128)(2,1)S(1)}, bf16[256,1280]{1,0:T(8,128)(2,1)S(1)}, u32[]{:S(2)}, u32[]{:S(2)}) collective-permute-start(bf16[256,1280]{1,0:T(8,128)(2,1)S(1)} %shard_map.231.refs_1_.refs_2_), channel_id=1, source_target_pairs={{0,4},{4,0},{1,5},{5,1},{2,6},{6,2},{3,7},{7,3},{8,12},{12,8},{9,1... | collective-permute-start | bytes 1966088 | tf_op jit(solution)/shard_map/ppermute | solution.py:24
  98.4 25.3 %collective-permute-start.27 = (bf16[256,1280]{1,0:T(8,128)(2,1)S(1)}, bf16[256,1280]{1,0:T(8,128)(2,1)S(1)}, u32[]{:S(2)}, u32[]{:S(2)}) collective-permute-start(bf16[256,1280]{1,0:T(8,128)(2,1)S(1)} %shard_map.231.refs_1_.refs_2_), channel_id=1, source_target_pairs={{0,2},{2,0},{1,3},{3,1},{4,6},{6,4},{5,7},{7,5},{8,10},{10,8},{9,1... | collective-permute-start | bytes 1966088 | tf_op jit(solution)/shard_map/ppermute | solution.py:24
  103.7 32.9 %collective-permute-start.24 = (bf16[256,1280]{1,0:T(8,128)(2,1)S(1)}, bf16[256,1280]{1,0:T(8,128)(2,1)S(1)}, u32[]{:S(2)}, u32[]{:S(2)}) collective-permute-start(bf16[256,1280]{1,0:T(8,128)(2,1)S(1)} %collective-permute-done.23.refs_10_.refs_3_.refs_2_), channel_id=1, source_target_pairs={{0,4},{4,0},{1,5},{5,1},{2,6},{6,2},{3,7},{7,3},{8,12},{12,8},{9,1... | collective-permute-start | bytes 1966088 | tf_op jit(solution)/shard_map/ppermute | solution.py:24
  109.6 27.4 %collective-permute-start.25 = (bf16[256,1280]{1,0:T(8,128)(2,1)S(1)}, bf16[256,1280]{1,0:T(8,128)(2,1)S(1)}, u32[]{:S(2)}, u32[]{:S(2)}) collective-permute-start(bf16[256,1280]{1,0:T(8,128)(2,1)S(1)} %collective-permute-done.23.refs_10_.refs_3_.refs_2_), channel_id=1, source_target_pairs={{0,2},{2,0},{1,3},{3,1},{4,6},{6,4},{5,7},{7,5},{8,10},{10,8},{9,1... | collective-permute-start | bytes 1966088 | tf_op jit(solution)/shard_map/ppermute | solution.py:24
  203.0 22.9 %collective-permute-start.49 = (bf16[256,1024]{1,0:T(8,128)(2,1)S(1)}, bf16[256,1024]{1,0:T(8,128)(2,1)S(1)}, u32[]{:S(2)}, u32[]{:S(2)}) collective-permute-start(bf16[256,1024]{1,0:T(8,128)(2,1)S(1)} %get-tuple-element.142.refs_11_), channel_id=1, source_target_pairs={{0,2},{2,0},{1,3},{3,1},{4,6},{6,4},{5,7},{7,5},{8,10},{10,8},{9,1... | collective-permute-start | bytes 1572872 | tf_op jit(solution)/shard_map/ppermute | solution.py:24
  228.8 39.5 %collective-permute-start.53 = (bf16[512,1024]{1,0:T(8,128)(2,1)S(1)}, bf16[512,1024]{1,0:T(8,128)(2,1)S(1)}, u32[]{:S(2)}, u32[]{:S(2)}) collective-permute-start(bf16[512,1024]{1,0:T(8,128)(2,1)S(1)} %shard_map.256.refs_7_), channel_id=1, source_target_pairs={{0,2},{2,0},{1,3},{3,1},{4,6},{6,4},{5,7},{7,5},{8,10},{10,8},{9,1... | collective-permute-start | bytes 3145736 | tf_op jit(solution)/shard_map/ppermute | solution.py:24
  230.2 38.1 %collective-permute-start.52 = (bf16[512,1024]{1,0:T(8,128)(2,1)S(1)}, bf16[512,1024]{1,0:T(8,128)(2,1)S(1)}, u32[]{:S(2)}, u32[]{:S(2)}) collective-permute-start(bf16[512,1024]{1,0:T(8,128)(2,1)S(1)} %shard_map.255.refs_2_), channel_id=1, source_target_pairs={{0,4},{4,0},{1,5},{5,1},{2,6},{6,2},{3,7},{7,3},{8,12},{12,8},{9,1... | collective-permute-start | bytes 3145736 | tf_op jit(solution)/shard_map/ppermute | solution.py:24
  230.7 35.6 %collective-permute-start.55 = (bf16[256,1024]{1,0:T(8,128)(2,1)}, bf16[256,1024]{1,0:T(8,128)(2,1)S(1)}, u32[]{:S(2)}, u32[]{:S(2)}) collective-permute-start(bf16[256,1024]{1,0:T(8,128)(2,1)} %get-tuple-element.149.refs_2_), channel_id=1, source_target_pairs={{0,2},{2,0},{1,3},{3,1},{4,6},{6,4},{5,7},{7,5},{8,10},{10,8},{9,1... | collective-permute-start | bytes 1572872 | tf_op jit(solution)/shard_map/ppermute | solution.py:24
  232.4 34.4 %collective-permute-start.54 = (bf16[256,1024]{1,0:T(8,128)(2,1)}, bf16[256,1024]{1,0:T(8,128)(2,1)S(1)}, u32[]{:S(2)}, u32[]{:S(2)}) collective-permute-start(bf16[256,1024]{1,0:T(8,128)(2,1)} %get-tuple-element.161), channel_id=1, source_target_pairs={{0,4},{4,0},{1,5},{5,1},{2,6},{6,2},{3,7},{7,3},{8,12},{12,8},{9,1... | collective-permute-start | bytes 1572872 | tf_op jit(solution)/shard_map/ppermute | solution.py:24
  272.2 39.1 %collective-permute-start.68 = (bf16[512,1024]{1,0:T(8,128)(2,1)S(1)}, bf16[512,1024]{1,0:T(8,128)(2,1)}, u32[]{:S(2)}, u32[]{:S(2)}) collective-permute-start(bf16[512,1024]{1,0:T(8,128)(2,1)S(1)} %shard_map.264.refs_3_), channel_id=1, source_target_pairs={{0,2},{2,0},{1,3},{3,1},{4,6},{6,4},{5,7},{7,5},{8,10},{10,8},{9,1... | collective-permute-start | bytes 3145736 | tf_op jit(solution)/shard_map/ppermute | solution.py:24
  273.6 49.4 %collective-permute-start.67 = (bf16[512,1024]{1,0:T(8,128)(2,1)S(1)}, bf16[512,1024]{1,0:T(8,128)(2,1)}, u32[]{:S(2)}, u32[]{:S(2)}) collective-permute-start(bf16[512,1024]{1,0:T(8,128)(2,1)S(1)} %shard_map.263.refs_2_), channel_id=1, source_target_pairs={{0,4},{4,0},{1,5},{5,1},{2,6},{6,2},{3,7},{7,3},{8,12},{12,8},{9,1... | collective-permute-start | bytes 3145736 | tf_op jit(solution)/shard_map/ppermute | solution.py:24
  274.1 26.0 %collective-permute-start.61 = (bf16[256,1024]{1,0:T(8,128)(2,1)}, bf16[256,1024]{1,0:T(8,128)(2,1)S(1)}, u32[]{:S(2)}, u32[]{:S(2)}) collective-permute-start(bf16[256,1024]{1,0:T(8,128)(2,1)} %get-tuple-element.181), channel_id=1, source_target_pairs={{0,8},{8,0},{16,24},{24,16},{1,9},{9,1},{17,25},{25,17},{2,10},{10... | collective-permute-start | bytes 1572872 | tf_op jit(solution)/shard_map/ppermute | solution.py:28
  282.2 23.6 %collective-permute-start.60 = (bf16[256,768]{1,0:T(8,128)(2,1)S(1)}, bf16[256,768]{1,0:T(8,128)(2,1)S(1)}, u32[]{:S(2)}, u32[]{:S(2)}) collective-permute-start(bf16[256,768]{1,0:T(8,128)(2,1)S(1)} %get-tuple-element.170.refs_8_), channel_id=1, source_target_pairs={{0,2},{2,0},{1,3},{3,1},{4,6},{6,4},{5,7},{7,5},{8,10},{10,8},{9,1... | collective-permute-start | bytes 1179656 | tf_op jit(solution)/shard_map/ppermute | solution.py:24
  283.2 23.7 %collective-permute-start.59 = (bf16[256,768]{1,0:T(8,128)(2,1)S(1)}, bf16[256,768]{1,0:T(8,128)(2,1)S(1)}, u32[]{:S(2)}, u32[]{:S(2)}) collective-permute-start(bf16[256,768]{1,0:T(8,128)(2,1)S(1)} %get-tuple-element.179), channel_id=1, source_target_pairs={{0,4},{4,0},{1,5},{5,1},{2,6},{6,2},{3,7},{7,3},{8,12},{12,8},{9,1... | collective-permute-start | bytes 1179656 | tf_op jit(solution)/shard_map/ppermute | solution.py:24
  313.0 33.6 %collective-permute-start.64 = (bf16[512,768]{1,0:T(8,128)(2,1)S(1)}, bf16[512,768]{1,0:T(8,128)(2,1)S(1)}, u32[]{:S(2)}, u32[]{:S(2)}) collective-permute-start(bf16[512,768]{1,0:T(8,128)(2,1)S(1)} %shard_map.273.refs_12_), channel_id=1, source_target_pairs={{0,2},{2,0},{1,3},{3,1},{4,6},{6,4},{5,7},{7,5},{8,10},{10,8},{9,1... | collective-permute-start | bytes 2359304 | tf_op jit(solution)/shard_map/ppermute | solution.py:24
  314.4 32.3 %collective-permute-start.63 = (bf16[512,768]{1,0:T(8,128)(2,1)S(1)}, bf16[512,768]{1,0:T(8,128)(2,1)S(1)}, u32[]{:S(2)}, u32[]{:S(2)}) collective-permute-start(bf16[512,768]{1,0:T(8,128)(2,1)S(1)} %shard_map.272.refs_2_), channel_id=1, source_target_pairs={{0,4},{4,0},{1,5},{5,1},{2,6},{6,2},{3,7},{7,3},{8,12},{12,8},{9,1... | collective-permute-start | bytes 2359304 | tf_op jit(solution)/shard_map/ppermute | solution.py:24
  323.0 23.6 %collective-permute-start.65 = (bf16[256,1280]{1,0:T(8,128)(2,1)S(1)}, bf16[256,1280]{1,0:T(8,128)(2,1)S(1)}, u32[]{:S(2)}, u32[]{:S(2)}) collective-permute-start(bf16[256,1280]{1,0:T(8,128)(2,1)S(1)} %get-tuple-element.188.refs_7_), channel_id=1, source_target_pairs={{0,2},{2,0},{1,3},{3,1},{4,6},{6,4},{5,7},{7,5},{8,10},{10,8},{9,1... | collective-permute-start | bytes 1966088 | tf_op jit(solution)/shard_map/ppermute | solution.py:24
  324.5 23.8 %collective-permute-start.62 = (bf16[256,1280]{1,0:T(8,128)(2,1)}, bf16[256,1280]{1,0:T(8,128)(2,1)S(1)}, u32[]{:S(2)}, u32[]{:S(2)}) collective-permute-start(bf16[256,1280]{1,0:T(8,128)(2,1)} %get-tuple-element.186), channel_id=1, source_target_pairs={{0,4},{4,0},{1,5},{5,1},{2,6},{6,2},{3,7},{7,3},{8,12},{12,8},{9,1... | collective-permute-start | bytes 1966088 | tf_op jit(solution)/shard_map/ppermute | solution.py:24
  348.8 42.7 %collective-permute-start.81 = (bf16[512,1280]{1,0:T(8,128)(2,1)S(1)}, bf16[512,1280]{1,0:T(8,128)(2,1)S(1)}, u32[]{:S(2)}, u32[]{:S(2)}) collective-permute-start(bf16[512,1280]{1,0:T(8,128)(2,1)S(1)} %shard_map.282.refs_9_), channel_id=1, source_target_pairs={{0,2},{2,0},{1,3},{3,1},{4,6},{6,4},{5,7},{7,5},{8,10},{10,8},{9,1... | collective-permute-start | bytes 3932168 | tf_op jit(solution)/shard_map/ppermute | solution.py:24
  350.2 41.3 %collective-permute-start.80 = (bf16[512,1280]{1,0:T(8,128)(2,1)S(1)}, bf16[512,1280]{1,0:T(8,128)(2,1)S(1)}, u32[]{:S(2)}, u32[]{:S(2)}) collective-permute-start(bf16[512,1280]{1,0:T(8,128)(2,1)S(1)} %shard_map.281.refs_4_), channel_id=1, source_target_pairs={{0,4},{4,0},{1,5},{5,1},{2,6},{6,2},{3,7},{7,3},{8,12},{12,8},{9,1... | collective-permute-start | bytes 3932168 | tf_op jit(solution)/shard_map/ppermute | solution.py:24
  (147 other events, 1752.6 us)

commit v7 on v6

--- a/solution.py
+++ b/solution.py
@@ -550,7 +550,7 @@
     return rowwise(kernel, [info, values, gain], [(values.shape, BF)], deps=deps)[0]
 
 
-def add_norm(info, rows, both, gain):
+def add_norm(info, rows, both, gain, deps=()):
     own, *others = both
 
     def kernel(info_ref, row_ref, own_ref, got_ref, gain_ref, hidden_ref, norm_ref):
@@ -558,7 +558,7 @@
         hidden_ref[...] = hidden
         norm_ref[...] = (hidden * inverse_rms(hidden) * gain_ref[...]).astype(BF)
 
-    return rowwise(kernel, [info, rows, own, *swap_all(others), gain], [(rows.shape, F32), (rows.shape, BF)])
+    return rowwise(kernel, [info, rows, own, *swap_all(others), gain], [(rows.shape, F32), (rows.shape, BF)], deps=deps)
 
 
 def add_out(info, hidden, both):
@@ -963,18 +963,18 @@
                     add_part(sums[which], "state", grads[len(tiles) * size :])
             for which in range(2):
                 columns = slice(which * lanes + h * HEAD_DIM, which * lanes + (h + 1) * HEAD_DIM)
-                state_out_ref[0, :, columns] = sums[which]["state"]
+                state_out_ref[0, :, columns] = sums[which]["state"].astype(BF)
                 for j in range(2):
                     here = pl.ds(start(0, j), size)
-                    own_ref[0, here, columns] = sums[which][(b, j)]
+                    own_ref[0, here, columns] = sums[which][(b, j)].astype(BF)
                     if b > 0:
-                        before_ref[0][0, here, columns] = sums[which][(b - 1, j)]
+                        before_ref[0][0, here, columns] = sums[which][(b - 1, j)].astype(BF)
 
     pairs = int(token_pairs(b, heads, count_states))
-    outputs = [((2, BLOCK, lanes), BF), ((2, BLOCK, 2 * lanes), F32), ((2, count_states, 2 * lanes), F32)]
+    outputs = [((2, BLOCK, lanes), BF), ((2, BLOCK, 2 * lanes), BF), ((2, count_states, 2 * lanes), BF)]
     out_specs = [block_spec(BLOCK, lanes), block_spec(BLOCK, 2 * lanes), block_spec(count_states, 2 * lanes)]
     if b > 0:
-        outputs.append(((2, BLOCK, 2 * lanes), F32))
+        outputs.append(((2, BLOCK, 2 * lanes), BF))
         out_specs.append(block_spec(BLOCK, 2 * lanes))
     return call(
         kernel,
@@ -1028,11 +1028,11 @@
                 sums = [part if old is None else old + part for old, part in zip(sums, (dk, dv))]
             for which, to in ((0, key), (1, value)):
                 columns = slice(which * lanes + h * HEAD_DIM, which * lanes + (h + 1) * HEAD_DIM)
-                state_out_ref[0, :, to] = (sums[which][:count_states] + sum_ref[0, :, columns]).astype(BF)
+                state_out_ref[0, :, to] = (sums[which][:count_states] + sum_ref[0, :, columns].astype(F32)).astype(BF)
                 for j in range(2):
                     total = sums[which][count_states + j * size : count_states + (j + 1) * size]
                     for ref in token_sum_refs:
-                        total = total + ref[0, rows[j], columns]
+                        total = total + ref[0, rows[j], columns].astype(F32)
                     token_out_ref[0, rows[j], columns] = total.astype(BF)
 
     pairs = 2 * heads * count_states * (count_states + BLOCK)
@@ -1136,7 +1136,7 @@
     mixed = []
     for b in range(blocks):
         proj_wait, state_wait, merge_wait, token_wait = (
-            (up.ring, [], up.low + [down.got], up.high) if b == 0 else (up.far, [], down.ring, down.low)
+            (up.ring, [], up.low + [down.got], up.high) if b == 0 else ([], up.far, down.ring, down.low)
         )
         state_proj = project(*state_norm, w_mid, at_state, 3 * head, 3 * head, deps=proj_wait)
         state_flat, state_logs = forward_states(b, blocks, info, token_proj, state_proj, deps=state_wait)
@@ -1162,7 +1162,7 @@
     hidden_norm = pair(hidden_own)
     activated, slope = project(*hidden_norm, w_up, 0, ff, ff // 2, activate=True)
 
-    down_grad = Reduce(outer([([dy_pair], [activated], 1)], ff // 2, split=True))
+    down_grad = Reduce(outer([([dy_pair], [activated], 1)], ff // 2, split=True, long=True))
     grad_up = project(*dy_pair, w_down, 0, ff, ff // 2, gate=slope, long=True)
     both = merge([[grad_up]], w_up, 0, halves=2)
     up_grad = Reduce(outer([([hidden_norm], [grad_up], 1)], ff // 2, split=True))
@@ -1203,7 +1203,7 @@
         return grad_state, low
 
     last = blocks - 1
-    tokens_back(last)
+    tokens_back(last, long=True)
     both, later = states_back(last, [])
     for b in range(last - 1, -1, -1):
         tokens_back(b)
@@ -1241,8 +1241,8 @@
     up_grad.third()
     down_grad.finish()
     late_grad.second(early_grad.next)
+    early_grad.third()
     out_both = merge([[activated]], w_down, 0, halves=2)
-    early_grad.third()
     up_grad.fourth()
     near, far = add_small(info, near, far, 2)
     far = swap_z(far, 2)

time: 439 us -> 431 us (0.982)
  starting transfers between devices: 86.2 us -> 80.1 us
  waiting for transfers between devices: 146 us -> 152 us
  local copies, waits for them, and re-layouts: 35.2 us -> 30.4 us
    unnamed x163 -> x285, local copies, waits for them, and re-layouts: 29.1 us -> 24.3 us
  transfers between devices with their start and end apart: 91 -> 91, of which waited for: 36 -> 39; matrix products, arithmetic and copies ran while one was open for 1% -> 1% of each run, Pallas kernels for 36% -> 36%
where the time goes in v7:
time: 431 us; the launch traced here: 427 us
  Pallas kernels  161 us (37%)
  waiting for transfers between devices  152 us (35%)
  starting transfers between devices  80.1 us (19%)
  local copies, waits for them, and re-layouts  30.4 us (7%)
    pallas_call x81, Pallas kernels, call(): pl.pallas_call(run, grid=grid, in_specs=list(in_specs) + [pl.BlockSpec(me...  161 us
    ppermute x71, waiting for transfers between devices, swap(): return lax.ppermute(array, axis, [(0, 1), (1, 0)])  85.7 us
    ppermute x20, waiting for transfers between devices, swap_z(): return lax.ppermute(array, 'z', [(i, i ^ bit) for i in range(RING)])  66 us
    ppermute x71, starting transfers between devices, swap(): return lax.ppermute(array, axis, [(0, 1), (1, 0)])  53.2 us
    ppermute x20, starting transfers between devices, swap_z(): return lax.ppermute(array, 'z', [(i, i ^ bit) for i in range(RING)])  26.9 us
    unnamed x285, local copies, waits for them, and re-layouts  24.3 us
  transfers between devices with their start and end apart: 91, of which 39 were waited for; matrix products, arithmetic and copies ran while one was open for 1% of the time, Pallas kernels for 36%

profile of v7, /device:TPU:0, one launch (start us, length us, event | category | flops | bytes accessed | tf_op | source)
XLA Modules:
  0.0 426.8 jit_solution(9795109596352278361)
XLA Ops:
  10.9 6.7 %collective-permute-done.2.refs_1_ = bf16[128,768]{1,0:T(8,128)(2,1)S(1)} collective-permute-done((bf16[128,768]{1,0:T(8,128)(2,1)S(1)}, bf16[128,768]{1,0:T(8,128)(2,1)S(1)}, u32[]{:S(2)}, u32[]{:S(2)}) %collective-permute-start.2) | collective-permute-done | bytes 196640 | tf_op jit(solution)/shard_map/ppermute | solution.py:28
  49.1 11.7 %collective-permute-done.22.refs_1_ = bf16[128,1280]{1,0:T(8,128)(2,1)S(1)} collective-permute-done((bf16[128,1280]{1,0:T(8,128)(2,1)S(1)}, bf16[128,1280]{1,0:T(8,128)(2,1)S(1)}, u32[]{:S(2)}, u32[]{:S(2)}) %collective-permute-start.22) | collective-permute-done | bytes 327712 | tf_op jit(solution)/shard_map/ppermute | solution.py:28
  68.3 5.3 %collective-permute-done.15.refs_3_.refs_2_ = bf16[256,1024]{1,0:T(8,128)(2,1)S(1)} collective-permute-done((bf16[256,1024]{1,0:T(8,128)(2,1)S(1)}, bf16[256,1024]{1,0:T(8,128)(2,1)S(1)}, u32[]{:S(2)}, u32[]{:S(2)}) %collective-permute-start.15) | collective-permute-done | bytes 524320 | tf_op jit(solution)/shard_map/ppermute | solution.py:28
  77.5 5.8 %shard_map.230.refs_4_.refs_1_ = bf16[2,1024,768]{2,1,0:T(8,128)(2,1)S(1)} custom-call(bf16[512,1024]{1,0:T(8,128)(2,1)S(1)} %shard_map.226.refs_3_.refs_0_.refs_4_, bf16[512,1024]{1,0:T(8,128)(2,1)S(1)} %collective-permute-done.7.refs_1_.refs_5_, bf16[256,768]{1,0:T(8,128)(2,1)S(1)} %shard_map.220.refs_2_.refs_4_, ...), custom_call_target="tpu_custom_call" | custom-call | flops 32212254 | bytes 83886 | tf_op jit(solution)/shard_map/pallas_call | solution.py:120
  113.6 5.0 %shard_map.236 = (bf16[2,512,256]{2,1,0:T(8,128)(2,1)S(1)}, f32[2,512,128]{2,1,0:T(8,128)S(1)}) custom-call(s32[19]{0:T(128)S(1)} %copy-done.113, bf16[2,1024,768]{2,1,0:T(8,128)(2,1)S(1)} %shard_map.230.refs_4_.refs_1_, bf16[2,512,768]{2,1,0:T(8,128)(2,1)S(1)} %shard_map.235.refs_2_), custom_call_target="tpu_custom_call" | custom-call | flops 10737418 | bytes 57672 | tf_op jit(solution)/shard_map/pallas_call | solution.py:120
  125.8 10.7 %collective-permute-done.24.refs_3_.refs_5_.refs_4_ = bf16[256,1280]{1,0:T(8,128)(2,1)S(1)} collective-permute-done((bf16[256,1280]{1,0:T(8,128)(2,1)S(1)}, bf16[256,1280]{1,0:T(8,128)(2,1)S(1)}, u32[]{:S(2)}, u32[]{:S(2)}) %collective-permute-start.24) | collective-permute-done | bytes 655392 | tf_op jit(solution)/shard_map/ppermute | solution.py:24
  151.7 5.1 %collective-permute-done.35.refs_3_.refs_8_.refs_7_ = bf16[256,1280]{1,0:T(8,128)(2,1)S(1)} collective-permute-done((bf16[256,1280]{1,0:T(8,128)(2,1)S(1)}, bf16[256,1280]{1,0:T(8,128)(2,1)S(1)}, u32[]{:S(2)}, u32[]{:S(2)}) %collective-permute-start.35) | collective-permute-done | bytes 655392 | tf_op jit(solution)/shard_map/ppermute | solution.py:24
  156.8 5.0 %shard_map.244 = (bf16[2,512,256]{2,1,0:T(8,128)(2,1)S(1)}, f32[2,512,128]{2,1,0:T(8,128)S(1)}) custom-call(s32[19]{0:T(128)S(1)} %copy-done.113, bf16[2,1024,768]{2,1,0:T(8,128)(2,1)S(1)} %shard_map.230.refs_4_.refs_1_, bf16[2,512,768]{2,1,0:T(8,128)(2,1)S(1)} %shard_map.243.refs_2_, bf16[256,1280]{1,0:T(8,128)(2,1)S(1)} %collective-permute-done.35.refs_3_.refs_8_.refs_7_, ...), custom_call_target="tpu_custom_call" | custom-call | flops 10737418 | bytes 57672 | tf_op jit(solution)/shard_map/pallas_call | solution.py:120
  166.2 5.8 %shard_map.246 = (bf16[2,512,256]{2,1,0:T(8,128)(2,1)S(1)}, f32[2,512,128]{2,1,0:T(8,128)S(1)}) custom-call(s32[19]{0:T(128)S(1)} %copy-done.113, bf16[2,1024,768]{2,1,0:T(8,128)(2,1)S(1)} %shard_map.230.refs_4_.refs_1_, bf16[2,512,768]{2,1,0:T(8,128)(2,1)S(1)} %shard_map.243.refs_2_, bf16[256,1024]{1,0:T(8,128)(2,1)S(1)} %collective-permute-done.33.refs_3_.refs_4_, ...), custom_call_target="tpu_custom_call" | custom-call | flops 12079595 | bytes 57672 | tf_op jit(solution)/shard_map/pallas_call | solution.py:120
  186.8 9.0 %shard_map.250 = (bf16[2,1024,1024]{2,1,0:T(8,128)(2,1)S(1)}, bf16[2,1024,1024]{2,1,0:T(8,128)(2,1)S(1)}) custom-call(bf16[512,1024]{1,0:T(8,128)(2,1)S(1)} %get-tuple-element.138.refs_0_, bf16[512,1024]{1,0:T(8,128)(2,1)S(1)} %collective-permute-done.42.refs_1_, bf16[256,1280]{1,0:T(8,128)(2,1)S(1)} %shard_map.231.refs_1_.refs_2_, ...), custom_call_target="tpu_custom_call" | custom-call | flops 42949672 | bytes 157286 | tf_op jit(solution)/shard_map/pallas_call | solution.py:120
  195.9 5.4 %shard_map.251 = (bf16[256,1024]{1,0:T(8,128)(2,1)S(1)}, bf16[512,1024]{1,0:T(8,128)(2,1)S(1)}, bf16[512,1024]{1,0:T(8,128)(2,1)S(1)}, bf16[512,1024]{1,0:T(8,128)(2,1)S(1)}, bf16[256,1024]{1,0:T(8,128)(2,1)S(1)}) custom-call(bf16[512,1024]{1,0:T(8,128)(2,1)S(1)} %shard_map.240.refs_10_.refs_0_.refs_6_, ...), custom_call_target="tpu_custom_call" | custom-call | flops 99999997952 | bytes 104857 | tf_op jit(solution)/shard_map/pallas_call | solution.py:120
  203.4 5.7 %shard_map.252.refs_0_.refs_2_ = bf16[2,1024,1024]{2,1,0:T(8,128)(2,1)S(1)} custom-call(bf16[512,1024]{1,0:T(8,128)(2,1)S(1)} %shard_map.240.refs_10_.refs_0_.refs_6_, bf16[512,1024]{1,0:T(8,128)(2,1)S(1)} %collective-permute-done.45.refs_1_, bf16[256,1024]{1,0:T(8,128)(2,1)S(1)} %shard_map.242.refs_10_.refs_2_.refs_1_, ...), custom_call_target="tpu_custom_call" | custom-call | flops 99999997952 | bytes 146800 | tf_op jit(solution)/shard_map/pallas_call | solution.py:120
  214.9 5.7 %shard_map.254 = (bf16[256,1024]{1,0:T(8,128)(2,1)S(1)}, bf16[512,1024]{1,0:T(8,128)(2,1)S(1)}, bf16[512,1024]{1,0:T(8,128)(2,1)S(1)}, bf16[512,1024]{1,0:T(8,128)(2,1)S(1)}, bf16[256,1024]{1,0:T(8,128)(2,1)S(1)}) custom-call(bf16[512,1024]{1,0:T(8,128)(2,1)S(1)} %copy-done.51, bf16[512,1024]{1,0:T(8,128)(2,1)S(1)} %copy-done.53, ...), custom_call_target="tpu_custom_call" | custom-call | flops 42949672 | bytes 104857 | tf_op jit(solution)/shard_map/pallas_call | solution.py:120
  230.2 11.3 %shard_map.259 = (bf16[2,512,256]{2,1,0:T(8,128)(2,1)S(1)}, bf16[2,512,512]{2,1,0:T(8,128)(2,1)S(1)}, bf16[2,512,512]{2,1,0:T(8,128)(2,1)S(1)}, bf16[2,512,512]{2,1,0:T(8,128)(2,1)S(1)}) custom-call(s32[19]{0:T(128)S(1)} %copy-done.114, bf16[2,1024,768]{2,1,0:T(8,128)(2,1)S(1)} %copy-done.3, bf16[2,512,768]{2,1,0:T(8,128)(2,1)S(1)} %copy-done.25, ...), custom_call_target="tpu_custom_call" | custom-call | flops 99999997952 | bytes 99615 | tf_op jit(solution)/shard_map/pallas_call | solution.py:120
  241.6 9.1 %shard_map.260 = (bf16[2,512,768]{2,1,0:T(8,128)(2,1)S(1)}, bf16[2,512,512]{2,1,0:T(8,128)(2,1)S(1)}) custom-call(s32[19]{0:T(128)S(1)} %copy-done.114, bf16[2,1024,768]{2,1,0:T(8,128)(2,1)S(1)} %copy-done.3, bf16[2,512,768]{2,1,0:T(8,128)(2,1)S(1)} %copy-done.25, f32[2,512,128]{2,1,0:T(8,128)S(1)} %copy-done.76, bf16[2,512,256]{2,1,0:T(8,128)(2,1)S(1)} %copy-done.45, ...), custom_call_target="tpu_custom_call" | custom-call | flops 26843544 | bytes 104858 | tf_op jit(solution)/shard_map/pallas_call | solution.py:120
  252.8 8.0 %shard_map.262 = (bf16[2,512,256]{2,1,0:T(8,128)(2,1)S(1)}, bf16[2,512,512]{2,1,0:T(8,128)(2,1)S(1)}, bf16[2,512,512]{2,1,0:T(8,128)(2,1)S(1)}) custom-call(s32[19]{0:T(128)S(1)} %copy-done.114, bf16[2,1024,768]{2,1,0:T(8,128)(2,1)S(1)} %copy-done.3, bf16[2,512,768]{2,1,0:T(8,128)(2,1)S(1)} %copy-done.27, f32[2,512,128]{2,1,0:T(8,128)S(1)} %copy-done.79, ...), custom_call_target="tpu_custom_call" | custom-call | flops 23488102 | bytes 89129 | tf_op jit(solution)/shard_map/pallas_call | solution.py:120
  282.4 9.4 %shard_map.269 = (bf16[2,512,768]{2,1,0:T(8,128)(2,1)S(1)}, bf16[2,512,512]{2,1,0:T(8,128)(2,1)S(1)}) custom-call(s32[19]{0:T(128)S(1)} %copy-done.114, bf16[2,1024,768]{2,1,0:T(8,128)(2,1)S(1)} %copy-done.3, bf16[2,512,768]{2,1,0:T(8,128)(2,1)S(1)} %copy-done.27, f32[2,512,128]{2,1,0:T(8,128)S(1)} %copy-done.111, ...), custom_call_target="tpu_custom_call" | custom-call | flops 99999997952 | bytes 115344 | tf_op jit(solution)/shard_map/pallas_call | solution.py:120
  293.7 5.5 %collective-permute-done.57.refs_1_ = bf16[256,768]{1,0:T(8,128)(2,1)S(1)} collective-permute-done((bf16[256,768]{1,0:T(8,128)(2,1)S(1)}, bf16[256,768]{1,0:T(8,128)(2,1)S(1)}, u32[]{:S(2)}, u32[]{:S(2)}) %collective-permute-start.57) | collective-permute-done | bytes 393248 | tf_op jit(solution)/shard_map/ppermute | solution.py:24
  310.7 5.6 %shard_map.276 = (bf16[256,1280]{1,0:T(8,128)(2,1)S(1)}, bf16[512,1280]{1,0:T(8,128)(2,1)S(1)}, bf16[512,1280]{1,0:T(8,128)(2,1)S(1)}, bf16[512,1280]{1,0:T(8,128)(2,1)S(1)}, bf16[256,1280]{1,0:T(8,128)(2,1)S(1)}) custom-call(bf16[512,1024]{1,0:T(8,128)(2,1)S(1)} %copy-done.21, bf16[512,1024]{1,0:T(8,128)(2,1)S(1)} %copy-done.33, ...), custom_call_target="tpu_custom_call" | custom-call | flops 53687092 | bytes 146800 | tf_op jit(solution)/shard_map/pallas_call | solution.py:120
  322.6 9.5 %collective-permute-done.66.refs_1_ = bf16[128,1024]{1,0:T(8,128)(2,1)S(1)} collective-permute-done((bf16[128,1024]{1,0:T(8,128)(2,1)S(1)}, bf16[128,1024]{1,0:T(8,128)(2,1)S(1)}, u32[]{:S(2)}, u32[]{:S(2)}) %collective-permute-start.66) | collective-permute-done | bytes 262176 | tf_op jit(solution)/shard_map/ppermute | solution.py:28
  333.0 7.1 %collective-permute-done.65.refs_1_ = bf16[256,1280]{1,0:T(8,128)(2,1)S(1)} collective-permute-done((bf16[256,1280]{1,0:T(8,128)(2,1)S(1)}, bf16[256,1280]{1,0:T(8,128)(2,1)S(1)}, u32[]{:S(2)}, u32[]{:S(2)}) %collective-permute-start.65) | collective-permute-done | bytes 655392 | tf_op jit(solution)/shard_map/ppermute | solution.py:24
  354.0 8.9 %collective-permute-done.74.refs_1_ = bf16[256,1024]{1,0:T(8,128)(2,1)S(1)} collective-permute-done((bf16[256,1024]{1,0:T(8,128)(2,1)S(1)}, bf16[256,1024]{1,0:T(8,128)(2,1)S(1)}, u32[]{:S(2)}, u32[]{:S(2)}) %collective-permute-start.74) | collective-permute-done | bytes 524320 | tf_op jit(solution)/shard_map/ppermute | solution.py:28
  369.3 9.1 %collective-permute-done.78.refs_1_ = bf16[256,768]{1,0:T(8,128)(2,1)S(1)} collective-permute-done((bf16[256,768]{1,0:T(8,128)(2,1)S(1)}, bf16[256,768]{1,0:T(8,128)(2,1)S(1)}, u32[]{:S(2)}, u32[]{:S(2)}) %collective-permute-start.78) | collective-permute-done | bytes 393248 | tf_op jit(solution)/shard_map/ppermute | solution.py:28
  392.9 7.3 %collective-permute-done.87.refs_3_ = bf16[256,1024]{1,0:T(8,128)(2,1)S(1)} collective-permute-done((bf16[256,1024]{1,0:T(8,128)(2,1)S(1)}, bf16[256,1024]{1,0:T(8,128)(2,1)S(1)}, u32[]{:S(2)}, u32[]{:S(2)}) %collective-permute-start.87) | collective-permute-done | bytes 524320 | tf_op jit(solution)/shard_map/ppermute | solution.py:24
  (543 shorter events, 245.9 us)
Async XLA Ops:
  8.4 24.0 %collective-permute-start = (bf16[256,1024]{1,0:T(8,128)(2,1)}, bf16[256,1024]{1,0:T(8,128)(2,1)}, u32[]{:S(2)}, u32[]{:S(2)}) collective-permute-start(bf16[256,1024]{1,0:T(8,128)(2,1)} %get-tuple-element.254), channel_id=1, source_target_pairs={{0,2},{2,0},{1,3},{3,1},{4,6},{6,4},{5,7},{7,5},{8,10},{10,8},{9,1... | collective-permute-start | bytes 1572872 | tf_op jit(solution)/shard_map/ppermute | solution.py:24
  40.0 35.9 %collective-permute-start.7 = (bf16[512,1024]{1,0:T(8,128)(2,1)S(1)}, bf16[512,1024]{1,0:T(8,128)(2,1)S(1)}, u32[]{:S(2)}, u32[]{:S(2)}) collective-permute-start(bf16[512,1024]{1,0:T(8,128)(2,1)S(1)} %shard_map.226.refs_3_.refs_0_.refs_4_), channel_id=1, source_target_pairs={{0,1},{1,0},{2,3},{3,2},{4,5},{5,4},{6,7},{7,6},{8,9},{9,8},{10,11... | collective-permute-start | bytes 3145736 | tf_op jit(solution)/shard_map/ppermute | solution.py:24
  63.0 24.1 %collective-permute-start.16 = (bf16[256,1024]{1,0:T(8,128)(2,1)S(1)}, bf16[256,1024]{1,0:T(8,128)(2,1)S(1)}, u32[]{:S(2)}, u32[]{:S(2)}) collective-permute-start(bf16[256,1024]{1,0:T(8,128)(2,1)S(1)} %shard_map.228.refs_2_.refs_1_), channel_id=1, source_target_pairs={{0,4},{4,0},{1,5},{5,1},{2,6},{6,2},{3,7},{7,3},{8,12},{12,8},{9,1... | collective-permute-start | bytes 1572872 | tf_op jit(solution)/shard_map/ppermute | solution.py:24
  76.0 22.4 %collective-permute-start.17 = (bf16[256,1024]{1,0:T(8,128)(2,1)S(1)}, bf16[256,1024]{1,0:T(8,128)(2,1)S(1)}, u32[]{:S(2)}, u32[]{:S(2)}) collective-permute-start(bf16[256,1024]{1,0:T(8,128)(2,1)S(1)} %collective-permute-done.15.refs_3_.refs_2_), channel_id=1, source_target_pairs={{0,4},{4,0},{1,5},{5,1},{2,6},{6,2},{3,7},{7,3},{8,12},{12,8},{9,1... | collective-permute-start | bytes 1572872 | tf_op jit(solution)/shard_map/ppermute | solution.py:24
  93.4 30.2 %collective-permute-start.26 = (bf16[256,1280]{1,0:T(8,128)(2,1)S(1)}, bf16[256,1280]{1,0:T(8,128)(2,1)S(1)}, u32[]{:S(2)}, u32[]{:S(2)}) collective-permute-start(bf16[256,1280]{1,0:T(8,128)(2,1)S(1)} %shard_map.231.refs_1_.refs_2_), channel_id=1, source_target_pairs={{0,4},{4,0},{1,5},{5,1},{2,6},{6,2},{3,7},{7,3},{8,12},{12,8},{9,1... | collective-permute-start | bytes 1966088 | tf_op jit(solution)/shard_map/ppermute | solution.py:24
  98.4 25.3 %collective-permute-start.27 = (bf16[256,1280]{1,0:T(8,128)(2,1)S(1)}, bf16[256,1280]{1,0:T(8,128)(2,1)S(1)}, u32[]{:S(2)}, u32[]{:S(2)}) collective-permute-start(bf16[256,1280]{1,0:T(8,128)(2,1)S(1)} %shard_map.231.refs_1_.refs_2_), channel_id=1, source_target_pairs={{0,2},{2,0},{1,3},{3,1},{4,6},{6,4},{5,7},{7,5},{8,10},{10,8},{9,1... | collective-permute-start | bytes 1966088 | tf_op jit(solution)/shard_map/ppermute | solution.py:24
  103.7 32.8 %collective-permute-start.24 = (bf16[256,1280]{1,0:T(8,128)(2,1)S(1)}, bf16[256,1280]{1,0:T(8,128)(2,1)S(1)}, u32[]{:S(2)}, u32[]{:S(2)}) collective-permute-start(bf16[256,1280]{1,0:T(8,128)(2,1)S(1)} %collective-permute-done.23.refs_10_.refs_3_.refs_2_), channel_id=1, source_target_pairs={{0,4},{4,0},{1,5},{5,1},{2,6},{6,2},{3,7},{7,3},{8,12},{12,8},{9,1... | collective-permute-start | bytes 1966088 | tf_op jit(solution)/shard_map/ppermute | solution.py:24
  109.6 27.4 %collective-permute-start.25 = (bf16[256,1280]{1,0:T(8,128)(2,1)S(1)}, bf16[256,1280]{1,0:T(8,128)(2,1)S(1)}, u32[]{:S(2)}, u32[]{:S(2)}) collective-permute-start(bf16[256,1280]{1,0:T(8,128)(2,1)S(1)} %collective-permute-done.23.refs_10_.refs_3_.refs_2_), channel_id=1, source_target_pairs={{0,2},{2,0},{1,3},{3,1},{4,6},{6,4},{5,7},{7,5},{8,10},{10,8},{9,1... | collective-permute-start | bytes 1966088 | tf_op jit(solution)/shard_map/ppermute | solution.py:24
  223.7 37.2 %collective-permute-start.55 = (bf16[256,1024]{1,0:T(8,128)(2,1)S(1)}, bf16[256,1024]{1,0:T(8,128)(2,1)S(1)}, u32[]{:S(2)}, u32[]{:S(2)}) collective-permute-start(bf16[256,1024]{1,0:T(8,128)(2,1)S(1)} %get-tuple-element.148.refs_2_), channel_id=1, source_target_pairs={{0,2},{2,0},{1,3},{3,1},{4,6},{6,4},{5,7},{7,5},{8,10},{10,8},{9,1... | collective-permute-start | bytes 1572872 | tf_op jit(solution)/shard_map/ppermute | solution.py:24
  224.4 36.9 %collective-permute-start.54 = (bf16[256,1024]{1,0:T(8,128)(2,1)S(1)}, bf16[256,1024]{1,0:T(8,128)(2,1)S(1)}, u32[]{:S(2)}, u32[]{:S(2)}) collective-permute-start(bf16[256,1024]{1,0:T(8,128)(2,1)S(1)} %get-tuple-element.162), channel_id=1, source_target_pairs={{0,4},{4,0},{1,5},{5,1},{2,6},{6,2},{3,7},{7,3},{8,12},{12,8},{9,1... | collective-permute-start | bytes 1572872 | tf_op jit(solution)/shard_map/ppermute | solution.py:24
  225.8 36.3 %collective-permute-start.53 = (bf16[512,1024]{1,0:T(8,128)(2,1)S(1)}, bf16[512,1024]{1,0:T(8,128)(2,1)S(1)}, u32[]{:S(2)}, u32[]{:S(2)}) collective-permute-start(bf16[512,1024]{1,0:T(8,128)(2,1)S(1)} %shard_map.256.refs_7_), channel_id=1, source_target_pairs={{0,2},{2,0},{1,3},{3,1},{4,6},{6,4},{5,7},{7,5},{8,10},{10,8},{9,1... | collective-permute-start | bytes 3145736 | tf_op jit(solution)/shard_map/ppermute | solution.py:24
  226.3 35.9 %collective-permute-start.52 = (bf16[512,1024]{1,0:T(8,128)(2,1)S(1)}, bf16[512,1024]{1,0:T(8,128)(2,1)S(1)}, u32[]{:S(2)}, u32[]{:S(2)}) collective-permute-start(bf16[512,1024]{1,0:T(8,128)(2,1)S(1)} %shard_map.255.refs_2_), channel_id=1, source_target_pairs={{0,4},{4,0},{1,5},{5,1},{2,6},{6,2},{3,7},{7,3},{8,12},{12,8},{9,1... | collective-permute-start | bytes 3145736 | tf_op jit(solution)/shard_map/ppermute | solution.py:24
  265.6 39.1 %collective-permute-start.68 = (bf16[512,1024]{1,0:T(8,128)(2,1)S(1)}, bf16[512,1024]{1,0:T(8,128)(2,1)S(1)}, u32[]{:S(2)}, u32[]{:S(2)}) collective-permute-start(bf16[512,1024]{1,0:T(8,128)(2,1)S(1)} %shard_map.264.refs_3_), channel_id=1, source_target_pairs={{0,2},{2,0},{1,3},{3,1},{4,6},{6,4},{5,7},{7,5},{8,10},{10,8},{9,1... | collective-permute-start | bytes 3145736 | tf_op jit(solution)/shard_map/ppermute | solution.py:24
  266.3 50.1 %collective-permute-start.67 = (bf16[512,1024]{1,0:T(8,128)(2,1)S(1)}, bf16[512,1024]{1,0:T(8,128)(2,1)S(1)}, u32[]{:S(2)}, u32[]{:S(2)}) collective-permute-start(bf16[512,1024]{1,0:T(8,128)(2,1)S(1)} %shard_map.263.refs_2_), channel_id=1, source_target_pairs={{0,4},{4,0},{1,5},{5,1},{2,6},{6,2},{3,7},{7,3},{8,12},{12,8},{9,1... | collective-permute-start | bytes 3145736 | tf_op jit(solution)/shard_map/ppermute | solution.py:24
  267.7 25.9 %collective-permute-start.58 = (bf16[256,1024]{1,0:T(8,128)(2,1)}, bf16[256,1024]{1,0:T(8,128)(2,1)S(1)}, u32[]{:S(2)}, u32[]{:S(2)}) collective-permute-start(bf16[256,1024]{1,0:T(8,128)(2,1)} %get-tuple-element.170), channel_id=1, source_target_pairs={{0,8},{8,0},{16,24},{24,16},{1,9},{9,1},{17,25},{25,17},{2,10},{10... | collective-permute-start | bytes 1572872 | tf_op jit(solution)/shard_map/ppermute | solution.py:28
  275.7 23.4 %collective-permute-start.57 = (bf16[256,768]{1,0:T(8,128)(2,1)S(1)}, bf16[256,768]{1,0:T(8,128)(2,1)S(1)}, u32[]{:S(2)}, u32[]{:S(2)}) collective-permute-start(bf16[256,768]{1,0:T(8,128)(2,1)S(1)} %get-tuple-element.169.refs_8_), channel_id=1, source_target_pairs={{0,2},{2,0},{1,3},{3,1},{4,6},{6,4},{5,7},{7,5},{8,10},{10,8},{9,1... | collective-permute-start | bytes 1179656 | tf_op jit(solution)/shard_map/ppermute | solution.py:24
  276.3 23.3 %collective-permute-start.60 = (bf16[256,768]{1,0:T(8,128)(2,1)S(1)}, bf16[256,768]{1,0:T(8,128)(2,1)S(1)}, u32[]{:S(2)}, u32[]{:S(2)}) collective-permute-start(bf16[256,768]{1,0:T(8,128)(2,1)S(1)} %get-tuple-element.179), channel_id=1, source_target_pairs={{0,4},{4,0},{1,5},{5,1},{2,6},{6,2},{3,7},{7,3},{8,12},{12,8},{9,1... | collective-permute-start | bytes 1179656 | tf_op jit(solution)/shard_map/ppermute | solution.py:24
  306.4 33.6 %collective-permute-start.61 = (bf16[512,768]{1,0:T(8,128)(2,1)S(1)}, bf16[512,768]{1,0:T(8,128)(2,1)S(1)}, u32[]{:S(2)}, u32[]{:S(2)}) collective-permute-start(bf16[512,768]{1,0:T(8,128)(2,1)S(1)} %shard_map.273.refs_12_), channel_id=1, source_target_pairs={{0,2},{2,0},{1,3},{3,1},{4,6},{6,4},{5,7},{7,5},{8,10},{10,8},{9,1... | collective-permute-start | bytes 2359304 | tf_op jit(solution)/shard_map/ppermute | solution.py:24
  307.1 33.0 %collective-permute-start.59 = (bf16[512,768]{1,0:T(8,128)(2,1)S(1)}, bf16[512,768]{1,0:T(8,128)(2,1)S(1)}, u32[]{:S(2)}, u32[]{:S(2)}) collective-permute-start(bf16[512,768]{1,0:T(8,128)(2,1)S(1)} %shard_map.272.refs_2_), channel_id=1, source_target_pairs={{0,4},{4,0},{1,5},{5,1},{2,6},{6,2},{3,7},{7,3},{8,12},{12,8},{9,1... | collective-permute-start | bytes 2359304 | tf_op jit(solution)/shard_map/ppermute | solution.py:24
  316.4 23.7 %collective-permute-start.65 = (bf16[256,1280]{1,0:T(8,128)(2,1)S(1)}, bf16[256,1280]{1,0:T(8,128)(2,1)S(1)}, u32[]{:S(2)}, u32[]{:S(2)}) collective-permute-start(bf16[256,1280]{1,0:T(8,128)(2,1)S(1)} %get-tuple-element.189.refs_7_), channel_id=1, source_target_pairs={{0,2},{2,0},{1,3},{3,1},{4,6},{6,4},{5,7},{7,5},{8,10},{10,8},{9,1... | collective-permute-start | bytes 1966088 | tf_op jit(solution)/shard_map/ppermute | solution.py:24
  317.1 24.5 %collective-permute-start.64 = (bf16[256,1280]{1,0:T(8,128)(2,1)S(1)}, bf16[256,1280]{1,0:T(8,128)(2,1)S(1)}, u32[]{:S(2)}, u32[]{:S(2)}) collective-permute-start(bf16[256,1280]{1,0:T(8,128)(2,1)S(1)} %get-tuple-element.187), channel_id=1, source_target_pairs={{0,4},{4,0},{1,5},{5,1},{2,6},{6,2},{3,7},{7,3},{8,12},{12,8},{9,1... | collective-permute-start | bytes 1966088 | tf_op jit(solution)/shard_map/ppermute | solution.py:24
  342.3 42.0 %collective-permute-start.81 = (bf16[512,1280]{1,0:T(8,128)(2,1)S(1)}, bf16[512,1280]{1,0:T(8,128)(2,1)S(1)}, u32[]{:S(2)}, u32[]{:S(2)}) collective-permute-start(bf16[512,1280]{1,0:T(8,128)(2,1)S(1)} %shard_map.282.refs_3_), channel_id=1, source_target_pairs={{0,2},{2,0},{1,3},{3,1},{4,6},{6,4},{5,7},{7,5},{8,10},{10,8},{9,1... | collective-permute-start | bytes 3932168 | tf_op jit(solution)/shard_map/ppermute | solution.py:24
  343.0 41.3 %collective-permute-start.80 = (bf16[512,1280]{1,0:T(8,128)(2,1)S(1)}, bf16[512,1280]{1,0:T(8,128)(2,1)S(1)}, u32[]{:S(2)}, u32[]{:S(2)}) collective-permute-start(bf16[512,1280]{1,0:T(8,128)(2,1)S(1)} %shard_map.281.refs_4_), channel_id=1, source_target_pairs={{0,4},{4,0},{1,5},{5,1},{2,6},{6,2},{3,7},{7,3},{8,12},{12,8},{9,1... | collective-permute-start | bytes 3932168 | tf_op jit(solution)/shard_map/ppermute | solution.py:24
  392.3 20.5 %collective-permute-start.75 = (bf16[256,1024]{1,0:T(8,128)(2,1)S(1)}, bf16[256,1024]{1,0:T(8,128)(2,1)S(1)}, u32[]{:S(2)}, u32[]{:S(2)}) collective-permute-start(bf16[256,1024]{1,0:T(8,128)(2,1)S(1)} %get-tuple-element.210), channel_id=1, source_target_pairs={{0,2},{2,0},{1,3},{3,1},{4,6},{6,4},{5,7},{7,5},{8,10},{10,8},{9,1... | collective-permute-start | bytes 1572872 | tf_op jit(solution)/shard_map/ppermute | solution.py:24
  (208 other events, 3185.7 us)

commit v8 on v7

--- a/solution.py
+++ b/solution.py
@@ -638,7 +638,7 @@
     return rowwise(kernel, [info, grad, gate], [(grad.shape, BF)])[0]
 
 
-def back_state(info, grad, state, update, both, gate, gain):
+def back_state(info, grad, state, update, both, gate, gain, long=False):
     own, *others = both
     width = state.shape[1]
 
@@ -662,6 +662,7 @@
         kernel,
         [info, grad, state, update, own, *swap_all(others), gate, gain],
         [(state.shape, F32), (state.shape, BF), ((1, width), F32), ((1, width), F32)],
+        long=long,
     )
 
 
@@ -1196,7 +1197,7 @@
     def state_step(b, both, grad_state):
         state_before, update = kept[b][0], kept[b][-1]
         grad_state, low, gain_sum, gate_sum = back_state(
-            info, grad_state, state_before, update, both, gate_open, gains[1]
+            info, grad_state, state_before, update, both, gate_open, gains[1], long=b > 0
         )
         gain_sums.append(gain_sum)
         gate_sums.append(gate_sum)

time: 431 us -> 432 us (level)
  transfers between devices with their start and end apart: 91 -> 91, of which waited for: 39 -> 38; matrix products, arithmetic and copies ran while one was open for 1% -> 1% of each run, Pallas kernels for 36% -> 36%
where the time goes in v8:
time: 432 us; the launch traced here: 427 us
  Pallas kernels  160 us (37%)
  waiting for transfers between devices  155 us (36%)
  starting transfers between devices  79.9 us (18%)
  local copies, waits for them, and re-layouts  28.2 us (7%)
    pallas_call x81, Pallas kernels, call(): pl.pallas_call(run, grid=grid, in_specs=list(in_specs) + [pl.BlockSpec(me...  160 us
    ppermute x71, waiting for transfers between devices, swap(): return lax.ppermute(array, axis, [(0, 1), (1, 0)])  89.3 us
    ppermute x20, waiting for transfers between devices, swap_z(): return lax.ppermute(array, 'z', [(i, i ^ bit) for i in range(RING)])  66.2 us
    ppermute x71, starting transfers between devices, swap(): return lax.ppermute(array, axis, [(0, 1), (1, 0)])  53 us
    ppermute x20, starting transfers between devices, swap_z(): return lax.ppermute(array, 'z', [(i, i ^ bit) for i in range(RING)])  26.8 us
    unnamed x285, local copies, waits for them, and re-layouts  22 us
  transfers between devices with their start and end apart: 91, of which 38 were waited for; matrix products, arithmetic and copies ran while one was open for 1% of the time, Pallas kernels for 36%

profile of v8, /device:TPU:0, one launch (start us, length us, event | category | flops | bytes accessed | tf_op | source)
XLA Modules:
  0.0 427.3 jit_solution(10229474726850732965)
XLA Ops:
  10.9 6.7 %collective-permute-done.2.refs_1_ = bf16[128,768]{1,0:T(8,128)(2,1)S(1)} collective-permute-done((bf16[128,768]{1,0:T(8,128)(2,1)S(1)}, bf16[128,768]{1,0:T(8,128)(2,1)S(1)}, u32[]{:S(2)}, u32[]{:S(2)}) %collective-permute-start.2) | collective-permute-done | bytes 196640 | tf_op jit(solution)/shard_map/ppermute | solution.py:28
  49.1 11.7 %collective-permute-done.22.refs_1_ = bf16[128,1280]{1,0:T(8,128)(2,1)S(1)} collective-permute-done((bf16[128,1280]{1,0:T(8,128)(2,1)S(1)}, bf16[128,1280]{1,0:T(8,128)(2,1)S(1)}, u32[]{:S(2)}, u32[]{:S(2)}) %collective-permute-start.22) | collective-permute-done | bytes 327712 | tf_op jit(solution)/shard_map/ppermute | solution.py:28
  68.3 5.3 %collective-permute-done.15.refs_3_.refs_2_ = bf16[256,1024]{1,0:T(8,128)(2,1)S(1)} collective-permute-done((bf16[256,1024]{1,0:T(8,128)(2,1)S(1)}, bf16[256,1024]{1,0:T(8,128)(2,1)S(1)}, u32[]{:S(2)}, u32[]{:S(2)}) %collective-permute-start.15) | collective-permute-done | bytes 524320 | tf_op jit(solution)/shard_map/ppermute | solution.py:28
  77.5 5.8 %shard_map.230.refs_4_.refs_1_ = bf16[2,1024,768]{2,1,0:T(8,128)(2,1)S(1)} custom-call(bf16[512,1024]{1,0:T(8,128)(2,1)S(1)} %shard_map.226.refs_3_.refs_0_.refs_4_, bf16[512,1024]{1,0:T(8,128)(2,1)S(1)} %collective-permute-done.7.refs_1_.refs_5_, bf16[256,768]{1,0:T(8,128)(2,1)S(1)} %shard_map.220.refs_2_.refs_4_, ...), custom_call_target="tpu_custom_call" | custom-call | flops 32212254 | bytes 83886 | tf_op jit(solution)/shard_map/pallas_call | solution.py:120
  114.4 5.0 %shard_map.236 = (bf16[2,512,256]{2,1,0:T(8,128)(2,1)S(1)}, f32[2,512,128]{2,1,0:T(8,128)S(1)}) custom-call(s32[19]{0:T(128)S(1)} %copy-done.117, bf16[2,1024,768]{2,1,0:T(8,128)(2,1)S(1)} %shard_map.230.refs_4_.refs_1_, bf16[2,512,768]{2,1,0:T(8,128)(2,1)S(1)} %shard_map.235.refs_2_), custom_call_target="tpu_custom_call" | custom-call | flops 10737418 | bytes 57672 | tf_op jit(solution)/shard_map/pallas_call | solution.py:120
  125.8 10.7 %collective-permute-done.24.refs_3_.refs_5_.refs_4_ = bf16[256,1280]{1,0:T(8,128)(2,1)S(1)} collective-permute-done((bf16[256,1280]{1,0:T(8,128)(2,1)S(1)}, bf16[256,1280]{1,0:T(8,128)(2,1)S(1)}, u32[]{:S(2)}, u32[]{:S(2)}) %collective-permute-start.24) | collective-permute-done | bytes 655392 | tf_op jit(solution)/shard_map/ppermute | solution.py:24
  151.7 5.1 %collective-permute-done.35.refs_3_.refs_8_.refs_7_ = bf16[256,1280]{1,0:T(8,128)(2,1)S(1)} collective-permute-done((bf16[256,1280]{1,0:T(8,128)(2,1)S(1)}, bf16[256,1280]{1,0:T(8,128)(2,1)S(1)}, u32[]{:S(2)}, u32[]{:S(2)}) %collective-permute-start.35) | collective-permute-done | bytes 655392 | tf_op jit(solution)/shard_map/ppermute | solution.py:24
  156.8 5.0 %shard_map.244 = (bf16[2,512,256]{2,1,0:T(8,128)(2,1)S(1)}, f32[2,512,128]{2,1,0:T(8,128)S(1)}) custom-call(s32[19]{0:T(128)S(1)} %copy-done.117, bf16[2,1024,768]{2,1,0:T(8,128)(2,1)S(1)} %shard_map.230.refs_4_.refs_1_, bf16[2,512,768]{2,1,0:T(8,128)(2,1)S(1)} %shard_map.243.refs_2_, bf16[256,1280]{1,0:T(8,128)(2,1)S(1)} %collective-permute-done.35.refs_3_.refs_8_.refs_7_, ...), custom_call_target="tpu_custom_call" | custom-call | flops 10737418 | bytes 57672 | tf_op jit(solution)/shard_map/pallas_call | solution.py:120
  166.2 5.8 %shard_map.246 = (bf16[2,512,256]{2,1,0:T(8,128)(2,1)S(1)}, f32[2,512,128]{2,1,0:T(8,128)S(1)}) custom-call(s32[19]{0:T(128)S(1)} %copy-done.117, bf16[2,1024,768]{2,1,0:T(8,128)(2,1)S(1)} %shard_map.230.refs_4_.refs_1_, bf16[2,512,768]{2,1,0:T(8,128)(2,1)S(1)} %shard_map.243.refs_2_, bf16[256,1024]{1,0:T(8,128)(2,1)S(1)} %collective-permute-done.33.refs_3_.refs_4_, ...), custom_call_target="tpu_custom_call" | custom-call | flops 12079595 | bytes 57672 | tf_op jit(solution)/shard_map/pallas_call | solution.py:120
  186.8 9.0 %shard_map.250 = (bf16[2,1024,1024]{2,1,0:T(8,128)(2,1)S(1)}, bf16[2,1024,1024]{2,1,0:T(8,128)(2,1)S(1)}) custom-call(bf16[512,1024]{1,0:T(8,128)(2,1)S(1)} %get-tuple-element.138.refs_0_, bf16[512,1024]{1,0:T(8,128)(2,1)S(1)} %collective-permute-done.42.refs_1_, bf16[256,1280]{1,0:T(8,128)(2,1)S(1)} %shard_map.231.refs_1_.refs_2_, ...), custom_call_target="tpu_custom_call" | custom-call | flops 42949672 | bytes 157286 | tf_op jit(solution)/shard_map/pallas_call | solution.py:120
  195.9 5.4 %shard_map.251 = (bf16[256,1024]{1,0:T(8,128)(2,1)S(1)}, bf16[512,1024]{1,0:T(8,128)(2,1)S(1)}, bf16[512,1024]{1,0:T(8,128)(2,1)S(1)}, bf16[512,1024]{1,0:T(8,128)(2,1)S(1)}, bf16[256,1024]{1,0:T(8,128)(2,1)S(1)}) custom-call(bf16[512,1024]{1,0:T(8,128)(2,1)S(1)} %shard_map.240.refs_10_.refs_0_.refs_6_, ...), custom_call_target="tpu_custom_call" | custom-call | flops 99999997952 | bytes 104857 | tf_op jit(solution)/shard_map/pallas_call | solution.py:120
  203.4 5.7 %shard_map.252.refs_0_.refs_2_ = bf16[2,1024,1024]{2,1,0:T(8,128)(2,1)S(1)} custom-call(bf16[512,1024]{1,0:T(8,128)(2,1)S(1)} %shard_map.240.refs_10_.refs_0_.refs_6_, bf16[512,1024]{1,0:T(8,128)(2,1)S(1)} %collective-permute-done.45.refs_1_, bf16[256,1024]{1,0:T(8,128)(2,1)S(1)} %shard_map.242.refs_10_.refs_2_.refs_1_, ...), custom_call_target="tpu_custom_call" | custom-call | flops 99999997952 | bytes 146800 | tf_op jit(solution)/shard_map/pallas_call | solution.py:120
  214.9 5.7 %shard_map.254 = (bf16[256,1024]{1,0:T(8,128)(2,1)S(1)}, bf16[512,1024]{1,0:T(8,128)(2,1)S(1)}, bf16[512,1024]{1,0:T(8,128)(2,1)S(1)}, bf16[512,1024]{1,0:T(8,128)(2,1)S(1)}, bf16[256,1024]{1,0:T(8,128)(2,1)S(1)}) custom-call(bf16[512,1024]{1,0:T(8,128)(2,1)S(1)} %copy-done.51, bf16[512,1024]{1,0:T(8,128)(2,1)S(1)} %copy-done.53, ...), custom_call_target="tpu_custom_call" | custom-call | flops 42949672 | bytes 104857 | tf_op jit(solution)/shard_map/pallas_call | solution.py:120
  230.6 11.3 %shard_map.259 = (bf16[2,512,256]{2,1,0:T(8,128)(2,1)S(1)}, bf16[2,512,512]{2,1,0:T(8,128)(2,1)S(1)}, bf16[2,512,512]{2,1,0:T(8,128)(2,1)S(1)}, bf16[2,512,512]{2,1,0:T(8,128)(2,1)S(1)}) custom-call(s32[19]{0:T(128)S(1)} %copy-done.118, bf16[2,1024,768]{2,1,0:T(8,128)(2,1)S(1)} %copy-done.3, bf16[2,512,768]{2,1,0:T(8,128)(2,1)S(1)} %copy-done.25, ...), custom_call_target="tpu_custom_call" | custom-call | flops 99999997952 | bytes 99615 | tf_op jit(solution)/shard_map/pallas_call | solution.py:120
  242.0 9.1 %shard_map.260 = (bf16[2,512,768]{2,1,0:T(8,128)(2,1)S(1)}, bf16[2,512,512]{2,1,0:T(8,128)(2,1)S(1)}) custom-call(s32[19]{0:T(128)S(1)} %copy-done.118, bf16[2,1024,768]{2,1,0:T(8,128)(2,1)S(1)} %copy-done.3, bf16[2,512,768]{2,1,0:T(8,128)(2,1)S(1)} %copy-done.25, f32[2,512,128]{2,1,0:T(8,128)S(1)} %copy-done.82, bf16[2,512,256]{2,1,0:T(8,128)(2,1)S(1)} %copy-done.47, ...), custom_call_target="tpu_custom_call" | custom-call | flops 26843544 | bytes 104858 | tf_op jit(solution)/shard_map/pallas_call | solution.py:120
  253.6 8.0 %shard_map.262 = (bf16[2,512,256]{2,1,0:T(8,128)(2,1)S(1)}, bf16[2,512,512]{2,1,0:T(8,128)(2,1)S(1)}, bf16[2,512,512]{2,1,0:T(8,128)(2,1)S(1)}) custom-call(s32[19]{0:T(128)S(1)} %copy-done.118, bf16[2,1024,768]{2,1,0:T(8,128)(2,1)S(1)} %copy-done.3, bf16[2,512,768]{2,1,0:T(8,128)(2,1)S(1)} %copy-done.27, f32[2,512,128]{2,1,0:T(8,128)S(1)} %copy-done.85, ...), custom_call_target="tpu_custom_call" | custom-call | flops 23488102 | bytes 89129 | tf_op jit(solution)/shard_map/pallas_call | solution.py:120
  278.0 9.4 %shard_map.269 = (bf16[2,512,768]{2,1,0:T(8,128)(2,1)S(1)}, bf16[2,512,512]{2,1,0:T(8,128)(2,1)S(1)}) custom-call(s32[19]{0:T(128)S(1)} %copy-done.118, bf16[2,1024,768]{2,1,0:T(8,128)(2,1)S(1)} %copy-done.3, bf16[2,512,768]{2,1,0:T(8,128)(2,1)S(1)} %copy-done.27, f32[2,512,128]{2,1,0:T(8,128)S(1)} %copy-done.115, ...), custom_call_target="tpu_custom_call" | custom-call | flops 99999997952 | bytes 115344 | tf_op jit(solution)/shard_map/pallas_call | solution.py:120
  289.4 9.9 %collective-permute-done.57.refs_1_ = bf16[256,768]{1,0:T(8,128)(2,1)S(1)} collective-permute-done((bf16[256,768]{1,0:T(8,128)(2,1)S(1)}, bf16[256,768]{1,0:T(8,128)(2,1)S(1)}, u32[]{:S(2)}, u32[]{:S(2)}) %collective-permute-start.57) | collective-permute-done | bytes 393248 | tf_op jit(solution)/shard_map/ppermute | solution.py:24
  311.2 5.6 %shard_map.276 = (bf16[256,1280]{1,0:T(8,128)(2,1)S(1)}, bf16[512,1280]{1,0:T(8,128)(2,1)S(1)}, bf16[512,1280]{1,0:T(8,128)(2,1)S(1)}, bf16[512,1280]{1,0:T(8,128)(2,1)S(1)}, bf16[256,1280]{1,0:T(8,128)(2,1)S(1)}) custom-call(bf16[512,1024]{1,0:T(8,128)(2,1)S(1)} %copy-done.21, bf16[512,1024]{1,0:T(8,128)(2,1)S(1)} %copy-done.33, ...), custom_call_target="tpu_custom_call" | custom-call | flops 53687092 | bytes 146800 | tf_op jit(solution)/shard_map/pallas_call | solution.py:120
  323.1 9.5 %collective-permute-done.66.refs_1_ = bf16[128,1024]{1,0:T(8,128)(2,1)S(1)} collective-permute-done((bf16[128,1024]{1,0:T(8,128)(2,1)S(1)}, bf16[128,1024]{1,0:T(8,128)(2,1)S(1)}, u32[]{:S(2)}, u32[]{:S(2)}) %collective-permute-start.66) | collective-permute-done | bytes 262176 | tf_op jit(solution)/shard_map/ppermute | solution.py:28
  333.4 7.1 %collective-permute-done.65.refs_1_ = bf16[256,1280]{1,0:T(8,128)(2,1)S(1)} collective-permute-done((bf16[256,1280]{1,0:T(8,128)(2,1)S(1)}, bf16[256,1280]{1,0:T(8,128)(2,1)S(1)}, u32[]{:S(2)}, u32[]{:S(2)}) %collective-permute-start.65) | collective-permute-done | bytes 655392 | tf_op jit(solution)/shard_map/ppermute | solution.py:24
  354.5 8.9 %collective-permute-done.74.refs_1_ = bf16[256,1024]{1,0:T(8,128)(2,1)S(1)} collective-permute-done((bf16[256,1024]{1,0:T(8,128)(2,1)S(1)}, bf16[256,1024]{1,0:T(8,128)(2,1)S(1)}, u32[]{:S(2)}, u32[]{:S(2)}) %collective-permute-start.74) | collective-permute-done | bytes 524320 | tf_op jit(solution)/shard_map/ppermute | solution.py:28
  369.7 9.1 %collective-permute-done.78.refs_1_ = bf16[256,768]{1,0:T(8,128)(2,1)S(1)} collective-permute-done((bf16[256,768]{1,0:T(8,128)(2,1)S(1)}, bf16[256,768]{1,0:T(8,128)(2,1)S(1)}, u32[]{:S(2)}, u32[]{:S(2)}) %collective-permute-start.78) | collective-permute-done | bytes 393248 | tf_op jit(solution)/shard_map/ppermute | solution.py:28
  393.3 7.4 %collective-permute-done.87.refs_3_ = bf16[256,1024]{1,0:T(8,128)(2,1)S(1)} collective-permute-done((bf16[256,1024]{1,0:T(8,128)(2,1)S(1)}, bf16[256,1024]{1,0:T(8,128)(2,1)S(1)}, u32[]{:S(2)}, u32[]{:S(2)}) %collective-permute-start.87) | collective-permute-done | bytes 524320 | tf_op jit(solution)/shard_map/ppermute | solution.py:24
  (543 shorter events, 241.8 us)
Async XLA Ops:
  8.4 24.0 %collective-permute-start = (bf16[256,1024]{1,0:T(8,128)(2,1)}, bf16[256,1024]{1,0:T(8,128)(2,1)}, u32[]{:S(2)}, u32[]{:S(2)}) collective-permute-start(bf16[256,1024]{1,0:T(8,128)(2,1)} %get-tuple-element.254), channel_id=1, source_target_pairs={{0,2},{2,0},{1,3},{3,1},{4,6},{6,4},{5,7},{7,5},{8,10},{10,8},{9,1... | collective-permute-start | bytes 1572872 | tf_op jit(solution)/shard_map/ppermute | solution.py:24
  40.0 35.9 %collective-permute-start.7 = (bf16[512,1024]{1,0:T(8,128)(2,1)S(1)}, bf16[512,1024]{1,0:T(8,128)(2,1)S(1)}, u32[]{:S(2)}, u32[]{:S(2)}) collective-permute-start(bf16[512,1024]{1,0:T(8,128)(2,1)S(1)} %shard_map.226.refs_3_.refs_0_.refs_4_), channel_id=1, source_target_pairs={{0,1},{1,0},{2,3},{3,2},{4,5},{5,4},{6,7},{7,6},{8,9},{9,8},{10,11... | collective-permute-start | bytes 3145736 | tf_op jit(solution)/shard_map/ppermute | solution.py:24
  63.0 24.1 %collective-permute-start.16 = (bf16[256,1024]{1,0:T(8,128)(2,1)S(1)}, bf16[256,1024]{1,0:T(8,128)(2,1)S(1)}, u32[]{:S(2)}, u32[]{:S(2)}) collective-permute-start(bf16[256,1024]{1,0:T(8,128)(2,1)S(1)} %shard_map.228.refs_2_.refs_1_), channel_id=1, source_target_pairs={{0,4},{4,0},{1,5},{5,1},{2,6},{6,2},{3,7},{7,3},{8,12},{12,8},{9,1... | collective-permute-start | bytes 1572872 | tf_op jit(solution)/shard_map/ppermute | solution.py:24
  76.0 22.4 %collective-permute-start.17 = (bf16[256,1024]{1,0:T(8,128)(2,1)S(1)}, bf16[256,1024]{1,0:T(8,128)(2,1)S(1)}, u32[]{:S(2)}, u32[]{:S(2)}) collective-permute-start(bf16[256,1024]{1,0:T(8,128)(2,1)S(1)} %collective-permute-done.15.refs_3_.refs_2_), channel_id=1, source_target_pairs={{0,4},{4,0},{1,5},{5,1},{2,6},{6,2},{3,7},{7,3},{8,12},{12,8},{9,1... | collective-permute-start | bytes 1572872 | tf_op jit(solution)/shard_map/ppermute | solution.py:24
  93.4 30.2 %collective-permute-start.26 = (bf16[256,1280]{1,0:T(8,128)(2,1)S(1)}, bf16[256,1280]{1,0:T(8,128)(2,1)S(1)}, u32[]{:S(2)}, u32[]{:S(2)}) collective-permute-start(bf16[256,1280]{1,0:T(8,128)(2,1)S(1)} %shard_map.231.refs_1_.refs_2_), channel_id=1, source_target_pairs={{0,4},{4,0},{1,5},{5,1},{2,6},{6,2},{3,7},{7,3},{8,12},{12,8},{9,1... | collective-permute-start | bytes 1966088 | tf_op jit(solution)/shard_map/ppermute | solution.py:24
  98.4 25.3 %collective-permute-start.27 = (bf16[256,1280]{1,0:T(8,128)(2,1)S(1)}, bf16[256,1280]{1,0:T(8,128)(2,1)S(1)}, u32[]{:S(2)}, u32[]{:S(2)}) collective-permute-start(bf16[256,1280]{1,0:T(8,128)(2,1)S(1)} %shard_map.231.refs_1_.refs_2_), channel_id=1, source_target_pairs={{0,2},{2,0},{1,3},{3,1},{4,6},{6,4},{5,7},{7,5},{8,10},{10,8},{9,1... | collective-permute-start | bytes 1966088 | tf_op jit(solution)/shard_map/ppermute | solution.py:24
  103.7 32.8 %collective-permute-start.24 = (bf16[256,1280]{1,0:T(8,128)(2,1)S(1)}, bf16[256,1280]{1,0:T(8,128)(2,1)S(1)}, u32[]{:S(2)}, u32[]{:S(2)}) collective-permute-start(bf16[256,1280]{1,0:T(8,128)(2,1)S(1)} %collective-permute-done.23.refs_10_.refs_3_.refs_2_), channel_id=1, source_target_pairs={{0,4},{4,0},{1,5},{5,1},{2,6},{6,2},{3,7},{7,3},{8,12},{12,8},{9,1... | collective-permute-start | bytes 1966088 | tf_op jit(solution)/shard_map/ppermute | solution.py:24
  109.6 27.4 %collective-permute-start.25 = (bf16[256,1280]{1,0:T(8,128)(2,1)S(1)}, bf16[256,1280]{1,0:T(8,128)(2,1)S(1)}, u32[]{:S(2)}, u32[]{:S(2)}) collective-permute-start(bf16[256,1280]{1,0:T(8,128)(2,1)S(1)} %collective-permute-done.23.refs_10_.refs_3_.refs_2_), channel_id=1, source_target_pairs={{0,2},{2,0},{1,3},{3,1},{4,6},{6,4},{5,7},{7,5},{8,10},{10,8},{9,1... | collective-permute-start | bytes 1966088 | tf_op jit(solution)/shard_map/ppermute | solution.py:24
  223.7 37.9 %collective-permute-start.55 = (bf16[256,1024]{1,0:T(8,128)(2,1)S(1)}, bf16[256,1024]{1,0:T(8,128)(2,1)S(1)}, u32[]{:S(2)}, u32[]{:S(2)}) collective-permute-start(bf16[256,1024]{1,0:T(8,128)(2,1)S(1)} %get-tuple-element.148.refs_2_), channel_id=1, source_target_pairs={{0,2},{2,0},{1,3},{3,1},{4,6},{6,4},{5,7},{7,5},{8,10},{10,8},{9,1... | collective-permute-start | bytes 1572872 | tf_op jit(solution)/shard_map/ppermute | solution.py:24
  224.4 37.7 %collective-permute-start.54 = (bf16[256,1024]{1,0:T(8,128)(2,1)S(1)}, bf16[256,1024]{1,0:T(8,128)(2,1)S(1)}, u32[]{:S(2)}, u32[]{:S(2)}) collective-permute-start(bf16[256,1024]{1,0:T(8,128)(2,1)S(1)} %get-tuple-element.162), channel_id=1, source_target_pairs={{0,4},{4,0},{1,5},{5,1},{2,6},{6,2},{3,7},{7,3},{8,12},{12,8},{9,1... | collective-permute-start | bytes 1572872 | tf_op jit(solution)/shard_map/ppermute | solution.py:24
  225.8 36.7 %collective-permute-start.53 = (bf16[512,1024]{1,0:T(8,128)(2,1)S(1)}, bf16[512,1024]{1,0:T(8,128)(2,1)S(1)}, u32[]{:S(2)}, u32[]{:S(2)}) collective-permute-start(bf16[512,1024]{1,0:T(8,128)(2,1)S(1)} %shard_map.256.refs_7_), channel_id=1, source_target_pairs={{0,2},{2,0},{1,3},{3,1},{4,6},{6,4},{5,7},{7,5},{8,10},{10,8},{9,1... | collective-permute-start | bytes 3145736 | tf_op jit(solution)/shard_map/ppermute | solution.py:24
  226.3 36.2 %collective-permute-start.52 = (bf16[512,1024]{1,0:T(8,128)(2,1)S(1)}, bf16[512,1024]{1,0:T(8,128)(2,1)S(1)}, u32[]{:S(2)}, u32[]{:S(2)}) collective-permute-start(bf16[512,1024]{1,0:T(8,128)(2,1)S(1)} %shard_map.255.refs_2_), channel_id=1, source_target_pairs={{0,4},{4,0},{1,5},{5,1},{2,6},{6,2},{3,7},{7,3},{8,12},{12,8},{9,1... | collective-permute-start | bytes 3145736 | tf_op jit(solution)/shard_map/ppermute | solution.py:24
  265.4 39.8 %collective-permute-start.68 = (bf16[512,1024]{1,0:T(8,128)(2,1)S(1)}, bf16[512,1024]{1,0:T(8,128)(2,1)S(1)}, u32[]{:S(2)}, u32[]{:S(2)}) collective-permute-start(bf16[512,1024]{1,0:T(8,128)(2,1)S(1)} %shard_map.264.refs_3_), channel_id=1, source_target_pairs={{0,2},{2,0},{1,3},{3,1},{4,6},{6,4},{5,7},{7,5},{8,10},{10,8},{9,1... | collective-permute-start | bytes 3145736 | tf_op jit(solution)/shard_map/ppermute | solution.py:24
  266.0 50.8 %collective-permute-start.67 = (bf16[512,1024]{1,0:T(8,128)(2,1)S(1)}, bf16[512,1024]{1,0:T(8,128)(2,1)S(1)}, u32[]{:S(2)}, u32[]{:S(2)}) collective-permute-start(bf16[512,1024]{1,0:T(8,128)(2,1)S(1)} %shard_map.263.refs_2_), channel_id=1, source_target_pairs={{0,4},{4,0},{1,5},{5,1},{2,6},{6,2},{3,7},{7,3},{8,12},{12,8},{9,1... | collective-permute-start | bytes 3145736 | tf_op jit(solution)/shard_map/ppermute | solution.py:24
  267.5 21.8 %collective-permute-start.58 = (bf16[256,1024]{1,0:T(8,128)(2,1)S(1)}, bf16[256,1024]{1,0:T(8,128)(2,1)S(1)}, u32[]{:S(2)}, u32[]{:S(2)}) collective-permute-start(bf16[256,1024]{1,0:T(8,128)(2,1)S(1)} %get-tuple-element.170), channel_id=1, source_target_pairs={{0,8},{8,0},{16,24},{24,16},{1,9},{9,1},{17,25},{25,17},{2,10},{10... | collective-permute-start | bytes 1572872 | tf_op jit(solution)/shard_map/ppermute | solution.py:28
  274.8 24.5 %collective-permute-start.57 = (bf16[256,768]{1,0:T(8,128)(2,1)S(1)}, bf16[256,768]{1,0:T(8,128)(2,1)S(1)}, u32[]{:S(2)}, u32[]{:S(2)}) collective-permute-start(bf16[256,768]{1,0:T(8,128)(2,1)S(1)} %get-tuple-element.169.refs_8_), channel_id=1, source_target_pairs={{0,2},{2,0},{1,3},{3,1},{4,6},{6,4},{5,7},{7,5},{8,10},{10,8},{9,1... | collective-permute-start | bytes 1179656 | tf_op jit(solution)/shard_map/ppermute | solution.py:24
  275.4 24.3 %collective-permute-start.60 = (bf16[256,768]{1,0:T(8,128)(2,1)S(1)}, bf16[256,768]{1,0:T(8,128)(2,1)S(1)}, u32[]{:S(2)}, u32[]{:S(2)}) collective-permute-start(bf16[256,768]{1,0:T(8,128)(2,1)S(1)} %get-tuple-element.179), channel_id=1, source_target_pairs={{0,4},{4,0},{1,5},{5,1},{2,6},{6,2},{3,7},{7,3},{8,12},{12,8},{9,1... | collective-permute-start | bytes 1179656 | tf_op jit(solution)/shard_map/ppermute | solution.py:24
  306.9 33.6 %collective-permute-start.61 = (bf16[512,768]{1,0:T(8,128)(2,1)S(1)}, bf16[512,768]{1,0:T(8,128)(2,1)S(1)}, u32[]{:S(2)}, u32[]{:S(2)}) collective-permute-start(bf16[512,768]{1,0:T(8,128)(2,1)S(1)} %shard_map.273.refs_12_), channel_id=1, source_target_pairs={{0,2},{2,0},{1,3},{3,1},{4,6},{6,4},{5,7},{7,5},{8,10},{10,8},{9,1... | collective-permute-start | bytes 2359304 | tf_op jit(solution)/shard_map/ppermute | solution.py:24
  307.5 33.0 %collective-permute-start.59 = (bf16[512,768]{1,0:T(8,128)(2,1)S(1)}, bf16[512,768]{1,0:T(8,128)(2,1)S(1)}, u32[]{:S(2)}, u32[]{:S(2)}) collective-permute-start(bf16[512,768]{1,0:T(8,128)(2,1)S(1)} %shard_map.272.refs_2_), channel_id=1, source_target_pairs={{0,4},{4,0},{1,5},{5,1},{2,6},{6,2},{3,7},{7,3},{8,12},{12,8},{9,1... | collective-permute-start | bytes 2359304 | tf_op jit(solution)/shard_map/ppermute | solution.py:24
  316.8 23.7 %collective-permute-start.65 = (bf16[256,1280]{1,0:T(8,128)(2,1)S(1)}, bf16[256,1280]{1,0:T(8,128)(2,1)S(1)}, u32[]{:S(2)}, u32[]{:S(2)}) collective-permute-start(bf16[256,1280]{1,0:T(8,128)(2,1)S(1)} %get-tuple-element.189.refs_7_), channel_id=1, source_target_pairs={{0,2},{2,0},{1,3},{3,1},{4,6},{6,4},{5,7},{7,5},{8,10},{10,8},{9,1... | collective-permute-start | bytes 1966088 | tf_op jit(solution)/shard_map/ppermute | solution.py:24
  317.4 24.7 %collective-permute-start.64 = (bf16[256,1280]{1,0:T(8,128)(2,1)S(1)}, bf16[256,1280]{1,0:T(8,128)(2,1)S(1)}, u32[]{:S(2)}, u32[]{:S(2)}) collective-permute-start(bf16[256,1280]{1,0:T(8,128)(2,1)S(1)} %get-tuple-element.187), channel_id=1, source_target_pairs={{0,4},{4,0},{1,5},{5,1},{2,6},{6,2},{3,7},{7,3},{8,12},{12,8},{9,1... | collective-permute-start | bytes 1966088 | tf_op jit(solution)/shard_map/ppermute | solution.py:24
  342.7 42.1 %collective-permute-start.81 = (bf16[512,1280]{1,0:T(8,128)(2,1)S(1)}, bf16[512,1280]{1,0:T(8,128)(2,1)S(1)}, u32[]{:S(2)}, u32[]{:S(2)}) collective-permute-start(bf16[512,1280]{1,0:T(8,128)(2,1)S(1)} %shard_map.282.refs_3_), channel_id=1, source_target_pairs={{0,2},{2,0},{1,3},{3,1},{4,6},{6,4},{5,7},{7,5},{8,10},{10,8},{9,1... | collective-permute-start | bytes 3932168 | tf_op jit(solution)/shard_map/ppermute | solution.py:24
  343.4 41.3 %collective-permute-start.80 = (bf16[512,1280]{1,0:T(8,128)(2,1)S(1)}, bf16[512,1280]{1,0:T(8,128)(2,1)S(1)}, u32[]{:S(2)}, u32[]{:S(2)}) collective-permute-start(bf16[512,1280]{1,0:T(8,128)(2,1)S(1)} %shard_map.281.refs_4_), channel_id=1, source_target_pairs={{0,4},{4,0},{1,5},{5,1},{2,6},{6,2},{3,7},{7,3},{8,12},{12,8},{9,1... | collective-permute-start | bytes 3932168 | tf_op jit(solution)/shard_map/ppermute | solution.py:24
  392.7 20.3 %collective-permute-start.75 = (bf16[256,1024]{1,0:T(8,128)(2,1)S(1)}, bf16[256,1024]{1,0:T(8,128)(2,1)S(1)}, u32[]{:S(2)}, u32[]{:S(2)}) collective-permute-start(bf16[256,1024]{1,0:T(8,128)(2,1)S(1)} %get-tuple-element.210), channel_id=1, source_target_pairs={{0,2},{2,0},{1,3},{3,1},{4,6},{6,4},{5,7},{7,5},{8,10},{10,8},{9,1... | collective-permute-start | bytes 1572872 | tf_op jit(solution)/shard_map/ppermute | solution.py:24
  (208 other events, 3193.1 us)
